TPU v7x, 1024 devices: a whole 4x4x32 slice. The times are simulated.
1024 devices in a mesh: blk: 64 (over z_lo, x, core), group: 16 (over y, z_hi).
Axes of the slice: x: 4, y: 4, z: 32 (z_hi: 4, z_lo: 8; z = z_hi * 8 + z_lo), core: 2. Of those that a mesh axis runs over, the one named last changes fastest.
Arguments:
- image_feats: bfloat16 [131072, 1152], P(('blk', 'group')), may hold values from -0.19921875 to 0.19921875
- text_feats: bfloat16 [131072, 1152], P(('blk', 'group')), may hold values from -0.19921875 to 0.19921875
- positive: int32 [1024, 128], P(('blk', 'group')), may hold values from 0 to 127, each once within a row
- scale: float32 [1], replicated, may hold values from 5 to 20
- bias: float32 [1], replicated, may hold values from -4 to -1
Outputs:
- loss_rows: float32 [131072], P(('blk', 'group'))
- image_grad: float32 [131072, 1152], P(('blk', 'group'))
- text_grad: float32 [131072, 1152], P(('blk', 'group'))
Inputs may be any that keep to these rules, and one draw needn't show every extreme that they name: Each row of positive is a permutation of 0 to 127.
All inputs are finite; a program needn't handle non-finite values.
Results may differ from a plain program's by a relative error of at most 0.0041.
Values may be sent and summed in bfloat16 or wider, within the bound.
No kernel may reach another device: no remote copies, remote signals or barrier semaphores. Data moves between devices by JAX's collectives and lax.ppermute only.
A program may use at most 32 MiB of HBM per device.

v0:
```python
import jax
import jax.numpy as jnp
from jax import lax
from jax.sharding import PartitionSpec as P

SPAN = 8


def passed_along(x, axis, by):
    size = lax.axis_size(axis)
    return lax.ppermute(x, axis, [(i, (i + by) % size) for i in range(size)])


def normalize(values):
    floats = values.astype(jnp.float32)
    inverse = lax.rsqrt(jnp.sum(floats * floats, axis=-1, keepdims=True) + 1e-06)
    return (floats * inverse, inverse)


def pair_terms(logit, sign):
    return (jax.nn.softplus(-sign * logit), -sign * jax.nn.sigmoid(-sign * logit))


def by_rows(left, right):
    return lax.dot_general(
        left, right, (((1,), (1,)), ((), ())), preferred_element_type=jnp.float32
    )


def by_cols(left, right):
    return lax.dot_general(
        left, right, (((0,), (0,)), ((), ())), preferred_element_type=jnp.float32
    )


def local(image_feats, text_feats, positive, scale, bias):
    tau = scale[0]
    offset = bias[0]
    rows = image_feats.shape[0]
    x_norm, x_inv = normalize(image_feats)
    y_norm, y_inv = normalize(text_feats)
    x_half = x_norm.astype(jnp.bfloat16)
    y_half = y_norm.astype(jnp.bfloat16)
    blocks = [y_half]
    current = y_half
    for step in range(1, SPAN):
        current = passed_along(current, "blk", 1)
        blocks.append(current)
    inner = jnp.concatenate(blocks, axis=0)
    outer = passed_along(y_half, "group", 1)
    window = jnp.concatenate([inner, outer], axis=0)
    width = window.shape[0]
    equal = positive[0][:, None] == jnp.arange(rows, dtype=jnp.int32)[None, :]
    own_sign = jnp.where(equal, 1.0, -1.0).astype(jnp.float32)
    sign = jnp.concatenate([own_sign, -jnp.ones((rows, width - rows), jnp.float32)], axis=1)
    logit = tau * by_rows(x_half, window) + offset
    loss, slope = pair_terms(logit, sign)
    loss_rows = jnp.sum(loss, axis=-1) / jnp.float32(width)
    slope_half = slope.astype(jnp.bfloat16)
    grad_x = tau * jnp.dot(slope_half, window, preferred_element_type=jnp.float32)
    terms = by_cols(slope_half, x_half)
    inner_terms = terms[: SPAN * rows].reshape(SPAN, rows, terms.shape[1])
    outer_terms = terms[SPAN * rows :]
    total = inner_terms[SPAN - 1]
    for step in range(SPAN - 1, 0, -1):
        total = passed_along(total, "blk", -1) + inner_terms[step - 1]
    total = total + passed_along(outer_terms, "group", -1)
    grad_y = tau * total
    image_grad = (grad_x - x_norm * jnp.sum(x_norm * grad_x, axis=-1, keepdims=True)) * x_inv
    text_grad = (grad_y - y_norm * jnp.sum(y_norm * grad_y, axis=-1, keepdims=True)) * y_inv
    return (loss_rows, image_grad, text_grad)


def solution(mesh):
    placed = (
        P(("blk", "group"), None),
        P(("blk", "group"), None),
        P(("blk", "group"), None),
        P(),
        P(),
    )
    return jax.shard_map(
        local,
        mesh=mesh,
        in_specs=placed,
        out_specs=(P(("blk", "group")), P(("blk", "group"), None), P(("blk", "group"), None)),
        check_vma=False,
    )
```

profile of v0, /device:TPU:144, one launch (start us, length us, event | category | flops | bytes accessed | tf_op | source)
XLA Modules:
  0.0 334.9 jit_solution(3903314067805163957)
XLA Ops:
  0.6 1.1 fusion.15
  1.7 1.1 constant_dynamic-update-slice_fusion.8
  2.8 0.0 copy-start.1
  2.8 2.1 collective-permute-start
  4.9 9.4 %collective-permute-done = bf16[128,1152]{1,0:T(8,128)(2,1)S(1)} collective-permute-done((bf16[128,1152]{1,0:T(8,128)(2,1)S(1)}, bf16[128,1152]{1,0:T(8,128)(2,1)S(1)}, u32[]{:S(2)}, u32[]{:S(2)}) %collective-permute-start) | collective-permute-done | bytes 294944 | tf_op jit(solution)/shard_map/ppermute | solution.py:11
  14.3 1.9 collective-permute-start.1
  16.3 9.4 %collective-permute-done.1 = bf16[128,1152]{1,0:T(8,128)(2,1)S(1)} collective-permute-done((bf16[128,1152]{1,0:T(8,128)(2,1)S(1)}, bf16[128,1152]{1,0:T(8,128)(2,1)S(1)}, u32[]{:S(2)}, u32[]{:S(2)}) %collective-permute-start.1) | collective-permute-done | bytes 294944 | tf_op jit(solution)/shard_map/ppermute | solution.py:11
  25.7 1.9 collective-permute-start.2
  27.6 15.7 %collective-permute-start.7 = (bf16[128,1152]{1,0:T(8,128)(2,1)S(1)}, bf16[128,1152]{1,0:T(8,128)(2,1)S(1)}, u32[]{:S(2)}, u32[]{:S(2)}) collective-permute-start(bf16[128,1152]{1,0:T(8,128)(2,1)S(1)} %get-tuple-element.6), channel_id=1, source_target_pairs={{0,1},{1,2},{2,3},{3,4},{4,5},{5,6},{6,7},{7,8},{8,9},{9,10},{10,1... | collective-permute-start | bytes 884744 | tf_op jit(solution)/shard_map/ppermute | solution.py:11
  43.3 1.1 fusion.11
  44.4 1.9 collective-permute-start.3
  47.7 0.7 fusion.22
  48.4 46.0 %collective-permute-done.3 = bf16[128,1152]{1,0:T(8,128)(2,1)S(1)} collective-permute-done((bf16[128,1152]{1,0:T(8,128)(2,1)S(1)}, bf16[128,1152]{1,0:T(8,128)(2,1)S(1)}, u32[]{:S(2)}, u32[]{:S(2)}) %collective-permute-start.3) | collective-permute-done | bytes 294944 | tf_op jit(solution)/shard_map/ppermute | solution.py:11
  94.5 1.9 collective-permute-start.4
  96.5 9.4 %collective-permute-done.4 = bf16[128,1152]{1,0:T(8,128)(2,1)S(1)} collective-permute-done((bf16[128,1152]{1,0:T(8,128)(2,1)S(1)}, bf16[128,1152]{1,0:T(8,128)(2,1)S(1)}, u32[]{:S(2)}, u32[]{:S(2)}) %collective-permute-start.4) | collective-permute-done | bytes 294944 | tf_op jit(solution)/shard_map/ppermute | solution.py:11
  105.8 1.9 collective-permute-start.5
  107.8 9.4 %collective-permute-done.5 = bf16[128,1152]{1,0:T(8,128)(2,1)S(1)} collective-permute-done((bf16[128,1152]{1,0:T(8,128)(2,1)S(1)}, bf16[128,1152]{1,0:T(8,128)(2,1)S(1)}, u32[]{:S(2)}, u32[]{:S(2)}) %collective-permute-start.5) | collective-permute-done | bytes 294944 | tf_op jit(solution)/shard_map/ppermute | solution.py:11
  117.2 1.9 collective-permute-start.6
  119.2 9.4 %collective-permute-done.6 = bf16[128,1152]{1,0:T(8,128)(2,1)S(1)} collective-permute-done((bf16[128,1152]{1,0:T(8,128)(2,1)S(1)}, bf16[128,1152]{1,0:T(8,128)(2,1)S(1)}, u32[]{:S(2)}, u32[]{:S(2)}) %collective-permute-start.6) | collective-permute-done | bytes 294944 | tf_op jit(solution)/shard_map/ppermute | solution.py:11
  128.6 1.1 fusion.16
  129.7 0.9 fusion.19
  130.7 1.9 collective-permute-start.8
  132.7 7.4 %collective-permute-done.8 = f32[128,1152]{1,0:T(8,128)S(1)} collective-permute-done((f32[128,1152]{1,0:T(8,128)S(1)}, f32[128,1152]{1,0:T(8,128)S(1)}, u32[]{:S(2)}, u32[]{:S(2)}) %collective-permute-start.8) | collective-permute-done | bytes 589856 | tf_op jit(solution)/shard_map/ppermute | solution.py:11
  140.0 0.1 slice_add_fusion.6
  140.1 7.1 %collective-permute-start.9 = (f32[128,1152]{1,0:T(8,128)S(1)}, f32[128,1152]{1,0:T(8,128)S(1)}, u32[]{:S(2)}, u32[]{:S(2)}) collective-permute-start(f32[128,1152]{1,0:T(8,128)S(1)} %slice_add_fusion.6), channel_id=1, source_target_pairs={{0,1008},{16,0},{32,16},{48,32},{64,48},{80,64},{96,80},{112,96},{... | collective-permute-start | bytes 1769480 | tf_op jit(solution)/shard_map/ppermute | solution.py:11
  147.3 7.4 %collective-permute-done.9 = f32[128,1152]{1,0:T(8,128)S(1)} collective-permute-done((f32[128,1152]{1,0:T(8,128)S(1)}, f32[128,1152]{1,0:T(8,128)S(1)}, u32[]{:S(2)}, u32[]{:S(2)}) %collective-permute-start.9) | collective-permute-done | bytes 589856 | tf_op jit(solution)/shard_map/ppermute | solution.py:11
  154.6 0.1 slice_add_fusion.5
  154.7 7.1 %collective-permute-start.10 = (f32[128,1152]{1,0:T(8,128)S(1)}, f32[128,1152]{1,0:T(8,128)S(1)}, u32[]{:S(2)}, u32[]{:S(2)}) collective-permute-start(f32[128,1152]{1,0:T(8,128)S(1)} %slice_add_fusion.5), channel_id=1, source_target_pairs={{0,1008},{16,0},{32,16},{48,32},{64,48},{80,64},{96,80},{112,96},{... | collective-permute-start | bytes 1769480 | tf_op jit(solution)/shard_map/ppermute | solution.py:11
  161.9 7.4 %collective-permute-done.10 = f32[128,1152]{1,0:T(8,128)S(1)} collective-permute-done((f32[128,1152]{1,0:T(8,128)S(1)}, f32[128,1152]{1,0:T(8,128)S(1)}, u32[]{:S(2)}, u32[]{:S(2)}) %collective-permute-start.10) | collective-permute-done | bytes 589856 | tf_op jit(solution)/shard_map/ppermute | solution.py:11
  169.2 0.1 slice_add_fusion.4
  169.3 7.1 %collective-permute-start.11 = (f32[128,1152]{1,0:T(8,128)S(1)}, f32[128,1152]{1,0:T(8,128)S(1)}, u32[]{:S(2)}, u32[]{:S(2)}) collective-permute-start(f32[128,1152]{1,0:T(8,128)S(1)} %slice_add_fusion.4), channel_id=1, source_target_pairs={{0,1008},{16,0},{32,16},{48,32},{64,48},{80,64},{96,80},{112,96},{... | collective-permute-start | bytes 1769480 | tf_op jit(solution)/shard_map/ppermute | solution.py:11
  176.5 7.4 %collective-permute-done.11 = f32[128,1152]{1,0:T(8,128)S(1)} collective-permute-done((f32[128,1152]{1,0:T(8,128)S(1)}, f32[128,1152]{1,0:T(8,128)S(1)}, u32[]{:S(2)}, u32[]{:S(2)}) %collective-permute-start.11) | collective-permute-done | bytes 589856 | tf_op jit(solution)/shard_map/ppermute | solution.py:11
  183.9 0.1 slice_add_fusion.3
  183.9 7.1 %collective-permute-start.12 = (f32[128,1152]{1,0:T(8,128)S(1)}, f32[128,1152]{1,0:T(8,128)S(1)}, u32[]{:S(2)}, u32[]{:S(2)}) collective-permute-start(f32[128,1152]{1,0:T(8,128)S(1)} %slice_add_fusion.3), channel_id=1, source_target_pairs={{0,1008},{16,0},{32,16},{48,32},{64,48},{80,64},{96,80},{112,96},{... | collective-permute-start | bytes 1769480 | tf_op jit(solution)/shard_map/ppermute | solution.py:11
  191.1 7.4 %collective-permute-done.12 = f32[128,1152]{1,0:T(8,128)S(1)} collective-permute-done((f32[128,1152]{1,0:T(8,128)S(1)}, f32[128,1152]{1,0:T(8,128)S(1)}, u32[]{:S(2)}, u32[]{:S(2)}) %collective-permute-start.12) | collective-permute-done | bytes 589856 | tf_op jit(solution)/shard_map/ppermute | solution.py:11
  198.5 0.1 slice_add_fusion.2
  198.5 7.1 %collective-permute-start.13 = (f32[128,1152]{1,0:T(8,128)S(1)}, f32[128,1152]{1,0:T(8,128)S(1)}, u32[]{:S(2)}, u32[]{:S(2)}) collective-permute-start(f32[128,1152]{1,0:T(8,128)S(1)} %slice_add_fusion.2), channel_id=1, source_target_pairs={{0,1008},{16,0},{32,16},{48,32},{64,48},{80,64},{96,80},{112,96},{... | collective-permute-start | bytes 1769480 | tf_op jit(solution)/shard_map/ppermute | solution.py:11
  205.7 0.7 fusion.8
  206.4 6.6 %collective-permute-done.13 = f32[128,1152]{1,0:T(8,128)S(1)} collective-permute-done((f32[128,1152]{1,0:T(8,128)S(1)}, f32[128,1152]{1,0:T(8,128)S(1)}, u32[]{:S(2)}, u32[]{:S(2)}) %collective-permute-start.13) | collective-permute-done | bytes 589856 | tf_op jit(solution)/shard_map/ppermute | solution.py:11
  213.1 0.1 slice_add_fusion.1
  213.2 7.1 %collective-permute-start.14 = (f32[128,1152]{1,0:T(8,128)S(1)}, f32[128,1152]{1,0:T(8,128)S(1)}, u32[]{:S(2)}, u32[]{:S(2)}) collective-permute-start(f32[128,1152]{1,0:T(8,128)S(1)} %get-tuple-element.7), channel_id=1, source_target_pairs={{0,1008},{16,0},{32,16},{48,32},{64,48},{80,64},{96,80},{112,96},{... | collective-permute-start | bytes 1769480 | tf_op jit(solution)/shard_map/ppermute | solution.py:11
  220.3 52.6 %collective-permute-start.15 = (f32[128,1152]{1,0:T(8,128)S(1)}, f32[128,1152]{1,0:T(8,128)S(1)}, u32[]{:S(2)}, u32[]{:S(2)}) collective-permute-start(f32[128,1152]{1,0:T(8,128)S(1)} %get-tuple-element.8), channel_id=1, source_target_pairs={{0,15},{1,0},{2,1},{3,2},{4,3},{5,4},{6,5},{7,6},{8,7},{9,8},{10,9... | collective-permute-start | bytes 1769480 | tf_op jit(solution)/shard_map/ppermute | solution.py:11
  272.9 0.5 broadcast_multiply_fusion
  273.4 1.0 fusion.10
  274.4 42.1 %collective-permute-done.14 = f32[128,1152]{1,0:T(8,128)S(1)} collective-permute-done((f32[128,1152]{1,0:T(8,128)S(1)}, f32[128,1152]{1,0:T(8,128)S(1)}, u32[]{:S(2)}, u32[]{:S(2)}) %collective-permute-start.14) | collective-permute-done | bytes 589856 | tf_op jit(solution)/shard_map/ppermute | solution.py:11
  316.5 17.1 %collective-permute-done.15 = f32[128,1152]{1,0:T(8,128)S(1)} collective-permute-done((f32[128,1152]{1,0:T(8,128)S(1)}, f32[128,1152]{1,0:T(8,128)S(1)}, u32[]{:S(2)}, u32[]{:S(2)}) %collective-permute-start.15) | collective-permute-done | bytes 589856 | tf_op jit(solution)/shard_map/ppermute | solution.py:11
  333.6 0.3 fusion.12
  333.8 1.0 fusion.14
  (16 shorter events, 0.3 us)
Async XLA Ops:
  2.8 125.8 %copy-start.1 = (bf16[128,1152]{1,0:T(8,128)(2,1)S(1)}, bf16[128,1152]{1,0:T(8,128)(2,1)}, u32[]{:S(2)}) copy-start(bf16[128,1152]{1,0:T(8,128)(2,1)} %param.5) | copy-start | bytes 884740
  2.8 11.5 %collective-permute-start = (bf16[128,1152]{1,0:T(8,128)(2,1)S(1)}, bf16[128,1152]{1,0:T(8,128)(2,1)S(1)}, u32[]{:S(2)}, u32[]{:S(2)}) collective-permute-start(bf16[128,1152]{1,0:T(8,128)(2,1)S(1)} %get-tuple-element.6), channel_id=1, source_target_pairs={{0,16},{16,32},{32,48},{48,64},{64,80},{80,96},{96,112},{112,128},... | collective-permute-start | bytes 884744 | tf_op jit(solution)/shard_map/ppermute | solution.py:11
  14.3 11.4 %collective-permute-start.1 = (bf16[128,1152]{1,0:T(8,128)(2,1)S(1)}, bf16[128,1152]{1,0:T(8,128)(2,1)S(1)}, u32[]{:S(2)}, u32[]{:S(2)}) collective-permute-start(bf16[128,1152]{1,0:T(8,128)(2,1)S(1)} %collective-permute-done), channel_id=1, source_target_pairs={{0,16},{16,32},{32,48},{48,64},{64,80},{80,96},{96,112},{112,128},... | collective-permute-start | bytes 884744 | tf_op jit(solution)/shard_map/ppermute | solution.py:11
  25.7 18.8 %collective-permute-start.2 = (bf16[128,1152]{1,0:T(8,128)(2,1)S(1)}, bf16[128,1152]{1,0:T(8,128)(2,1)S(1)}, u32[]{:S(2)}, u32[]{:S(2)}) collective-permute-start(bf16[128,1152]{1,0:T(8,128)(2,1)S(1)} %collective-permute-done.1), channel_id=1, source_target_pairs={{0,16},{16,32},{32,48},{48,64},{64,80},{80,96},{96,112},{112,128},... | collective-permute-start | bytes 884744 | tf_op jit(solution)/shard_map/ppermute | solution.py:11
  27.6 101.0 %collective-permute-start.7 = (bf16[128,1152]{1,0:T(8,128)(2,1)S(1)}, bf16[128,1152]{1,0:T(8,128)(2,1)S(1)}, u32[]{:S(2)}, u32[]{:S(2)}) collective-permute-start(bf16[128,1152]{1,0:T(8,128)(2,1)S(1)} %get-tuple-element.6), channel_id=1, source_target_pairs={{0,1},{1,2},{2,3},{3,4},{4,5},{5,6},{6,7},{7,8},{8,9},{9,10},{10,1... | collective-permute-start | bytes 884744 | tf_op jit(solution)/shard_map/ppermute | solution.py:11
  44.4 50.0 %collective-permute-start.3 = (bf16[128,1152]{1,0:T(8,128)(2,1)S(1)}, bf16[128,1152]{1,0:T(8,128)(2,1)S(1)}, u32[]{:S(2)}, u32[]{:S(2)}) collective-permute-start(bf16[128,1152]{1,0:T(8,128)(2,1)S(1)} %collective-permute-done.2), channel_id=1, source_target_pairs={{0,16},{16,32},{32,48},{48,64},{64,80},{80,96},{96,112},{112,128},... | collective-permute-start | bytes 884744 | tf_op jit(solution)/shard_map/ppermute | solution.py:11
  94.5 11.4 %collective-permute-start.4 = (bf16[128,1152]{1,0:T(8,128)(2,1)S(1)}, bf16[128,1152]{1,0:T(8,128)(2,1)S(1)}, u32[]{:S(2)}, u32[]{:S(2)}) collective-permute-start(bf16[128,1152]{1,0:T(8,128)(2,1)S(1)} %collective-permute-done.3), channel_id=1, source_target_pairs={{0,16},{16,32},{32,48},{48,64},{64,80},{80,96},{96,112},{112,128},... | collective-permute-start | bytes 884744 | tf_op jit(solution)/shard_map/ppermute | solution.py:11
  105.8 11.4 %collective-permute-start.5 = (bf16[128,1152]{1,0:T(8,128)(2,1)S(1)}, bf16[128,1152]{1,0:T(8,128)(2,1)S(1)}, u32[]{:S(2)}, u32[]{:S(2)}) collective-permute-start(bf16[128,1152]{1,0:T(8,128)(2,1)S(1)} %collective-permute-done.4), channel_id=1, source_target_pairs={{0,16},{16,32},{32,48},{48,64},{64,80},{80,96},{96,112},{112,128},... | collective-permute-start | bytes 884744 | tf_op jit(solution)/shard_map/ppermute | solution.py:11
  117.2 11.4 %collective-permute-start.6 = (bf16[128,1152]{1,0:T(8,128)(2,1)S(1)}, bf16[128,1152]{1,0:T(8,128)(2,1)S(1)}, u32[]{:S(2)}, u32[]{:S(2)}) collective-permute-start(bf16[128,1152]{1,0:T(8,128)(2,1)S(1)} %collective-permute-done.5), channel_id=1, source_target_pairs={{0,16},{16,32},{32,48},{48,64},{64,80},{80,96},{96,112},{112,128},... | collective-permute-start | bytes 884744 | tf_op jit(solution)/shard_map/ppermute | solution.py:11
  130.7 9.3 %collective-permute-start.8 = (f32[128,1152]{1,0:T(8,128)S(1)}, f32[128,1152]{1,0:T(8,128)S(1)}, u32[]{:S(2)}, u32[]{:S(2)}) collective-permute-start(f32[128,1152]{1,0:T(8,128)S(1)} %slice.53), channel_id=1, source_target_pairs={{0,1008},{16,0},{32,16},{48,32},{64,48},{80,64},{96,80},{112,96},{... | collective-permute-start | bytes 1769480 | tf_op jit(solution)/shard_map/ppermute | solution.py:11
  140.1 14.5 %collective-permute-start.9 = (f32[128,1152]{1,0:T(8,128)S(1)}, f32[128,1152]{1,0:T(8,128)S(1)}, u32[]{:S(2)}, u32[]{:S(2)}) collective-permute-start(f32[128,1152]{1,0:T(8,128)S(1)} %slice_add_fusion.6), channel_id=1, source_target_pairs={{0,1008},{16,0},{32,16},{48,32},{64,48},{80,64},{96,80},{112,96},{... | collective-permute-start | bytes 1769480 | tf_op jit(solution)/shard_map/ppermute | solution.py:11
  154.7 14.5 %collective-permute-start.10 = (f32[128,1152]{1,0:T(8,128)S(1)}, f32[128,1152]{1,0:T(8,128)S(1)}, u32[]{:S(2)}, u32[]{:S(2)}) collective-permute-start(f32[128,1152]{1,0:T(8,128)S(1)} %slice_add_fusion.5), channel_id=1, source_target_pairs={{0,1008},{16,0},{32,16},{48,32},{64,48},{80,64},{96,80},{112,96},{... | collective-permute-start | bytes 1769480 | tf_op jit(solution)/shard_map/ppermute | solution.py:11
  169.3 14.5 %collective-permute-start.11 = (f32[128,1152]{1,0:T(8,128)S(1)}, f32[128,1152]{1,0:T(8,128)S(1)}, u32[]{:S(2)}, u32[]{:S(2)}) collective-permute-start(f32[128,1152]{1,0:T(8,128)S(1)} %slice_add_fusion.4), channel_id=1, source_target_pairs={{0,1008},{16,0},{32,16},{48,32},{64,48},{80,64},{96,80},{112,96},{... | collective-permute-start | bytes 1769480 | tf_op jit(solution)/shard_map/ppermute | solution.py:11
  183.9 14.5 %collective-permute-start.12 = (f32[128,1152]{1,0:T(8,128)S(1)}, f32[128,1152]{1,0:T(8,128)S(1)}, u32[]{:S(2)}, u32[]{:S(2)}) collective-permute-start(f32[128,1152]{1,0:T(8,128)S(1)} %slice_add_fusion.3), channel_id=1, source_target_pairs={{0,1008},{16,0},{32,16},{48,32},{64,48},{80,64},{96,80},{112,96},{... | collective-permute-start | bytes 1769480 | tf_op jit(solution)/shard_map/ppermute | solution.py:11
  198.5 14.5 %collective-permute-start.13 = (f32[128,1152]{1,0:T(8,128)S(1)}, f32[128,1152]{1,0:T(8,128)S(1)}, u32[]{:S(2)}, u32[]{:S(2)}) collective-permute-start(f32[128,1152]{1,0:T(8,128)S(1)} %slice_add_fusion.2), channel_id=1, source_target_pairs={{0,1008},{16,0},{32,16},{48,32},{64,48},{80,64},{96,80},{112,96},{... | collective-permute-start | bytes 1769480 | tf_op jit(solution)/shard_map/ppermute | solution.py:11
  206.4 127.1 %copy-start = (bf16[128,1152]{1,0:T(8,128)(2,1)S(1)}, bf16[128,1152]{1,0:T(8,128)(2,1)}, u32[]{:S(2)}) copy-start(bf16[128,1152]{1,0:T(8,128)(2,1)} %param.6) | copy-start | bytes 884740
  213.2 103.3 %collective-permute-start.14 = (f32[128,1152]{1,0:T(8,128)S(1)}, f32[128,1152]{1,0:T(8,128)S(1)}, u32[]{:S(2)}, u32[]{:S(2)}) collective-permute-start(f32[128,1152]{1,0:T(8,128)S(1)} %get-tuple-element.7), channel_id=1, source_target_pairs={{0,1008},{16,0},{32,16},{48,32},{64,48},{80,64},{96,80},{112,96},{... | collective-permute-start | bytes 1769480 | tf_op jit(solution)/shard_map/ppermute | solution.py:11
  220.3 113.2 %collective-permute-start.15 = (f32[128,1152]{1,0:T(8,128)S(1)}, f32[128,1152]{1,0:T(8,128)S(1)}, u32[]{:S(2)}, u32[]{:S(2)}) collective-permute-start(f32[128,1152]{1,0:T(8,128)S(1)} %get-tuple-element.8), channel_id=1, source_target_pairs={{0,15},{1,0},{2,1},{3,2},{4,3},{5,4},{6,5},{7,6},{8,7},{9,8},{10,9... | collective-permute-start | bytes 1769480 | tf_op jit(solution)/shard_map/ppermute | solution.py:11
where the time goes:
time: 336 us; the launch traced here: 335 us
  waiting for transfers between devices  196 us (58%)
  starting transfers between devices  127 us (38%)
  other arithmetic  7.38 us (2%)
    ppermute x16, waiting for transfers between devices, passed_along(): return lax.ppermute(x, axis, [(i, (i + by) % size) for i in range(size)])  196 us
    ppermute x16, starting transfers between devices, passed_along(): return lax.ppermute(x, axis, [(i, (i + by) % size) for i in range(size)])  127 us
  transfers between devices with their start and end apart: 16, of which 14 were waited for; matrix products, arithmetic and copies ran while one was open for 1% of the time, Pallas kernels for 0%

commit v1 on v0

v1 whole, which is shorter than its diff:
```python
import functools

import jax
import jax.numpy as jnp
from jax import lax
from jax.experimental import pallas as pl
from jax.experimental.pallas import tpu as pltpu
from jax.sharding import PartitionSpec as P

SPAN = 8
CORES = 2
CHIPS = SPAN // CORES
F32 = jnp.float32
BF16 = jnp.bfloat16


def shifted(x, axis, by):
    size = lax.axis_size(axis)
    return lax.ppermute(x, axis, [(i, (i + by) % size) for i in range(size)])


def in_row(x, by):
    pairs = []
    for i in range(lax.axis_size("blk")):
        first, place = i - i % SPAN, i % SPAN
        pairs.append((i, first + (place + CORES * by) % SPAN))
    return lax.ppermute(x, "blk", pairs)


def to_twin(x):
    return lax.ppermute(x, "blk", [(i, i ^ 1) for i in range(lax.axis_size("blk"))])


def row_inverse(values):
    floats = values.astype(F32)
    return lax.rsqrt(jnp.sum(floats * floats, axis=-1, keepdims=True) + 1e-06)


def along_lanes(column):
    rows = column.shape[0]
    return jnp.broadcast_to(column, (rows, rows)).T


def by_rows(left, right):
    return lax.dot_general(left, right, (((1,), (1,)), ((), ())), preferred_element_type=F32)


def by_cols(left, right):
    return lax.dot_general(left, right, (((0,), (0,)), ((), ())), preferred_element_type=F32)


def product(left, right):
    return jnp.dot(left, right, preferred_element_type=F32)


def loss_and_slope(u):
    small = jnp.exp(-jnp.abs(u))
    whole = 1.0 + small
    return (
        jnp.maximum(u, 0.0) + jnp.log1p(small),
        jnp.where(u >= 0.0, 1.0, small) / whole,
    )


def inner_kernel(scale, bias, x_ref, y_ref, pos_ref, *rest):
    pairs, (loss_ref, gx_ref, gy_ref) = rest[:-3], rest[-3:]
    tau, offset = scale[0], bias[0]
    rows = x_ref.shape[0]
    x, y = x_ref[...], y_ref[...]
    x_inv, y_inv = row_inverse(x), row_inverse(y)
    x_tau, y_tau = x_inv * tau, y_inv * tau
    y_lanes = along_lanes(y_inv)
    own = by_rows(x, y) * x_tau * y_lanes + offset
    place = lax.broadcasted_iota(jnp.int32, (rows, rows), 1)
    equal = pos_ref[...] == place
    away = jnp.where(equal, -1.0, 1.0)
    loss, slope = loss_and_slope(away * own)
    slope = slope * away
    gx = product((slope * y_lanes).astype(BF16), y)
    gy = by_cols((slope * x_inv).astype(BF16), x)
    for ref in pairs:
        other = ref[:rows, :]
        lanes = along_lanes(row_inverse(other))
        add, slope = loss_and_slope(by_rows(x, other) * x_tau * lanes + offset)
        loss = loss + add
        gx = gx + product((slope * lanes).astype(BF16), other)
        other = ref[rows:, :]
        lanes = along_lanes(row_inverse(other))
        _, slope = loss_and_slope(by_rows(y, other) * y_tau * lanes + offset)
        gy = gy + product((slope * lanes).astype(BF16), other)
    loss_ref[...] = loss
    gx_ref[...] = gx
    gy_ref[...] = gy


def outer_kernel(scale, bias, x_ref, y_ref, yg_ref, xg_ref, loss_in, gx_in, gy_in, loss_ref, ix_ref, ty_ref):
    tau, offset = scale[0], bias[0]
    rows = x_ref.shape[0]
    x, y = x_ref[...], y_ref[...]
    x_inv, y_inv = row_inverse(x), row_inverse(y)
    other = yg_ref[...]
    lanes = along_lanes(row_inverse(other))
    add, slope = loss_and_slope(by_rows(x, other) * (x_inv * tau) * lanes + offset)
    loss_ref[...] = jnp.sum((loss_in[...] + add).T, axis=0, keepdims=True) / F32((SPAN + 1) * rows)
    gx = (gx_in[...] + product((slope * lanes).astype(BF16), other)) * tau
    xn = x.astype(F32) * x_inv
    ix_ref[...] = (gx - xn * jnp.sum(xn * gx, axis=-1, keepdims=True)) * x_inv
    other = xg_ref[...]
    lanes = along_lanes(row_inverse(other))
    _, slope = loss_and_slope(by_rows(y, other) * (y_inv * tau) * lanes + offset)
    gy = (gy_in[...] + product((slope * lanes).astype(BF16), other)) * tau
    yn = y.astype(F32) * y_inv
    ty_ref[...] = (gy - yn * jnp.sum(yn * gy, axis=-1, keepdims=True)) * y_inv


def call(kernel, outs, flops, scale, bias, *args):
    return pl.pallas_call(
        kernel,
        out_shape=[jax.ShapeDtypeStruct(shape, F32) for shape in outs],
        in_specs=[pl.BlockSpec(memory_space=pltpu.SMEM)] * 2
        + [pl.BlockSpec(memory_space=pltpu.VMEM)] * len(args),
        out_specs=[pl.BlockSpec(memory_space=pltpu.VMEM)] * len(outs),
        compiler_params=pltpu.CompilerParams(vmem_limit_bytes=40 * 1024 * 1024),
        cost_estimate=pl.CostEstimate(flops=flops, bytes_accessed=8 * 1024 * 1024, transcendentals=0),
    )(scale, bias, *args)


def local(image_feats, text_feats, positive, scale, bias):
    x, y = image_feats, text_feats
    rows, width = x.shape
    place = lax.axis_index("blk") % SPAN
    chip, core = place // CORES, place % CORES
    y_back = shifted(y, "blk", SPAN)
    x_next = shifted(x, "blk", -SPAN)
    y_outer = shifted(y, "group", 1)
    x_outer = shifted(x, "group", -1)
    up = jnp.concatenate([y, x_next], axis=0)
    down = jnp.concatenate([y_back, x], axis=0)
    pairs = [in_row(jnp.where(chip + by < CHIPS, up, down), by) for by in range(1, CHIPS)]
    twins = [to_twin(jnp.where(core == 0, up, down))] + [to_twin(pair) for pair in pairs]
    block = (rows, width)
    work = 2 * rows * rows * width
    loss, gx, gy = call(
        inner_kernel, [(rows, rows), block, block], work * 31, scale, bias, x, y,
        positive.reshape(rows, 1), *pairs, *twins,
    )
    loss, image_grad, text_grad = call(
        outer_kernel, [(1, rows), block, block], work * 4, scale, bias, x, y, y_outer, x_outer, loss, gx, gy
    )
    return (loss[0], image_grad, text_grad)


def solution(mesh):
    rows = P(("blk", "group"), None)
    return jax.shard_map(
        local,
        mesh=mesh,
        in_specs=(rows, rows, rows, P(), P()),
        out_specs=(P(("blk", "group")), rows, rows),
        check_vma=False,
    )
```

time: 336 us -> 146 us (0.43)
  the two profiles are of different devices: /device:TPU:144 before, /device:TPU:97 now
where the time goes in v1:
time: 146 us
  waiting for transfers between devices  75.1 us (51%)
  starting transfers between devices  55.2 us (38%)
  Pallas kernels  9.82 us (7%)
  local copies, waits for them, and re-layouts  3.31 us (2%)
  between operations  2.17 us (1%)
    ppermute x4, waiting for transfers between devices, shifted(): return lax.ppermute(x, axis, [(i, (i + by) % size) for i in range(size)])  59.3 us
    ppermute x4, starting transfers between devices, shifted(): return lax.ppermute(x, axis, [(i, (i + by) % size) for i in range(size)])  28.2 us
    ppermute x3, waiting for transfers between devices, in_row(): return lax.ppermute(x, 'blk', pairs)  15.8 us
    ppermute x4, starting transfers between devices, to_twin(): lax.ppermute(x, 'blk', [(i, i ^ 1) for i in range(lax.axis_size('blk'))])  13.9 us
    ppermute x3, starting transfers between devices, in_row(): return lax.ppermute(x, 'blk', pairs)  13.1 us
    pallas_call x2, Pallas kernels, call(): pl.pallas_call(kernel, out_shape=[jax.ShapeDtypeStruct(shape, F32) for sh...  9.82 us
  transfers between devices with their start and end apart: 11, of which 5 were waited for; matrix products, arithmetic and copies ran while one was open for 1% of the time, Pallas kernels for 5%

profile of v1, /device:TPU:97, one launch (start us, length us, event | category | flops | bytes accessed | tf_op | source)
XLA Modules:
  0.0 145.8 jit_solution(1453355170030898050)
XLA Ops:
  0.6 4.8 %collective-permute-start.3 = (bf16[128,1152]{1,0:T(8,128)(2,1)}, bf16[128,1152]{1,0:T(8,128)(2,1)S(1)}, u32[]{:S(2)}, u32[]{:S(2)}) collective-permute-start(bf16[128,1152]{1,0:T(8,128)(2,1)} %y_ref.3), channel_id=1, source_target_pairs={{0,128},{16,144},{32,160},{48,176},{64,192},{80,208},{96,224},{112... | collective-permute-start | bytes 884744 | tf_op jit(solution)/shard_map/ppermute | solution.py:19
  5.4 1.9 %collective-permute-start.2 = (bf16[128,1152]{1,0:T(8,128)(2,1)}, bf16[128,1152]{1,0:T(8,128)(2,1)S(1)}, u32[]{:S(2)}, u32[]{:S(2)}) collective-permute-start(bf16[128,1152]{1,0:T(8,128)(2,1)} %x_ref.3), channel_id=1, source_target_pairs={{0,896},{16,912},{32,928},{48,944},{64,960},{80,976},{96,992},{112... | collective-permute-start | bytes 884744 | tf_op jit(solution)/shard_map/ppermute | solution.py:19
  7.4 1.0 constant_dynamic-update-slice_fusion.1
  8.4 0.0 copy-start
  8.4 3.0 %collective-permute-done.3 = bf16[128,1152]{1,0:T(8,128)(2,1)S(1)} collective-permute-done((bf16[128,1152]{1,0:T(8,128)(2,1)}, bf16[128,1152]{1,0:T(8,128)(2,1)S(1)}, u32[]{:S(2)}, u32[]{:S(2)}) %collective-permute-start.3) | collective-permute-done | bytes 294944 | tf_op jit(solution)/shard_map/ppermute | solution.py:19
  11.4 0.0 copy-done
  11.4 8.8 %collective-permute-done.2 = bf16[128,1152]{1,0:T(8,128)(2,1)S(1)} collective-permute-done((bf16[128,1152]{1,0:T(8,128)(2,1)}, bf16[128,1152]{1,0:T(8,128)(2,1)S(1)}, u32[]{:S(2)}, u32[]{:S(2)}) %collective-permute-start.2) | collective-permute-done | bytes 294944 | tf_op jit(solution)/shard_map/ppermute | solution.py:19
  20.3 0.0 copy-start.1
  20.3 0.2 broadcast_select_fusion
  20.5 7.5 %collective-permute-start.6 = (bf16[256,1152]{1,0:T(8,128)(2,1)S(1)}, bf16[256,1152]{1,0:T(8,128)(2,1)S(1)}, u32[]{:S(2)}, u32[]{:S(2)}) collective-permute-start(bf16[256,1152]{1,0:T(8,128)(2,1)S(1)} %get-tuple-element.16), channel_id=1, source_target_pairs={{0,96},{16,112},{32,0},{48,16},{64,32},{80,48},{96,64},{112,80},{1... | collective-permute-start | bytes 1769480 | tf_op jit(solution)/shard_map/ppermute | solution.py:27
  28.1 1.9 %collective-permute-start.4 = (bf16[256,1152]{1,0:T(8,128)(2,1)S(1)}, bf16[256,1152]{1,0:T(8,128)(2,1)S(1)}, u32[]{:S(2)}, u32[]{:S(2)}) collective-permute-start(bf16[256,1152]{1,0:T(8,128)(2,1)S(1)} %get-tuple-element.18), channel_id=1, source_target_pairs={{0,32},{16,48},{32,64},{48,80},{64,96},{80,112},{96,0},{112,16},{1... | collective-permute-start | bytes 1769480 | tf_op jit(solution)/shard_map/ppermute | solution.py:27
  30.0 3.6 %collective-permute-start.5 = (bf16[256,1152]{1,0:T(8,128)(2,1)S(1)}, bf16[256,1152]{1,0:T(8,128)(2,1)S(1)}, u32[]{:S(2)}, u32[]{:S(2)}) collective-permute-start(bf16[256,1152]{1,0:T(8,128)(2,1)S(1)} %get-tuple-element.17), channel_id=1, source_target_pairs={{0,64},{16,80},{32,96},{48,112},{64,0},{80,16},{96,32},{112,48},{1... | collective-permute-start | bytes 1769480 | tf_op jit(solution)/shard_map/ppermute | solution.py:27
  33.6 3.3 %collective-permute-start.7 = (bf16[256,1152]{1,0:T(8,128)(2,1)S(1)}, bf16[256,1152]{1,0:T(8,128)(2,1)S(1)}, u32[]{:S(2)}, u32[]{:S(2)}) collective-permute-start(bf16[256,1152]{1,0:T(8,128)(2,1)S(1)} %get-tuple-element.15), channel_id=1, source_target_pairs={{0,16},{16,0},{32,48},{48,32},{64,80},{80,64},{96,112},{112,96},{1... | collective-permute-start | bytes 1769480 | tf_op jit(solution)/shard_map/ppermute | solution.py:31
  36.9 15.8 %collective-permute-done.6.rest_2_ = bf16[256,1152]{1,0:T(8,128)(2,1)S(1)} collective-permute-done((bf16[256,1152]{1,0:T(8,128)(2,1)S(1)}, bf16[256,1152]{1,0:T(8,128)(2,1)S(1)}, u32[]{:S(2)}, u32[]{:S(2)}) %collective-permute-start.6) | collective-permute-done | bytes 589856 | tf_op jit(solution)/shard_map/ppermute | solution.py:27
  52.7 3.4 %collective-permute-start.10 = (bf16[256,1152]{1,0:T(8,128)(2,1)S(1)}, bf16[256,1152]{1,0:T(8,128)(2,1)S(1)}, u32[]{:S(2)}, u32[]{:S(2)}) collective-permute-start(bf16[256,1152]{1,0:T(8,128)(2,1)S(1)} %collective-permute-done.6.rest_2_), channel_id=1, source_target_pairs={{0,16},{16,0},{32,48},{48,32},{64,80},{80,64},{96,112},{112,96},{1... | collective-permute-start | bytes 1769480 | tf_op jit(solution)/shard_map/ppermute | solution.py:31
  56.1 0.0 collective-permute-done.4.rest_0_
  56.1 5.3 %collective-permute-start.8 = (bf16[256,1152]{1,0:T(8,128)(2,1)S(1)}, bf16[256,1152]{1,0:T(8,128)(2,1)}, u32[]{:S(2)}, u32[]{:S(2)}) collective-permute-start(bf16[256,1152]{1,0:T(8,128)(2,1)S(1)} %collective-permute-done.4.rest_0_), channel_id=1, source_target_pairs={{0,16},{16,0},{32,48},{48,32},{64,80},{80,64},{96,112},{112,96},{1... | collective-permute-start | bytes 1769480 | tf_op jit(solution)/shard_map/ppermute | solution.py:31
  61.5 0.0 collective-permute-done.5.rest_1_
  61.5 1.9 %collective-permute-start.9 = (bf16[256,1152]{1,0:T(8,128)(2,1)S(1)}, bf16[256,1152]{1,0:T(8,128)(2,1)}, u32[]{:S(2)}, u32[]{:S(2)}) collective-permute-start(bf16[256,1152]{1,0:T(8,128)(2,1)S(1)} %collective-permute-done.5.rest_1_), channel_id=1, source_target_pairs={{0,16},{16,0},{32,48},{48,32},{64,80},{80,64},{96,112},{112,96},{1... | collective-permute-start | bytes 1769480 | tf_op jit(solution)/shard_map/ppermute | solution.py:31
  63.4 0.0 copy-done.1
  63.4 15.4 %collective-permute-start = (bf16[128,1152]{1,0:T(8,128)(2,1)S(1)}, bf16[128,1152]{1,0:T(8,128)(2,1)}, u32[]{:S(2)}, u32[]{:S(2)}) collective-permute-start(bf16[128,1152]{1,0:T(8,128)(2,1)S(1)} %copy-done.1), channel_id=1, source_target_pairs={{0,1},{1,2},{2,3},{3,4},{4,5},{5,6},{6,7},{7,8},{8,9},{9,10},{10,1... | collective-permute-start | bytes 884744 | tf_op jit(solution)/shard_map/ppermute | solution.py:19
  78.9 0.0 collective-permute-done.7.rest_3_
  78.9 6.0 %collective-permute-start.1 = (bf16[128,1152]{1,0:T(8,128)(2,1)S(1)}, bf16[128,1152]{1,0:T(8,128)(2,1)}, u32[]{:S(2)}, u32[]{:S(2)}) collective-permute-start(bf16[128,1152]{1,0:T(8,128)(2,1)S(1)} %copy-done), channel_id=1, source_target_pairs={{0,15},{1,0},{2,1},{3,2},{4,3},{5,4},{6,5},{7,6},{8,7},{9,8},{10,9... | collective-permute-start | bytes 884744 | tf_op jit(solution)/shard_map/ppermute | solution.py:19
  86.2 0.0 copy-start.3
  86.2 0.6 copy-done.3
  86.9 0.7 copy.8.pos_ref
  87.6 0.0 collective-permute-done.10.rest_6_
  87.6 0.0 collective-permute-done.8.rest_4_
  87.6 0.0 collective-permute-done.9.rest_5_
  87.6 0.0 copy-start.2
  87.6 0.8 copy-done.2
  88.5 6.7 %shard_map.76 = (f32[128,128]{1,0:T(8,128)S(1)}, f32[128,1152]{1,0:T(8,128)S(1)}, f32[128,1152]{1,0:T(8,128)S(1)}) custom-call(f32[1]{0:T(128)S(6)} %copy.11.scale, f32[1]{0:T(128)S(6)} %copy.12.bias, bf16[128,1152]{1,0:T(8,128)(2,1)S(1)} %copy-done, bf16[128,1152]{1,0:T(8,128)(2,1)S(1)} %copy-done.1, s32[128,1]{1,0:T(8,128)S(1)} %copy-done.2, ...), custom_call_target="tpu_custom_call" | custom-call | flops 1170210816 | bytes 8388608 | tf_op jit(solution)/shard_map/pallas_call | solution.py:117
  95.2 29.3 %collective-permute-done.yg_ref = bf16[128,1152]{1,0:T(8,128)(2,1)} collective-permute-done((bf16[128,1152]{1,0:T(8,128)(2,1)S(1)}, bf16[128,1152]{1,0:T(8,128)(2,1)}, u32[]{:S(2)}, u32[]{:S(2)}) %collective-permute-start) | collective-permute-done | bytes 294944 | tf_op jit(solution)/shard_map/ppermute | solution.py:19
  124.5 18.2 %collective-permute-done.1.xg_ref = bf16[128,1152]{1,0:T(8,128)(2,1)} collective-permute-done((bf16[128,1152]{1,0:T(8,128)(2,1)S(1)}, bf16[128,1152]{1,0:T(8,128)(2,1)}, u32[]{:S(2)}, u32[]{:S(2)}) %collective-permute-start.1) | collective-permute-done | bytes 294944 | tf_op jit(solution)/shard_map/ppermute | solution.py:19
  142.7 3.1 %shard_map.77 = (f32[1,128]{1,0:T(1,128)}, f32[128,1152]{1,0:T(8,128)}, f32[128,1152]{1,0:T(8,128)}) custom-call(f32[1]{0:T(128)S(6)} %copy.11.scale, f32[1]{0:T(128)S(6)} %copy.12.bias, bf16[128,1152]{1,0:T(8,128)(2,1)S(1)} %copy-done, bf16[128,1152]{1,0:T(8,128)(2,1)S(1)} %copy-done.1, bf16[128,1152]{1,0:T(8,128)(2,1)} %collective-permute-done.yg_ref, ...), custom_call_target="tpu_custom_call" | custom-call | flops 150994944 | bytes 8388608 | tf_op jit(solution)/shard_map/pallas_call | solution.py:117
  (3 shorter events, 0.1 us)
Async XLA Ops:
  0.6 10.7 %collective-permute-start.3 = (bf16[128,1152]{1,0:T(8,128)(2,1)}, bf16[128,1152]{1,0:T(8,128)(2,1)S(1)}, u32[]{:S(2)}, u32[]{:S(2)}) collective-permute-start(bf16[128,1152]{1,0:T(8,128)(2,1)} %y_ref.3), channel_id=1, source_target_pairs={{0,128},{16,144},{32,160},{48,176},{64,192},{80,208},{96,224},{112... | collective-permute-start | bytes 884744 | tf_op jit(solution)/shard_map/ppermute | solution.py:19
  5.4 14.8 %collective-permute-start.2 = (bf16[128,1152]{1,0:T(8,128)(2,1)}, bf16[128,1152]{1,0:T(8,128)(2,1)S(1)}, u32[]{:S(2)}, u32[]{:S(2)}) collective-permute-start(bf16[128,1152]{1,0:T(8,128)(2,1)} %x_ref.3), channel_id=1, source_target_pairs={{0,896},{16,912},{32,928},{48,944},{64,960},{80,976},{96,992},{112... | collective-permute-start | bytes 884744 | tf_op jit(solution)/shard_map/ppermute | solution.py:19
  8.4 3.0 %copy-start = (bf16[128,1152]{1,0:T(8,128)(2,1)S(1)}, bf16[128,1152]{1,0:T(8,128)(2,1)}, u32[]{:S(2)}) copy-start(bf16[128,1152]{1,0:T(8,128)(2,1)} %x_ref.3) | copy-start | bytes 884740
  20.3 43.1 %copy-start.1 = (bf16[128,1152]{1,0:T(8,128)(2,1)S(1)}, bf16[128,1152]{1,0:T(8,128)(2,1)}, u32[]{:S(2)}) copy-start(bf16[128,1152]{1,0:T(8,128)(2,1)} %y_ref.3) | copy-start | bytes 884740
  20.5 32.2 %collective-permute-start.6 = (bf16[256,1152]{1,0:T(8,128)(2,1)S(1)}, bf16[256,1152]{1,0:T(8,128)(2,1)S(1)}, u32[]{:S(2)}, u32[]{:S(2)}) collective-permute-start(bf16[256,1152]{1,0:T(8,128)(2,1)S(1)} %get-tuple-element.16), channel_id=1, source_target_pairs={{0,96},{16,112},{32,0},{48,16},{64,32},{80,48},{96,64},{112,80},{1... | collective-permute-start | bytes 1769480 | tf_op jit(solution)/shard_map/ppermute | solution.py:27
  28.1 28.1 %collective-permute-start.4 = (bf16[256,1152]{1,0:T(8,128)(2,1)S(1)}, bf16[256,1152]{1,0:T(8,128)(2,1)S(1)}, u32[]{:S(2)}, u32[]{:S(2)}) collective-permute-start(bf16[256,1152]{1,0:T(8,128)(2,1)S(1)} %get-tuple-element.18), channel_id=1, source_target_pairs={{0,32},{16,48},{32,64},{48,80},{64,96},{80,112},{96,0},{112,16},{1... | collective-permute-start | bytes 1769480 | tf_op jit(solution)/shard_map/ppermute | solution.py:27
  30.0 31.5 %collective-permute-start.5 = (bf16[256,1152]{1,0:T(8,128)(2,1)S(1)}, bf16[256,1152]{1,0:T(8,128)(2,1)S(1)}, u32[]{:S(2)}, u32[]{:S(2)}) collective-permute-start(bf16[256,1152]{1,0:T(8,128)(2,1)S(1)} %get-tuple-element.17), channel_id=1, source_target_pairs={{0,64},{16,80},{32,96},{48,112},{64,0},{80,16},{96,32},{112,48},{1... | collective-permute-start | bytes 1769480 | tf_op jit(solution)/shard_map/ppermute | solution.py:27
  33.6 45.2 %collective-permute-start.7 = (bf16[256,1152]{1,0:T(8,128)(2,1)S(1)}, bf16[256,1152]{1,0:T(8,128)(2,1)S(1)}, u32[]{:S(2)}, u32[]{:S(2)}) collective-permute-start(bf16[256,1152]{1,0:T(8,128)(2,1)S(1)} %get-tuple-element.15), channel_id=1, source_target_pairs={{0,16},{16,0},{32,48},{48,32},{64,80},{80,64},{96,112},{112,96},{1... | collective-permute-start | bytes 1769480 | tf_op jit(solution)/shard_map/ppermute | solution.py:31
  52.7 34.9 %collective-permute-start.10 = (bf16[256,1152]{1,0:T(8,128)(2,1)S(1)}, bf16[256,1152]{1,0:T(8,128)(2,1)S(1)}, u32[]{:S(2)}, u32[]{:S(2)}) collective-permute-start(bf16[256,1152]{1,0:T(8,128)(2,1)S(1)} %collective-permute-done.6.rest_2_), channel_id=1, source_target_pairs={{0,16},{16,0},{32,48},{48,32},{64,80},{80,64},{96,112},{112,96},{1... | collective-permute-start | bytes 1769480 | tf_op jit(solution)/shard_map/ppermute | solution.py:31
  56.1 31.5 %collective-permute-start.8 = (bf16[256,1152]{1,0:T(8,128)(2,1)S(1)}, bf16[256,1152]{1,0:T(8,128)(2,1)}, u32[]{:S(2)}, u32[]{:S(2)}) collective-permute-start(bf16[256,1152]{1,0:T(8,128)(2,1)S(1)} %collective-permute-done.4.rest_0_), channel_id=1, source_target_pairs={{0,16},{16,0},{32,48},{48,32},{64,80},{80,64},{96,112},{112,96},{1... | collective-permute-start | bytes 1769480 | tf_op jit(solution)/shard_map/ppermute | solution.py:31
  61.5 26.2 %collective-permute-start.9 = (bf16[256,1152]{1,0:T(8,128)(2,1)S(1)}, bf16[256,1152]{1,0:T(8,128)(2,1)}, u32[]{:S(2)}, u32[]{:S(2)}) collective-permute-start(bf16[256,1152]{1,0:T(8,128)(2,1)S(1)} %collective-permute-done.5.rest_1_), channel_id=1, source_target_pairs={{0,16},{16,0},{32,48},{48,32},{64,80},{80,64},{96,112},{112,96},{1... | collective-permute-start | bytes 1769480 | tf_op jit(solution)/shard_map/ppermute | solution.py:31
  63.4 61.1 %collective-permute-start = (bf16[128,1152]{1,0:T(8,128)(2,1)S(1)}, bf16[128,1152]{1,0:T(8,128)(2,1)}, u32[]{:S(2)}, u32[]{:S(2)}) collective-permute-start(bf16[128,1152]{1,0:T(8,128)(2,1)S(1)} %copy-done.1), channel_id=1, source_target_pairs={{0,1},{1,2},{2,3},{3,4},{4,5},{5,6},{6,7},{7,8},{8,9},{9,10},{10,1... | collective-permute-start | bytes 884744 | tf_op jit(solution)/shard_map/ppermute | solution.py:19
  78.9 63.8 %collective-permute-start.1 = (bf16[128,1152]{1,0:T(8,128)(2,1)S(1)}, bf16[128,1152]{1,0:T(8,128)(2,1)}, u32[]{:S(2)}, u32[]{:S(2)}) collective-permute-start(bf16[128,1152]{1,0:T(8,128)(2,1)S(1)} %copy-done), channel_id=1, source_target_pairs={{0,15},{1,0},{2,1},{3,2},{4,3},{5,4},{6,5},{7,6},{8,7},{9,8},{10,9... | collective-permute-start | bytes 884744 | tf_op jit(solution)/shard_map/ppermute | solution.py:19
  86.2 0.7 copy-start.3
  87.6 0.8 copy-start.2

commit v2 on v1

--- a/solution.py
+++ b/solution.py
@@ -71,9 +71,9 @@
     x_tau, y_tau = x_inv * tau, y_inv * tau
     y_lanes = along_lanes(y_inv)
     own = by_rows(x, y) * x_tau * y_lanes + offset
-    place = lax.broadcasted_iota(jnp.int32, (rows, rows), 1)
-    equal = pos_ref[...] == place
-    away = jnp.where(equal, -1.0, 1.0)
+    place = lax.broadcasted_iota(jnp.int32, (rows, rows), 1).astype(F32)
+    match = jnp.broadcast_to(pos_ref[...].astype(F32), (rows, rows)).T
+    away = jnp.where(match == place, -1.0, 1.0)
     loss, slope = loss_and_slope(away * own)
     slope = slope * away
     gx = product((slope * y_lanes).astype(BF16), y)
@@ -134,16 +134,28 @@
     x_next = shifted(x, "blk", -SPAN)
     y_outer = shifted(y, "group", 1)
     x_outer = shifted(x, "group", -1)
-    up = jnp.concatenate([y, x_next], axis=0)
-    down = jnp.concatenate([y_back, x], axis=0)
-    pairs = [in_row(jnp.where(chip + by < CHIPS, up, down), by) for by in range(1, CHIPS)]
-    twins = [to_twin(jnp.where(core == 0, up, down))] + [to_twin(pair) for pair in pairs]
     block = (rows, width)
     work = 2 * rows * rows * width
-    loss, gx, gy = call(
-        inner_kernel, [(rows, rows), block, block], work * 31, scale, bias, x, y,
-        positive.reshape(rows, 1), *pairs, *twins,
-    )
+
+    def inner(_):
+        up = jnp.concatenate([y, x_next], axis=0)
+        down = jnp.concatenate([y_back, x], axis=0)
+        sends = [jnp.where(chip + by < CHIPS, up, down) for by in range(1, CHIPS)]
+        twins = [to_twin(jnp.where(core == 0, up, down))]
+        sends[1], twins[0] = lax.optimization_barrier((sends[1], twins[0]))
+        pairs = [in_row(sends[by - 1], by) for by in range(1, CHIPS)]
+        twins += [to_twin(pair) for pair in pairs]
+        loss, gx, gy = call(
+            inner_kernel, [(rows, rows), block, block], work * 31, scale, bias, x, y,
+            positive, *pairs, *twins,
+        )
+        return loss, gx, gy
+
+    def skip(_):
+        return jnp.zeros((rows, rows), F32), jnp.zeros(block, F32), jnp.zeros(block, F32)
+
+    go = lax.optimization_barrier(jnp.int32(1))
+    loss, gx, gy = lax.cond(go > 0, inner, skip, 0)
     loss, image_grad, text_grad = call(
         outer_kernel, [(1, rows), block, block], work * 4, scale, bias, x, y, y_outer, x_outer, loss, gx, gy
     )

time: 146 us -> 132 us (0.904)
  the two profiles are of different devices: /device:TPU:97 before, /device:TPU:1 now
where the time goes in v2:
time: 132 us; the launch traced here: 131 us
  starting transfers between devices  93.2 us (71%)
  waiting for transfers between devices  23.9 us (18%)
  Pallas kernels  9.84 us (7%)
  between operations  2.04 us (2%)
  local copies, waits for them, and re-layouts  2 us (2%)
    ppermute x4, starting transfers between devices, to_twin(): lax.ppermute(x, 'blk', [(i, i ^ 1) for i in range(lax.axis_size('blk'))])  45 us
    ppermute x4, starting transfers between devices, shifted(): return lax.ppermute(x, axis, [(i, (i + by) % size) for i in range(size)])  39.8 us
    ppermute x3, waiting for transfers between devices, in_row(): return lax.ppermute(x, 'blk', pairs)  22.2 us
    pallas_call x2, Pallas kernels, call(): pl.pallas_call(kernel, out_shape=[jax.ShapeDtypeStruct(shape, F32) for sh...  9.84 us
    ppermute x3, starting transfers between devices, in_row(): return lax.ppermute(x, 'blk', pairs)  8.41 us
  transfers between devices with their start and end apart: 11, of which 2 were waited for; matrix products, arithmetic and copies ran while one was open for 1% of the time, Pallas kernels for 5%

profile of v2, /device:TPU:1, one launch (start us, length us, event | category | flops | bytes accessed | tf_op | source)
XLA Modules:
  0.0 131.4 jit_solution(937342183599694252)
XLA Ops:
  0.6 4.4 %collective-permute-start.10 = (bf16[128,1152]{1,0:T(8,128)(2,1)}, bf16[128,1152]{1,0:T(8,128)(2,1)S(1)}, u32[]{:S(2)}, u32[]{:S(2)}) collective-permute-start(bf16[128,1152]{1,0:T(8,128)(2,1)} %y_ref.1), channel_id=1, source_target_pairs={{0,128},{16,144},{32,160},{48,176},{64,192},{80,208},{96,224},{112... | collective-permute-start | bytes 884744 | tf_op jit(solution)/shard_map/ppermute | solution.py:19
  5.0 11.3 %collective-permute-start.9 = (bf16[128,1152]{1,0:T(8,128)(2,1)}, bf16[128,1152]{1,0:T(8,128)(2,1)S(1)}, u32[]{:S(2)}, u32[]{:S(2)}) collective-permute-start(bf16[128,1152]{1,0:T(8,128)(2,1)} %x_ref.1), channel_id=1, source_target_pairs={{0,896},{16,912},{32,928},{48,944},{64,960},{80,976},{96,992},{112... | collective-permute-start | bytes 884744 | tf_op jit(solution)/shard_map/ppermute | solution.py:19
  16.3 15.4 %collective-permute-start.7 = (bf16[128,1152]{1,0:T(8,128)(2,1)}, bf16[128,1152]{1,0:T(8,128)(2,1)S(1)}, u32[]{:S(2)}, u32[]{:S(2)}) collective-permute-start(bf16[128,1152]{1,0:T(8,128)(2,1)} %y_ref.1), channel_id=1, source_target_pairs={{0,1},{1,2},{2,3},{3,4},{4,5},{5,6},{6,7},{7,8},{8,9},{9,10},{10,1... | collective-permute-start | bytes 884744 | tf_op jit(solution)/shard_map/ppermute | solution.py:19
  31.7 8.7 %collective-permute-start.8 = (bf16[128,1152]{1,0:T(8,128)(2,1)}, bf16[128,1152]{1,0:T(8,128)(2,1)S(1)}, u32[]{:S(2)}, u32[]{:S(2)}) collective-permute-start(bf16[128,1152]{1,0:T(8,128)(2,1)} %x_ref.1), channel_id=1, source_target_pairs={{0,15},{1,0},{2,1},{3,2},{4,3},{5,4},{6,5},{7,6},{8,7},{9,8},{10,9... | collective-permute-start | bytes 884744 | tf_op jit(solution)/shard_map/ppermute | solution.py:19
  41.1 0.0 copy-start.2
  41.8 0.0 collective-permute-done.10
  41.8 0.0 collective-permute-done.9
  41.8 0.0 copy-done.2
  41.8 86.4 %conditional.1 = ((f32[128,128]{1,0:T(8,128)S(1)}, f32[128,1152]{1,0:T(8,128)S(1)}, f32[128,1152]{1,0:T(8,128)S(1)})) conditional(s32[]{:T(128)} %convert_element_type.3, () %tuple.16, (s32[]{:T(128)}, bf16[128,1152]{1,0:T(8,128)(2,1)}, bf16[128,1152]{1,0:T(8,128)(2,1)S(1)}, bf16[128,1152]{1,0:T(8,128)(2,1)S(1)}, bf16[128,1152]{1,0:T(8,128)(2,1)}, ...), branch_computations={%region_0.1_spmd, %region_1.2_spmd} | conditional | flops 1171390464 | bytes 33161748 | solution.py:158
  41.9 1.0 constant_dynamic-update-slice_fusion.1
  42.9 0.0 copy-start.1
  42.9 0.9 copy-done.1
  43.8 0.1 constant_dynamic-update-slice_fusion
  43.9 0.0 copy-start
  43.9 0.2 broadcast_select_fusion
  44.1 38.0 %collective-permute-start.1 = (bf16[256,1152]{1,0:T(8,128)(2,1)S(1)}, bf16[256,1152]{1,0:T(8,128)(2,1)S(1)}, u32[]{:S(2)}, u32[]{:S(2)}) collective-permute-start(bf16[256,1152]{1,0:T(8,128)(2,1)S(1)} %get-tuple-element.72), channel_id=1, source_target_pairs={{0,16},{16,0},{32,48},{48,32},{64,80},{80,64},{96,112},{112,96},{1... | collective-permute-start | bytes 1769480 | tf_op jit(solution)/shard_map/cond/branch_1_fun/ppermute | solution.py:31
  82.1 1.9 %collective-permute-start = (bf16[256,1152]{1,0:T(8,128)(2,1)S(1)}, bf16[256,1152]{1,0:T(8,128)(2,1)S(1)}, u32[]{:S(2)}, u32[]{:S(2)}) collective-permute-start(bf16[256,1152]{1,0:T(8,128)(2,1)S(1)} %get-tuple-element.74), channel_id=1, source_target_pairs={{0,32},{16,48},{32,64},{48,80},{64,96},{80,112},{96,0},{112,16},{1... | collective-permute-start | bytes 1769480 | tf_op jit(solution)/shard_map/cond/branch_1_fun/ppermute | solution.py:27
  84.1 4.6 %collective-permute-start.3 = (bf16[256,1152]{1,0:T(8,128)(2,1)S(1)}, bf16[256,1152]{1,0:T(8,128)(2,1)S(1)}, u32[]{:S(2)}, u32[]{:S(2)}) collective-permute-start(bf16[256,1152]{1,0:T(8,128)(2,1)S(1)} %get-tuple-element.71), channel_id=1, source_target_pairs={{0,96},{16,112},{32,0},{48,16},{64,32},{80,48},{96,64},{112,80},{1... | collective-permute-start | bytes 1769480 | tf_op jit(solution)/shard_map/cond/branch_1_fun/ppermute | solution.py:27
  88.6 0.0 collective-permute-done.1.rest_3_
  88.6 1.9 %collective-permute-start.2 = (bf16[256,1152]{1,0:T(8,128)(2,1)S(1)}, bf16[256,1152]{1,0:T(8,128)(2,1)S(1)}, u32[]{:S(2)}, u32[]{:S(2)}) collective-permute-start(bf16[256,1152]{1,0:T(8,128)(2,1)S(1)} %get-tuple-element.27), channel_id=1, source_target_pairs={{0,64},{16,80},{32,96},{48,112},{64,0},{80,16},{96,32},{112,48},{1... | collective-permute-start | bytes 1769480 | tf_op jit(solution)/shard_map/cond/branch_1_fun/ppermute | solution.py:27
  90.6 22.2 %collective-permute-done.rest_0_ = bf16[256,1152]{1,0:T(8,128)(2,1)S(1)} collective-permute-done((bf16[256,1152]{1,0:T(8,128)(2,1)S(1)}, bf16[256,1152]{1,0:T(8,128)(2,1)S(1)}, u32[]{:S(2)}, u32[]{:S(2)}) %collective-permute-start) | collective-permute-done | bytes 589856 | tf_op jit(solution)/shard_map/cond/branch_1_fun/ppermute | solution.py:27
  112.8 2.7 %collective-permute-start.4 = (bf16[256,1152]{1,0:T(8,128)(2,1)S(1)}, bf16[256,1152]{1,0:T(8,128)(2,1)S(1)}, u32[]{:S(2)}, u32[]{:S(2)}) collective-permute-start(bf16[256,1152]{1,0:T(8,128)(2,1)S(1)} %collective-permute-done.rest_0_), channel_id=1, source_target_pairs={{0,16},{16,0},{32,48},{48,32},{64,80},{80,64},{96,112},{112,96},{1... | collective-permute-start | bytes 1769480 | tf_op jit(solution)/shard_map/cond/branch_1_fun/ppermute | solution.py:31
  115.5 0.0 collective-permute-done.3.rest_2_
  115.5 1.9 %collective-permute-start.6 = (bf16[256,1152]{1,0:T(8,128)(2,1)S(1)}, bf16[256,1152]{1,0:T(8,128)(2,1)S(1)}, u32[]{:S(2)}, u32[]{:S(2)}) collective-permute-start(bf16[256,1152]{1,0:T(8,128)(2,1)S(1)} %collective-permute-done.3.rest_2_), channel_id=1, source_target_pairs={{0,16},{16,0},{32,48},{48,32},{64,80},{80,64},{96,112},{112,96},{1... | collective-permute-start | bytes 1769480 | tf_op jit(solution)/shard_map/cond/branch_1_fun/ppermute | solution.py:31
  117.5 0.0 collective-permute-done.2.rest_1_
  117.5 2.4 %collective-permute-start.5 = (bf16[256,1152]{1,0:T(8,128)(2,1)S(1)}, bf16[256,1152]{1,0:T(8,128)(2,1)S(1)}, u32[]{:S(2)}, u32[]{:S(2)}) collective-permute-start(bf16[256,1152]{1,0:T(8,128)(2,1)S(1)} %collective-permute-done.2.rest_1_), channel_id=1, source_target_pairs={{0,16},{16,0},{32,48},{48,32},{64,80},{80,64},{96,112},{112,96},{1... | collective-permute-start | bytes 1769480 | tf_op jit(solution)/shard_map/cond/branch_1_fun/ppermute | solution.py:31
  119.9 0.0 collective-permute-done.4.rest_4_
  119.9 0.0 collective-permute-done.6.rest_6_
  119.9 1.6 %collective-permute-done.5.rest_5_ = bf16[256,1152]{1,0:T(8,128)(2,1)S(1)} collective-permute-done((bf16[256,1152]{1,0:T(8,128)(2,1)S(1)}, bf16[256,1152]{1,0:T(8,128)(2,1)S(1)}, u32[]{:S(2)}, u32[]{:S(2)}) %collective-permute-start.5) | collective-permute-done | bytes 589856 | tf_op jit(solution)/shard_map/cond/branch_1_fun/ppermute | solution.py:31
  121.5 0.0 copy-done
  121.5 6.7 %branch_1_fun.1 = (f32[128,128]{1,0:T(8,128)S(1)}, f32[128,1152]{1,0:T(8,128)S(1)}, f32[128,1152]{1,0:T(8,128)S(1)}) custom-call(f32[1]{0:T(128)} %get-tuple-element.18.scale, f32[1]{0:T(128)} %get-tuple-element.19.bias, bf16[128,1152]{1,0:T(8,128)(2,1)S(1)} %copy-done.1, bf16[128,1152]{1,0:T(8,128)(2,1)S(1)} %copy-done, ...), custom_call_target="tpu_custom_call" | custom-call | flops 1170210816 | bytes 8388608 | tf_op jit(solution)/shard_map/cond/branch_1_fun/pallas_call | solution.py:117
  128.2 0.0 collective-permute-done.7.yg_ref
  128.2 0.0 collective-permute-done.8.xg_ref
  128.3 3.1 %shard_map.77 = (f32[1,128]{1,0:T(1,128)}, f32[128,1152]{1,0:T(8,128)}, f32[128,1152]{1,0:T(8,128)}) custom-call(f32[1]{0:T(128)S(6)} %copy.17.scale, f32[1]{0:T(128)S(6)} %copy.18.bias, bf16[128,1152]{1,0:T(8,128)(2,1)} %x_ref.1, bf16[128,1152]{1,0:T(8,128)(2,1)} %y_ref.1, bf16[128,1152]{1,0:T(8,128)(2,1)S(1)} %collective-permute-done.7.yg_ref, ...), custom_call_target="tpu_custom_call" | custom-call | flops 150994944 | bytes 8388608 | tf_op jit(solution)/shard_map/pallas_call | solution.py:117
  (1 shorter events, 0.0 us)
Async XLA Ops:
  0.6 41.2 %collective-permute-start.10 = (bf16[128,1152]{1,0:T(8,128)(2,1)}, bf16[128,1152]{1,0:T(8,128)(2,1)S(1)}, u32[]{:S(2)}, u32[]{:S(2)}) collective-permute-start(bf16[128,1152]{1,0:T(8,128)(2,1)} %y_ref.1), channel_id=1, source_target_pairs={{0,128},{16,144},{32,160},{48,176},{64,192},{80,208},{96,224},{112... | collective-permute-start | bytes 884744 | tf_op jit(solution)/shard_map/ppermute | solution.py:19
  5.0 36.8 %collective-permute-start.9 = (bf16[128,1152]{1,0:T(8,128)(2,1)}, bf16[128,1152]{1,0:T(8,128)(2,1)S(1)}, u32[]{:S(2)}, u32[]{:S(2)}) collective-permute-start(bf16[128,1152]{1,0:T(8,128)(2,1)} %x_ref.1), channel_id=1, source_target_pairs={{0,896},{16,912},{32,928},{48,944},{64,960},{80,976},{96,992},{112... | collective-permute-start | bytes 884744 | tf_op jit(solution)/shard_map/ppermute | solution.py:19
  16.3 112.0 %collective-permute-start.7 = (bf16[128,1152]{1,0:T(8,128)(2,1)}, bf16[128,1152]{1,0:T(8,128)(2,1)S(1)}, u32[]{:S(2)}, u32[]{:S(2)}) collective-permute-start(bf16[128,1152]{1,0:T(8,128)(2,1)} %y_ref.1), channel_id=1, source_target_pairs={{0,1},{1,2},{2,3},{3,4},{4,5},{5,6},{6,7},{7,8},{8,9},{9,10},{10,1... | collective-permute-start | bytes 884744 | tf_op jit(solution)/shard_map/ppermute | solution.py:19
  31.7 96.5 %collective-permute-start.8 = (bf16[128,1152]{1,0:T(8,128)(2,1)}, bf16[128,1152]{1,0:T(8,128)(2,1)S(1)}, u32[]{:S(2)}, u32[]{:S(2)}) collective-permute-start(bf16[128,1152]{1,0:T(8,128)(2,1)} %x_ref.1), channel_id=1, source_target_pairs={{0,15},{1,0},{2,1},{3,2},{4,3},{5,4},{6,5},{7,6},{8,7},{9,8},{10,9... | collective-permute-start | bytes 884744 | tf_op jit(solution)/shard_map/ppermute | solution.py:19
  41.1 0.7 copy-start.2
  42.9 1.0 copy-start.1
  43.9 77.6 %copy-start = (bf16[128,1152]{1,0:T(8,128)(2,1)S(1)}, bf16[128,1152]{1,0:T(8,128)(2,1)}, u32[]{:S(2)}) copy-start(bf16[128,1152]{1,0:T(8,128)(2,1)} %get-tuple-element.21.y_ref) | copy-start | bytes 884740 | tf_op jit(solution)/shard_map/cond
  44.1 44.5 %collective-permute-start.1 = (bf16[256,1152]{1,0:T(8,128)(2,1)S(1)}, bf16[256,1152]{1,0:T(8,128)(2,1)S(1)}, u32[]{:S(2)}, u32[]{:S(2)}) collective-permute-start(bf16[256,1152]{1,0:T(8,128)(2,1)S(1)} %get-tuple-element.72), channel_id=1, source_target_pairs={{0,16},{16,0},{32,48},{48,32},{64,80},{80,64},{96,112},{112,96},{1... | collective-permute-start | bytes 1769480 | tf_op jit(solution)/shard_map/cond/branch_1_fun/ppermute | solution.py:31
  82.1 30.7 %collective-permute-start = (bf16[256,1152]{1,0:T(8,128)(2,1)S(1)}, bf16[256,1152]{1,0:T(8,128)(2,1)S(1)}, u32[]{:S(2)}, u32[]{:S(2)}) collective-permute-start(bf16[256,1152]{1,0:T(8,128)(2,1)S(1)} %get-tuple-element.74), channel_id=1, source_target_pairs={{0,32},{16,48},{32,64},{48,80},{64,96},{80,112},{96,0},{112,16},{1... | collective-permute-start | bytes 1769480 | tf_op jit(solution)/shard_map/cond/branch_1_fun/ppermute | solution.py:27
  84.1 31.5 %collective-permute-start.3 = (bf16[256,1152]{1,0:T(8,128)(2,1)S(1)}, bf16[256,1152]{1,0:T(8,128)(2,1)S(1)}, u32[]{:S(2)}, u32[]{:S(2)}) collective-permute-start(bf16[256,1152]{1,0:T(8,128)(2,1)S(1)} %get-tuple-element.71), channel_id=1, source_target_pairs={{0,96},{16,112},{32,0},{48,16},{64,32},{80,48},{96,64},{112,80},{1... | collective-permute-start | bytes 1769480 | tf_op jit(solution)/shard_map/cond/branch_1_fun/ppermute | solution.py:27
  88.6 28.8 %collective-permute-start.2 = (bf16[256,1152]{1,0:T(8,128)(2,1)S(1)}, bf16[256,1152]{1,0:T(8,128)(2,1)S(1)}, u32[]{:S(2)}, u32[]{:S(2)}) collective-permute-start(bf16[256,1152]{1,0:T(8,128)(2,1)S(1)} %get-tuple-element.27), channel_id=1, source_target_pairs={{0,64},{16,80},{32,96},{48,112},{64,0},{80,16},{96,32},{112,48},{1... | collective-permute-start | bytes 1769480 | tf_op jit(solution)/shard_map/cond/branch_1_fun/ppermute | solution.py:27
  112.8 7.1 %collective-permute-start.4 = (bf16[256,1152]{1,0:T(8,128)(2,1)S(1)}, bf16[256,1152]{1,0:T(8,128)(2,1)S(1)}, u32[]{:S(2)}, u32[]{:S(2)}) collective-permute-start(bf16[256,1152]{1,0:T(8,128)(2,1)S(1)} %collective-permute-done.rest_0_), channel_id=1, source_target_pairs={{0,16},{16,0},{32,48},{48,32},{64,80},{80,64},{96,112},{112,96},{1... | collective-permute-start | bytes 1769480 | tf_op jit(solution)/shard_map/cond/branch_1_fun/ppermute | solution.py:31
  115.5 4.4 %collective-permute-start.6 = (bf16[256,1152]{1,0:T(8,128)(2,1)S(1)}, bf16[256,1152]{1,0:T(8,128)(2,1)S(1)}, u32[]{:S(2)}, u32[]{:S(2)}) collective-permute-start(bf16[256,1152]{1,0:T(8,128)(2,1)S(1)} %collective-permute-done.3.rest_2_), channel_id=1, source_target_pairs={{0,16},{16,0},{32,48},{48,32},{64,80},{80,64},{96,112},{112,96},{1... | collective-permute-start | bytes 1769480 | tf_op jit(solution)/shard_map/cond/branch_1_fun/ppermute | solution.py:31
  117.5 4.0 %collective-permute-start.5 = (bf16[256,1152]{1,0:T(8,128)(2,1)S(1)}, bf16[256,1152]{1,0:T(8,128)(2,1)S(1)}, u32[]{:S(2)}, u32[]{:S(2)}) collective-permute-start(bf16[256,1152]{1,0:T(8,128)(2,1)S(1)} %collective-permute-done.2.rest_1_), channel_id=1, source_target_pairs={{0,16},{16,0},{32,48},{48,32},{64,80},{80,64},{96,112},{112,96},{1... | collective-permute-start | bytes 1769480 | tf_op jit(solution)/shard_map/cond/branch_1_fun/ppermute | solution.py:31

commit v3 on v2

--- a/solution.py
+++ b/solution.py
@@ -24,6 +24,18 @@
     for i in range(lax.axis_size("blk")):
         first, place = i - i % SPAN, i % SPAN
         pairs.append((i, first + (place + CORES * by) % SPAN))
+    return lax.ppermute(x, "blk", pairs)
+
+
+def next_row(x, by):
+    size = lax.axis_size("blk")
+    pairs = [(i, i + SPAN * by) for i in range(size) if 0 <= i + SPAN * by < size]
+    return lax.ppermute(x, "blk", pairs)
+
+
+def around(x):
+    last = lax.axis_size("blk") - SPAN
+    pairs = [(last + i, i) for i in range(SPAN)] + [(i, last + i) for i in range(SPAN)]
     return lax.ppermute(x, "blk", pairs)
 
 
@@ -128,18 +140,21 @@
 def local(image_feats, text_feats, positive, scale, bias):
     x, y = image_feats, text_feats
     rows, width = x.shape
-    place = lax.axis_index("blk") % SPAN
+    index = lax.axis_index("blk")
+    place = index % SPAN
     chip, core = place // CORES, place % CORES
-    y_back = shifted(y, "blk", SPAN)
-    x_next = shifted(x, "blk", -SPAN)
+    last = lax.axis_size("blk") - SPAN
+    wrapped = around(jnp.where(index >= last, y, x))
+    y_back = next_row(y, 1)
+    x_next = next_row(x, -1)
     y_outer = shifted(y, "group", 1)
     x_outer = shifted(x, "group", -1)
     block = (rows, width)
     work = 2 * rows * rows * width
 
     def inner(_):
-        up = jnp.concatenate([y, x_next], axis=0)
-        down = jnp.concatenate([y_back, x], axis=0)
+        up = jnp.concatenate([y, jnp.where(index >= last, wrapped, x_next)], axis=0)
+        down = jnp.concatenate([jnp.where(index < SPAN, wrapped, y_back), x], axis=0)
         sends = [jnp.where(chip + by < CHIPS, up, down) for by in range(1, CHIPS)]
         twins = [to_twin(jnp.where(core == 0, up, down))]
         sends[1], twins[0] = lax.optimization_barrier((sends[1], twins[0]))

time: 132 us -> 129 us (0.977)
  the two profiles are of different devices: /device:TPU:1 before, /device:TPU:313 now
where the time goes in v3:
time: 129 us
  starting transfers between devices  67.2 us (52%)
  waiting for transfers between devices  47.2 us (37%)
  Pallas kernels  9.69 us (8%)
  other arithmetic  2.55 us (2%)
  between operations  2.03 us (2%)
    ppermute x4, starting transfers between devices, to_twin(): lax.ppermute(x, 'blk', [(i, i ^ 1) for i in range(lax.axis_size('blk'))])  26.7 us
    ppermute x2, waiting for transfers between devices, next_row(): return lax.ppermute(x, 'blk', pairs)  23.3 us
    ppermute x3, waiting for transfers between devices, in_row(): return lax.ppermute(x, 'blk', pairs)  21.9 us
    ppermute x2, starting transfers between devices, next_row(): return lax.ppermute(x, 'blk', pairs)  15.9 us
    ppermute x2, starting transfers between devices, shifted(): return lax.ppermute(x, axis, [(i, (i + by) % size) for i in range(size)])  14 us
    ppermute x3, starting transfers between devices, in_row(): return lax.ppermute(x, 'blk', pairs)  9.93 us
    pallas_call x2, Pallas kernels, call(): pl.pallas_call(kernel, out_shape=[jax.ShapeDtypeStruct(shape, F32) for sh...  9.69 us
  transfers between devices with their start and end apart: 12, of which 4 were waited for; matrix products, arithmetic and copies ran while one was open for 1% of the time, Pallas kernels for 5%

profile of v3, /device:TPU:313, one launch (start us, length us, event | category | flops | bytes accessed | tf_op | source)
XLA Modules:
  0.0 128.8 jit_solution(16901234558892761776)
XLA Ops:
  0.6 0.0 copy-start
  0.6 0.0 copy-start.1
  0.7 0.0 copy-start.2
  0.7 1.1 broadcast_select_fusion.6
  1.7 0.7 collective-permute-start.9
  2.4 0.0 copy-done
  2.4 13.9 %collective-permute-start.10 = (bf16[128,1152]{1,0:T(8,128)(2,1)S(1)}, bf16[128,1152]{1,0:T(8,128)(2,1)S(1)}, u32[]{:S(2)}, u32[]{:S(2)}) collective-permute-start(bf16[128,1152]{1,0:T(8,128)(2,1)S(1)} %copy-done), channel_id=1, source_target_pairs={{128,0},{144,16},{160,32},{176,48},{192,64},{208,80},{224,96},{240... | collective-permute-start | bytes 884744 | tf_op jit(solution)/shard_map/ppermute | solution.py:33
  16.4 0.0 copy-done.1
  16.4 1.9 %collective-permute-start.11 = (bf16[128,1152]{1,0:T(8,128)(2,1)S(1)}, bf16[128,1152]{1,0:T(8,128)(2,1)S(1)}, u32[]{:S(2)}, u32[]{:S(2)}) collective-permute-start(bf16[128,1152]{1,0:T(8,128)(2,1)S(1)} %copy-done.1), channel_id=1, source_target_pairs={{0,128},{16,144},{32,160},{48,176},{64,192},{80,208},{96,224},{112... | collective-permute-start | bytes 884744 | tf_op jit(solution)/shard_map/ppermute | solution.py:33
  18.3 7.9 %collective-permute-start.7 = (bf16[128,1152]{1,0:T(8,128)(2,1)S(1)}, bf16[128,1152]{1,0:T(8,128)(2,1)S(1)}, u32[]{:S(2)}, u32[]{:S(2)}) collective-permute-start(bf16[128,1152]{1,0:T(8,128)(2,1)S(1)} %copy-done.1), channel_id=1, source_target_pairs={{0,1},{1,2},{2,3},{3,4},{4,5},{5,6},{6,7},{7,8},{8,9},{9,10},{10,1... | collective-permute-start | bytes 884744 | tf_op jit(solution)/shard_map/ppermute | solution.py:19
  26.3 6.1 %collective-permute-start.8 = (bf16[128,1152]{1,0:T(8,128)(2,1)S(1)}, bf16[128,1152]{1,0:T(8,128)(2,1)S(1)}, u32[]{:S(2)}, u32[]{:S(2)}) collective-permute-start(bf16[128,1152]{1,0:T(8,128)(2,1)S(1)} %copy-done), channel_id=1, source_target_pairs={{0,15},{1,0},{2,1},{3,2},{4,3},{5,4},{6,5},{7,6},{8,7},{9,8},{10,9... | collective-permute-start | bytes 884744 | tf_op jit(solution)/shard_map/ppermute | solution.py:19
  33.6 0.0 collective-permute-done.9
  33.6 23.3 %collective-permute-done.10 = bf16[128,1152]{1,0:T(8,128)(2,1)S(1)} collective-permute-done((bf16[128,1152]{1,0:T(8,128)(2,1)S(1)}, bf16[128,1152]{1,0:T(8,128)(2,1)S(1)}, u32[]{:S(2)}, u32[]{:S(2)}) %collective-permute-start.10) | collective-permute-done | bytes 294944 | tf_op jit(solution)/shard_map/ppermute | solution.py:33
  57.0 0.0 collective-permute-done.11
  57.0 0.0 copy-done.2
  57.0 68.9 %conditional.1 = ((f32[128,128]{1,0:T(8,128)}, f32[128,1152]{1,0:T(8,128)S(1)}, f32[128,1152]{1,0:T(8,128)S(1)})) conditional(s32[]{:T(128)} %convert_element_type.3, () %tuple.28, (s32[]{:T(128)}, s32[]{:T(128)}, s32[]{:T(128)}, bf16[128,1152]{1,0:T(8,128)(2,1)S(1)}, bf16[128,1152]{1,0:T(8,128)(2,1)S(1)}, /*index=5*/bf16[128,1152]{1,0:T(8,128)(2,1)S(1)}, ...), branch_computations={%region_0.1_spmd, %region_1.2_spmd} | conditional | flops 1176403968 | bytes 31097448 | solution.py:173
  57.0 0.1 broadcast_select_fusion.5
  57.0 1.3 %broadcast_select_fusion = (bf16[256,1152]{1,0:T(8,128)(2,1)}, bf16[256,1152]{1,0:T(8,128)(2,1)S(1)}, bf16[256,1152]{1,0:T(8,128)(2,1)}) fusion(pred[]{:T(512)S(6)} %lt.20, bf16[128,1152]{1,0:T(8,128)(2,1)S(1)} %get-tuple-element.67.x_ref, bf16[128,1152]{1,0:T(8,128)(2,1)S(1)} %get-tuple-element.112, bf16[128,1152]{1,0:T(8,128)(2,1)S(1)} %get-tuple-element.111, ...), kind=kLoop, calls=%fused_computation.2 | loop fusion | flops 3244032 | bytes 2949123 | tf_op jit(solution)/shard_map/cond/branch_1_fun/jit(_where)/select_n | solution.py:158
  58.3 18.9 %collective-permute-start.1 = (bf16[256,1152]{1,0:T(8,128)(2,1)}, bf16[256,1152]{1,0:T(8,128)(2,1)S(1)}, u32[]{:S(2)}, u32[]{:S(2)}) collective-permute-start(bf16[256,1152]{1,0:T(8,128)(2,1)} %get-tuple-element.110), channel_id=1, source_target_pairs={{0,16},{16,0},{32,48},{48,32},{64,80},{80,64},{96,112},{112,96},{1... | collective-permute-start | bytes 1769480 | tf_op jit(solution)/shard_map/cond/branch_1_fun/ppermute | solution.py:43
  77.2 4.4 %collective-permute-start.3 = (bf16[256,1152]{1,0:T(8,128)(2,1)}, bf16[256,1152]{1,0:T(8,128)(2,1)S(1)}, u32[]{:S(2)}, u32[]{:S(2)}) collective-permute-start(bf16[256,1152]{1,0:T(8,128)(2,1)} %get-tuple-element.108), channel_id=1, source_target_pairs={{0,96},{16,112},{32,0},{48,16},{64,32},{80,48},{96,64},{112,80},{1... | collective-permute-start | bytes 1769480 | tf_op jit(solution)/shard_map/cond/branch_1_fun/ppermute | solution.py:27
  81.6 0.1 broadcast_select_fusion.3
  81.8 1.9 %collective-permute-start = (bf16[256,1152]{1,0:T(8,128)(2,1)S(1)}, bf16[256,1152]{1,0:T(8,128)(2,1)S(1)}, u32[]{:S(2)}, u32[]{:S(2)}) collective-permute-start(bf16[256,1152]{1,0:T(8,128)(2,1)S(1)} %broadcast_select_fusion.3), channel_id=1, source_target_pairs={{0,32},{16,48},{32,64},{48,80},{64,96},{80,112},{96,0},{112,16},{1... | collective-permute-start | bytes 1769480 | tf_op jit(solution)/shard_map/cond/branch_1_fun/ppermute | solution.py:27
  83.7 0.0 collective-permute-done.1.rest_3_
  83.7 3.6 %collective-permute-start.2 = (bf16[256,1152]{1,0:T(8,128)(2,1)S(1)}, bf16[256,1152]{1,0:T(8,128)(2,1)S(1)}, u32[]{:S(2)}, u32[]{:S(2)}) collective-permute-start(bf16[256,1152]{1,0:T(8,128)(2,1)S(1)} %get-tuple-element.76), channel_id=1, source_target_pairs={{0,64},{16,80},{32,96},{48,112},{64,0},{80,16},{96,32},{112,48},{1... | collective-permute-start | bytes 1769480 | tf_op jit(solution)/shard_map/cond/branch_1_fun/ppermute | solution.py:27
  87.4 19.8 %collective-permute-done.3.rest_2_ = bf16[256,1152]{1,0:T(8,128)(2,1)S(1)} collective-permute-done((bf16[256,1152]{1,0:T(8,128)(2,1)}, bf16[256,1152]{1,0:T(8,128)(2,1)S(1)}, u32[]{:S(2)}, u32[]{:S(2)}) %collective-permute-start.3) | collective-permute-done | bytes 589856 | tf_op jit(solution)/shard_map/cond/branch_1_fun/ppermute | solution.py:27
  107.2 2.9 %collective-permute-start.6 = (bf16[256,1152]{1,0:T(8,128)(2,1)S(1)}, bf16[256,1152]{1,0:T(8,128)(2,1)S(1)}, u32[]{:S(2)}, u32[]{:S(2)}) collective-permute-start(bf16[256,1152]{1,0:T(8,128)(2,1)S(1)} %collective-permute-done.3.rest_2_), channel_id=1, source_target_pairs={{0,16},{16,0},{32,48},{48,32},{64,80},{80,64},{96,112},{112,96},{1... | collective-permute-start | bytes 1769480 | tf_op jit(solution)/shard_map/cond/branch_1_fun/ppermute | solution.py:43
  110.1 2.1 %collective-permute-done.rest_0_ = bf16[256,1152]{1,0:T(8,128)(2,1)S(1)} collective-permute-done((bf16[256,1152]{1,0:T(8,128)(2,1)S(1)}, bf16[256,1152]{1,0:T(8,128)(2,1)S(1)}, u32[]{:S(2)}, u32[]{:S(2)}) %collective-permute-start) | collective-permute-done | bytes 589856 | tf_op jit(solution)/shard_map/cond/branch_1_fun/ppermute | solution.py:27
  112.2 3.0 %collective-permute-start.4 = (bf16[256,1152]{1,0:T(8,128)(2,1)S(1)}, bf16[256,1152]{1,0:T(8,128)(2,1)S(1)}, u32[]{:S(2)}, u32[]{:S(2)}) collective-permute-start(bf16[256,1152]{1,0:T(8,128)(2,1)S(1)} %collective-permute-done.rest_0_), channel_id=1, source_target_pairs={{0,16},{16,0},{32,48},{48,32},{64,80},{80,64},{96,112},{112,96},{1... | collective-permute-start | bytes 1769480 | tf_op jit(solution)/shard_map/cond/branch_1_fun/ppermute | solution.py:43
  115.2 0.0 collective-permute-done.2.rest_1_
  115.2 1.9 %collective-permute-start.5 = (bf16[256,1152]{1,0:T(8,128)(2,1)S(1)}, bf16[256,1152]{1,0:T(8,128)(2,1)S(1)}, u32[]{:S(2)}, u32[]{:S(2)}) collective-permute-start(bf16[256,1152]{1,0:T(8,128)(2,1)S(1)} %collective-permute-done.2.rest_1_), channel_id=1, source_target_pairs={{0,16},{16,0},{32,48},{48,32},{64,80},{80,64},{96,112},{112,96},{1... | collective-permute-start | bytes 1769480 | tf_op jit(solution)/shard_map/cond/branch_1_fun/ppermute | solution.py:43
  117.1 0.0 collective-permute-done.6.rest_6_
  117.1 0.0 collective-permute-done.4.rest_4_
  117.2 1.9 %collective-permute-done.5.rest_5_ = bf16[256,1152]{1,0:T(8,128)(2,1)S(1)} collective-permute-done((bf16[256,1152]{1,0:T(8,128)(2,1)S(1)}, bf16[256,1152]{1,0:T(8,128)(2,1)S(1)}, u32[]{:S(2)}, u32[]{:S(2)}) %collective-permute-start.5) | collective-permute-done | bytes 589856 | tf_op jit(solution)/shard_map/cond/branch_1_fun/ppermute | solution.py:43
  119.1 6.8 %branch_1_fun.1 = (f32[128,128]{1,0:T(8,128)}, f32[128,1152]{1,0:T(8,128)S(1)}, f32[128,1152]{1,0:T(8,128)S(1)}) custom-call(f32[1]{0:T(128)} %get-tuple-element.65.scale, f32[1]{0:T(128)} %get-tuple-element.66.bias, bf16[128,1152]{1,0:T(8,128)(2,1)S(1)} %get-tuple-element.67.x_ref, bf16[128,1152]{1,0:T(8,128)(2,1)S(1)} %get-tuple-element.68.y_ref, ...), custom_call_target="tpu_custom_call" | custom-call | flops 1170210816 | bytes 8388608 | tf_op jit(solution)/shard_map/cond/branch_1_fun/pallas_call | solution.py:129
  125.9 0.0 collective-permute-done.7.yg_ref
  125.9 0.0 collective-permute-done.8.xg_ref
  125.9 2.9 %shard_map.77 = (f32[1,128]{1,0:T(1,128)}, f32[128,1152]{1,0:T(8,128)}, f32[128,1152]{1,0:T(8,128)}) custom-call(f32[1]{0:T(128)S(6)} %copy.15.scale, f32[1]{0:T(128)S(6)} %copy.16.bias, bf16[128,1152]{1,0:T(8,128)(2,1)S(1)} %copy-done, bf16[128,1152]{1,0:T(8,128)(2,1)S(1)} %copy-done.1, bf16[128,1152]{1,0:T(8,128)(2,1)S(1)} %collective-permute-done.7.yg_ref, ...), custom_call_target="tpu_custom_call" | custom-call | flops 150994944 | bytes 8388608 | tf_op jit(solution)/shard_map/pallas_call | solution.py:129
Async XLA Ops:
  0.6 1.8 %copy-start = (bf16[128,1152]{1,0:T(8,128)(2,1)S(1)}, bf16[128,1152]{1,0:T(8,128)(2,1)}, u32[]{:S(2)}) copy-start(bf16[128,1152]{1,0:T(8,128)(2,1)} %x_ref.1) | copy-start | bytes 884740
  0.6 15.7 %copy-start.1 = (bf16[128,1152]{1,0:T(8,128)(2,1)S(1)}, bf16[128,1152]{1,0:T(8,128)(2,1)}, u32[]{:S(2)}) copy-start(bf16[128,1152]{1,0:T(8,128)(2,1)} %y_ref.1) | copy-start | bytes 884740
  0.7 56.3 %copy-start.2 = (s32[1,128]{1,0:T(1,128)S(1)}, s32[1,128]{1,0:T(1,128)}, u32[]{:S(2)}) copy-start(s32[1,128]{1,0:T(1,128)} %param.9) | copy-start | bytes 1540
  1.7 31.9 %collective-permute-start.9 = (bf16[128,1152]{1,0:T(8,128)(2,1)S(1)}, bf16[128,1152]{1,0:T(8,128)(2,1)S(1)}, u32[]{:S(2)}, u32[]{:S(2)}) collective-permute-start(bf16[128,1152]{1,0:T(8,128)(2,1)S(1)} %broadcast_select_fusion.6), channel_id=1, source_target_pairs={{896,0},{912,16},{928,32},{944,48},{960,64},{976,80},{992,96},{100... | collective-permute-start | bytes 884744 | tf_op jit(solution)/shard_map/ppermute | solution.py:39
  2.4 54.5 %collective-permute-start.10 = (bf16[128,1152]{1,0:T(8,128)(2,1)S(1)}, bf16[128,1152]{1,0:T(8,128)(2,1)S(1)}, u32[]{:S(2)}, u32[]{:S(2)}) collective-permute-start(bf16[128,1152]{1,0:T(8,128)(2,1)S(1)} %copy-done), channel_id=1, source_target_pairs={{128,0},{144,16},{160,32},{176,48},{192,64},{208,80},{224,96},{240... | collective-permute-start | bytes 884744 | tf_op jit(solution)/shard_map/ppermute | solution.py:33
  16.4 40.6 %collective-permute-start.11 = (bf16[128,1152]{1,0:T(8,128)(2,1)S(1)}, bf16[128,1152]{1,0:T(8,128)(2,1)S(1)}, u32[]{:S(2)}, u32[]{:S(2)}) collective-permute-start(bf16[128,1152]{1,0:T(8,128)(2,1)S(1)} %copy-done.1), channel_id=1, source_target_pairs={{0,128},{16,144},{32,160},{48,176},{64,192},{80,208},{96,224},{112... | collective-permute-start | bytes 884744 | tf_op jit(solution)/shard_map/ppermute | solution.py:33
  18.3 107.6 %collective-permute-start.7 = (bf16[128,1152]{1,0:T(8,128)(2,1)S(1)}, bf16[128,1152]{1,0:T(8,128)(2,1)S(1)}, u32[]{:S(2)}, u32[]{:S(2)}) collective-permute-start(bf16[128,1152]{1,0:T(8,128)(2,1)S(1)} %copy-done.1), channel_id=1, source_target_pairs={{0,1},{1,2},{2,3},{3,4},{4,5},{5,6},{6,7},{7,8},{8,9},{9,10},{10,1... | collective-permute-start | bytes 884744 | tf_op jit(solution)/shard_map/ppermute | solution.py:19
  26.3 99.7 %collective-permute-start.8 = (bf16[128,1152]{1,0:T(8,128)(2,1)S(1)}, bf16[128,1152]{1,0:T(8,128)(2,1)S(1)}, u32[]{:S(2)}, u32[]{:S(2)}) collective-permute-start(bf16[128,1152]{1,0:T(8,128)(2,1)S(1)} %copy-done), channel_id=1, source_target_pairs={{0,15},{1,0},{2,1},{3,2},{4,3},{5,4},{6,5},{7,6},{8,7},{9,8},{10,9... | collective-permute-start | bytes 884744 | tf_op jit(solution)/shard_map/ppermute | solution.py:19
  58.3 25.4 %collective-permute-start.1 = (bf16[256,1152]{1,0:T(8,128)(2,1)}, bf16[256,1152]{1,0:T(8,128)(2,1)S(1)}, u32[]{:S(2)}, u32[]{:S(2)}) collective-permute-start(bf16[256,1152]{1,0:T(8,128)(2,1)} %get-tuple-element.110), channel_id=1, source_target_pairs={{0,16},{16,0},{32,48},{48,32},{64,80},{80,64},{96,112},{112,96},{1... | collective-permute-start | bytes 1769480 | tf_op jit(solution)/shard_map/cond/branch_1_fun/ppermute | solution.py:43
  77.2 29.9 %collective-permute-start.3 = (bf16[256,1152]{1,0:T(8,128)(2,1)}, bf16[256,1152]{1,0:T(8,128)(2,1)S(1)}, u32[]{:S(2)}, u32[]{:S(2)}) collective-permute-start(bf16[256,1152]{1,0:T(8,128)(2,1)} %get-tuple-element.108), channel_id=1, source_target_pairs={{0,96},{16,112},{32,0},{48,16},{64,32},{80,48},{96,64},{112,80},{1... | collective-permute-start | bytes 1769480 | tf_op jit(solution)/shard_map/cond/branch_1_fun/ppermute | solution.py:27
  81.8 30.4 %collective-permute-start = (bf16[256,1152]{1,0:T(8,128)(2,1)S(1)}, bf16[256,1152]{1,0:T(8,128)(2,1)S(1)}, u32[]{:S(2)}, u32[]{:S(2)}) collective-permute-start(bf16[256,1152]{1,0:T(8,128)(2,1)S(1)} %broadcast_select_fusion.3), channel_id=1, source_target_pairs={{0,32},{16,48},{32,64},{48,80},{64,96},{80,112},{96,0},{112,16},{1... | collective-permute-start | bytes 1769480 | tf_op jit(solution)/shard_map/cond/branch_1_fun/ppermute | solution.py:27
  83.7 31.5 %collective-permute-start.2 = (bf16[256,1152]{1,0:T(8,128)(2,1)S(1)}, bf16[256,1152]{1,0:T(8,128)(2,1)S(1)}, u32[]{:S(2)}, u32[]{:S(2)}) collective-permute-start(bf16[256,1152]{1,0:T(8,128)(2,1)S(1)} %get-tuple-element.76), channel_id=1, source_target_pairs={{0,64},{16,80},{32,96},{48,112},{64,0},{80,16},{96,32},{112,48},{1... | collective-permute-start | bytes 1769480 | tf_op jit(solution)/shard_map/cond/branch_1_fun/ppermute | solution.py:27
  107.2 9.9 %collective-permute-start.6 = (bf16[256,1152]{1,0:T(8,128)(2,1)S(1)}, bf16[256,1152]{1,0:T(8,128)(2,1)S(1)}, u32[]{:S(2)}, u32[]{:S(2)}) collective-permute-start(bf16[256,1152]{1,0:T(8,128)(2,1)S(1)} %collective-permute-done.3.rest_2_), channel_id=1, source_target_pairs={{0,16},{16,0},{32,48},{48,32},{64,80},{80,64},{96,112},{112,96},{1... | collective-permute-start | bytes 1769480 | tf_op jit(solution)/shard_map/cond/branch_1_fun/ppermute | solution.py:43
  112.2 5.0 %collective-permute-start.4 = (bf16[256,1152]{1,0:T(8,128)(2,1)S(1)}, bf16[256,1152]{1,0:T(8,128)(2,1)S(1)}, u32[]{:S(2)}, u32[]{:S(2)}) collective-permute-start(bf16[256,1152]{1,0:T(8,128)(2,1)S(1)} %collective-permute-done.rest_0_), channel_id=1, source_target_pairs={{0,16},{16,0},{32,48},{48,32},{64,80},{80,64},{96,112},{112,96},{1... | collective-permute-start | bytes 1769480 | tf_op jit(solution)/shard_map/cond/branch_1_fun/ppermute | solution.py:43
  115.2 3.9 %collective-permute-start.5 = (bf16[256,1152]{1,0:T(8,128)(2,1)S(1)}, bf16[256,1152]{1,0:T(8,128)(2,1)S(1)}, u32[]{:S(2)}, u32[]{:S(2)}) collective-permute-start(bf16[256,1152]{1,0:T(8,128)(2,1)S(1)} %collective-permute-done.2.rest_1_), channel_id=1, source_target_pairs={{0,16},{16,0},{32,48},{48,32},{64,80},{80,64},{96,112},{112,96},{1... | collective-permute-start | bytes 1769480 | tf_op jit(solution)/shard_map/cond/branch_1_fun/ppermute | solution.py:43

commit v4 on v3

--- a/solution.py
+++ b/solution.py
@@ -14,9 +14,17 @@
 BF16 = jnp.bfloat16
 
 
-def shifted(x, axis, by):
-    size = lax.axis_size(axis)
-    return lax.ppermute(x, axis, [(i, (i + by) % size) for i in range(size)])
+def along_ring(x, by):
+    blks, groups = lax.axis_size("blk"), lax.axis_size("group")
+    length = blks // SPAN
+    pairs = []
+    for blk in range(blks):
+        row, place = divmod(blk, SPAN)
+        for group in range(groups):
+            to = (group * length + row + by) % (groups * length)
+            to_blk, to_group = to % length * SPAN + place, to // length
+            pairs.append((blk * groups + group, to_blk * groups + to_group))
+    return lax.ppermute(x, ("blk", "group"), pairs)
 
 
 def in_row(x, by):
@@ -24,12 +32,6 @@
     for i in range(lax.axis_size("blk")):
         first, place = i - i % SPAN, i % SPAN
         pairs.append((i, first + (place + CORES * by) % SPAN))
-    return lax.ppermute(x, "blk", pairs)
-
-
-def next_row(x, by):
-    size = lax.axis_size("blk")
-    pairs = [(i, i + SPAN * by) for i in range(size) if 0 <= i + SPAN * by < size]
     return lax.ppermute(x, "blk", pairs)
 
 
@@ -145,10 +147,12 @@
     chip, core = place // CORES, place % CORES
     last = lax.axis_size("blk") - SPAN
     wrapped = around(jnp.where(index >= last, y, x))
-    y_back = next_row(y, 1)
-    x_next = next_row(x, -1)
-    y_outer = shifted(y, "group", 1)
-    x_outer = shifted(x, "group", -1)
+    length = lax.axis_size("blk") // SPAN
+    y_back = along_ring(y, 1)
+    x_next = along_ring(x, -1)
+    y_back, x_next, wrapped = lax.optimization_barrier((y_back, x_next, wrapped))
+    y_outer = along_ring(y_back, length - 1)
+    x_outer = along_ring(x_next, 1 - length)
     block = (rows, width)
     work = 2 * rows * rows * width
 

time: 129 us -> 113 us (0.88)
  the two profiles are of different devices: /device:TPU:313 before, /device:TPU:1 now
where the time goes in v4:
time: 113 us; the launch traced here: 112 us
  starting transfers between devices  67.4 us (60%)
  waiting for transfers between devices  29.2 us (26%)
  Pallas kernels  9.68 us (9%)
  other arithmetic  3.53 us (3%)
  between operations  2.04 us (2%)
    ppermute x4, starting transfers between devices, along_ring(): return lax.ppermute(x, ('blk', 'group'), pairs)  31.6 us
    ppermute x3, waiting for transfers between devices, in_row(): return lax.ppermute(x, 'blk', pairs)  21.9 us
    ppermute x1, starting transfers between devices, around(): return lax.ppermute(x, 'blk', pairs)  13.7 us
    ppermute x4, starting transfers between devices, to_twin(): lax.ppermute(x, 'blk', [(i, i ^ 1) for i in range(lax.axis_size('blk'))])  12.1 us
    ppermute x3, starting transfers between devices, in_row(): return lax.ppermute(x, 'blk', pairs)  9.93 us
    pallas_call x2, Pallas kernels, call(): pl.pallas_call(kernel, out_shape=[jax.ShapeDtypeStruct(shape, F32) for sh...  9.68 us
    ppermute x4, waiting for transfers between devices, along_ring(): return lax.ppermute(x, ('blk', 'group'), pairs)  5.33 us
  transfers between devices with their start and end apart: 12, of which 5 were waited for; matrix products, arithmetic and copies ran while one was open for 2% of the time, Pallas kernels for 6%

profile of v4, /device:TPU:1, one launch (start us, length us, event | category | flops | bytes accessed | tf_op | source)
XLA Modules:
  0.0 112.0 jit_solution(17179238137868322422)
XLA Ops:
  0.6 0.0 copy-start
  0.6 0.0 copy-start.1
  0.7 0.0 copy-start.2
  0.7 1.1 broadcast_select_fusion.6
  1.7 13.7 %collective-permute-start.9 = (bf16[128,1152]{1,0:T(8,128)(2,1)S(1)}, bf16[128,1152]{1,0:T(8,128)(2,1)S(1)}, u32[]{:S(2)}, u32[]{:S(2)}) collective-permute-start(bf16[128,1152]{1,0:T(8,128)(2,1)S(1)} %broadcast_select_fusion.6), channel_id=1, source_target_pairs={{896,0},{912,16},{928,32},{944,48},{960,64},{976,80},{992,96},{100... | collective-permute-start | bytes 884744 | tf_op jit(solution)/shard_map/ppermute | solution.py:41
  15.5 0.0 copy-done.1
  15.5 1.9 %collective-permute-start.7 = (bf16[128,1152]{1,0:T(8,128)(2,1)S(1)}, bf16[128,1152]{1,0:T(8,128)(2,1)}, u32[]{:S(2)}, u32[]{:S(2)}) collective-permute-start(bf16[128,1152]{1,0:T(8,128)(2,1)S(1)} %copy-done.1), channel_id=1, source_target_pairs={{0,128},{1,129},{2,130},{3,131},{4,132},{5,133},{6,134},{7,135},{8... | collective-permute-start | bytes 884744 | tf_op jit(solution)/shard_map/ppermute | solution.py:27
  17.4 0.0 copy-done
  17.4 14.5 %collective-permute-start.8 = (bf16[128,1152]{1,0:T(8,128)(2,1)S(1)}, bf16[128,1152]{1,0:T(8,128)(2,1)}, u32[]{:S(2)}, u32[]{:S(2)}) collective-permute-start(bf16[128,1152]{1,0:T(8,128)(2,1)S(1)} %copy-done), channel_id=1, source_target_pairs={{0,911},{1,896},{2,897},{3,898},{4,899},{5,900},{6,901},{7,902},{8... | collective-permute-start | bytes 884744 | tf_op jit(solution)/shard_map/ppermute | solution.py:27
  31.9 0.0 collective-permute-done.9
  31.9 4.6 %collective-permute-done.7 = bf16[128,1152]{1,0:T(8,128)(2,1)} collective-permute-done((bf16[128,1152]{1,0:T(8,128)(2,1)S(1)}, bf16[128,1152]{1,0:T(8,128)(2,1)}, u32[]{:S(2)}, u32[]{:S(2)}) %collective-permute-start.7) | collective-permute-done | bytes 294944 | tf_op jit(solution)/shard_map/ppermute | solution.py:27
  36.5 0.8 collective-permute-done.8
  37.2 6.3 %collective-permute-start.10 = (bf16[128,1152]{1,0:T(8,128)(2,1)}, bf16[128,1152]{1,0:T(8,128)(2,1)S(1)}, u32[]{:S(2)}, u32[]{:S(2)}) collective-permute-start(bf16[128,1152]{1,0:T(8,128)(2,1)} %collective-permute-done.7), channel_id=1, source_target_pairs={{0,896},{1,897},{2,898},{3,899},{4,900},{5,901},{6,902},{7,903},{8... | collective-permute-start | bytes 884744 | tf_op jit(solution)/shard_map/ppermute | solution.py:27
  43.6 8.8 %collective-permute-start.11 = (bf16[128,1152]{1,0:T(8,128)(2,1)}, bf16[128,1152]{1,0:T(8,128)(2,1)S(1)}, u32[]{:S(2)}, u32[]{:S(2)}) collective-permute-start(bf16[128,1152]{1,0:T(8,128)(2,1)} %collective-permute-done.8), channel_id=1, source_target_pairs={{0,143},{1,128},{2,129},{3,130},{4,131},{5,132},{6,133},{7,134},{8... | collective-permute-start | bytes 884744 | tf_op jit(solution)/shard_map/ppermute | solution.py:27
  53.7 0.0 copy-done.2
  53.8 55.4 %conditional.1 = ((f32[128,128]{1,0:T(8,128)}, f32[128,1152]{1,0:T(8,128)S(1)}, f32[128,1152]{1,0:T(8,128)S(1)})) conditional(s32[]{:T(128)} %convert_element_type.3, () %tuple.30, (s32[]{:T(128)}, s32[]{:T(128)}, s32[]{:T(128)}, bf16[128,1152]{1,0:T(8,128)(2,1)S(1)}, bf16[128,1152]{1,0:T(8,128)(2,1)}, /*index=5*/bf16[128,1152]{1,0:T(8,128)(2,1)S(1)}, ...), branch_computations={%region_0.1_spmd, %region_1.2_spmd} | conditional | flops 1176403968 | bytes 31097448 | solution.py:177
  53.8 1.0 broadcast_select_fusion.5
  54.8 1.3 %broadcast_select_fusion = (bf16[256,1152]{1,0:T(8,128)(2,1)}, bf16[256,1152]{1,0:T(8,128)(2,1)S(1)}, bf16[256,1152]{1,0:T(8,128)(2,1)}) fusion(pred[]{:T(512)S(6)} %lt.20, bf16[128,1152]{1,0:T(8,128)(2,1)S(1)} %get-tuple-element.67.x_ref, bf16[128,1152]{1,0:T(8,128)(2,1)S(1)} %get-tuple-element.118, bf16[128,1152]{1,0:T(8,128)(2,1)S(1)} %get-tuple-element.117, ...), kind=kLoop, calls=%fused_computation.2 | loop fusion | flops 3244032 | bytes 2949123 | tf_op jit(solution)/shard_map/cond/branch_1_fun/jit(_where)/select_n | solution.py:162
  56.1 4.3 %collective-permute-start.1 = (bf16[256,1152]{1,0:T(8,128)(2,1)}, bf16[256,1152]{1,0:T(8,128)(2,1)S(1)}, u32[]{:S(2)}, u32[]{:S(2)}) collective-permute-start(bf16[256,1152]{1,0:T(8,128)(2,1)} %get-tuple-element.116), channel_id=1, source_target_pairs={{0,16},{16,0},{32,48},{48,32},{64,80},{80,64},{96,112},{112,96},{1... | collective-permute-start | bytes 1769480 | tf_op jit(solution)/shard_map/cond/branch_1_fun/ppermute | solution.py:45
  60.5 4.4 %collective-permute-start.3 = (bf16[256,1152]{1,0:T(8,128)(2,1)}, bf16[256,1152]{1,0:T(8,128)(2,1)S(1)}, u32[]{:S(2)}, u32[]{:S(2)}) collective-permute-start(bf16[256,1152]{1,0:T(8,128)(2,1)} %get-tuple-element.114), channel_id=1, source_target_pairs={{0,96},{16,112},{32,0},{48,16},{64,32},{80,48},{96,64},{112,80},{1... | collective-permute-start | bytes 1769480 | tf_op jit(solution)/shard_map/cond/branch_1_fun/ppermute | solution.py:35
  64.9 0.1 broadcast_select_fusion.3
  65.0 1.9 %collective-permute-start = (bf16[256,1152]{1,0:T(8,128)(2,1)S(1)}, bf16[256,1152]{1,0:T(8,128)(2,1)S(1)}, u32[]{:S(2)}, u32[]{:S(2)}) collective-permute-start(bf16[256,1152]{1,0:T(8,128)(2,1)S(1)} %broadcast_select_fusion.3), channel_id=1, source_target_pairs={{0,32},{16,48},{32,64},{48,80},{64,96},{80,112},{96,0},{112,16},{1... | collective-permute-start | bytes 1769480 | tf_op jit(solution)/shard_map/cond/branch_1_fun/ppermute | solution.py:35
  66.9 0.0 collective-permute-done.1.rest_3_
  66.9 3.6 %collective-permute-start.2 = (bf16[256,1152]{1,0:T(8,128)(2,1)S(1)}, bf16[256,1152]{1,0:T(8,128)(2,1)S(1)}, u32[]{:S(2)}, u32[]{:S(2)}) collective-permute-start(bf16[256,1152]{1,0:T(8,128)(2,1)S(1)} %get-tuple-element.76), channel_id=1, source_target_pairs={{0,64},{16,80},{32,96},{48,112},{64,0},{80,16},{96,32},{112,48},{1... | collective-permute-start | bytes 1769480 | tf_op jit(solution)/shard_map/cond/branch_1_fun/ppermute | solution.py:35
  70.6 19.8 %collective-permute-done.3.rest_2_ = bf16[256,1152]{1,0:T(8,128)(2,1)S(1)} collective-permute-done((bf16[256,1152]{1,0:T(8,128)(2,1)}, bf16[256,1152]{1,0:T(8,128)(2,1)S(1)}, u32[]{:S(2)}, u32[]{:S(2)}) %collective-permute-start.3) | collective-permute-done | bytes 589856 | tf_op jit(solution)/shard_map/cond/branch_1_fun/ppermute | solution.py:35
  90.4 2.9 %collective-permute-start.6 = (bf16[256,1152]{1,0:T(8,128)(2,1)S(1)}, bf16[256,1152]{1,0:T(8,128)(2,1)S(1)}, u32[]{:S(2)}, u32[]{:S(2)}) collective-permute-start(bf16[256,1152]{1,0:T(8,128)(2,1)S(1)} %collective-permute-done.3.rest_2_), channel_id=1, source_target_pairs={{0,16},{16,0},{32,48},{48,32},{64,80},{80,64},{96,112},{112,96},{1... | collective-permute-start | bytes 1769480 | tf_op jit(solution)/shard_map/cond/branch_1_fun/ppermute | solution.py:45
  93.3 2.1 %collective-permute-done.rest_0_ = bf16[256,1152]{1,0:T(8,128)(2,1)S(1)} collective-permute-done((bf16[256,1152]{1,0:T(8,128)(2,1)S(1)}, bf16[256,1152]{1,0:T(8,128)(2,1)S(1)}, u32[]{:S(2)}, u32[]{:S(2)}) %collective-permute-start) | collective-permute-done | bytes 589856 | tf_op jit(solution)/shard_map/cond/branch_1_fun/ppermute | solution.py:35
  95.4 3.0 %collective-permute-start.4 = (bf16[256,1152]{1,0:T(8,128)(2,1)S(1)}, bf16[256,1152]{1,0:T(8,128)(2,1)S(1)}, u32[]{:S(2)}, u32[]{:S(2)}) collective-permute-start(bf16[256,1152]{1,0:T(8,128)(2,1)S(1)} %collective-permute-done.rest_0_), channel_id=1, source_target_pairs={{0,16},{16,0},{32,48},{48,32},{64,80},{80,64},{96,112},{112,96},{1... | collective-permute-start | bytes 1769480 | tf_op jit(solution)/shard_map/cond/branch_1_fun/ppermute | solution.py:45
  98.4 0.0 collective-permute-done.2.rest_1_
  98.4 1.9 %collective-permute-start.5 = (bf16[256,1152]{1,0:T(8,128)(2,1)S(1)}, bf16[256,1152]{1,0:T(8,128)(2,1)S(1)}, u32[]{:S(2)}, u32[]{:S(2)}) collective-permute-start(bf16[256,1152]{1,0:T(8,128)(2,1)S(1)} %collective-permute-done.2.rest_1_), channel_id=1, source_target_pairs={{0,16},{16,0},{32,48},{48,32},{64,80},{80,64},{96,112},{112,96},{1... | collective-permute-start | bytes 1769480 | tf_op jit(solution)/shard_map/cond/branch_1_fun/ppermute | solution.py:45
  100.3 0.0 collective-permute-done.6.rest_6_
  100.3 0.0 collective-permute-done.4.rest_4_
  100.4 1.9 %collective-permute-done.5.rest_5_ = bf16[256,1152]{1,0:T(8,128)(2,1)S(1)} collective-permute-done((bf16[256,1152]{1,0:T(8,128)(2,1)S(1)}, bf16[256,1152]{1,0:T(8,128)(2,1)S(1)}, u32[]{:S(2)}, u32[]{:S(2)}) %collective-permute-start.5) | collective-permute-done | bytes 589856 | tf_op jit(solution)/shard_map/cond/branch_1_fun/ppermute | solution.py:45
  102.3 6.8 %branch_1_fun.1 = (f32[128,128]{1,0:T(8,128)}, f32[128,1152]{1,0:T(8,128)S(1)}, f32[128,1152]{1,0:T(8,128)S(1)}) custom-call(f32[1]{0:T(128)} %get-tuple-element.65.scale, f32[1]{0:T(128)} %get-tuple-element.66.bias, bf16[128,1152]{1,0:T(8,128)(2,1)S(1)} %get-tuple-element.67.x_ref, bf16[128,1152]{1,0:T(8,128)(2,1)S(1)} %get-tuple-element.68.y_ref, ...), custom_call_target="tpu_custom_call" | custom-call | flops 1170210816 | bytes 8388608 | tf_op jit(solution)/shard_map/cond/branch_1_fun/pallas_call | solution.py:131
  109.1 0.0 collective-permute-done.10.yg_ref
  109.1 0.0 collective-permute-done.11.xg_ref
  109.1 2.9 %shard_map.77 = (f32[1,128]{1,0:T(1,128)}, f32[128,1152]{1,0:T(8,128)}, f32[128,1152]{1,0:T(8,128)}) custom-call(f32[1]{0:T(128)S(6)} %copy.15.scale, f32[1]{0:T(128)S(6)} %copy.16.bias, bf16[128,1152]{1,0:T(8,128)(2,1)S(1)} %copy-done, bf16[128,1152]{1,0:T(8,128)(2,1)S(1)} %copy-done.1, bf16[128,1152]{1,0:T(8,128)(2,1)S(1)} %collective-permute-done.10.yg_ref, ...), custom_call_target="tpu_custom_call" | custom-call | flops 150994944 | bytes 8388608 | tf_op jit(solution)/shard_map/pallas_call | solution.py:131
Async XLA Ops:
  0.6 16.8 %copy-start = (bf16[128,1152]{1,0:T(8,128)(2,1)S(1)}, bf16[128,1152]{1,0:T(8,128)(2,1)}, u32[]{:S(2)}) copy-start(bf16[128,1152]{1,0:T(8,128)(2,1)} %x_ref.1) | copy-start | bytes 884740
  0.6 14.8 %copy-start.1 = (bf16[128,1152]{1,0:T(8,128)(2,1)S(1)}, bf16[128,1152]{1,0:T(8,128)(2,1)}, u32[]{:S(2)}) copy-start(bf16[128,1152]{1,0:T(8,128)(2,1)} %y_ref.1) | copy-start | bytes 884740
  0.7 53.1 %copy-start.2 = (s32[1,128]{1,0:T(1,128)S(1)}, s32[1,128]{1,0:T(1,128)}, u32[]{:S(2)}) copy-start(s32[1,128]{1,0:T(1,128)} %param.9) | copy-start | bytes 1540
  1.7 30.2 %collective-permute-start.9 = (bf16[128,1152]{1,0:T(8,128)(2,1)S(1)}, bf16[128,1152]{1,0:T(8,128)(2,1)S(1)}, u32[]{:S(2)}, u32[]{:S(2)}) collective-permute-start(bf16[128,1152]{1,0:T(8,128)(2,1)S(1)} %broadcast_select_fusion.6), channel_id=1, source_target_pairs={{896,0},{912,16},{928,32},{944,48},{960,64},{976,80},{992,96},{100... | collective-permute-start | bytes 884744 | tf_op jit(solution)/shard_map/ppermute | solution.py:41
  15.5 21.0 %collective-permute-start.7 = (bf16[128,1152]{1,0:T(8,128)(2,1)S(1)}, bf16[128,1152]{1,0:T(8,128)(2,1)}, u32[]{:S(2)}, u32[]{:S(2)}) collective-permute-start(bf16[128,1152]{1,0:T(8,128)(2,1)S(1)} %copy-done.1), channel_id=1, source_target_pairs={{0,128},{1,129},{2,130},{3,131},{4,132},{5,133},{6,134},{7,135},{8... | collective-permute-start | bytes 884744 | tf_op jit(solution)/shard_map/ppermute | solution.py:27
  17.4 19.8 %collective-permute-start.8 = (bf16[128,1152]{1,0:T(8,128)(2,1)S(1)}, bf16[128,1152]{1,0:T(8,128)(2,1)}, u32[]{:S(2)}, u32[]{:S(2)}) collective-permute-start(bf16[128,1152]{1,0:T(8,128)(2,1)S(1)} %copy-done), channel_id=1, source_target_pairs={{0,911},{1,896},{2,897},{3,898},{4,899},{5,900},{6,901},{7,902},{8... | collective-permute-start | bytes 884744 | tf_op jit(solution)/shard_map/ppermute | solution.py:27
  37.2 71.9 %collective-permute-start.10 = (bf16[128,1152]{1,0:T(8,128)(2,1)}, bf16[128,1152]{1,0:T(8,128)(2,1)S(1)}, u32[]{:S(2)}, u32[]{:S(2)}) collective-permute-start(bf16[128,1152]{1,0:T(8,128)(2,1)} %collective-permute-done.7), channel_id=1, source_target_pairs={{0,896},{1,897},{2,898},{3,899},{4,900},{5,901},{6,902},{7,903},{8... | collective-permute-start | bytes 884744 | tf_op jit(solution)/shard_map/ppermute | solution.py:27
  43.6 65.5 %collective-permute-start.11 = (bf16[128,1152]{1,0:T(8,128)(2,1)}, bf16[128,1152]{1,0:T(8,128)(2,1)S(1)}, u32[]{:S(2)}, u32[]{:S(2)}) collective-permute-start(bf16[128,1152]{1,0:T(8,128)(2,1)} %collective-permute-done.8), channel_id=1, source_target_pairs={{0,143},{1,128},{2,129},{3,130},{4,131},{5,132},{6,133},{7,134},{8... | collective-permute-start | bytes 884744 | tf_op jit(solution)/shard_map/ppermute | solution.py:27
  56.1 10.8 %collective-permute-start.1 = (bf16[256,1152]{1,0:T(8,128)(2,1)}, bf16[256,1152]{1,0:T(8,128)(2,1)S(1)}, u32[]{:S(2)}, u32[]{:S(2)}) collective-permute-start(bf16[256,1152]{1,0:T(8,128)(2,1)} %get-tuple-element.116), channel_id=1, source_target_pairs={{0,16},{16,0},{32,48},{48,32},{64,80},{80,64},{96,112},{112,96},{1... | collective-permute-start | bytes 1769480 | tf_op jit(solution)/shard_map/cond/branch_1_fun/ppermute | solution.py:45
  60.5 29.9 %collective-permute-start.3 = (bf16[256,1152]{1,0:T(8,128)(2,1)}, bf16[256,1152]{1,0:T(8,128)(2,1)S(1)}, u32[]{:S(2)}, u32[]{:S(2)}) collective-permute-start(bf16[256,1152]{1,0:T(8,128)(2,1)} %get-tuple-element.114), channel_id=1, source_target_pairs={{0,96},{16,112},{32,0},{48,16},{64,32},{80,48},{96,64},{112,80},{1... | collective-permute-start | bytes 1769480 | tf_op jit(solution)/shard_map/cond/branch_1_fun/ppermute | solution.py:35
  65.0 30.4 %collective-permute-start = (bf16[256,1152]{1,0:T(8,128)(2,1)S(1)}, bf16[256,1152]{1,0:T(8,128)(2,1)S(1)}, u32[]{:S(2)}, u32[]{:S(2)}) collective-permute-start(bf16[256,1152]{1,0:T(8,128)(2,1)S(1)} %broadcast_select_fusion.3), channel_id=1, source_target_pairs={{0,32},{16,48},{32,64},{48,80},{64,96},{80,112},{96,0},{112,16},{1... | collective-permute-start | bytes 1769480 | tf_op jit(solution)/shard_map/cond/branch_1_fun/ppermute | solution.py:35
  66.9 31.5 %collective-permute-start.2 = (bf16[256,1152]{1,0:T(8,128)(2,1)S(1)}, bf16[256,1152]{1,0:T(8,128)(2,1)S(1)}, u32[]{:S(2)}, u32[]{:S(2)}) collective-permute-start(bf16[256,1152]{1,0:T(8,128)(2,1)S(1)} %get-tuple-element.76), channel_id=1, source_target_pairs={{0,64},{16,80},{32,96},{48,112},{64,0},{80,16},{96,32},{112,48},{1... | collective-permute-start | bytes 1769480 | tf_op jit(solution)/shard_map/cond/branch_1_fun/ppermute | solution.py:35
  90.4 9.9 %collective-permute-start.6 = (bf16[256,1152]{1,0:T(8,128)(2,1)S(1)}, bf16[256,1152]{1,0:T(8,128)(2,1)S(1)}, u32[]{:S(2)}, u32[]{:S(2)}) collective-permute-start(bf16[256,1152]{1,0:T(8,128)(2,1)S(1)} %collective-permute-done.3.rest_2_), channel_id=1, source_target_pairs={{0,16},{16,0},{32,48},{48,32},{64,80},{80,64},{96,112},{112,96},{1... | collective-permute-start | bytes 1769480 | tf_op jit(solution)/shard_map/cond/branch_1_fun/ppermute | solution.py:45
  95.4 5.0 %collective-permute-start.4 = (bf16[256,1152]{1,0:T(8,128)(2,1)S(1)}, bf16[256,1152]{1,0:T(8,128)(2,1)S(1)}, u32[]{:S(2)}, u32[]{:S(2)}) collective-permute-start(bf16[256,1152]{1,0:T(8,128)(2,1)S(1)} %collective-permute-done.rest_0_), channel_id=1, source_target_pairs={{0,16},{16,0},{32,48},{48,32},{64,80},{80,64},{96,112},{112,96},{1... | collective-permute-start | bytes 1769480 | tf_op jit(solution)/shard_map/cond/branch_1_fun/ppermute | solution.py:45
  98.4 3.9 %collective-permute-start.5 = (bf16[256,1152]{1,0:T(8,128)(2,1)S(1)}, bf16[256,1152]{1,0:T(8,128)(2,1)S(1)}, u32[]{:S(2)}, u32[]{:S(2)}) collective-permute-start(bf16[256,1152]{1,0:T(8,128)(2,1)S(1)} %collective-permute-done.2.rest_1_), channel_id=1, source_target_pairs={{0,16},{16,0},{32,48},{48,32},{64,80},{80,64},{96,112},{112,96},{1... | collective-permute-start | bytes 1769480 | tf_op jit(solution)/shard_map/cond/branch_1_fun/ppermute | solution.py:45

commit v5 on v4

v5 whole, which is shorter than its diff:
```python
import functools

import jax
import jax.numpy as jnp
from jax import lax
from jax.experimental import pallas as pl
from jax.experimental.pallas import tpu as pltpu
from jax.sharding import PartitionSpec as P

SPAN = 8
CORES = 2
CHIPS = SPAN // CORES
F32 = jnp.float32
BF16 = jnp.bfloat16


def along_ring(x, by):
    blks, groups = lax.axis_size("blk"), lax.axis_size("group")
    length = blks // SPAN
    pairs = []
    for blk in range(blks):
        row, place = divmod(blk, SPAN)
        for group in range(groups):
            to = (group * length + row + by) % (groups * length)
            to_blk, to_group = to % length * SPAN + place, to // length
            pairs.append((blk * groups + group, to_blk * groups + to_group))
    return lax.ppermute(x, ("blk", "group"), pairs)


def in_row(x, by):
    pairs = []
    for i in range(lax.axis_size("blk")):
        first, place = i - i % SPAN, i % SPAN
        pairs.append((i, first + (place + CORES * by) % SPAN))
    return lax.ppermute(x, "blk", pairs)


def around(x):
    last = lax.axis_size("blk") - SPAN
    pairs = [(last + i, i) for i in range(SPAN)] + [(i, last + i) for i in range(SPAN)]
    return lax.ppermute(x, "blk", pairs)


def to_twin(x):
    return lax.ppermute(x, "blk", [(i, i ^ 1) for i in range(lax.axis_size("blk"))])


def row_inverse(values):
    floats = values.astype(F32)
    return lax.rsqrt(jnp.sum(floats * floats, axis=-1, keepdims=True) + 1e-06)


def unit_rows(values):
    return (values.astype(F32) * row_inverse(values)).astype(BF16)


def by_rows(left, right):
    return lax.dot_general(left, right, (((1,), (1,)), ((), ())), preferred_element_type=F32)


def by_cols(left, right):
    return lax.dot_general(left, right, (((0,), (0,)), ((), ())), preferred_element_type=F32)


def product(left, right):
    return jnp.dot(left, right, preferred_element_type=F32)


def loss_and_slope(u):
    small = jnp.exp(-jnp.abs(u))
    whole = 1.0 + small
    return (
        jnp.maximum(u, 0.0) + jnp.log1p(small),
        jnp.where(u >= 0.0, 1.0, small) / whole,
    )


TEXT, IMAGE = 0, 1


def add_block(other, role, tau, offset, units_ref, loss_ref, grads_ref):
    unit = unit_rows(other)
    loss, slope = loss_and_slope(tau * by_rows(units_ref[role], unit) + offset)
    loss_ref[...] += jnp.where(role == TEXT, loss, 0.0)
    grads_ref[role] += product(slope.astype(BF16), unit)


def add_blocks(roles, refs, tau, offset, units_ref, loss_ref, grads_ref):
    rows = units_ref.shape[1]
    singles, twin = refs[:-1], refs[-1]
    for by, ref in enumerate(singles, 1):
        add_block(ref[...], roles[by], tau, offset, units_ref, loss_ref, grads_ref)
    for by in range(CHIPS):
        add_block(twin[by * rows : (by + 1) * rows, :], roles[by], tau, offset, units_ref, loss_ref, grads_ref)


def first_kernel(scale, bias, roles, x_ref, y_ref, pos_ref, *rest):
    refs, (loss_ref, grads_ref, units_ref) = rest[:-3], rest[-3:]
    tau, offset = scale[0], bias[0]
    rows = x_ref.shape[0]
    x, y = unit_rows(x_ref[...]), unit_rows(y_ref[...])
    units_ref[IMAGE] = y
    units_ref[TEXT] = x
    logit = tau * by_rows(x, y) + offset
    place = lax.broadcasted_iota(jnp.int32, (rows, rows), 1).astype(F32)
    match = jnp.broadcast_to(pos_ref[...].astype(F32), (rows, rows)).T
    away = jnp.where(match == place, -1.0, 1.0)
    loss, slope = loss_and_slope(away * logit)
    slope = (slope * away).astype(BF16)
    loss_ref[...] = loss
    grads_ref[TEXT] = product(slope, y)
    grads_ref[IMAGE] = by_cols(slope, x)
    add_blocks(roles, refs, tau, offset, units_ref, loss_ref, grads_ref)


def second_kernel(scale, bias, roles, units_ref, loss_in, grads_in, *rest):
    refs, (loss_ref, grads_ref) = rest[:-2], rest[-2:]
    loss_ref[...] = loss_in[...]
    grads_ref[...] = grads_in[...]
    add_blocks(roles, refs, scale[0], bias[0], units_ref, loss_ref, grads_ref)


def last_kernel(scale, bias, x_ref, y_ref, yg_ref, xg_ref, units_ref, loss_in, grads_in, loss_ref, ix_ref, ty_ref):
    tau, offset = scale[0], bias[0]
    rows = x_ref.shape[0]
    unit = unit_rows(yg_ref[...])
    add, slope = loss_and_slope(tau * by_rows(units_ref[TEXT], unit) + offset)
    loss_ref[...] = jnp.sum((loss_in[...] + add).T, axis=0, keepdims=True) / F32((SPAN + 1) * rows)
    gx = (grads_in[TEXT] + product(slope.astype(BF16), unit)) * tau
    x = x_ref[...]
    x_inv = row_inverse(x)
    xn = x.astype(F32) * x_inv
    ix_ref[...] = (gx - xn * jnp.sum(xn * gx, axis=-1, keepdims=True)) * x_inv
    unit = unit_rows(xg_ref[...])
    _, slope = loss_and_slope(tau * by_rows(units_ref[IMAGE], unit) + offset)
    gy = (grads_in[IMAGE] + product(slope.astype(BF16), unit)) * tau
    y = y_ref[...]
    y_inv = row_inverse(y)
    yn = y.astype(F32) * y_inv
    ty_ref[...] = (gy - yn * jnp.sum(yn * gy, axis=-1, keepdims=True)) * y_inv


def call(kernel, outs, blocks, scalars, *args):
    flops = blocks * 4 * 128 * 128 * 1152
    return pl.pallas_call(
        kernel,
        out_shape=[jax.ShapeDtypeStruct(shape, kind) for shape, kind in outs],
        in_specs=[pl.BlockSpec(memory_space=pltpu.SMEM)] * len(scalars)
        + [pl.BlockSpec(memory_space=pltpu.VMEM)] * len(args),
        out_specs=[pl.BlockSpec(memory_space=pltpu.VMEM)] * len(outs),
        compiler_params=pltpu.CompilerParams(vmem_limit_bytes=40 * 1024 * 1024),
        cost_estimate=pl.CostEstimate(flops=flops, bytes_accessed=blocks * 1024 * 1024, transcendentals=0),
    )(*scalars, *args)


def local(image_feats, text_feats, positive, scale, bias):
    x, y = image_feats, text_feats
    rows, width = x.shape
    index = lax.axis_index("blk")
    place = index % SPAN
    chip, core = place // CORES, place % CORES
    last = lax.axis_size("blk") - SPAN
    length = lax.axis_size("blk") // SPAN
    shifts = range(1, CHIPS)
    wrapped = around(jnp.where(index >= last, y, x))
    y_back = along_ring(y, 1)
    x_next = along_ring(x, -1)
    first = {by: jnp.where(chip + by < CHIPS, y, x) for by in shifts}
    got = {by: in_row(first[by], by) for by in (1, CHIPS - 1)}
    first[2], got[1] = lax.optimization_barrier((first[2], got[1]))
    got[2] = in_row(first[2], 2)
    got = [got[by] for by in shifts]
    y_back, x_next, wrapped = lax.optimization_barrier((y_back, x_next, wrapped))
    y_outer = along_ring(y_back, length - 1)
    x_outer = along_ring(x_next, 1 - length)
    loss_out, grads_out = ((rows, rows), F32), ((2, rows, width), F32)
    units_out = ((2, rows, width), BF16)
    roles = jnp.stack([1 - core] + [(chip < by).astype(jnp.int32) for by in shifts])

    def inner(_):
        twin = to_twin(jnp.concatenate([jnp.where(core == 0, y, x)] + got, axis=0))
        loss, grads, units = call(
            first_kernel, [loss_out, grads_out, units_out], 8, (scale, bias, roles), x, y, positive, *got, twin
        )
        text = jnp.where(index < SPAN, wrapped, y_back)
        image = jnp.where(index >= last, wrapped, x_next)
        then = [jnp.where(chip + by < CHIPS, image, text) for by in shifts]
        then[1], twin = lax.optimization_barrier((then[1], twin))
        later = [in_row(block, by) for by, block in zip(shifts, then)]
        twin = to_twin(jnp.concatenate([jnp.where(core == 0, image, text)] + later, axis=0))
        loss, grads = call(
            second_kernel, [loss_out, grads_out], 7, (scale, bias, 1 - roles), units, loss, grads, *later, twin
        )
        return loss, grads, units

    def skip(_):
        return tuple(jnp.zeros(*out) for out in (loss_out, grads_out, units_out))

    go = lax.optimization_barrier(jnp.int32(1))
    loss, grads, units = lax.cond(go > 0, inner, skip, 0)
    block = ((rows, width), F32)
    loss, image_grad, text_grad = call(
        last_kernel, [((1, rows), F32), block, block], 2, (scale, bias), x, y, y_outer, x_outer, units, loss, grads
    )
    return (loss[0], image_grad, text_grad)


def solution(mesh):
    rows = P(("blk", "group"), None)
    return jax.shard_map(
        local,
        mesh=mesh,
        in_specs=(rows, rows, rows, P(), P()),
        out_specs=(P(("blk", "group")), rows, rows),
        check_vma=False,
    )
```

time: 113 us -> 104 us (0.920)
  waiting for transfers between devices: 29.2 us -> 10.1 us
  Pallas kernels: 9.68 us -> 15 us
  starting transfers between devices: 67.4 us -> 71.7 us
  local copies, waits for them, and re-layouts: 0.01 us -> 1.54 us
    ppermute x3 -> x6, waiting for transfers between devices: 21.9 us -> 10.1 us  [in_row(): return lax.ppermute(x, 'blk', pairs)]
    ppermute x3 -> x6, starting transfers between devices: 9.93 us -> 19.4 us  [in_row(): return lax.ppermute(x, 'blk', pairs)]
    pallas_call x2 -> x3, Pallas kernels: 9.68 us -> 15 us  [call(): pl.pallas_call(kernel, out_shape=[jax.ShapeDtypeStruct(shape, kind) for s...]
    ppermute x4, waiting for transfers between devices: 5.33 us -> 0.01 us  [along_ring(): return lax.ppermute(x, ('blk', 'group'), pairs)]
    ppermute x4 -> x2, starting transfers between devices: 12.1 us -> 7.87 us  [to_twin(): lax.ppermute(x, 'blk', [(i, i ^ 1) for i in range(lax.axis_size('blk'))])]
    ppermute x4 -> x2, waiting for transfers between devices: 1.96 us -> 0.01 us  [to_twin(): lax.ppermute(x, 'blk', [(i, i ^ 1) for i in range(lax.axis_size('blk'))])]
  transfers between devices with their start and end apart: 12 -> 13, of which waited for: 5 -> 2; matrix products, arithmetic and copies ran while one was open for 2% -> 1% of each run, Pallas kernels for 6% -> 11%
where the time goes in v5:
time: 104 us
  starting transfers between devices  71.7 us (69%)
  Pallas kernels  15 us (14%)
  waiting for transfers between devices  10.1 us (10%)
  other arithmetic  2.76 us (3%)
  between operations  2.15 us (2%)
  local copies, waits for them, and re-layouts  1.54 us (1%)
    ppermute x4, starting transfers between devices, along_ring(): return lax.ppermute(x, ('blk', 'group'), pairs)  31.6 us
    ppermute x6, starting transfers between devices, in_row(): return lax.ppermute(x, 'blk', pairs)  19.4 us
    pallas_call x3, Pallas kernels, call(): pl.pallas_call(kernel, out_shape=[jax.ShapeDtypeStruct(shape, kind) for s...  15 us
    ppermute x1, starting transfers between devices, around(): return lax.ppermute(x, 'blk', pairs)  12.9 us
    ppermute x6, waiting for transfers between devices, in_row(): return lax.ppermute(x, 'blk', pairs)  10.1 us
    ppermute x2, starting transfers between devices, to_twin(): lax.ppermute(x, 'blk', [(i, i ^ 1) for i in range(lax.axis_size('blk'))])  7.87 us
  transfers between devices with their start and end apart: 13, of which 2 were waited for; matrix products, arithmetic and copies ran while one was open for 1% of the time, Pallas kernels for 11%

profile of v5, /device:TPU:1, one launch (start us, length us, event | category | flops | bytes accessed | tf_op | source)
XLA Modules:
  0.0 103.5 jit_solution(1626427156654599959)
XLA Ops:
  0.6 0.0 copy-start
  0.6 0.0 copy-start.1
  0.7 0.0 copy-start.9
  0.7 1.2 %broadcast_select_fusion.7 = (bf16[128,1152]{1,0:T(8,128)(2,1)S(1)}, bf16[128,1152]{1,0:T(8,128)(2,1)S(1)}, bf16[128,1152]{1,0:T(8,128)(2,1)S(1)}, bf16[128,1152]{1,0:T(8,128)(2,1)S(1)}) fusion(bf16[128,1152]{1,0:T(8,128)(2,1)} %y_ref.1, bf16[128,1152]{1,0:T(8,128)(2,1)} %x_ref.1, pred[]{:T(512)S(6)} %lt.47, pred[]{:T(512)S(6)} %lt.46, pred[]{:T(512)S(6)} %lt.45, ...), kind=kLoop, calls=%fused_computation.10 | loop fusion | flops 589824 | bytes 1769476 | tf_op jit(solution)/shard_map/jit(_where)/select_n | solution.py:168
  1.9 3.9 %collective-permute-start.10 = (bf16[128,1152]{1,0:T(8,128)(2,1)S(1)}, bf16[128,1152]{1,0:T(8,128)(2,1)S(1)}, u32[]{:S(2)}, u32[]{:S(2)}) collective-permute-start(bf16[128,1152]{1,0:T(8,128)(2,1)S(1)} %get-tuple-element.85), channel_id=1, source_target_pairs={{0,32},{16,48},{32,64},{48,80},{64,96},{80,112},{96,0},{112,16},{1... | collective-permute-start | bytes 884744 | tf_op jit(solution)/shard_map/ppermute | solution.py:35
  5.9 12.9 %collective-permute-start.7 = (bf16[128,1152]{1,0:T(8,128)(2,1)S(1)}, bf16[128,1152]{1,0:T(8,128)(2,1)S(1)}, u32[]{:S(2)}, u32[]{:S(2)}) collective-permute-start(bf16[128,1152]{1,0:T(8,128)(2,1)S(1)} %get-tuple-element.87), channel_id=1, source_target_pairs={{896,0},{912,16},{928,32},{944,48},{960,64},{976,80},{992,96},{100... | collective-permute-start | bytes 884744 | tf_op jit(solution)/shard_map/ppermute | solution.py:41
  18.8 1.9 %collective-permute-start.5 = (bf16[128,1152]{1,0:T(8,128)(2,1)S(1)}, bf16[128,1152]{1,0:T(8,128)(2,1)}, u32[]{:S(2)}, u32[]{:S(2)}) collective-permute-start(bf16[128,1152]{1,0:T(8,128)(2,1)S(1)} %copy-done.1), channel_id=1, source_target_pairs={{0,128},{1,129},{2,130},{3,131},{4,132},{5,133},{6,134},{7,135},{8... | collective-permute-start | bytes 884744 | tf_op jit(solution)/shard_map/ppermute | solution.py:27
  20.7 14.5 %collective-permute-start.6 = (bf16[128,1152]{1,0:T(8,128)(2,1)S(1)}, bf16[128,1152]{1,0:T(8,128)(2,1)}, u32[]{:S(2)}, u32[]{:S(2)}) collective-permute-start(bf16[128,1152]{1,0:T(8,128)(2,1)S(1)} %copy-done), channel_id=1, source_target_pairs={{0,911},{1,896},{2,897},{3,898},{4,899},{5,900},{6,901},{7,902},{8... | collective-permute-start | bytes 884744 | tf_op jit(solution)/shard_map/ppermute | solution.py:27
  35.2 3.4 %collective-permute-start.12 = (bf16[128,1152]{1,0:T(8,128)(2,1)S(1)}, bf16[128,1152]{1,0:T(8,128)(2,1)S(1)}, u32[]{:S(2)}, u32[]{:S(2)}) collective-permute-start(bf16[128,1152]{1,0:T(8,128)(2,1)S(1)} %get-tuple-element.84), channel_id=1, source_target_pairs={{0,96},{16,112},{32,0},{48,16},{64,32},{80,48},{96,64},{112,80},{1... | collective-permute-start | bytes 884744 | tf_op jit(solution)/shard_map/ppermute | solution.py:35
  38.6 0.0 collective-permute-done.10
  38.6 3.4 %collective-permute-start.11 = (bf16[128,1152]{1,0:T(8,128)(2,1)S(1)}, bf16[128,1152]{1,0:T(8,128)(2,1)S(1)}, u32[]{:S(2)}, u32[]{:S(2)}) collective-permute-start(bf16[128,1152]{1,0:T(8,128)(2,1)S(1)} %get-tuple-element.68), channel_id=1, source_target_pairs={{0,64},{16,80},{32,96},{48,112},{64,0},{80,16},{96,32},{112,48},{1... | collective-permute-start | bytes 884744 | tf_op jit(solution)/shard_map/ppermute | solution.py:35
  42.1 0.0 collective-permute-done.7
  42.1 0.0 copy-start.8
  42.1 0.0 collective-permute-done.5
  42.1 0.0 collective-permute-done.6
  42.1 0.7 copy-done.8
  42.8 3.8 %collective-permute-start.8 = (bf16[128,1152]{1,0:T(8,128)(2,1)}, bf16[128,1152]{1,0:T(8,128)(2,1)S(1)}, u32[]{:S(2)}, u32[]{:S(2)}) collective-permute-start(bf16[128,1152]{1,0:T(8,128)(2,1)} %collective-permute-done.5), channel_id=1, source_target_pairs={{0,896},{1,897},{2,898},{3,899},{4,900},{5,901},{6,902},{7,903},{8... | collective-permute-start | bytes 884744 | tf_op jit(solution)/shard_map/ppermute | solution.py:27
  46.6 11.4 %collective-permute-start.9 = (bf16[128,1152]{1,0:T(8,128)(2,1)}, bf16[128,1152]{1,0:T(8,128)(2,1)S(1)}, u32[]{:S(2)}, u32[]{:S(2)}) collective-permute-start(bf16[128,1152]{1,0:T(8,128)(2,1)} %collective-permute-done.6), channel_id=1, source_target_pairs={{0,143},{1,128},{2,129},{3,130},{4,131},{5,132},{6,133},{7,134},{8... | collective-permute-start | bytes 884744 | tf_op jit(solution)/shard_map/ppermute | solution.py:27
  59.3 0.1 pad_add_fusion
  59.4 0.0 collective-permute-done.12
  59.4 0.0 collective-permute-done.11
  59.4 40.9 %conditional.1 = (f32[128,128]{1,0:T(8,128)}, f32[2,128,1152]{2,1,0:T(8,128)S(1)}, bf16[2,128,1152]{2,1,0:T(8,128)(2,1)}) conditional(s32[]{:T(128)} %convert_element_type.2, () %tuple.20, (s32[4]{0:T(128)S(1)}, s32[]{:T(128)}, bf16[128,1152]{1,0:T(8,128)(2,1)S(1)}, bf16[128,1152]{1,0:T(8,128)(2,1)S(1)}, bf16[128,1152]{1,0:T(8,128)(2,1)S(1)}, ...), branch_computations={%region_0.1_spmd, %region_1.2_spmd} | conditional | flops 1142931456 | bytes 44630536 | solution.py:200
  59.4 0.0 copy-start.2
  59.5 0.6 copy-done.2
  60.1 0.1 copy-done.4
  60.2 0.1 copy-done.6
  60.3 0.1 pad_maximum_fusion
  60.4 4.5 %collective-permute-start = (bf16[512,1152]{1,0:T(8,128)(2,1)S(1)}, bf16[512,1152]{1,0:T(8,128)(2,1)S(1)}, u32[]{:S(2)}, u32[]{:S(2)}) collective-permute-start(bf16[512,1152]{1,0:T(8,128)(2,1)S(1)} %pad_maximum_fusion), channel_id=1, source_target_pairs={{0,16},{16,0},{32,48},{48,32},{64,80},{80,64},{96,112},{112,96},{1... | collective-permute-start | bytes 3538952 | tf_op jit(solution)/shard_map/cond/branch_1_fun/ppermute | solution.py:45
  65.0 1.1 %broadcast_select_fusion.5 = (bf16[128,1152]{1,0:T(8,128)(2,1)S(1)}, bf16[128,1152]{1,0:T(8,128)(2,1)S(1)}, bf16[128,1152]{1,0:T(8,128)(2,1)S(1)}) fusion(pred[]{:T(512)S(6)} %eq.6, bf16[128,1152]{1,0:T(8,128)(2,1)} %get-tuple-element.45, bf16[128,1152]{1,0:T(8,128)(2,1)} %get-tuple-element.47, pred[]{:T(512)S(6)} %lt.29, ...), kind=kLoop, calls=%fused_computation.7 | loop fusion | flops 442368 | bytes 1769475 | tf_op jit(solution)/shard_map/cond/branch_1_fun/jit(_where)/select_n | solution.py:190
  66.1 0.1 broadcast_select_fusion
  66.2 2.2 %collective-permute-start.1 = (bf16[128,1152]{1,0:T(8,128)(2,1)S(1)}, bf16[128,1152]{1,0:T(8,128)(2,1)S(1)}, u32[]{:S(2)}, u32[]{:S(2)}) collective-permute-start(bf16[128,1152]{1,0:T(8,128)(2,1)S(1)} %get-tuple-element.83), channel_id=1, source_target_pairs={{0,32},{16,48},{32,64},{48,80},{64,96},{80,112},{96,0},{112,16},{1... | collective-permute-start | bytes 884744 | tf_op jit(solution)/shard_map/cond/branch_1_fun/ppermute | solution.py:35
  68.5 4.3 %collective-permute-start.3 = (bf16[128,1152]{1,0:T(8,128)(2,1)S(1)}, bf16[128,1152]{1,0:T(8,128)(2,1)S(1)}, u32[]{:S(2)}, u32[]{:S(2)}) collective-permute-start(bf16[128,1152]{1,0:T(8,128)(2,1)S(1)} %get-tuple-element.81), channel_id=1, source_target_pairs={{0,96},{16,112},{32,0},{48,16},{64,32},{80,48},{96,64},{112,80},{1... | collective-permute-start | bytes 884744 | tf_op jit(solution)/shard_map/cond/branch_1_fun/ppermute | solution.py:35
  72.7 0.0 collective-permute-done.rest_3_
  72.7 2.1 %collective-permute-start.2 = (bf16[128,1152]{1,0:T(8,128)(2,1)S(1)}, bf16[128,1152]{1,0:T(8,128)(2,1)S(1)}, u32[]{:S(2)}, u32[]{:S(2)}) collective-permute-start(bf16[128,1152]{1,0:T(8,128)(2,1)S(1)} %get-tuple-element.48), channel_id=1, source_target_pairs={{0,64},{16,80},{32,96},{48,112},{64,0},{80,16},{96,32},{112,48},{1... | collective-permute-start | bytes 884744 | tf_op jit(solution)/shard_map/cond/branch_1_fun/ppermute | solution.py:35
  74.9 3.1 %collective-permute-done.1.rest_0_ = bf16[128,1152]{1,0:T(8,128)(2,1)S(1)} collective-permute-done((bf16[128,1152]{1,0:T(8,128)(2,1)S(1)}, bf16[128,1152]{1,0:T(8,128)(2,1)S(1)}, u32[]{:S(2)}, u32[]{:S(2)}) %collective-permute-start.1) | collective-permute-done | bytes 294944 | tf_op jit(solution)/shard_map/cond/branch_1_fun/ppermute | solution.py:35
  78.0 7.0 %collective-permute-done.3.rest_2_ = bf16[128,1152]{1,0:T(8,128)(2,1)S(1)} collective-permute-done((bf16[128,1152]{1,0:T(8,128)(2,1)S(1)}, bf16[128,1152]{1,0:T(8,128)(2,1)S(1)}, u32[]{:S(2)}, u32[]{:S(2)}) %collective-permute-start.3) | collective-permute-done | bytes 294944 | tf_op jit(solution)/shard_map/cond/branch_1_fun/ppermute | solution.py:35
  85.0 0.0 collective-permute-done.2.rest_1_
  85.0 0.1 pad_maximum_fusion.1
  85.1 3.3 %collective-permute-start.4 = (bf16[512,1152]{1,0:T(8,128)(2,1)S(1)}, bf16[512,1152]{1,0:T(8,128)(2,1)S(1)}, u32[]{:S(2)}, u32[]{:S(2)}) collective-permute-start(bf16[512,1152]{1,0:T(8,128)(2,1)S(1)} %pad_maximum_fusion.1), channel_id=1, source_target_pairs={{0,16},{16,0},{32,48},{48,32},{64,80},{80,64},{96,112},{112,96},{1... | collective-permute-start | bytes 3538952 | tf_op jit(solution)/shard_map/cond/branch_1_fun/ppermute | solution.py:45
  88.5 0.0 copy-done.3
  88.5 0.0 copy-done.5
  88.5 0.0 copy-done.7
  88.5 6.0 %branch_1_fun.2 = (f32[128,128]{1,0:T(8,128)S(1)}, f32[2,128,1152]{2,1,0:T(8,128)S(1)}, bf16[2,128,1152]{2,1,0:T(8,128)(2,1)}) custom-call(f32[1]{0:T(128)} %get-tuple-element.30.scale, f32[1]{0:T(128)} %get-tuple-element.31.bias, s32[4]{0:T(128)S(1)} %get-tuple-element.32.roles, bf16[128,1152]{1,0:T(8,128)(2,1)S(1)} %get-tuple-element.33.x_ref, ...), custom_call_target="tpu_custom_call" | custom-call | flops 603979776 | bytes 8388608 | tf_op jit(solution)/shard_map/cond/branch_1_fun/pallas_call | solution.py:145
  94.5 0.0 collective-permute-done.4.rest_3_
  94.5 5.9 %branch_1_fun.3 = (f32[128,128]{1,0:T(8,128)}, f32[2,128,1152]{2,1,0:T(8,128)S(1)}) custom-call(f32[1]{0:T(128)} %get-tuple-element.30.scale, f32[1]{0:T(128)} %get-tuple-element.31.bias, s32[4]{0:T(128)S(1)} %broadcast_subtract_fusion.roles, bf16[2,128,1152]{2,1,0:T(8,128)(2,1)} %get-tuple-element.93.units_ref, f32[128,128]{1,0:T(8,128)S(1)} %get-tuple-element.41.loss_in, ...), custom_call_target="tpu_custom_call" | custom-call | flops 528482304 | bytes 7340032 | tf_op jit(solution)/shard_map/cond/branch_1_fun/pallas_call | solution.py:145
  100.3 0.0 collective-permute-done.8.yg_ref
  100.3 0.0 collective-permute-done.9.xg_ref
  100.3 3.2 %shard_map.77 = (f32[1,128]{1,0:T(1,128)}, f32[128,1152]{1,0:T(8,128)}, f32[128,1152]{1,0:T(8,128)}) custom-call(f32[1]{0:T(128)S(6)} %copy.15.scale, f32[1]{0:T(128)S(6)} %copy.16.bias, bf16[128,1152]{1,0:T(8,128)(2,1)S(1)} %copy-done, bf16[128,1152]{1,0:T(8,128)(2,1)S(1)} %copy-done.1, bf16[128,1152]{1,0:T(8,128)(2,1)S(1)} %collective-permute-done.8.yg_ref, ...), custom_call_target="tpu_custom_call" | custom-call | flops 150994944 | bytes 2097152 | tf_op jit(solution)/shard_map/pallas_call | solution.py:145
  (10 shorter events, 0.1 us)
Async XLA Ops:
  0.6 20.1 %copy-start = (bf16[128,1152]{1,0:T(8,128)(2,1)S(1)}, bf16[128,1152]{1,0:T(8,128)(2,1)}, u32[]{:S(2)}) copy-start(bf16[128,1152]{1,0:T(8,128)(2,1)} %x_ref.1) | copy-start | bytes 884740
  0.6 18.1 %copy-start.1 = (bf16[128,1152]{1,0:T(8,128)(2,1)S(1)}, bf16[128,1152]{1,0:T(8,128)(2,1)}, u32[]{:S(2)}) copy-start(bf16[128,1152]{1,0:T(8,128)(2,1)} %y_ref.1) | copy-start | bytes 884740
  0.7 58.8 %copy-start.9 = (s32[1,128]{1,0:T(1,128)S(1)}, s32[1,128]{1,0:T(1,128)}, u32[]{:S(2)}) copy-start(s32[1,128]{1,0:T(1,128)} %param.9) | copy-start | bytes 1540
  1.9 36.7 %collective-permute-start.10 = (bf16[128,1152]{1,0:T(8,128)(2,1)S(1)}, bf16[128,1152]{1,0:T(8,128)(2,1)S(1)}, u32[]{:S(2)}, u32[]{:S(2)}) collective-permute-start(bf16[128,1152]{1,0:T(8,128)(2,1)S(1)} %get-tuple-element.85), channel_id=1, source_target_pairs={{0,32},{16,48},{32,64},{48,80},{64,96},{80,112},{96,0},{112,16},{1... | collective-permute-start | bytes 884744 | tf_op jit(solution)/shard_map/ppermute | solution.py:35
  5.9 36.2 %collective-permute-start.7 = (bf16[128,1152]{1,0:T(8,128)(2,1)S(1)}, bf16[128,1152]{1,0:T(8,128)(2,1)S(1)}, u32[]{:S(2)}, u32[]{:S(2)}) collective-permute-start(bf16[128,1152]{1,0:T(8,128)(2,1)S(1)} %get-tuple-element.87), channel_id=1, source_target_pairs={{896,0},{912,16},{928,32},{944,48},{960,64},{976,80},{992,96},{100... | collective-permute-start | bytes 884744 | tf_op jit(solution)/shard_map/ppermute | solution.py:41
  18.8 23.3 %collective-permute-start.5 = (bf16[128,1152]{1,0:T(8,128)(2,1)S(1)}, bf16[128,1152]{1,0:T(8,128)(2,1)}, u32[]{:S(2)}, u32[]{:S(2)}) collective-permute-start(bf16[128,1152]{1,0:T(8,128)(2,1)S(1)} %copy-done.1), channel_id=1, source_target_pairs={{0,128},{1,129},{2,130},{3,131},{4,132},{5,133},{6,134},{7,135},{8... | collective-permute-start | bytes 884744 | tf_op jit(solution)/shard_map/ppermute | solution.py:27
  20.7 21.4 %collective-permute-start.6 = (bf16[128,1152]{1,0:T(8,128)(2,1)S(1)}, bf16[128,1152]{1,0:T(8,128)(2,1)}, u32[]{:S(2)}, u32[]{:S(2)}) collective-permute-start(bf16[128,1152]{1,0:T(8,128)(2,1)S(1)} %copy-done), channel_id=1, source_target_pairs={{0,911},{1,896},{2,897},{3,898},{4,899},{5,900},{6,901},{7,902},{8... | collective-permute-start | bytes 884744 | tf_op jit(solution)/shard_map/ppermute | solution.py:27
  35.2 24.2 %collective-permute-start.12 = (bf16[128,1152]{1,0:T(8,128)(2,1)S(1)}, bf16[128,1152]{1,0:T(8,128)(2,1)S(1)}, u32[]{:S(2)}, u32[]{:S(2)}) collective-permute-start(bf16[128,1152]{1,0:T(8,128)(2,1)S(1)} %get-tuple-element.84), channel_id=1, source_target_pairs={{0,96},{16,112},{32,0},{48,16},{64,32},{80,48},{96,64},{112,80},{1... | collective-permute-start | bytes 884744 | tf_op jit(solution)/shard_map/ppermute | solution.py:35
  38.6 20.8 %collective-permute-start.11 = (bf16[128,1152]{1,0:T(8,128)(2,1)S(1)}, bf16[128,1152]{1,0:T(8,128)(2,1)S(1)}, u32[]{:S(2)}, u32[]{:S(2)}) collective-permute-start(bf16[128,1152]{1,0:T(8,128)(2,1)S(1)} %get-tuple-element.68), channel_id=1, source_target_pairs={{0,64},{16,80},{32,96},{48,112},{64,0},{80,16},{96,32},{112,48},{1... | collective-permute-start | bytes 884744 | tf_op jit(solution)/shard_map/ppermute | solution.py:35
  42.1 0.7 copy-start.8
  42.8 57.5 %collective-permute-start.8 = (bf16[128,1152]{1,0:T(8,128)(2,1)}, bf16[128,1152]{1,0:T(8,128)(2,1)S(1)}, u32[]{:S(2)}, u32[]{:S(2)}) collective-permute-start(bf16[128,1152]{1,0:T(8,128)(2,1)} %collective-permute-done.5), channel_id=1, source_target_pairs={{0,896},{1,897},{2,898},{3,899},{4,900},{5,901},{6,902},{7,903},{8... | collective-permute-start | bytes 884744 | tf_op jit(solution)/shard_map/ppermute | solution.py:27
  46.6 53.7 %collective-permute-start.9 = (bf16[128,1152]{1,0:T(8,128)(2,1)}, bf16[128,1152]{1,0:T(8,128)(2,1)S(1)}, u32[]{:S(2)}, u32[]{:S(2)}) collective-permute-start(bf16[128,1152]{1,0:T(8,128)(2,1)} %collective-permute-done.6), channel_id=1, source_target_pairs={{0,143},{1,128},{2,129},{3,130},{4,131},{5,132},{6,133},{7,134},{8... | collective-permute-start | bytes 884744 | tf_op jit(solution)/shard_map/ppermute | solution.py:27
  59.4 0.7 copy-start.2
  59.4 0.8 copy-start.4
  59.4 0.9 copy-start.6
  60.4 12.3 %collective-permute-start = (bf16[512,1152]{1,0:T(8,128)(2,1)S(1)}, bf16[512,1152]{1,0:T(8,128)(2,1)S(1)}, u32[]{:S(2)}, u32[]{:S(2)}) collective-permute-start(bf16[512,1152]{1,0:T(8,128)(2,1)S(1)} %pad_maximum_fusion), channel_id=1, source_target_pairs={{0,16},{16,0},{32,48},{48,32},{64,80},{80,64},{96,112},{112,96},{1... | collective-permute-start | bytes 3538952 | tf_op jit(solution)/shard_map/cond/branch_1_fun/ppermute | solution.py:45
  66.2 11.7 %collective-permute-start.1 = (bf16[128,1152]{1,0:T(8,128)(2,1)S(1)}, bf16[128,1152]{1,0:T(8,128)(2,1)S(1)}, u32[]{:S(2)}, u32[]{:S(2)}) collective-permute-start(bf16[128,1152]{1,0:T(8,128)(2,1)S(1)} %get-tuple-element.83), channel_id=1, source_target_pairs={{0,32},{16,48},{32,64},{48,80},{64,96},{80,112},{96,0},{112,16},{1... | collective-permute-start | bytes 884744 | tf_op jit(solution)/shard_map/cond/branch_1_fun/ppermute | solution.py:35
  68.5 16.5 %collective-permute-start.3 = (bf16[128,1152]{1,0:T(8,128)(2,1)S(1)}, bf16[128,1152]{1,0:T(8,128)(2,1)S(1)}, u32[]{:S(2)}, u32[]{:S(2)}) collective-permute-start(bf16[128,1152]{1,0:T(8,128)(2,1)S(1)} %get-tuple-element.81), channel_id=1, source_target_pairs={{0,96},{16,112},{32,0},{48,16},{64,32},{80,48},{96,64},{112,80},{1... | collective-permute-start | bytes 884744 | tf_op jit(solution)/shard_map/cond/branch_1_fun/ppermute | solution.py:35
  72.7 12.3 %collective-permute-start.2 = (bf16[128,1152]{1,0:T(8,128)(2,1)S(1)}, bf16[128,1152]{1,0:T(8,128)(2,1)S(1)}, u32[]{:S(2)}, u32[]{:S(2)}) collective-permute-start(bf16[128,1152]{1,0:T(8,128)(2,1)S(1)} %get-tuple-element.48), channel_id=1, source_target_pairs={{0,64},{16,80},{32,96},{48,112},{64,0},{80,16},{96,32},{112,48},{1... | collective-permute-start | bytes 884744 | tf_op jit(solution)/shard_map/cond/branch_1_fun/ppermute | solution.py:35
  85.0 3.5 %copy-start.3 = (bf16[128,1152]{1,0:T(8,128)(2,1)S(1)}, bf16[128,1152]{1,0:T(8,128)(2,1)}, u32[]{:S(2)}) copy-start(bf16[128,1152]{1,0:T(8,128)(2,1)} %copy-done.2) | copy-start | bytes 884740 | tf_op jit(solution)/shard_map/cond
  85.0 3.5 %copy-start.5 = (bf16[128,1152]{1,0:T(8,128)(2,1)S(1)}, bf16[128,1152]{1,0:T(8,128)(2,1)}, u32[]{:S(2)}) copy-start(bf16[128,1152]{1,0:T(8,128)(2,1)} %copy-done.4) | copy-start | bytes 884740 | tf_op jit(solution)/shard_map/cond
  85.0 3.5 %copy-start.7 = (bf16[128,1152]{1,0:T(8,128)(2,1)S(1)}, bf16[128,1152]{1,0:T(8,128)(2,1)}, u32[]{:S(2)}) copy-start(bf16[128,1152]{1,0:T(8,128)(2,1)} %copy-done.6) | copy-start | bytes 884740 | tf_op jit(solution)/shard_map/cond
  85.1 9.3 %collective-permute-start.4 = (bf16[512,1152]{1,0:T(8,128)(2,1)S(1)}, bf16[512,1152]{1,0:T(8,128)(2,1)S(1)}, u32[]{:S(2)}, u32[]{:S(2)}) collective-permute-start(bf16[512,1152]{1,0:T(8,128)(2,1)S(1)} %pad_maximum_fusion.1), channel_id=1, source_target_pairs={{0,16},{16,0},{32,48},{48,32},{64,80},{80,64},{96,112},{112,96},{1... | collective-permute-start | bytes 3538952 | tf_op jit(solution)/shard_map/cond/branch_1_fun/ppermute | solution.py:45

commit v6 on v5

--- a/solution.py
+++ b/solution.py
@@ -87,11 +87,11 @@
 
 def add_blocks(roles, refs, tau, offset, units_ref, loss_ref, grads_ref):
     rows = units_ref.shape[1]
-    singles, twin = refs[:-1], refs[-1]
-    for by, ref in enumerate(singles, 1):
-        add_block(ref[...], roles[by], tau, offset, units_ref, loss_ref, grads_ref)
-    for by in range(CHIPS):
-        add_block(twin[by * rows : (by + 1) * rows, :], roles[by], tau, offset, units_ref, loss_ref, grads_ref)
+    at = 0
+    for ref in refs:
+        for first in range(0, ref.shape[0], rows):
+            add_block(ref[first : first + rows, :], roles[at], tau, offset, units_ref, loss_ref, grads_ref)
+            at += 1
 
 
 def first_kernel(scale, bias, roles, x_ref, y_ref, pos_ref, *rest):
@@ -113,31 +113,31 @@
     add_blocks(roles, refs, tau, offset, units_ref, loss_ref, grads_ref)
 
 
-def second_kernel(scale, bias, roles, units_ref, loss_in, grads_in, *rest):
+def next_kernel(scale, bias, roles, units_ref, loss_in, grads_in, *rest):
     refs, (loss_ref, grads_ref) = rest[:-2], rest[-2:]
     loss_ref[...] = loss_in[...]
     grads_ref[...] = grads_in[...]
     add_blocks(roles, refs, scale[0], bias[0], units_ref, loss_ref, grads_ref)
 
 
-def last_kernel(scale, bias, x_ref, y_ref, yg_ref, xg_ref, units_ref, loss_in, grads_in, loss_ref, ix_ref, ty_ref):
-    tau, offset = scale[0], bias[0]
+def outer_grad(tau, offset, feats_ref, other_ref, unit, before):
+    other = unit_rows(other_ref[...])
+    loss, slope = loss_and_slope(tau * by_rows(unit, other) + offset)
+    grad = (before + product(slope.astype(BF16), other)) * tau
+    feats = feats_ref[...]
+    inverse = row_inverse(feats)
+    norm = feats.astype(F32) * inverse
+    return loss, (grad - norm * jnp.sum(norm * grad, axis=-1, keepdims=True)) * inverse
+
+
+def image_kernel(scale, bias, x_ref, other_ref, units_ref, loss_in, grads_in, loss_ref, out_ref):
+    loss, out_ref[...] = outer_grad(scale[0], bias[0], x_ref, other_ref, units_ref[TEXT], grads_in[TEXT])
     rows = x_ref.shape[0]
-    unit = unit_rows(yg_ref[...])
-    add, slope = loss_and_slope(tau * by_rows(units_ref[TEXT], unit) + offset)
-    loss_ref[...] = jnp.sum((loss_in[...] + add).T, axis=0, keepdims=True) / F32((SPAN + 1) * rows)
-    gx = (grads_in[TEXT] + product(slope.astype(BF16), unit)) * tau
-    x = x_ref[...]
-    x_inv = row_inverse(x)
-    xn = x.astype(F32) * x_inv
-    ix_ref[...] = (gx - xn * jnp.sum(xn * gx, axis=-1, keepdims=True)) * x_inv
-    unit = unit_rows(xg_ref[...])
-    _, slope = loss_and_slope(tau * by_rows(units_ref[IMAGE], unit) + offset)
-    gy = (grads_in[IMAGE] + product(slope.astype(BF16), unit)) * tau
-    y = y_ref[...]
-    y_inv = row_inverse(y)
-    yn = y.astype(F32) * y_inv
-    ty_ref[...] = (gy - yn * jnp.sum(yn * gy, axis=-1, keepdims=True)) * y_inv
+    loss_ref[...] = jnp.sum((loss_in[...] + loss).T, axis=0, keepdims=True) / F32((SPAN + 1) * rows)
+
+
+def text_kernel(scale, bias, y_ref, other_ref, units_ref, grads_in, out_ref):
+    _, out_ref[...] = outer_grad(scale[0], bias[0], y_ref, other_ref, units_ref[IMAGE], grads_in[IMAGE])
 
 
 def call(kernel, outs, blocks, scalars, *args):
@@ -170,12 +170,12 @@
     first[2], got[1] = lax.optimization_barrier((first[2], got[1]))
     got[2] = in_row(first[2], 2)
     got = [got[by] for by in shifts]
-    y_back, x_next, wrapped = lax.optimization_barrier((y_back, x_next, wrapped))
     y_outer = along_ring(y_back, length - 1)
     x_outer = along_ring(x_next, 1 - length)
     loss_out, grads_out = ((rows, rows), F32), ((2, rows, width), F32)
     units_out = ((2, rows, width), BF16)
-    roles = jnp.stack([1 - core] + [(chip < by).astype(jnp.int32) for by in shifts])
+    from_chips = [(chip < by).astype(jnp.int32) for by in shifts]
+    roles = jnp.stack(from_chips + [1 - core] + from_chips)
 
     def inner(_):
         twin = to_twin(jnp.concatenate([jnp.where(core == 0, y, x)] + got, axis=0))
@@ -187,9 +187,14 @@
         then = [jnp.where(chip + by < CHIPS, image, text) for by in shifts]
         then[1], twin = lax.optimization_barrier((then[1], twin))
         later = [in_row(block, by) for by, block in zip(shifts, then)]
+        *later, loss = lax.optimization_barrier((*later, loss))
         twin = to_twin(jnp.concatenate([jnp.where(core == 0, image, text)] + later, axis=0))
+        outs, count = [loss_out, grads_out], len(later)
         loss, grads = call(
-            second_kernel, [loss_out, grads_out], 7, (scale, bias, 1 - roles), units, loss, grads, *later, twin
+            next_kernel, outs, count, (scale, bias, 1 - roles[:count]), units, loss, grads, *later
+        )
+        loss, grads = call(
+            next_kernel, outs, count + 1, (scale, bias, 1 - roles[count:]), units, loss, grads, twin
         )
         return loss, grads, units
 
@@ -199,9 +204,10 @@
     go = lax.optimization_barrier(jnp.int32(1))
     loss, grads, units = lax.cond(go > 0, inner, skip, 0)
     block = ((rows, width), F32)
-    loss, image_grad, text_grad = call(
-        last_kernel, [((1, rows), F32), block, block], 2, (scale, bias), x, y, y_outer, x_outer, units, loss, grads
+    loss, image_grad = call(
+        image_kernel, [((1, rows), F32), block], 1, (scale, bias), x, y_outer, units, loss, grads
     )
+    (text_grad,) = call(text_kernel, [block], 1, (scale, bias), y, x_outer, units, grads)
     return (loss[0], image_grad, text_grad)
 
 

time: 104 us -> 100 us (0.962)
  the two profiles are of different devices: /device:TPU:1 before, /device:TPU:32 now
where the time goes in v6:
time: 100 us; the launch traced here: 99.6 us
  starting transfers between devices  60.7 us (61%)
  Pallas kernels  19.9 us (20%)
  waiting for transfers between devices  11.9 us (12%)
  other arithmetic  3.77 us (4%)
  between operations  2.14 us (2%)
  local copies, waits for them, and re-layouts  1.05 us (1%)
    ppermute x4, starting transfers between devices, along_ring(): return lax.ppermute(x, ('blk', 'group'), pairs)  36.1 us
    ppermute x6, starting transfers between devices, in_row(): return lax.ppermute(x, 'blk', pairs)  20.1 us
    pallas_call x5, Pallas kernels, call(): pl.pallas_call(kernel, out_shape=[jax.ShapeDtypeStruct(shape, kind) for s...  19.9 us
    ppermute x6, waiting for transfers between devices, in_row(): return lax.ppermute(x, 'blk', pairs)  6.11 us
    ppermute x4, waiting for transfers between devices, along_ring(): return lax.ppermute(x, ('blk', 'group'), pairs)  5.76 us
    ppermute x2, starting transfers between devices, to_twin(): lax.ppermute(x, 'blk', [(i, i ^ 1) for i in range(lax.axis_size('blk'))])  3.83 us
  transfers between devices with their start and end apart: 13, of which 2 were waited for; matrix products, arithmetic and copies ran while one was open for 3% of the time, Pallas kernels for 17%

profile of v6, /device:TPU:32, one launch (start us, length us, event | category | flops | bytes accessed | tf_op | source)
XLA Modules:
  0.0 99.6 jit_solution(5061436938765300694)
XLA Ops:
  0.7 1.2 %broadcast_select_fusion.7 = (bf16[128,1152]{1,0:T(8,128)(2,1)S(1)}, bf16[128,1152]{1,0:T(8,128)(2,1)S(1)}, bf16[128,1152]{1,0:T(8,128)(2,1)S(1)}, bf16[128,1152]{1,0:T(8,128)(2,1)S(1)}) fusion(bf16[128,1152]{1,0:T(8,128)(2,1)} %y_ref.1, bf16[128,1152]{1,0:T(8,128)(2,1)} %x_ref.1, pred[]{:T(512)S(6)} %ge.6, pred[]{:T(512)S(6)} %lt.47, pred[]{:T(512)S(6)} %lt.46, ...), kind=kLoop, calls=%fused_computation.11 | loop fusion | flops 589824 | bytes 1769476 | tf_op jit(solution)/shard_map/jit(_where)/select_n | solution.py:165
  1.9 3.4 %collective-permute-start.7 = (bf16[128,1152]{1,0:T(8,128)(2,1)S(1)}, bf16[128,1152]{1,0:T(8,128)(2,1)S(1)}, u32[]{:S(2)}, u32[]{:S(2)}) collective-permute-start(bf16[128,1152]{1,0:T(8,128)(2,1)S(1)} %get-tuple-element.84), channel_id=1, source_target_pairs={{0,32},{16,48},{32,64},{48,80},{64,96},{80,112},{96,0},{112,16},{1... | collective-permute-start | bytes 884744 | tf_op jit(solution)/shard_map/ppermute | solution.py:35
  5.4 13.2 %collective-permute-start.11 = (bf16[128,1152]{1,0:T(8,128)(2,1)S(1)}, bf16[128,1152]{1,0:T(8,128)(2,1)}, u32[]{:S(2)}, u32[]{:S(2)}) collective-permute-start(bf16[128,1152]{1,0:T(8,128)(2,1)S(1)} %copy-done), channel_id=1, source_target_pairs={{0,911},{1,896},{2,897},{3,898},{4,899},{5,900},{6,901},{7,902},{8... | collective-permute-start | bytes 884744 | tf_op jit(solution)/shard_map/ppermute | solution.py:27
  18.6 1.9 %collective-permute-start.5 = (bf16[128,1152]{1,0:T(8,128)(2,1)S(1)}, bf16[128,1152]{1,0:T(8,128)(2,1)}, u32[]{:S(2)}, u32[]{:S(2)}) collective-permute-start(bf16[128,1152]{1,0:T(8,128)(2,1)S(1)} %copy-done.1), channel_id=1, source_target_pairs={{0,128},{1,129},{2,130},{3,131},{4,132},{5,133},{6,134},{7,135},{8... | collective-permute-start | bytes 884744 | tf_op jit(solution)/shard_map/ppermute | solution.py:27
  20.5 0.7 collective-permute-start.10
  21.2 5.1 %collective-permute-start.9 = (bf16[128,1152]{1,0:T(8,128)(2,1)S(1)}, bf16[128,1152]{1,0:T(8,128)(2,1)S(1)}, u32[]{:S(2)}, u32[]{:S(2)}) collective-permute-start(bf16[128,1152]{1,0:T(8,128)(2,1)S(1)} %get-tuple-element.83), channel_id=1, source_target_pairs={{0,96},{16,112},{32,0},{48,16},{64,32},{80,48},{96,64},{112,80},{1... | collective-permute-start | bytes 884744 | tf_op jit(solution)/shard_map/ppermute | solution.py:35
  26.3 0.0 collective-permute-done.7
  26.3 1.9 %collective-permute-start.8 = (bf16[128,1152]{1,0:T(8,128)(2,1)S(1)}, bf16[128,1152]{1,0:T(8,128)(2,1)S(1)}, u32[]{:S(2)}, u32[]{:S(2)}) collective-permute-start(bf16[128,1152]{1,0:T(8,128)(2,1)S(1)} %get-tuple-element.68), channel_id=1, source_target_pairs={{0,64},{16,80},{32,96},{48,112},{64,0},{80,16},{96,32},{112,48},{1... | collective-permute-start | bytes 884744 | tf_op jit(solution)/shard_map/ppermute | solution.py:35
  28.3 0.0 collective-permute-done.11
  28.3 15.2 %collective-permute-start.12 = (bf16[128,1152]{1,0:T(8,128)(2,1)}, bf16[128,1152]{1,0:T(8,128)(2,1)S(1)}, u32[]{:S(2)}, u32[]{:S(2)}) collective-permute-start(bf16[128,1152]{1,0:T(8,128)(2,1)} %collective-permute-done.11), channel_id=1, source_target_pairs={{0,143},{1,128},{2,129},{3,130},{4,131},{5,132},{6,133},{7,134},{8... | collective-permute-start | bytes 884744 | tf_op jit(solution)/shard_map/ppermute | solution.py:27
  43.4 0.0 collective-permute-done.5
  43.4 5.9 %collective-permute-start.6 = (bf16[128,1152]{1,0:T(8,128)(2,1)}, bf16[128,1152]{1,0:T(8,128)(2,1)S(1)}, u32[]{:S(2)}, u32[]{:S(2)}) collective-permute-start(bf16[128,1152]{1,0:T(8,128)(2,1)} %collective-permute-done.5), channel_id=1, source_target_pairs={{0,896},{1,897},{2,898},{3,899},{4,900},{5,901},{6,902},{7,903},{8... | collective-permute-start | bytes 884744 | tf_op jit(solution)/shard_map/ppermute | solution.py:27
  50.6 0.1 stack.34
  50.7 0.0 collective-permute-done.10
  50.7 0.0 collective-permute-done.9
  50.7 0.0 collective-permute-done.8
  50.7 0.0 copy-done.10
  50.8 37.8 %conditional.1 = (f32[128,128]{1,0:T(8,128)}, f32[2,128,1152]{2,1,0:T(8,128)S(1)}, bf16[2,128,1152]{2,1,0:T(8,128)(2,1)}) conditional(s32[]{:T(128)} %convert_element_type.2, () %tuple.19, (s32[7]{0:T(128)S(1)}, s32[]{:T(128)}, bf16[128,1152]{1,0:T(8,128)(2,1)S(1)}, bf16[128,1152]{1,0:T(8,128)(2,1)S(1)}, bf16[128,1152]{1,0:T(8,128)(2,1)S(1)}, ...), branch_computations={%region_0.1_spmd, %region_1.2_spmd} | conditional | flops 1142931456 | bytes 46989912 | solution.py:205
  50.8 0.0 copy-start.2
  50.8 0.0 copy-start.6
  50.8 0.7 copy-done.8
  51.5 0.0 copy-done.2
  51.6 0.1 copy-done.4
  51.7 0.1 copy-done.6
  51.8 1.1 %pad_maximum_fusion = bf16[512,1152]{1,0:T(8,128)(2,1)} fusion(bf16[128,1152]{1,0:T(8,128)(2,1)S(1)} %get-tuple-element.38.rest_2_, bf16[128,1152]{1,0:T(8,128)(2,1)S(1)} %get-tuple-element.37.rest_1_, bf16[128,1152]{1,0:T(8,128)(2,1)S(1)} %get-tuple-element.36.rest_0_, bf16[128,1152]{1,0:T(8,128)(2,1)S(1)} %broadcast_select_fusion.6), kind=kLoop, calls=%fused_computation | loop fusion | flops 4718592 | bytes 2359296 | tf_op jit(solution)/shard_map/cond/branch_1_fun/concatenate | solution.py:181
  52.9 1.9 %collective-permute-start = (bf16[512,1152]{1,0:T(8,128)(2,1)}, bf16[512,1152]{1,0:T(8,128)(2,1)S(1)}, u32[]{:S(2)}, u32[]{:S(2)}) collective-permute-start(bf16[512,1152]{1,0:T(8,128)(2,1)} %pad_maximum_fusion), channel_id=1, source_target_pairs={{0,16},{16,0},{32,48},{48,32},{64,80},{80,64},{96,112},{112,96},{1... | collective-permute-start | bytes 3538952 | tf_op jit(solution)/shard_map/cond/branch_1_fun/ppermute | solution.py:45
  54.8 1.1 %broadcast_select_fusion.5 = (bf16[128,1152]{1,0:T(8,128)(2,1)S(1)}, bf16[128,1152]{1,0:T(8,128)(2,1)S(1)}, bf16[128,1152]{1,0:T(8,128)(2,1)S(1)}) fusion(pred[]{:T(512)S(6)} %eq.6, bf16[128,1152]{1,0:T(8,128)(2,1)S(1)} %copy-done.9, bf16[128,1152]{1,0:T(8,128)(2,1)} %get-tuple-element.45, pred[]{:T(512)S(6)} %lt.29, bf16[128,1152]{1,0:T(8,128)(2,1)} %get-tuple-element.44, ...), kind=kLoop, calls=%fused_computation.7 | loop fusion | flops 442368 | bytes 1769475 | tf_op jit(solution)/shard_map/cond/branch_1_fun/jit(_where)/select_n | solution.py:191
  56.0 0.0 copy-start.3
  56.0 0.0 copy-start.7
  56.0 0.1 broadcast_select_fusion
  56.1 3.2 %collective-permute-start.3 = (bf16[128,1152]{1,0:T(8,128)(2,1)S(1)}, bf16[128,1152]{1,0:T(8,128)(2,1)S(1)}, u32[]{:S(2)}, u32[]{:S(2)}) collective-permute-start(bf16[128,1152]{1,0:T(8,128)(2,1)S(1)} %get-tuple-element.79), channel_id=1, source_target_pairs={{0,96},{16,112},{32,0},{48,16},{64,32},{80,48},{96,64},{112,80},{1... | collective-permute-start | bytes 884744 | tf_op jit(solution)/shard_map/cond/branch_1_fun/ppermute | solution.py:35
  59.3 2.8 %collective-permute-start.1 = (bf16[128,1152]{1,0:T(8,128)(2,1)S(1)}, bf16[128,1152]{1,0:T(8,128)(2,1)S(1)}, u32[]{:S(2)}, u32[]{:S(2)}) collective-permute-start(bf16[128,1152]{1,0:T(8,128)(2,1)S(1)} %get-tuple-element.81), channel_id=1, source_target_pairs={{0,32},{16,48},{32,64},{48,80},{64,96},{80,112},{96,0},{112,16},{1... | collective-permute-start | bytes 884744 | tf_op jit(solution)/shard_map/cond/branch_1_fun/ppermute | solution.py:35
  62.1 0.0 collective-permute-done.rest_3_
  62.1 3.6 %collective-permute-start.2 = (bf16[128,1152]{1,0:T(8,128)(2,1)S(1)}, bf16[128,1152]{1,0:T(8,128)(2,1)S(1)}, u32[]{:S(2)}, u32[]{:S(2)}) collective-permute-start(bf16[128,1152]{1,0:T(8,128)(2,1)S(1)} %get-tuple-element.46), channel_id=1, source_target_pairs={{0,64},{16,80},{32,96},{48,112},{64,0},{80,16},{96,32},{112,48},{1... | collective-permute-start | bytes 884744 | tf_op jit(solution)/shard_map/cond/branch_1_fun/ppermute | solution.py:35
  65.8 6.0 %branch_1_fun.3 = (f32[128,128]{1,0:T(8,128)S(1)}, f32[2,128,1152]{2,1,0:T(8,128)S(1)}, bf16[2,128,1152]{2,1,0:T(8,128)(2,1)}) custom-call(f32[1]{0:T(128)} %get-tuple-element.30.scale, f32[1]{0:T(128)} %get-tuple-element.31.bias, s32[7]{0:T(128)S(1)} %get-tuple-element.32.roles, bf16[128,1152]{1,0:T(8,128)(2,1)S(1)} %get-tuple-element.33.x_ref, ...), custom_call_target="tpu_custom_call" | custom-call | flops 603979776 | bytes 8388608 | tf_op jit(solution)/shard_map/cond/branch_1_fun/pallas_call | solution.py:145
  71.7 0.0 collective-permute-done.3.rest_2_
  71.7 6.1 %collective-permute-done.1.rest_0_ = bf16[128,1152]{1,0:T(8,128)(2,1)S(1)} collective-permute-done((bf16[128,1152]{1,0:T(8,128)(2,1)S(1)}, bf16[128,1152]{1,0:T(8,128)(2,1)S(1)}, u32[]{:S(2)}, u32[]{:S(2)}) %collective-permute-start.1) | collective-permute-done | bytes 294944 | tf_op jit(solution)/shard_map/cond/branch_1_fun/ppermute | solution.py:35
  77.8 0.0 collective-permute-done.2.rest_1_
  77.9 0.1 pad_maximum_fusion.1
  77.9 1.9 %collective-permute-start.4 = (bf16[512,1152]{1,0:T(8,128)(2,1)S(1)}, bf16[512,1152]{1,0:T(8,128)(2,1)S(1)}, u32[]{:S(2)}, u32[]{:S(2)}) collective-permute-start(bf16[512,1152]{1,0:T(8,128)(2,1)S(1)} %pad_maximum_fusion.1), channel_id=1, source_target_pairs={{0,16},{16,0},{32,48},{48,32},{64,80},{80,64},{96,112},{112,96},{1... | collective-permute-start | bytes 3538952 | tf_op jit(solution)/shard_map/cond/branch_1_fun/ppermute | solution.py:45
  79.9 0.1 slice_subtract_fusion.1.roles
  80.0 3.9 %branch_1_fun.4 = (f32[128,128]{1,0:T(8,128)S(1)}, f32[2,128,1152]{2,1,0:T(8,128)S(1)}) custom-call(f32[1]{0:T(128)} %get-tuple-element.30.scale, f32[1]{0:T(128)} %get-tuple-element.31.bias, s32[3]{0:T(128)S(1)} %slice_subtract_fusion.roles, bf16[2,128,1152]{2,1,0:T(8,128)(2,1)} %get-tuple-element.91.units_ref, f32[128,128]{1,0:T(8,128)S(1)} %get-tuple-element.48.loss_in, ...), custom_call_target="tpu_custom_call" | custom-call | flops 226492416 | bytes 3145728 | tf_op jit(solution)/shard_map/cond/branch_1_fun/pallas_call | solution.py:145
  83.8 0.0 collective-permute-done.4.rest_0_
  83.9 4.7 %branch_1_fun.5 = (f32[128,128]{1,0:T(8,128)}, f32[2,128,1152]{2,1,0:T(8,128)S(1)}) custom-call(f32[1]{0:T(128)} %get-tuple-element.30.scale, f32[1]{0:T(128)} %get-tuple-element.31.bias, s32[4]{0:T(128)S(1)} %slice_subtract_fusion.1.roles, bf16[2,128,1152]{2,1,0:T(8,128)(2,1)} %get-tuple-element.91.units_ref, f32[128,128]{1,0:T(8,128)S(1)} %get-tuple-element.53.loss_in, ...), custom_call_target="tpu_custom_call" | custom-call | flops 301989888 | bytes 4194304 | tf_op jit(solution)/shard_map/cond/branch_1_fun/pallas_call | solution.py:145
  88.5 0.0 collective-permute-done.12.other_ref
  88.5 2.7 %shard_map.78 = f32[128,1152]{1,0:T(8,128)} custom-call(f32[1]{0:T(128)S(6)} %copy.15.scale, f32[1]{0:T(128)S(6)} %copy.16.bias, bf16[128,1152]{1,0:T(8,128)(2,1)S(1)} %copy-done.1, bf16[128,1152]{1,0:T(8,128)(2,1)S(1)} %collective-permute-done.12.other_ref, bf16[2,128,1152]{2,1,0:T(8,128)(2,1)} %get-tuple-element.69.units_ref, ...), custom_call_target="tpu_custom_call" | custom-call | flops 75497472 | bytes 1048576 | tf_op jit(solution)/shard_map/pallas_call | solution.py:145
  91.2 5.8 %collective-permute-done.6.other_ref = bf16[128,1152]{1,0:T(8,128)(2,1)S(1)} collective-permute-done((bf16[128,1152]{1,0:T(8,128)(2,1)}, bf16[128,1152]{1,0:T(8,128)(2,1)S(1)}, u32[]{:S(2)}, u32[]{:S(2)}) %collective-permute-start.6) | collective-permute-done | bytes 294944 | tf_op jit(solution)/shard_map/ppermute | solution.py:27
  97.0 2.7 %shard_map.77 = (f32[1,128]{1,0:T(1,128)}, f32[128,1152]{1,0:T(8,128)}) custom-call(f32[1]{0:T(128)S(6)} %copy.15.scale, f32[1]{0:T(128)S(6)} %copy.16.bias, bf16[128,1152]{1,0:T(8,128)(2,1)S(1)} %copy-done, bf16[128,1152]{1,0:T(8,128)(2,1)S(1)} %collective-permute-done.6.other_ref, bf16[2,128,1152]{2,1,0:T(8,128)(2,1)} %get-tuple-element.69.units_ref, ...), custom_call_target="tpu_custom_call" | custom-call | flops 75497472 | bytes 1048576 | tf_op jit(solution)/shard_map/pallas_call | solution.py:145
  (15 shorter events, 0.1 us)
Async XLA Ops:
  0.6 17.9 %copy-start.1 = (bf16[128,1152]{1,0:T(8,128)(2,1)S(1)}, bf16[128,1152]{1,0:T(8,128)(2,1)}, u32[]{:S(2)}) copy-start(bf16[128,1152]{1,0:T(8,128)(2,1)} %y_ref.1) | copy-start | bytes 884740
  0.6 4.7 %copy-start = (bf16[128,1152]{1,0:T(8,128)(2,1)S(1)}, bf16[128,1152]{1,0:T(8,128)(2,1)}, u32[]{:S(2)}) copy-start(bf16[128,1152]{1,0:T(8,128)(2,1)} %x_ref.1) | copy-start | bytes 884740
  0.7 50.1 %copy-start.10 = (s32[1,128]{1,0:T(1,128)S(1)}, s32[1,128]{1,0:T(1,128)}, u32[]{:S(2)}) copy-start(s32[1,128]{1,0:T(1,128)} %param.9) | copy-start | bytes 1540
  1.9 24.4 %collective-permute-start.7 = (bf16[128,1152]{1,0:T(8,128)(2,1)S(1)}, bf16[128,1152]{1,0:T(8,128)(2,1)S(1)}, u32[]{:S(2)}, u32[]{:S(2)}) collective-permute-start(bf16[128,1152]{1,0:T(8,128)(2,1)S(1)} %get-tuple-element.84), channel_id=1, source_target_pairs={{0,32},{16,48},{32,64},{48,80},{64,96},{80,112},{96,0},{112,16},{1... | collective-permute-start | bytes 884744 | tf_op jit(solution)/shard_map/ppermute | solution.py:35
  5.4 22.9 %collective-permute-start.11 = (bf16[128,1152]{1,0:T(8,128)(2,1)S(1)}, bf16[128,1152]{1,0:T(8,128)(2,1)}, u32[]{:S(2)}, u32[]{:S(2)}) collective-permute-start(bf16[128,1152]{1,0:T(8,128)(2,1)S(1)} %copy-done), channel_id=1, source_target_pairs={{0,911},{1,896},{2,897},{3,898},{4,899},{5,900},{6,901},{7,902},{8... | collective-permute-start | bytes 884744 | tf_op jit(solution)/shard_map/ppermute | solution.py:27
  18.6 24.9 %collective-permute-start.5 = (bf16[128,1152]{1,0:T(8,128)(2,1)S(1)}, bf16[128,1152]{1,0:T(8,128)(2,1)}, u32[]{:S(2)}, u32[]{:S(2)}) collective-permute-start(bf16[128,1152]{1,0:T(8,128)(2,1)S(1)} %copy-done.1), channel_id=1, source_target_pairs={{0,128},{1,129},{2,130},{3,131},{4,132},{5,133},{6,134},{7,135},{8... | collective-permute-start | bytes 884744 | tf_op jit(solution)/shard_map/ppermute | solution.py:27
  20.5 30.2 %collective-permute-start.10 = (bf16[128,1152]{1,0:T(8,128)(2,1)S(1)}, bf16[128,1152]{1,0:T(8,128)(2,1)S(1)}, u32[]{:S(2)}, u32[]{:S(2)}) collective-permute-start(bf16[128,1152]{1,0:T(8,128)(2,1)S(1)} %get-tuple-element.82), channel_id=1, source_target_pairs={{896,0},{912,16},{928,32},{944,48},{960,64},{976,80},{992,96},{100... | collective-permute-start | bytes 884744 | tf_op jit(solution)/shard_map/ppermute | solution.py:41
  21.2 29.6 %collective-permute-start.9 = (bf16[128,1152]{1,0:T(8,128)(2,1)S(1)}, bf16[128,1152]{1,0:T(8,128)(2,1)S(1)}, u32[]{:S(2)}, u32[]{:S(2)}) collective-permute-start(bf16[128,1152]{1,0:T(8,128)(2,1)S(1)} %get-tuple-element.83), channel_id=1, source_target_pairs={{0,96},{16,112},{32,0},{48,16},{64,32},{80,48},{96,64},{112,80},{1... | collective-permute-start | bytes 884744 | tf_op jit(solution)/shard_map/ppermute | solution.py:35
  26.3 24.4 %collective-permute-start.8 = (bf16[128,1152]{1,0:T(8,128)(2,1)S(1)}, bf16[128,1152]{1,0:T(8,128)(2,1)S(1)}, u32[]{:S(2)}, u32[]{:S(2)}) collective-permute-start(bf16[128,1152]{1,0:T(8,128)(2,1)S(1)} %get-tuple-element.68), channel_id=1, source_target_pairs={{0,64},{16,80},{32,96},{48,112},{64,0},{80,16},{96,32},{112,48},{1... | collective-permute-start | bytes 884744 | tf_op jit(solution)/shard_map/ppermute | solution.py:35
  28.3 60.3 %collective-permute-start.12 = (bf16[128,1152]{1,0:T(8,128)(2,1)}, bf16[128,1152]{1,0:T(8,128)(2,1)S(1)}, u32[]{:S(2)}, u32[]{:S(2)}) collective-permute-start(bf16[128,1152]{1,0:T(8,128)(2,1)} %collective-permute-done.11), channel_id=1, source_target_pairs={{0,143},{1,128},{2,129},{3,130},{4,131},{5,132},{6,133},{7,134},{8... | collective-permute-start | bytes 884744 | tf_op jit(solution)/shard_map/ppermute | solution.py:27
  43.4 53.5 %collective-permute-start.6 = (bf16[128,1152]{1,0:T(8,128)(2,1)}, bf16[128,1152]{1,0:T(8,128)(2,1)S(1)}, u32[]{:S(2)}, u32[]{:S(2)}) collective-permute-start(bf16[128,1152]{1,0:T(8,128)(2,1)} %collective-permute-done.5), channel_id=1, source_target_pairs={{0,896},{1,897},{2,898},{3,899},{4,900},{5,901},{6,902},{7,903},{8... | collective-permute-start | bytes 884744 | tf_op jit(solution)/shard_map/ppermute | solution.py:27
  50.8 0.7 copy-start.8
  50.8 0.8 copy-start.2
  50.8 0.9 copy-start.4
  50.8 1.0 copy-start.6
  51.8 3.0 %copy-start.9 = (bf16[128,1152]{1,0:T(8,128)(2,1)S(1)}, bf16[128,1152]{1,0:T(8,128)(2,1)}, u32[]{:S(2)}) copy-start(bf16[128,1152]{1,0:T(8,128)(2,1)} %copy-done.8) | copy-start | bytes 884740 | tf_op jit(solution)/shard_map/cond
  52.9 9.2 %collective-permute-start = (bf16[512,1152]{1,0:T(8,128)(2,1)}, bf16[512,1152]{1,0:T(8,128)(2,1)S(1)}, u32[]{:S(2)}, u32[]{:S(2)}) collective-permute-start(bf16[512,1152]{1,0:T(8,128)(2,1)} %pad_maximum_fusion), channel_id=1, source_target_pairs={{0,16},{16,0},{32,48},{48,32},{64,80},{80,64},{96,112},{112,96},{1... | collective-permute-start | bytes 3538952 | tf_op jit(solution)/shard_map/cond/branch_1_fun/ppermute | solution.py:45
  56.0 9.8 %copy-start.3 = (bf16[128,1152]{1,0:T(8,128)(2,1)S(1)}, bf16[128,1152]{1,0:T(8,128)(2,1)}, u32[]{:S(2)}) copy-start(bf16[128,1152]{1,0:T(8,128)(2,1)} %copy-done.2) | copy-start | bytes 884740 | tf_op jit(solution)/shard_map/cond
  56.0 9.8 %copy-start.5 = (bf16[128,1152]{1,0:T(8,128)(2,1)S(1)}, bf16[128,1152]{1,0:T(8,128)(2,1)}, u32[]{:S(2)}) copy-start(bf16[128,1152]{1,0:T(8,128)(2,1)} %copy-done.4) | copy-start | bytes 884740 | tf_op jit(solution)/shard_map/cond
  56.0 9.8 %copy-start.7 = (bf16[128,1152]{1,0:T(8,128)(2,1)S(1)}, bf16[128,1152]{1,0:T(8,128)(2,1)}, u32[]{:S(2)}) copy-start(bf16[128,1152]{1,0:T(8,128)(2,1)} %copy-done.6) | copy-start | bytes 884740 | tf_op jit(solution)/shard_map/cond
  56.1 15.6 %collective-permute-start.3 = (bf16[128,1152]{1,0:T(8,128)(2,1)S(1)}, bf16[128,1152]{1,0:T(8,128)(2,1)S(1)}, u32[]{:S(2)}, u32[]{:S(2)}) collective-permute-start(bf16[128,1152]{1,0:T(8,128)(2,1)S(1)} %get-tuple-element.79), channel_id=1, source_target_pairs={{0,96},{16,112},{32,0},{48,16},{64,32},{80,48},{96,64},{112,80},{1... | collective-permute-start | bytes 884744 | tf_op jit(solution)/shard_map/cond/branch_1_fun/ppermute | solution.py:35
  59.3 18.6 %collective-permute-start.1 = (bf16[128,1152]{1,0:T(8,128)(2,1)S(1)}, bf16[128,1152]{1,0:T(8,128)(2,1)S(1)}, u32[]{:S(2)}, u32[]{:S(2)}) collective-permute-start(bf16[128,1152]{1,0:T(8,128)(2,1)S(1)} %get-tuple-element.81), channel_id=1, source_target_pairs={{0,32},{16,48},{32,64},{48,80},{64,96},{80,112},{96,0},{112,16},{1... | collective-permute-start | bytes 884744 | tf_op jit(solution)/shard_map/cond/branch_1_fun/ppermute | solution.py:35
  62.1 15.7 %collective-permute-start.2 = (bf16[128,1152]{1,0:T(8,128)(2,1)S(1)}, bf16[128,1152]{1,0:T(8,128)(2,1)S(1)}, u32[]{:S(2)}, u32[]{:S(2)}) collective-permute-start(bf16[128,1152]{1,0:T(8,128)(2,1)S(1)} %get-tuple-element.46), channel_id=1, source_target_pairs={{0,64},{16,80},{32,96},{48,112},{64,0},{80,16},{96,32},{112,48},{1... | collective-permute-start | bytes 884744 | tf_op jit(solution)/shard_map/cond/branch_1_fun/ppermute | solution.py:35
  77.9 5.9 %collective-permute-start.4 = (bf16[512,1152]{1,0:T(8,128)(2,1)S(1)}, bf16[512,1152]{1,0:T(8,128)(2,1)S(1)}, u32[]{:S(2)}, u32[]{:S(2)}) collective-permute-start(bf16[512,1152]{1,0:T(8,128)(2,1)S(1)} %pad_maximum_fusion.1), channel_id=1, source_target_pairs={{0,16},{16,0},{32,48},{48,32},{64,80},{80,64},{96,112},{112,96},{1... | collective-permute-start | bytes 3538952 | tf_op jit(solution)/shard_map/cond/branch_1_fun/ppermute | solution.py:45

commit v7 on v6

v7 whole, which is shorter than its diff:
```python
import functools

import jax
import jax.numpy as jnp
from jax import lax
from jax.experimental import pallas as pl
from jax.experimental.pallas import tpu as pltpu
from jax.sharding import PartitionSpec as P

SPAN = 8
CORES = 2
CHIPS = SPAN // CORES
F32 = jnp.float32
BF16 = jnp.bfloat16


def along_ring(x, by):
    blks, groups = lax.axis_size("blk"), lax.axis_size("group")
    length = blks // SPAN
    pairs = []
    for blk in range(blks):
        row, place = divmod(blk, SPAN)
        for group in range(groups):
            to = (group * length + row + by) % (groups * length)
            to_blk, to_group = to % length * SPAN + place, to // length
            pairs.append((blk * groups + group, to_blk * groups + to_group))
    return lax.ppermute(x, ("blk", "group"), pairs)


def in_row(x, by):
    pairs = []
    for i in range(lax.axis_size("blk")):
        first, place = i - i % SPAN, i % SPAN
        pairs.append((i, first + (place + CORES * by) % SPAN))
    return lax.ppermute(x, "blk", pairs)


def around(x):
    last = lax.axis_size("blk") - SPAN
    pairs = [(last + i, i) for i in range(SPAN)] + [(i, last + i) for i in range(SPAN)]
    return lax.ppermute(x, "blk", pairs)


def to_twin(x):
    return lax.ppermute(x, "blk", [(i, i ^ 1) for i in range(lax.axis_size("blk"))])


def row_inverse(values):
    floats = values.astype(F32)
    return lax.rsqrt(jnp.sum(floats * floats, axis=-1, keepdims=True) + 1e-06)


def unit_rows(values):
    return (values.astype(F32) * row_inverse(values)).astype(BF16)


def by_rows(left, right):
    return lax.dot_general(left, right, (((1,), (1,)), ((), ())), preferred_element_type=F32)


def by_cols(left, right):
    return lax.dot_general(left, right, (((0,), (0,)), ((), ())), preferred_element_type=F32)


def product(left, right):
    return jnp.dot(left, right, preferred_element_type=F32)


def loss_and_slope(u):
    small = jnp.exp(-jnp.abs(u))
    whole = 1.0 + small
    return (
        jnp.maximum(u, 0.0) + jnp.log1p(small),
        jnp.where(u >= 0.0, 1.0, small) / whole,
    )


TEXT, IMAGE = 0, 1


def add_blocks(roles, refs, tau, offset, units, loss_ref, grads_ref, stack_ref):
    rows = units.shape[0] // 2
    at = 0
    for ref in refs:
        for first in range(0, ref.shape[0], rows):
            stack_ref[at : at + rows, :] = unit_rows(ref[first : first + rows, :])
            at += rows
    stack = stack_ref[...]
    logits = tau * by_rows(stack, units) + offset
    slopes = []
    for i in range(at // rows):
        is_text = roles[i] == TEXT
        block = logits[i * rows : (i + 1) * rows, :]
        loss, slope = loss_and_slope(jnp.where(is_text, block[:, :rows], block[:, rows:]))
        loss_ref[...] += jnp.where(is_text, loss, 0.0)
        text, image = jnp.where(is_text, slope, 0.0), jnp.where(is_text, 0.0, slope)
        slopes.append(jnp.concatenate([text, image], axis=1).astype(BF16))
    grads_ref[...] += by_cols(jnp.concatenate(slopes, axis=0), stack)


def first_kernel(scale, bias, roles, x_ref, y_ref, pos_ref, *rest):
    refs, (loss_ref, grads_ref, units_ref, inverses_ref, stack_ref) = rest[:-5], rest[-5:]
    tau, offset = scale[0], bias[0]
    rows = x_ref.shape[0]
    for i, ref in enumerate((x_ref, y_ref)):
        inverse = row_inverse(ref[...])
        inverses_ref[i * rows : (i + 1) * rows, :] = inverse
        units_ref[i * rows : (i + 1) * rows, :] = (ref[...].astype(F32) * inverse).astype(BF16)
    units = units_ref[...]
    x, y = units[:rows, :], units[rows:, :]
    place = lax.broadcasted_iota(jnp.int32, (rows, rows), 0)
    away = jnp.where(place == pos_ref[...], -1.0, 1.0)
    loss, slope = loss_and_slope(away * (tau * by_rows(y, x) + offset))
    slope = (slope * away).astype(BF16)
    loss_ref[...] = loss
    grads_ref[:rows, :] = by_cols(slope, y)
    grads_ref[rows:, :] = product(slope, x)
    add_blocks(roles, refs, tau, offset, units, loss_ref, grads_ref, stack_ref)


def next_kernel(scale, bias, roles, units_ref, loss_in, grads_in, *rest):
    refs, (loss_ref, grads_ref, stack_ref) = rest[:-3], rest[-3:]
    loss_ref[...] = loss_in[...]
    grads_ref[...] = grads_in[...]
    add_blocks(roles, refs, scale[0], bias[0], units_ref[...], loss_ref, grads_ref, stack_ref)


def last_kernel(
    scale, bias, x_ref, y_ref, yg_ref, xg_ref, units_ref, inverses_ref, loss_in, grads_in, loss_ref, ix_ref, ty_ref
):
    tau, offset = scale[0], bias[0]
    rows = x_ref.shape[0]
    for i, (feats_ref, other_ref, out_ref) in enumerate(((x_ref, yg_ref, ix_ref), (y_ref, xg_ref, ty_ref))):
        own = slice(i * rows, (i + 1) * rows)
        other = unit_rows(other_ref[...])
        loss, slope = loss_and_slope(tau * by_rows(other, units_ref[own, :]) + offset)
        if i == TEXT:
            loss_ref[...] = jnp.sum(loss_in[...] + loss, axis=0, keepdims=True) / F32((SPAN + 1) * rows)
        grad = (grads_in[own, :] + by_cols(slope.astype(BF16), other)) * tau
        inverse = inverses_ref[own, :]
        norm = feats_ref[...].astype(F32) * inverse
        out_ref[...] = (grad - norm * jnp.sum(norm * grad, axis=-1, keepdims=True)) * inverse


def call(kernel, outs, blocks, scalars, *args, scratch=()):
    flops = blocks * 4 * 128 * 128 * 1152
    return pl.pallas_call(
        kernel,
        out_shape=[jax.ShapeDtypeStruct(shape, kind) for shape, kind in outs],
        in_specs=[pl.BlockSpec(memory_space=pltpu.SMEM)] * len(scalars)
        + [pl.BlockSpec(memory_space=pltpu.VMEM)] * len(args),
        out_specs=[pl.BlockSpec(memory_space=pltpu.VMEM)] * len(outs),
        scratch_shapes=scratch,
        compiler_params=pltpu.CompilerParams(vmem_limit_bytes=40 * 1024 * 1024),
        cost_estimate=pl.CostEstimate(flops=flops, bytes_accessed=blocks * 1024 * 1024, transcendentals=0),
    )(*scalars, *args)


def local(image_feats, text_feats, positive, scale, bias):
    x, y = image_feats, text_feats
    rows, width = x.shape
    index = lax.axis_index("blk")
    place = index % SPAN
    chip, core = place // CORES, place % CORES
    last = lax.axis_size("blk") - SPAN
    length = lax.axis_size("blk") // SPAN
    shifts = range(1, CHIPS)
    wrapped = around(jnp.where(index >= last, y, x))
    y_back = along_ring(y, 1)
    x_next = along_ring(x, -1)
    first = [jnp.where(chip + by < CHIPS, y, x) for by in shifts]
    nearest = in_row(first[0], 1)
    y_outer = along_ring(y_back, length - 1)
    x_outer = along_ring(x_next, 1 - length)
    double = 2 * rows
    loss_out, grads_out = ((rows, rows), F32), ((double, width), F32)
    units_out, inverses_out = ((double, width), BF16), ((double, 1), F32)
    from_chips = [(chip < by).astype(jnp.int32) for by in shifts]
    roles = jnp.stack(from_chips + [1 - core] + from_chips)

    def stack(blocks):
        return [pltpu.VMEM((blocks * rows, width), BF16)]

    def inner(_):
        text = jnp.where(index < SPAN, wrapped, y_back)
        image = jnp.where(index >= last, wrapped, x_next)
        then = [jnp.where(chip + by < CHIPS, image, text) for by in shifts]
        got = [nearest, in_row(first[1], 2), in_row(first[2], 3)]
        then[2], got[2] = lax.optimization_barrier((then[2], got[2]))
        twin = to_twin(jnp.concatenate([jnp.where(core == 0, y, x)] + got, axis=0))
        then[1], twin = lax.optimization_barrier((then[1], twin))
        loss, grads, units, inverses = call(
            first_kernel, [loss_out, grads_out, units_out, inverses_out], 8, (scale, bias, roles),
            x, y, positive, *got, twin, scratch=stack(7),
        )
        later = [in_row(block, by) for by, block in zip(shifts, then)]
        *later, loss = lax.optimization_barrier((*later, loss))
        twin = to_twin(jnp.concatenate([jnp.where(core == 0, image, text)] + later, axis=0))
        outs, count = [loss_out, grads_out], len(later)
        loss, grads = call(
            next_kernel, outs, count, (scale, bias, 1 - roles[:count]),
            units, loss, grads, *later, scratch=stack(count),
        )
        loss, grads = call(
            next_kernel, outs, count + 1, (scale, bias, 1 - roles[count:]),
            units, loss, grads, twin, scratch=stack(count + 1),
        )
        return loss, grads, units, inverses

    def skip(_):
        return tuple(jnp.zeros(*out) for out in (loss_out, grads_out, units_out, inverses_out))

    go = lax.optimization_barrier(jnp.int32(1))
    loss, grads, units, inverses = lax.cond(go > 0, inner, skip, 0)
    block = ((rows, width), F32)
    loss, image_grad, text_grad = call(
        last_kernel, [((1, rows), F32), block, block], 2, (scale, bias),
        x, y, y_outer, x_outer, units, inverses, loss, grads,
    )
    return (loss[0], image_grad, text_grad)


def solution(mesh):
    rows = P(("blk", "group"), None)
    return jax.shard_map(
        local,
        mesh=mesh,
        in_specs=(rows, rows, rows, P(), P()),
        out_specs=(P(("blk", "group")), rows, rows),
        check_vma=False,
    )
```

time: 100 us -> 123 us (1.23)
  the two profiles are of different devices: /device:TPU:32 before, /device:TPU:1 now
where the time goes in v7:
time: 123 us; the launch traced here: 121 us
  starting transfers between devices  65 us (53%)
  waiting for transfers between devices  34.5 us (28%)
  Pallas kernels  16.2 us (13%)
  other arithmetic  2.61 us (2%)
  between operations  2.12 us (2%)
    ppermute x4, starting transfers between devices, along_ring(): return lax.ppermute(x, ('blk', 'group'), pairs)  35.6 us
    ppermute x1, waiting for transfers between devices, around(): return lax.ppermute(x, 'blk', pairs)  22.4 us
    ppermute x6, starting transfers between devices, in_row(): return lax.ppermute(x, 'blk', pairs)  20.2 us
    pallas_call x4, Pallas kernels, call(): pl.pallas_call(kernel, out_shape=[jax.ShapeDtypeStruct(shape, kind) for s...  16.2 us
    ppermute x6, waiting for transfers between devices, in_row(): return lax.ppermute(x, 'blk', pairs)  12.1 us
    ppermute x2, starting transfers between devices, to_twin(): lax.ppermute(x, 'blk', [(i, i ^ 1) for i in range(lax.axis_size('blk'))])  7.21 us
  transfers between devices with their start and end apart: 13, of which 4 were waited for; matrix products, arithmetic and copies ran while one was open for 2% of the time, Pallas kernels for 11%

profile of v7, /device:TPU:1, one launch (start us, length us, event | category | flops | bytes accessed | tf_op | source)
XLA Modules:
  0.0 120.7 jit_solution(11614160712617437787)
XLA Ops:
  0.6 0.0 copy-start.1
  0.6 0.0 copy-start
  0.7 0.0 copy-start.2
  0.7 4.5 %collective-permute-start.7 = (bf16[128,1152]{1,0:T(8,128)(2,1)}, bf16[128,1152]{1,0:T(8,128)(2,1)}, u32[]{:S(2)}, u32[]{:S(2)}) collective-permute-start(bf16[128,1152]{1,0:T(8,128)(2,1)} %y_ref.1), channel_id=1, source_target_pairs={{0,128},{1,129},{2,130},{3,131},{4,132},{5,133},{6,134},{7,135},{8... | collective-permute-start | bytes 884744 | tf_op jit(solution)/shard_map/ppermute | solution.py:27
  5.2 19.2 %collective-permute-start.9 = (bf16[128,1152]{1,0:T(8,128)(2,1)}, bf16[128,1152]{1,0:T(8,128)(2,1)}, u32[]{:S(2)}, u32[]{:S(2)}) collective-permute-start(bf16[128,1152]{1,0:T(8,128)(2,1)} %x_ref.1), channel_id=1, source_target_pairs={{0,911},{1,896},{2,897},{3,898},{4,899},{5,900},{6,901},{7,902},{8... | collective-permute-start | bytes 884744 | tf_op jit(solution)/shard_map/ppermute | solution.py:27
  24.4 1.1 broadcast_select_fusion.9
  25.6 1.9 %collective-permute-start.11 = (bf16[128,1152]{1,0:T(8,128)(2,1)S(1)}, bf16[128,1152]{1,0:T(8,128)(2,1)S(1)}, u32[]{:S(2)}, u32[]{:S(2)}) collective-permute-start(bf16[128,1152]{1,0:T(8,128)(2,1)S(1)} %get-tuple-element.102), channel_id=1, source_target_pairs={{896,0},{912,16},{928,32},{944,48},{960,64},{976,80},{992,96},{100... | collective-permute-start | bytes 884744 | tf_op jit(solution)/shard_map/ppermute | solution.py:41
  27.5 3.1 %collective-permute-start.12 = (bf16[128,1152]{1,0:T(8,128)(2,1)S(1)}, bf16[128,1152]{1,0:T(8,128)(2,1)S(1)}, u32[]{:S(2)}, u32[]{:S(2)}) collective-permute-start(bf16[128,1152]{1,0:T(8,128)(2,1)S(1)} %get-tuple-element.101), channel_id=1, source_target_pairs={{0,32},{16,48},{32,64},{48,80},{64,96},{80,112},{96,0},{112,16},{1... | collective-permute-start | bytes 884744 | tf_op jit(solution)/shard_map/ppermute | solution.py:35
  30.6 0.0 collective-permute-done.9
  30.6 8.1 %collective-permute-start.10 = (bf16[128,1152]{1,0:T(8,128)(2,1)}, bf16[128,1152]{1,0:T(8,128)(2,1)S(1)}, u32[]{:S(2)}, u32[]{:S(2)}) collective-permute-start(bf16[128,1152]{1,0:T(8,128)(2,1)} %collective-permute-done.9), channel_id=1, source_target_pairs={{0,143},{1,128},{2,129},{3,130},{4,131},{5,132},{6,133},{7,134},{8... | collective-permute-start | bytes 884744 | tf_op jit(solution)/shard_map/ppermute | solution.py:27
  38.8 0.0 collective-permute-done.7
  38.8 3.8 %collective-permute-start.8 = (bf16[128,1152]{1,0:T(8,128)(2,1)}, bf16[128,1152]{1,0:T(8,128)(2,1)S(1)}, u32[]{:S(2)}, u32[]{:S(2)}) collective-permute-start(bf16[128,1152]{1,0:T(8,128)(2,1)} %collective-permute-done.7), channel_id=1, source_target_pairs={{0,896},{1,897},{2,898},{3,899},{4,900},{5,901},{6,902},{7,903},{8... | collective-permute-start | bytes 884744 | tf_op jit(solution)/shard_map/ppermute | solution.py:27
  43.9 0.1 stack.34
  43.9 22.4 %collective-permute-done.11 = bf16[128,1152]{1,0:T(8,128)(2,1)S(1)} collective-permute-done((bf16[128,1152]{1,0:T(8,128)(2,1)S(1)}, bf16[128,1152]{1,0:T(8,128)(2,1)S(1)}, u32[]{:S(2)}, u32[]{:S(2)}) %collective-permute-start.11) | collective-permute-done | bytes 294944 | tf_op jit(solution)/shard_map/ppermute | solution.py:41
  66.3 0.0 collective-permute-done.12
  66.3 0.0 copy-done.1
  66.3 0.0 copy-done
  66.3 0.0 copy-done.2
  66.3 51.0 %conditional.1 = (f32[128,128]{1,0:T(8,128)}, f32[256,1152]{1,0:T(8,128)S(1)}, bf16[256,1152]{1,0:T(8,128)(2,1)}, f32[256,1]{1,0:T(8,128)S(1)}) conditional(s32[]{:T(128)} %convert_element_type.2, () %tuple.19, (s32[7]{0:T(128)S(1)}, s32[]{:T(128)}, bf16[128,1152]{1,0:T(8,128)(2,1)S(1)}, bf16[128,1152]{1,0:T(8,128)(2,1)S(1)}, s32[]{:T(128)}, ...), branch_computations={%region_0.1_spmd, %region_1.2_spmd} | conditional | flops 1143226368 | bytes 40501716 | solution.py:214
  66.4 0.1 broadcast_select_fusion.2
  66.5 4.3 %collective-permute-start.1 = (bf16[128,1152]{1,0:T(8,128)(2,1)S(1)}, bf16[128,1152]{1,0:T(8,128)(2,1)S(1)}, u32[]{:S(2)}, u32[]{:S(2)}) collective-permute-start(bf16[128,1152]{1,0:T(8,128)(2,1)S(1)} %get-tuple-element.99), channel_id=1, source_target_pairs={{0,96},{16,112},{32,0},{48,16},{64,32},{80,48},{96,64},{112,80},{1... | collective-permute-start | bytes 884744 | tf_op jit(solution)/shard_map/cond/branch_1_fun/ppermute | solution.py:35
  70.7 2.6 %collective-permute-start = (bf16[128,1152]{1,0:T(8,128)(2,1)S(1)}, bf16[128,1152]{1,0:T(8,128)(2,1)S(1)}, u32[]{:S(2)}, u32[]{:S(2)}) collective-permute-start(bf16[128,1152]{1,0:T(8,128)(2,1)S(1)} %get-tuple-element.100), channel_id=1, source_target_pairs={{0,64},{16,80},{32,96},{48,112},{64,0},{80,16},{96,32},{112,48},{1... | collective-permute-start | bytes 884744 | tf_op jit(solution)/shard_map/cond/branch_1_fun/ppermute | solution.py:35
  73.3 1.1 broadcast_select_fusion.1
  74.4 0.1 broadcast_select_fusion
  74.5 2.6 %collective-permute-done.1.rest_2_ = bf16[128,1152]{1,0:T(8,128)(2,1)S(1)} collective-permute-done((bf16[128,1152]{1,0:T(8,128)(2,1)S(1)}, bf16[128,1152]{1,0:T(8,128)(2,1)S(1)}, u32[]{:S(2)}, u32[]{:S(2)}) %collective-permute-start.1) | collective-permute-done | bytes 294944 | tf_op jit(solution)/shard_map/cond/branch_1_fun/ppermute | solution.py:35
  77.1 4.6 %collective-permute-done.rest_1_ = bf16[128,1152]{1,0:T(8,128)(2,1)S(1)} collective-permute-done((bf16[128,1152]{1,0:T(8,128)(2,1)S(1)}, bf16[128,1152]{1,0:T(8,128)(2,1)S(1)}, u32[]{:S(2)}, u32[]{:S(2)}) %collective-permute-start) | collective-permute-done | bytes 294944 | tf_op jit(solution)/shard_map/cond/branch_1_fun/ppermute | solution.py:35
  81.7 0.1 pad_maximum_fusion
  81.8 4.5 %collective-permute-start.2 = (bf16[512,1152]{1,0:T(8,128)(2,1)S(1)}, bf16[512,1152]{1,0:T(8,128)(2,1)S(1)}, u32[]{:S(2)}, u32[]{:S(2)}) collective-permute-start(bf16[512,1152]{1,0:T(8,128)(2,1)S(1)} %pad_maximum_fusion), channel_id=1, source_target_pairs={{0,16},{16,0},{32,48},{48,32},{64,80},{80,64},{96,112},{112,96},{1... | collective-permute-start | bytes 3538952 | tf_op jit(solution)/shard_map/cond/branch_1_fun/ppermute | solution.py:45
  86.3 3.8 %collective-permute-start.3 = (bf16[128,1152]{1,0:T(8,128)(2,1)S(1)}, bf16[128,1152]{1,0:T(8,128)(2,1)S(1)}, u32[]{:S(2)}, u32[]{:S(2)}) collective-permute-start(bf16[128,1152]{1,0:T(8,128)(2,1)S(1)} %get-tuple-element.95), channel_id=1, source_target_pairs={{0,32},{16,48},{32,64},{48,80},{64,96},{80,112},{96,0},{112,16},{1... | collective-permute-start | bytes 884744 | tf_op jit(solution)/shard_map/cond/branch_1_fun/ppermute | solution.py:35
  90.1 3.4 %collective-permute-start.5 = (bf16[128,1152]{1,0:T(8,128)(2,1)S(1)}, bf16[128,1152]{1,0:T(8,128)(2,1)S(1)}, u32[]{:S(2)}, u32[]{:S(2)}) collective-permute-start(bf16[128,1152]{1,0:T(8,128)(2,1)S(1)} %get-tuple-element.61), channel_id=1, source_target_pairs={{0,96},{16,112},{32,0},{48,16},{64,32},{80,48},{96,64},{112,80},{1... | collective-permute-start | bytes 884744 | tf_op jit(solution)/shard_map/cond/branch_1_fun/ppermute | solution.py:35
  93.5 0.0 collective-permute-done.2.rest_3_
  93.5 3.1 %collective-permute-start.4 = (bf16[128,1152]{1,0:T(8,128)(2,1)S(1)}, bf16[128,1152]{1,0:T(8,128)(2,1)S(1)}, u32[]{:S(2)}, u32[]{:S(2)}) collective-permute-start(bf16[128,1152]{1,0:T(8,128)(2,1)S(1)} %get-tuple-element.60), channel_id=1, source_target_pairs={{0,64},{16,80},{32,96},{48,112},{64,0},{80,16},{96,32},{112,48},{1... | collective-permute-start | bytes 884744 | tf_op jit(solution)/shard_map/cond/branch_1_fun/ppermute | solution.py:35
  96.6 4.7 %branch_1_fun.3 = (f32[128,128]{1,0:T(8,128)S(1)}, f32[256,1152]{1,0:T(8,128)S(1)}, bf16[256,1152]{1,0:T(8,128)(2,1)}, f32[256,1]{1,0:T(8,128)S(1)}) custom-call(f32[1]{0:T(128)} %get-tuple-element.44.scale, f32[1]{0:T(128)} %get-tuple-element.45.bias, s32[7]{0:T(128)S(1)} %get-tuple-element.46.roles, bf16[128,1152]{1,0:T(8,128)(2,1)S(1)} %get-tuple-element.47.x_ref, ...), custom_call_target="tpu_custom_call" | custom-call | flops 603979776 | bytes 8388608 | tf_op jit(solution)/shard_map/cond/branch_1_fun/pallas_call | solution.py:147
  101.3 0.0 collective-permute-done.3.rest_0_
  101.3 0.0 collective-permute-done.5.rest_2_
  101.3 4.9 %collective-permute-done.4.rest_1_ = bf16[128,1152]{1,0:T(8,128)(2,1)S(1)} collective-permute-done((bf16[128,1152]{1,0:T(8,128)(2,1)S(1)}, bf16[128,1152]{1,0:T(8,128)(2,1)S(1)}, u32[]{:S(2)}, u32[]{:S(2)}) %collective-permute-start.4) | collective-permute-done | bytes 294944 | tf_op jit(solution)/shard_map/cond/branch_1_fun/ppermute | solution.py:35
  106.2 0.1 pad_maximum_fusion.1
  106.3 2.7 %collective-permute-start.6 = (bf16[512,1152]{1,0:T(8,128)(2,1)S(1)}, bf16[512,1152]{1,0:T(8,128)(2,1)S(1)}, u32[]{:S(2)}, u32[]{:S(2)}) collective-permute-start(bf16[512,1152]{1,0:T(8,128)(2,1)S(1)} %pad_maximum_fusion.1), channel_id=1, source_target_pairs={{0,16},{16,0},{32,48},{48,32},{64,80},{80,64},{96,112},{112,96},{1... | collective-permute-start | bytes 3538952 | tf_op jit(solution)/shard_map/cond/branch_1_fun/ppermute | solution.py:45
  109.0 0.1 slice_subtract_fusion.1.roles
  109.1 4.0 %branch_1_fun.4 = (f32[128,128]{1,0:T(8,128)S(1)}, f32[256,1152]{1,0:T(8,128)S(1)}) custom-call(f32[1]{0:T(128)} %get-tuple-element.44.scale, f32[1]{0:T(128)} %get-tuple-element.45.bias, s32[3]{0:T(128)S(1)} %slice_subtract_fusion.roles, bf16[256,1152]{1,0:T(8,128)(2,1)} %get-tuple-element.109.units_ref, f32[128,128]{1,0:T(8,128)S(1)} %get-tuple-element.63.loss_in, ...), custom_call_target="tpu_custom_call" | custom-call | flops 226492416 | bytes 3145728 | tf_op jit(solution)/shard_map/cond/branch_1_fun/pallas_call | solution.py:147
  113.1 0.0 collective-permute-done.6.rest_0_
  113.1 4.3 %branch_1_fun.5 = (f32[128,128]{1,0:T(8,128)}, f32[256,1152]{1,0:T(8,128)S(1)}) custom-call(f32[1]{0:T(128)} %get-tuple-element.44.scale, f32[1]{0:T(128)} %get-tuple-element.45.bias, s32[4]{0:T(128)S(1)} %slice_subtract_fusion.1.roles, bf16[256,1152]{1,0:T(8,128)(2,1)} %get-tuple-element.109.units_ref, f32[128,128]{1,0:T(8,128)S(1)} %get-tuple-element.68.loss_in, ...), custom_call_target="tpu_custom_call" | custom-call | flops 301989888 | bytes 4194304 | tf_op jit(solution)/shard_map/cond/branch_1_fun/pallas_call | solution.py:147
  117.4 0.0 collective-permute-done.10.xg_ref
  117.4 0.0 collective-permute-done.8.yg_ref
  117.4 3.3 %shard_map.77 = (f32[1,128]{1,0:T(1,128)}, f32[128,1152]{1,0:T(8,128)}, f32[128,1152]{1,0:T(8,128)}) custom-call(f32[1]{0:T(128)S(6)} %copy.17.scale, f32[1]{0:T(128)S(6)} %copy.18.bias, bf16[128,1152]{1,0:T(8,128)(2,1)S(1)} %copy-done, bf16[128,1152]{1,0:T(8,128)(2,1)S(1)} %copy-done.1, bf16[128,1152]{1,0:T(8,128)(2,1)S(1)} %collective-permute-done.8.yg_ref, ...), custom_call_target="tpu_custom_call" | custom-call | flops 150994944 | bytes 2097152 | tf_op jit(solution)/shard_map/pallas_call | solution.py:147
  (1 shorter events, 0.0 us)
Async XLA Ops:
  0.6 65.7 %copy-start.1 = (bf16[128,1152]{1,0:T(8,128)(2,1)S(1)}, bf16[128,1152]{1,0:T(8,128)(2,1)}, u32[]{:S(2)}) copy-start(bf16[128,1152]{1,0:T(8,128)(2,1)} %y_ref.1) | copy-start | bytes 884740
  0.6 65.7 %copy-start = (bf16[128,1152]{1,0:T(8,128)(2,1)S(1)}, bf16[128,1152]{1,0:T(8,128)(2,1)}, u32[]{:S(2)}) copy-start(bf16[128,1152]{1,0:T(8,128)(2,1)} %x_ref.1) | copy-start | bytes 884740
  0.7 65.7 %copy-start.2 = (s32[1,128]{1,0:T(1,128)S(1)}, s32[1,128]{1,0:T(1,128)}, u32[]{:S(2)}) copy-start(s32[1,128]{1,0:T(1,128)} %param.9) | copy-start | bytes 1540
  0.7 38.1 %collective-permute-start.7 = (bf16[128,1152]{1,0:T(8,128)(2,1)}, bf16[128,1152]{1,0:T(8,128)(2,1)}, u32[]{:S(2)}, u32[]{:S(2)}) collective-permute-start(bf16[128,1152]{1,0:T(8,128)(2,1)} %y_ref.1), channel_id=1, source_target_pairs={{0,128},{1,129},{2,130},{3,131},{4,132},{5,133},{6,134},{7,135},{8... | collective-permute-start | bytes 884744 | tf_op jit(solution)/shard_map/ppermute | solution.py:27
  5.2 25.4 %collective-permute-start.9 = (bf16[128,1152]{1,0:T(8,128)(2,1)}, bf16[128,1152]{1,0:T(8,128)(2,1)}, u32[]{:S(2)}, u32[]{:S(2)}) collective-permute-start(bf16[128,1152]{1,0:T(8,128)(2,1)} %x_ref.1), channel_id=1, source_target_pairs={{0,911},{1,896},{2,897},{3,898},{4,899},{5,900},{6,901},{7,902},{8... | collective-permute-start | bytes 884744 | tf_op jit(solution)/shard_map/ppermute | solution.py:27
  25.6 40.8 %collective-permute-start.11 = (bf16[128,1152]{1,0:T(8,128)(2,1)S(1)}, bf16[128,1152]{1,0:T(8,128)(2,1)S(1)}, u32[]{:S(2)}, u32[]{:S(2)}) collective-permute-start(bf16[128,1152]{1,0:T(8,128)(2,1)S(1)} %get-tuple-element.102), channel_id=1, source_target_pairs={{896,0},{912,16},{928,32},{944,48},{960,64},{976,80},{992,96},{100... | collective-permute-start | bytes 884744 | tf_op jit(solution)/shard_map/ppermute | solution.py:41
  27.5 38.8 %collective-permute-start.12 = (bf16[128,1152]{1,0:T(8,128)(2,1)S(1)}, bf16[128,1152]{1,0:T(8,128)(2,1)S(1)}, u32[]{:S(2)}, u32[]{:S(2)}) collective-permute-start(bf16[128,1152]{1,0:T(8,128)(2,1)S(1)} %get-tuple-element.101), channel_id=1, source_target_pairs={{0,32},{16,48},{32,64},{48,80},{64,96},{80,112},{96,0},{112,16},{1... | collective-permute-start | bytes 884744 | tf_op jit(solution)/shard_map/ppermute | solution.py:35
  30.6 86.8 %collective-permute-start.10 = (bf16[128,1152]{1,0:T(8,128)(2,1)}, bf16[128,1152]{1,0:T(8,128)(2,1)S(1)}, u32[]{:S(2)}, u32[]{:S(2)}) collective-permute-start(bf16[128,1152]{1,0:T(8,128)(2,1)} %collective-permute-done.9), channel_id=1, source_target_pairs={{0,143},{1,128},{2,129},{3,130},{4,131},{5,132},{6,133},{7,134},{8... | collective-permute-start | bytes 884744 | tf_op jit(solution)/shard_map/ppermute | solution.py:27
  38.8 78.6 %collective-permute-start.8 = (bf16[128,1152]{1,0:T(8,128)(2,1)}, bf16[128,1152]{1,0:T(8,128)(2,1)S(1)}, u32[]{:S(2)}, u32[]{:S(2)}) collective-permute-start(bf16[128,1152]{1,0:T(8,128)(2,1)} %collective-permute-done.7), channel_id=1, source_target_pairs={{0,896},{1,897},{2,898},{3,899},{4,900},{5,901},{6,902},{7,903},{8... | collective-permute-start | bytes 884744 | tf_op jit(solution)/shard_map/ppermute | solution.py:27
  66.5 10.6 %collective-permute-start.1 = (bf16[128,1152]{1,0:T(8,128)(2,1)S(1)}, bf16[128,1152]{1,0:T(8,128)(2,1)S(1)}, u32[]{:S(2)}, u32[]{:S(2)}) collective-permute-start(bf16[128,1152]{1,0:T(8,128)(2,1)S(1)} %get-tuple-element.99), channel_id=1, source_target_pairs={{0,96},{16,112},{32,0},{48,16},{64,32},{80,48},{96,64},{112,80},{1... | collective-permute-start | bytes 884744 | tf_op jit(solution)/shard_map/cond/branch_1_fun/ppermute | solution.py:35
  70.7 11.0 %collective-permute-start = (bf16[128,1152]{1,0:T(8,128)(2,1)S(1)}, bf16[128,1152]{1,0:T(8,128)(2,1)S(1)}, u32[]{:S(2)}, u32[]{:S(2)}) collective-permute-start(bf16[128,1152]{1,0:T(8,128)(2,1)S(1)} %get-tuple-element.100), channel_id=1, source_target_pairs={{0,64},{16,80},{32,96},{48,112},{64,0},{80,16},{96,32},{112,48},{1... | collective-permute-start | bytes 884744 | tf_op jit(solution)/shard_map/cond/branch_1_fun/ppermute | solution.py:35
  81.8 11.7 %collective-permute-start.2 = (bf16[512,1152]{1,0:T(8,128)(2,1)S(1)}, bf16[512,1152]{1,0:T(8,128)(2,1)S(1)}, u32[]{:S(2)}, u32[]{:S(2)}) collective-permute-start(bf16[512,1152]{1,0:T(8,128)(2,1)S(1)} %pad_maximum_fusion), channel_id=1, source_target_pairs={{0,16},{16,0},{32,48},{48,32},{64,80},{80,64},{96,112},{112,96},{1... | collective-permute-start | bytes 3538952 | tf_op jit(solution)/shard_map/cond/branch_1_fun/ppermute | solution.py:45
  86.3 15.0 %collective-permute-start.3 = (bf16[128,1152]{1,0:T(8,128)(2,1)S(1)}, bf16[128,1152]{1,0:T(8,128)(2,1)S(1)}, u32[]{:S(2)}, u32[]{:S(2)}) collective-permute-start(bf16[128,1152]{1,0:T(8,128)(2,1)S(1)} %get-tuple-element.95), channel_id=1, source_target_pairs={{0,32},{16,48},{32,64},{48,80},{64,96},{80,112},{96,0},{112,16},{1... | collective-permute-start | bytes 884744 | tf_op jit(solution)/shard_map/cond/branch_1_fun/ppermute | solution.py:35
  90.1 11.2 %collective-permute-start.5 = (bf16[128,1152]{1,0:T(8,128)(2,1)S(1)}, bf16[128,1152]{1,0:T(8,128)(2,1)S(1)}, u32[]{:S(2)}, u32[]{:S(2)}) collective-permute-start(bf16[128,1152]{1,0:T(8,128)(2,1)S(1)} %get-tuple-element.61), channel_id=1, source_target_pairs={{0,96},{16,112},{32,0},{48,16},{64,32},{80,48},{96,64},{112,80},{1... | collective-permute-start | bytes 884744 | tf_op jit(solution)/shard_map/cond/branch_1_fun/ppermute | solution.py:35
  93.5 12.7 %collective-permute-start.4 = (bf16[128,1152]{1,0:T(8,128)(2,1)S(1)}, bf16[128,1152]{1,0:T(8,128)(2,1)S(1)}, u32[]{:S(2)}, u32[]{:S(2)}) collective-permute-start(bf16[128,1152]{1,0:T(8,128)(2,1)S(1)} %get-tuple-element.60), channel_id=1, source_target_pairs={{0,64},{16,80},{32,96},{48,112},{64,0},{80,16},{96,32},{112,48},{1... | collective-permute-start | bytes 884744 | tf_op jit(solution)/shard_map/cond/branch_1_fun/ppermute | solution.py:35
  106.3 6.8 %collective-permute-start.6 = (bf16[512,1152]{1,0:T(8,128)(2,1)S(1)}, bf16[512,1152]{1,0:T(8,128)(2,1)S(1)}, u32[]{:S(2)}, u32[]{:S(2)}) collective-permute-start(bf16[512,1152]{1,0:T(8,128)(2,1)S(1)} %pad_maximum_fusion.1), channel_id=1, source_target_pairs={{0,16},{16,0},{32,48},{48,32},{64,80},{80,64},{96,112},{112,96},{1... | collective-permute-start | bytes 3538952 | tf_op jit(solution)/shard_map/cond/branch_1_fun/ppermute | solution.py:45

commit v8 on v7

--- a/solution.py
+++ b/solution.py
@@ -169,14 +169,16 @@
     y_back = along_ring(y, 1)
     x_next = along_ring(x, -1)
     first = [jnp.where(chip + by < CHIPS, y, x) for by in shifts]
-    nearest = in_row(first[0], 1)
-    y_outer = along_ring(y_back, length - 1)
-    x_outer = along_ring(x_next, 1 - length)
+    near, far = in_row(first[0], 1), in_row(first[2], 3)
+    y_outer, wrapped = lax.optimization_barrier((y_back, wrapped))
+    x_outer, wrapped = lax.optimization_barrier((x_next, wrapped))
+    y_outer = along_ring(y_outer, length - 1)
+    x_outer = along_ring(x_outer, 1 - length)
     double = 2 * rows
     loss_out, grads_out = ((rows, rows), F32), ((double, width), F32)
     units_out, inverses_out = ((double, width), BF16), ((double, 1), F32)
-    from_chips = [(chip < by).astype(jnp.int32) for by in shifts]
-    roles = jnp.stack(from_chips + [1 - core] + from_chips)
+    near_role, middle_role, far_role = [(chip < by).astype(jnp.int32) for by in shifts]
+    twin_role = 1 - core
 
     def stack(blocks):
         return [pltpu.VMEM((blocks * rows, width), BF16)]
@@ -185,26 +187,25 @@
         text = jnp.where(index < SPAN, wrapped, y_back)
         image = jnp.where(index >= last, wrapped, x_next)
         then = [jnp.where(chip + by < CHIPS, image, text) for by in shifts]
-        got = [nearest, in_row(first[1], 2), in_row(first[2], 3)]
-        then[2], got[2] = lax.optimization_barrier((then[2], got[2]))
-        twin = to_twin(jnp.concatenate([jnp.where(core == 0, y, x)] + got, axis=0))
-        then[1], twin = lax.optimization_barrier((then[1], twin))
+        mine, other = jnp.where(core == 0, y, x), jnp.where(core == 0, image, text)
+        twin = to_twin(jnp.concatenate([mine, near, far], axis=0))
+        middle = in_row(first[1], 2)
+        then[2], twin = lax.optimization_barrier((then[2], twin))
+        then[1], middle = lax.optimization_barrier((then[1], middle))
+        scalars = (scale, bias, jnp.stack([near_role, far_role, twin_role, near_role, far_role]))
         loss, grads, units, inverses = call(
-            first_kernel, [loss_out, grads_out, units_out, inverses_out], 8, (scale, bias, roles),
-            x, y, positive, *got, twin, scratch=stack(7),
+            first_kernel, [loss_out, grads_out, units_out, inverses_out], 6, scalars,
+            x, y, positive, near, far, twin, scratch=stack(5),
         )
-        later = [in_row(block, by) for by, block in zip(shifts, then)]
+        later = [in_row(block, by) for by, block in zip(shifts, then)] + [middle]
         *later, loss = lax.optimization_barrier((*later, loss))
-        twin = to_twin(jnp.concatenate([jnp.where(core == 0, image, text)] + later, axis=0))
-        outs, count = [loss_out, grads_out], len(later)
-        loss, grads = call(
-            next_kernel, outs, count, (scale, bias, 1 - roles[:count]),
-            units, loss, grads, *later, scratch=stack(count),
-        )
-        loss, grads = call(
-            next_kernel, outs, count + 1, (scale, bias, 1 - roles[count:]),
-            units, loss, grads, twin, scratch=stack(count + 1),
-        )
+        twin = to_twin(jnp.concatenate([other] + later, axis=0))
+        later_roles = [1 - near_role, 1 - middle_role, 1 - far_role, middle_role]
+        for roles, refs in ((later_roles, later), ([1 - twin_role] + later_roles, [twin])):
+            loss, grads = call(
+                next_kernel, [loss_out, grads_out], len(roles), (scale, bias, jnp.stack(roles)),
+                units, loss, grads, *refs, scratch=stack(len(roles)),
+            )
         return loss, grads, units, inverses
 
     def skip(_):

time: 123 us -> 110 us (0.89); the launches traced: 121 us -> 109 us
  waiting for transfers between devices: 34.5 us -> 8.3 us
  local copies, waits for them, and re-layouts: 0.1 us -> 5.22 us
  starting transfers between devices: 65 us -> 69.8 us
  other arithmetic: 2.61 us -> 5.18 us
  Pallas kernels: 16.2 us -> 18.5 us
    ppermute x1, waiting for transfers between devices: 22.4 us -> 0.01 us  [around(): return lax.ppermute(x, 'blk', pairs)]
    ppermute x1, starting transfers between devices: 1.92 us -> 13.7 us  [around(): return lax.ppermute(x, 'blk', pairs)]
    ppermute x4, starting transfers between devices: 35.6 us -> 29.6 us  [along_ring(): return lax.ppermute(x, ('blk', 'group'), pairs)]
    cond x0 -> x13, local copies, waits for them, and re-layouts: none -> 4.3 us
    ppermute x6, waiting for transfers between devices: 12.1 us -> 8.28 us  [in_row(): return lax.ppermute(x, 'blk', pairs)]
    pallas_call x4, Pallas kernels: 16.2 us -> 18.5 us  [call(): pl.pallas_call(kernel, out_shape=[jax.ShapeDtypeStruct(shape, kind) for s...]
    cond x0 -> x1, other arithmetic: none -> 1.84 us
  transfers between devices with their start and end apart: 13 -> 13, of which waited for: 4 -> 3; matrix products, arithmetic and copies ran while one was open for 2% -> 6% of each run, Pallas kernels for 11% -> 13%
where the time goes in v8:
time: 110 us; the launch traced here: 109 us
  starting transfers between devices  69.8 us (63%)
  Pallas kernels  18.5 us (17%)
  waiting for transfers between devices  8.3 us (8%)
  local copies, waits for them, and re-layouts  5.22 us (5%)
  other arithmetic  5.18 us (5%)
  between operations  2.12 us (2%)
    ppermute x4, starting transfers between devices, along_ring(): return lax.ppermute(x, ('blk', 'group'), pairs)  29.6 us
    ppermute x6, starting transfers between devices, in_row(): return lax.ppermute(x, 'blk', pairs)  20.2 us
    pallas_call x4, Pallas kernels, call(): pl.pallas_call(kernel, out_shape=[jax.ShapeDtypeStruct(shape, kind) for s...  18.5 us
    ppermute x1, starting transfers between devices, around(): return lax.ppermute(x, 'blk', pairs)  13.7 us
    ppermute x6, waiting for transfers between devices, in_row(): return lax.ppermute(x, 'blk', pairs)  8.28 us
    ppermute x2, starting transfers between devices, to_twin(): lax.ppermute(x, 'blk', [(i, i ^ 1) for i in range(lax.axis_size('blk'))])  6.31 us
    cond x13, local copies, waits for them, and re-layouts  4.3 us
  transfers between devices with their start and end apart: 13, of which 3 were waited for; matrix products, arithmetic and copies ran while one was open for 6% of the time, Pallas kernels for 13%

profile of v8, /device:TPU:1, one launch (start us, length us, event | category | flops | bytes accessed | tf_op | source)
XLA Modules:
  0.0 109.3 jit_solution(15606108520435201909)
XLA Ops:
  0.6 0.0 copy-start.2
  0.6 0.0 copy-start.3
  0.7 1.2 %broadcast_select_fusion.7 = (bf16[128,1152]{1,0:T(8,128)(2,1)S(1)}, bf16[128,1152]{1,0:T(8,128)(2,1)S(1)}, bf16[128,1152]{1,0:T(8,128)(2,1)S(1)}) fusion(bf16[128,1152]{1,0:T(8,128)(2,1)} %y_ref.1, bf16[128,1152]{1,0:T(8,128)(2,1)} %x_ref.1, pred[]{:T(512)S(6)} %lt.46, pred[]{:T(512)S(6)} %lt.45, pred[]{:T(512)S(6)} %ge.6), kind=kLoop, calls=%fused_computation.14 | loop fusion | flops 442368 | bytes 1474563 | tf_op jit(solution)/shard_map/jit(_where)/select_n | solution.py:171
  1.9 13.7 %collective-permute-start.7 = (bf16[128,1152]{1,0:T(8,128)(2,1)S(1)}, bf16[128,1152]{1,0:T(8,128)(2,1)S(1)}, u32[]{:S(2)}, u32[]{:S(2)}) collective-permute-start(bf16[128,1152]{1,0:T(8,128)(2,1)S(1)} %get-tuple-element.125), channel_id=1, source_target_pairs={{896,0},{912,16},{928,32},{944,48},{960,64},{976,80},{992,96},{100... | collective-permute-start | bytes 884744 | tf_op jit(solution)/shard_map/ppermute | solution.py:41
  15.6 1.9 %collective-permute-start.6 = (bf16[128,1152]{1,0:T(8,128)(2,1)S(1)}, bf16[128,1152]{1,0:T(8,128)(2,1)}, u32[]{:S(2)}, u32[]{:S(2)}) collective-permute-start(bf16[128,1152]{1,0:T(8,128)(2,1)S(1)} %copy-done.3), channel_id=1, source_target_pairs={{0,128},{1,129},{2,130},{3,131},{4,132},{5,133},{6,134},{7,135},{8... | collective-permute-start | bytes 884744 | tf_op jit(solution)/shard_map/ppermute | solution.py:27
  17.6 14.5 %collective-permute-start.9 = (bf16[128,1152]{1,0:T(8,128)(2,1)S(1)}, bf16[128,1152]{1,0:T(8,128)(2,1)}, u32[]{:S(2)}, u32[]{:S(2)}) collective-permute-start(bf16[128,1152]{1,0:T(8,128)(2,1)S(1)} %copy-done.2), channel_id=1, source_target_pairs={{0,911},{1,896},{2,897},{3,898},{4,899},{5,900},{6,901},{7,902},{8... | collective-permute-start | bytes 884744 | tf_op jit(solution)/shard_map/ppermute | solution.py:27
  32.1 3.1 %collective-permute-start.11 = (bf16[128,1152]{1,0:T(8,128)(2,1)S(1)}, bf16[128,1152]{1,0:T(8,128)(2,1)S(1)}, u32[]{:S(2)}, u32[]{:S(2)}) collective-permute-start(bf16[128,1152]{1,0:T(8,128)(2,1)S(1)} %get-tuple-element.124), channel_id=1, source_target_pairs={{0,32},{16,48},{32,64},{48,80},{64,96},{80,112},{96,0},{112,16},{1... | collective-permute-start | bytes 884744 | tf_op jit(solution)/shard_map/ppermute | solution.py:35
  35.2 3.4 %collective-permute-start.12 = (bf16[128,1152]{1,0:T(8,128)(2,1)S(1)}, bf16[128,1152]{1,0:T(8,128)(2,1)S(1)}, u32[]{:S(2)}, u32[]{:S(2)}) collective-permute-start(bf16[128,1152]{1,0:T(8,128)(2,1)S(1)} %get-tuple-element.123), channel_id=1, source_target_pairs={{0,96},{16,112},{32,0},{48,16},{64,32},{80,48},{96,64},{112,80},{1... | collective-permute-start | bytes 884744 | tf_op jit(solution)/shard_map/ppermute | solution.py:35
  38.6 0.0 collective-permute-done.7
  38.6 0.0 collective-permute-done.6
  38.6 0.0 collective-permute-done.9
  38.6 11.2 %collective-permute-start.10 = (bf16[128,1152]{1,0:T(8,128)(2,1)}, bf16[128,1152]{1,0:T(8,128)(2,1)S(1)}, u32[]{:S(2)}, u32[]{:S(2)}) collective-permute-start(bf16[128,1152]{1,0:T(8,128)(2,1)} %collective-permute-done.9), channel_id=1, source_target_pairs={{0,143},{1,128},{2,129},{3,130},{4,131},{5,132},{6,133},{7,134},{8... | collective-permute-start | bytes 884744 | tf_op jit(solution)/shard_map/ppermute | solution.py:27
  49.9 1.9 %collective-permute-start.8 = (bf16[128,1152]{1,0:T(8,128)(2,1)}, bf16[128,1152]{1,0:T(8,128)(2,1)S(1)}, u32[]{:S(2)}, u32[]{:S(2)}) collective-permute-start(bf16[128,1152]{1,0:T(8,128)(2,1)} %collective-permute-done.6), channel_id=1, source_target_pairs={{0,896},{1,897},{2,898},{3,899},{4,900},{5,901},{6,902},{7,903},{8... | collective-permute-start | bytes 884744 | tf_op jit(solution)/shard_map/ppermute | solution.py:27
  53.1 0.0 collective-permute-done.11
  53.1 52.5 %conditional.1 = (f32[128,128]{1,0:T(8,128)S(1)}, f32[256,1152]{1,0:T(8,128)}, bf16[256,1152]{1,0:T(8,128)(2,1)}, f32[256,1]{1,0:T(8,128)S(1)}) conditional(s32[]{:T(128)} %convert_element_type.12, () %tuple.23, (s32[]{:T(128)}, pred[]{:T(512)}, s32[]{:T(128)}, s32[]{:T(128)}, s32[]{:T(128)}, /*index=5*/s32[]{:T(128)}, s32[]{:T(128)}, ...), branch_computations={%region_0.1_spmd, %region_1.2_spmd} | conditional | flops 1136295936 | bytes 51413696 | solution.py:215
  53.1 0.0 copy-start.4
  53.1 0.0 copy-start.5
  53.2 0.1 broadcast_select_fusion
  53.3 0.6 copy-done.4
  53.9 0.1 copy-done.5
  54.0 0.1 copy-done.6
  54.1 1.0 pad_maximum_fusion
  55.1 3.0 %collective-permute-start = (bf16[384,1152]{1,0:T(8,128)(2,1)}, bf16[384,1152]{1,0:T(8,128)(2,1)S(1)}, u32[]{:S(2)}, u32[]{:S(2)}) collective-permute-start(bf16[384,1152]{1,0:T(8,128)(2,1)} %pad_maximum_fusion), channel_id=1, source_target_pairs={{0,16},{16,0},{32,48},{48,32},{64,80},{80,64},{96,112},{112,96},{1... | collective-permute-start | bytes 2654216 | tf_op jit(solution)/shard_map/cond/branch_1_fun/ppermute | solution.py:45
  58.0 4.4 %collective-permute-start.2 = (bf16[128,1152]{1,0:T(8,128)(2,1)S(1)}, bf16[128,1152]{1,0:T(8,128)(2,1)S(1)}, u32[]{:S(2)}, u32[]{:S(2)}) collective-permute-start(bf16[128,1152]{1,0:T(8,128)(2,1)S(1)} %get-tuple-element.118), channel_id=1, source_target_pairs={{0,64},{16,80},{32,96},{48,112},{64,0},{80,16},{96,32},{112,48},{1... | collective-permute-start | bytes 884744 | tf_op jit(solution)/shard_map/cond/branch_1_fun/ppermute | solution.py:35
  62.5 1.8 %select_dynamic-update-slice_fusion = (bf16[640,1152]{1,0:T(8,128)(2,1)}, bf16[128,1152]{1,0:T(8,128)(2,1)S(1)}, bf16[128,1152]{1,0:T(8,128)(2,1)S(1)}) fusion(pred[]{:T(512)S(6)} %eq.6, bf16[128,1152]{1,0:T(8,128)(2,1)S(1)} %get-tuple-element.68, bf16[128,1152]{1,0:T(8,128)(2,1)} %get-tuple-element.70, pred[]{:T(512)S(6)} %lt.31, ...), kind=kLoop, calls=%fused_computation.1 | loop fusion | flops 442367 | bytes 1769475 | tf_op jit(solution)/shard_map/cond
  64.3 1.0 broadcast_select_fusion.1
  65.3 2.2 %collective-permute-start.1 = (bf16[128,1152]{1,0:T(8,128)(2,1)}, bf16[128,1152]{1,0:T(8,128)(2,1)S(1)}, u32[]{:S(2)}, u32[]{:S(2)}) collective-permute-start(bf16[128,1152]{1,0:T(8,128)(2,1)} %get-tuple-element.121), channel_id=1, source_target_pairs={{0,32},{16,48},{32,64},{48,80},{64,96},{80,112},{96,0},{112,16},{1... | collective-permute-start | bytes 884744 | tf_op jit(solution)/shard_map/cond/branch_1_fun/ppermute | solution.py:35
  67.5 2.6 %collective-permute-done.2.rest_3_ = bf16[128,1152]{1,0:T(8,128)(2,1)S(1)} collective-permute-done((bf16[128,1152]{1,0:T(8,128)(2,1)S(1)}, bf16[128,1152]{1,0:T(8,128)(2,1)S(1)}, u32[]{:S(2)}, u32[]{:S(2)}) %collective-permute-start.2) | collective-permute-done | bytes 294944 | tf_op jit(solution)/shard_map/cond/branch_1_fun/ppermute | solution.py:35
  70.1 4.4 %collective-permute-start.3 = (bf16[128,1152]{1,0:T(8,128)(2,1)}, bf16[128,1152]{1,0:T(8,128)(2,1)S(1)}, u32[]{:S(2)}, u32[]{:S(2)}) collective-permute-start(bf16[128,1152]{1,0:T(8,128)(2,1)} %get-tuple-element.73), channel_id=1, source_target_pairs={{0,64},{16,80},{32,96},{48,112},{64,0},{80,16},{96,32},{112,48},{1... | collective-permute-start | bytes 884744 | tf_op jit(solution)/shard_map/cond/branch_1_fun/ppermute | solution.py:35
  74.5 0.0 collective-permute-done.rest_2_
  74.5 2.7 %collective-permute-start.4 = (bf16[128,1152]{1,0:T(8,128)(2,1)}, bf16[128,1152]{1,0:T(8,128)(2,1)S(1)}, u32[]{:S(2)}, u32[]{:S(2)}) collective-permute-start(bf16[128,1152]{1,0:T(8,128)(2,1)} %get-tuple-element.74), channel_id=1, source_target_pairs={{0,96},{16,112},{32,0},{48,16},{64,32},{80,48},{96,64},{112,80},{1... | collective-permute-start | bytes 884744 | tf_op jit(solution)/shard_map/cond/branch_1_fun/ppermute | solution.py:35
  77.3 0.1 stack.37.roles
  77.3 4.7 %branch_1_fun.3 = (f32[128,128]{1,0:T(8,128)S(1)}, f32[256,1152]{1,0:T(8,128)S(1)}, bf16[256,1152]{1,0:T(8,128)(2,1)}, f32[256,1]{1,0:T(8,128)S(1)}) custom-call(f32[1]{0:T(128)} %get-tuple-element.54.scale, f32[1]{0:T(128)} %get-tuple-element.55.bias, s32[5]{0:T(128)S(1)} %stack.37.roles, bf16[128,1152]{1,0:T(8,128)(2,1)S(1)} %get-tuple-element.61.x_ref, ...), custom_call_target="tpu_custom_call" | custom-call | flops 452984832 | bytes 6291456 | tf_op jit(solution)/shard_map/cond/branch_1_fun/pallas_call | solution.py:147
  82.1 0.0 collective-permute-done.1.rest_0_
  82.1 0.6 collective-permute-done.3.rest_1_
  82.7 5.1 %collective-permute-done.4.rest_2_ = bf16[128,1152]{1,0:T(8,128)(2,1)S(1)} collective-permute-done((bf16[128,1152]{1,0:T(8,128)(2,1)}, bf16[128,1152]{1,0:T(8,128)(2,1)S(1)}, u32[]{:S(2)}, u32[]{:S(2)}) %collective-permute-start.4) | collective-permute-done | bytes 294944 | tf_op jit(solution)/shard_map/cond/branch_1_fun/ppermute | solution.py:35
  87.8 0.7 constant_dynamic-update-slice_fusion.3
  88.6 0.7 constant_dynamic-update-slice_fusion.2
  89.3 0.7 constant_dynamic-update-slice_fusion.1
  90.0 0.7 constant_dynamic-update-slice_fusion
  90.8 3.3 %collective-permute-start.5 = (bf16[640,1152]{1,0:T(8,128)(2,1)}, bf16[640,1152]{1,0:T(8,128)(2,1)S(1)}, u32[]{:S(2)}, u32[]{:S(2)}) collective-permute-start(bf16[640,1152]{1,0:T(8,128)(2,1)} %constant_dynamic-update-slice_fusion), channel_id=1, source_target_pairs={{0,16},{16,0},{32,48},{48,32},{64,80},{80,64},{96,112},{112,96},{1... | collective-permute-start | bytes 4423688 | tf_op jit(solution)/shard_map/cond/branch_1_fun/ppermute | solution.py:45
  94.1 0.1 stack.10.roles
  94.2 0.1 pad_add_fusion.roles
  94.3 1.3 %copy-done.1 = f32[256,1152]{1,0:T(8,128)S(1)} copy-done((f32[256,1152]{1,0:T(8,128)S(1)}, f32[256,1152]{1,0:T(8,128)}, u32[]{:S(2)}) %copy-start.1) | copy-done | bytes 1179672 | tf_op jit(solution)/shard_map/cond
  95.6 4.3 %branch_1_fun.4 = (f32[128,128]{1,0:T(8,128)S(1)}, f32[256,1152]{1,0:T(8,128)S(1)}) custom-call(f32[1]{0:T(128)} %get-tuple-element.54.scale, f32[1]{0:T(128)} %get-tuple-element.55.bias, s32[4]{0:T(128)S(1)} %pad_add_fusion.roles, bf16[256,1152]{1,0:T(8,128)(2,1)} %get-tuple-element.132.units_ref, f32[128,128]{1,0:T(8,128)S(1)} %get-tuple-element.77.loss_in, ...), custom_call_target="tpu_custom_call" | custom-call | flops 301989888 | bytes 4194304 | tf_op jit(solution)/shard_map/cond/branch_1_fun/pallas_call | solution.py:147
  99.8 5.7 %branch_1_fun.5 = (f32[128,128]{1,0:T(8,128)S(1)}, f32[256,1152]{1,0:T(8,128)}) custom-call(f32[1]{0:T(128)} %get-tuple-element.54.scale, f32[1]{0:T(128)} %get-tuple-element.55.bias, s32[5]{0:T(128)S(1)} %stack.10.roles, bf16[256,1152]{1,0:T(8,128)(2,1)} %get-tuple-element.132.units_ref, f32[128,128]{1,0:T(8,128)S(1)} %get-tuple-element.83.loss_in, ...), custom_call_target="tpu_custom_call" | custom-call | flops 377487360 | bytes 5242880 | tf_op jit(solution)/shard_map/cond/branch_1_fun/pallas_call | solution.py:147
  105.6 0.0 collective-permute-done.10.xg_ref
  105.6 3.7 %shard_map.77 = (f32[1,128]{1,0:T(1,128)}, f32[128,1152]{1,0:T(8,128)}, f32[128,1152]{1,0:T(8,128)}) custom-call(f32[1]{0:T(128)S(6)} %copy.21.scale, f32[1]{0:T(128)S(6)} %copy.22.bias, bf16[128,1152]{1,0:T(8,128)(2,1)} %x_ref.1, bf16[128,1152]{1,0:T(8,128)(2,1)} %y_ref.1, bf16[128,1152]{1,0:T(8,128)(2,1)S(1)} %collective-permute-done.8.yg_ref, ...), custom_call_target="tpu_custom_call" | custom-call | flops 150994944 | bytes 2097152 | tf_op jit(solution)/shard_map/pallas_call | solution.py:147
  (11 shorter events, 0.0 us)
Async XLA Ops:
  0.6 16.9 %copy-start.2 = (bf16[128,1152]{1,0:T(8,128)(2,1)S(1)}, bf16[128,1152]{1,0:T(8,128)(2,1)}, u32[]{:S(2)}) copy-start(bf16[128,1152]{1,0:T(8,128)(2,1)} %x_ref.1) | copy-start | bytes 884740
  0.6 15.0 %copy-start.3 = (bf16[128,1152]{1,0:T(8,128)(2,1)S(1)}, bf16[128,1152]{1,0:T(8,128)(2,1)}, u32[]{:S(2)}) copy-start(bf16[128,1152]{1,0:T(8,128)(2,1)} %y_ref.1) | copy-start | bytes 884740
  0.7 52.5 %copy-start.7 = (s32[1,128]{1,0:T(1,128)S(1)}, s32[1,128]{1,0:T(1,128)}, u32[]{:S(2)}) copy-start(s32[1,128]{1,0:T(1,128)} %param.9) | copy-start | bytes 1540
  1.9 36.7 %collective-permute-start.7 = (bf16[128,1152]{1,0:T(8,128)(2,1)S(1)}, bf16[128,1152]{1,0:T(8,128)(2,1)S(1)}, u32[]{:S(2)}, u32[]{:S(2)}) collective-permute-start(bf16[128,1152]{1,0:T(8,128)(2,1)S(1)} %get-tuple-element.125), channel_id=1, source_target_pairs={{896,0},{912,16},{928,32},{944,48},{960,64},{976,80},{992,96},{100... | collective-permute-start | bytes 884744 | tf_op jit(solution)/shard_map/ppermute | solution.py:41
  15.6 23.0 %collective-permute-start.6 = (bf16[128,1152]{1,0:T(8,128)(2,1)S(1)}, bf16[128,1152]{1,0:T(8,128)(2,1)}, u32[]{:S(2)}, u32[]{:S(2)}) collective-permute-start(bf16[128,1152]{1,0:T(8,128)(2,1)S(1)} %copy-done.3), channel_id=1, source_target_pairs={{0,128},{1,129},{2,130},{3,131},{4,132},{5,133},{6,134},{7,135},{8... | collective-permute-start | bytes 884744 | tf_op jit(solution)/shard_map/ppermute | solution.py:27
  17.6 21.0 %collective-permute-start.9 = (bf16[128,1152]{1,0:T(8,128)(2,1)S(1)}, bf16[128,1152]{1,0:T(8,128)(2,1)}, u32[]{:S(2)}, u32[]{:S(2)}) collective-permute-start(bf16[128,1152]{1,0:T(8,128)(2,1)S(1)} %copy-done.2), channel_id=1, source_target_pairs={{0,911},{1,896},{2,897},{3,898},{4,899},{5,900},{6,901},{7,902},{8... | collective-permute-start | bytes 884744 | tf_op jit(solution)/shard_map/ppermute | solution.py:27
  32.1 21.0 %collective-permute-start.11 = (bf16[128,1152]{1,0:T(8,128)(2,1)S(1)}, bf16[128,1152]{1,0:T(8,128)(2,1)S(1)}, u32[]{:S(2)}, u32[]{:S(2)}) collective-permute-start(bf16[128,1152]{1,0:T(8,128)(2,1)S(1)} %get-tuple-element.124), channel_id=1, source_target_pairs={{0,32},{16,48},{32,64},{48,80},{64,96},{80,112},{96,0},{112,16},{1... | collective-permute-start | bytes 884744 | tf_op jit(solution)/shard_map/ppermute | solution.py:35
  35.2 17.9 %collective-permute-start.12 = (bf16[128,1152]{1,0:T(8,128)(2,1)S(1)}, bf16[128,1152]{1,0:T(8,128)(2,1)S(1)}, u32[]{:S(2)}, u32[]{:S(2)}) collective-permute-start(bf16[128,1152]{1,0:T(8,128)(2,1)S(1)} %get-tuple-element.123), channel_id=1, source_target_pairs={{0,96},{16,112},{32,0},{48,16},{64,32},{80,48},{96,64},{112,80},{1... | collective-permute-start | bytes 884744 | tf_op jit(solution)/shard_map/ppermute | solution.py:35
  38.6 67.0 %collective-permute-start.10 = (bf16[128,1152]{1,0:T(8,128)(2,1)}, bf16[128,1152]{1,0:T(8,128)(2,1)S(1)}, u32[]{:S(2)}, u32[]{:S(2)}) collective-permute-start(bf16[128,1152]{1,0:T(8,128)(2,1)} %collective-permute-done.9), channel_id=1, source_target_pairs={{0,143},{1,128},{2,129},{3,130},{4,131},{5,132},{6,133},{7,134},{8... | collective-permute-start | bytes 884744 | tf_op jit(solution)/shard_map/ppermute | solution.py:27
  49.9 55.7 %collective-permute-start.8 = (bf16[128,1152]{1,0:T(8,128)(2,1)}, bf16[128,1152]{1,0:T(8,128)(2,1)S(1)}, u32[]{:S(2)}, u32[]{:S(2)}) collective-permute-start(bf16[128,1152]{1,0:T(8,128)(2,1)} %collective-permute-done.6), channel_id=1, source_target_pairs={{0,896},{1,897},{2,898},{3,899},{4,900},{5,901},{6,902},{7,903},{8... | collective-permute-start | bytes 884744 | tf_op jit(solution)/shard_map/ppermute | solution.py:27
  53.1 0.7 copy-start.4
  53.1 0.8 copy-start.5
  53.2 0.9 copy-start.6
  55.1 19.4 %collective-permute-start = (bf16[384,1152]{1,0:T(8,128)(2,1)}, bf16[384,1152]{1,0:T(8,128)(2,1)S(1)}, u32[]{:S(2)}, u32[]{:S(2)}) collective-permute-start(bf16[384,1152]{1,0:T(8,128)(2,1)} %pad_maximum_fusion), channel_id=1, source_target_pairs={{0,16},{16,0},{32,48},{48,32},{64,80},{80,64},{96,112},{112,96},{1... | collective-permute-start | bytes 2654216 | tf_op jit(solution)/shard_map/cond/branch_1_fun/ppermute | solution.py:45
  58.0 12.0 %collective-permute-start.2 = (bf16[128,1152]{1,0:T(8,128)(2,1)S(1)}, bf16[128,1152]{1,0:T(8,128)(2,1)S(1)}, u32[]{:S(2)}, u32[]{:S(2)}) collective-permute-start(bf16[128,1152]{1,0:T(8,128)(2,1)S(1)} %get-tuple-element.118), channel_id=1, source_target_pairs={{0,64},{16,80},{32,96},{48,112},{64,0},{80,16},{96,32},{112,48},{1... | collective-permute-start | bytes 884744 | tf_op jit(solution)/shard_map/cond/branch_1_fun/ppermute | solution.py:35
  65.3 16.8 %collective-permute-start.1 = (bf16[128,1152]{1,0:T(8,128)(2,1)}, bf16[128,1152]{1,0:T(8,128)(2,1)S(1)}, u32[]{:S(2)}, u32[]{:S(2)}) collective-permute-start(bf16[128,1152]{1,0:T(8,128)(2,1)} %get-tuple-element.121), channel_id=1, source_target_pairs={{0,32},{16,48},{32,64},{48,80},{64,96},{80,112},{96,0},{112,16},{1... | collective-permute-start | bytes 884744 | tf_op jit(solution)/shard_map/cond/branch_1_fun/ppermute | solution.py:35
  70.1 12.6 %collective-permute-start.3 = (bf16[128,1152]{1,0:T(8,128)(2,1)}, bf16[128,1152]{1,0:T(8,128)(2,1)S(1)}, u32[]{:S(2)}, u32[]{:S(2)}) collective-permute-start(bf16[128,1152]{1,0:T(8,128)(2,1)} %get-tuple-element.73), channel_id=1, source_target_pairs={{0,64},{16,80},{32,96},{48,112},{64,0},{80,16},{96,32},{112,48},{1... | collective-permute-start | bytes 884744 | tf_op jit(solution)/shard_map/cond/branch_1_fun/ppermute | solution.py:35
  74.5 13.3 %collective-permute-start.4 = (bf16[128,1152]{1,0:T(8,128)(2,1)}, bf16[128,1152]{1,0:T(8,128)(2,1)S(1)}, u32[]{:S(2)}, u32[]{:S(2)}) collective-permute-start(bf16[128,1152]{1,0:T(8,128)(2,1)} %get-tuple-element.74), channel_id=1, source_target_pairs={{0,96},{16,112},{32,0},{48,16},{64,32},{80,48},{96,64},{112,80},{1... | collective-permute-start | bytes 884744 | tf_op jit(solution)/shard_map/cond/branch_1_fun/ppermute | solution.py:35
  82.1 8.0 %copy-start = (f32[256,1152]{1,0:T(8,128)}, f32[256,1152]{1,0:T(8,128)S(1)}, u32[]{:S(2)}) copy-start(f32[256,1152]{1,0:T(8,128)S(1)} %get-tuple-element.78.grads_in) | copy-start | bytes 3538948 | tf_op jit(solution)/shard_map/cond
  90.8 9.1 %collective-permute-start.5 = (bf16[640,1152]{1,0:T(8,128)(2,1)}, bf16[640,1152]{1,0:T(8,128)(2,1)S(1)}, u32[]{:S(2)}, u32[]{:S(2)}) collective-permute-start(bf16[640,1152]{1,0:T(8,128)(2,1)} %constant_dynamic-update-slice_fusion), channel_id=1, source_target_pairs={{0,16},{16,0},{32,48},{48,32},{64,80},{80,64},{96,112},{112,96},{1... | collective-permute-start | bytes 4423688 | tf_op jit(solution)/shard_map/cond/branch_1_fun/ppermute | solution.py:45
  94.3 1.3 %copy-start.1 = (f32[256,1152]{1,0:T(8,128)S(1)}, f32[256,1152]{1,0:T(8,128)}, u32[]{:S(2)}) copy-start(f32[256,1152]{1,0:T(8,128)} %copy-done) | copy-start | bytes 3538948 | tf_op jit(solution)/shard_map/cond

commit v9 on v8

--- a/solution.py
+++ b/solution.py
@@ -22,6 +22,20 @@
         row, place = divmod(blk, SPAN)
         for group in range(groups):
             to = (group * length + row + by) % (groups * length)
+            to_blk, to_group = to % length * SPAN + place, to // length
+            pairs.append((blk * groups + group, to_blk * groups + to_group))
+    return lax.ppermute(x, ("blk", "group"), pairs)
+
+
+def swapped_along_ring(x, by, odd):
+    blks, groups = lax.axis_size("blk"), lax.axis_size("group")
+    length = blks // SPAN
+    pairs = []
+    for blk in range(blks):
+        row, place = divmod(blk, SPAN)
+        for group in range(groups):
+            way = by if row % 2 == odd else -by
+            to = (group * length + row + way) % (groups * length)
             to_blk, to_group = to % length * SPAN + place, to // length
             pairs.append((blk * groups + group, to_blk * groups + to_group))
     return lax.ppermute(x, ("blk", "group"), pairs)
@@ -99,9 +113,20 @@
 
 
 def first_kernel(scale, bias, roles, x_ref, y_ref, pos_ref, *rest):
-    refs, (loss_ref, grads_ref, units_ref, inverses_ref, stack_ref) = rest[:-5], rest[-5:]
+    refs, (loss_ref, grads_ref, units_ref, inverses_ref, sent_ref, stack_ref) = rest[:-6], rest[-6:]
     tau, offset = scale[0], bias[0]
     rows = x_ref.shape[0]
+
+    @pl.when(roles[len(refs)] == TEXT)
+    def _():
+        sent_ref[:rows, :] = y_ref[...]
+
+    @pl.when(roles[len(refs)] != TEXT)
+    def _():
+        sent_ref[:rows, :] = x_ref[...]
+
+    for i, ref in enumerate(refs, 1):
+        sent_ref[i * rows : (i + 1) * rows, :] = ref[...]
     for i, ref in enumerate((x_ref, y_ref)):
         inverse = row_inverse(ref[...])
         inverses_ref[i * rows : (i + 1) * rows, :] = inverse
@@ -126,13 +151,15 @@
 
 
 def last_kernel(
-    scale, bias, x_ref, y_ref, yg_ref, xg_ref, units_ref, inverses_ref, loss_in, grads_in, loss_ref, ix_ref, ty_ref
+    scale, bias, odd, x_ref, y_ref, one_ref, two_ref, units_ref, inverses_ref, loss_in, grads_in, loss_ref, ix_ref, ty_ref
 ):
     tau, offset = scale[0], bias[0]
     rows = x_ref.shape[0]
-    for i, (feats_ref, other_ref, out_ref) in enumerate(((x_ref, yg_ref, ix_ref), (y_ref, xg_ref, ty_ref))):
+    one, two = one_ref[...].astype(F32), two_ref[...].astype(F32)
+    text, image = jnp.where(odd[0] == 1, one, two), jnp.where(odd[0] == 1, two, one)
+    for i, (feats_ref, other, out_ref) in enumerate(((x_ref, text, ix_ref), (y_ref, image, ty_ref))):
         own = slice(i * rows, (i + 1) * rows)
-        other = unit_rows(other_ref[...])
+        other = unit_rows(other)
         loss, slope = loss_and_slope(tau * by_rows(other, units_ref[own, :]) + offset)
         if i == TEXT:
             loss_ref[...] = jnp.sum(loss_in[...] + loss, axis=0, keepdims=True) / F32((SPAN + 1) * rows)
@@ -170,42 +197,46 @@
     x_next = along_ring(x, -1)
     first = [jnp.where(chip + by < CHIPS, y, x) for by in shifts]
     near, far = in_row(first[0], 1), in_row(first[2], 3)
-    y_outer, wrapped = lax.optimization_barrier((y_back, wrapped))
-    x_outer, wrapped = lax.optimization_barrier((x_next, wrapped))
-    y_outer = along_ring(y_outer, length - 1)
-    x_outer = along_ring(x_outer, 1 - length)
+    first[1], near = lax.optimization_barrier((first[1], near))
+    middle = in_row(first[1], 2)
+    odd = index // SPAN % 2
+    y_back, x_next, wrapped = lax.optimization_barrier((y_back, x_next, wrapped))
+    one = swapped_along_ring(jnp.where(odd == 0, y_back, x_next), length - 1, 0)
+    two = swapped_along_ring(jnp.where(odd == 1, y_back, x_next), length - 1, 1)
     double = 2 * rows
     loss_out, grads_out = ((rows, rows), F32), ((double, width), F32)
     units_out, inverses_out = ((double, width), BF16), ((double, 1), F32)
+    sent_out = ((CHIPS * rows, width), BF16)
     near_role, middle_role, far_role = [(chip < by).astype(jnp.int32) for by in shifts]
     twin_role = 1 - core
 
     def stack(blocks):
         return [pltpu.VMEM((blocks * rows, width), BF16)]
+
+    def more(roles, refs, units, loss, grads):
+        return call(
+            next_kernel, [loss_out, grads_out], len(roles), (scale, bias, jnp.stack(roles)),
+            units, loss, grads, *refs, scratch=stack(len(roles)),
+        )
 
     def inner(_):
         text = jnp.where(index < SPAN, wrapped, y_back)
         image = jnp.where(index >= last, wrapped, x_next)
         then = [jnp.where(chip + by < CHIPS, image, text) for by in shifts]
-        mine, other = jnp.where(core == 0, y, x), jnp.where(core == 0, image, text)
-        twin = to_twin(jnp.concatenate([mine, near, far], axis=0))
-        middle = in_row(first[1], 2)
-        then[2], twin = lax.optimization_barrier((then[2], twin))
-        then[1], middle = lax.optimization_barrier((then[1], middle))
-        scalars = (scale, bias, jnp.stack([near_role, far_role, twin_role, near_role, far_role]))
-        loss, grads, units, inverses = call(
-            first_kernel, [loss_out, grads_out, units_out, inverses_out], 6, scalars,
-            x, y, positive, near, far, twin, scratch=stack(5),
+        got_roles = [near_role, middle_role, far_role]
+        loss, grads, units, inverses, sent = call(
+            first_kernel, [loss_out, grads_out, units_out, inverses_out, sent_out], 4,
+            (scale, bias, jnp.stack(got_roles + [core])), x, y, positive, near, middle, far, scratch=stack(3),
         )
-        later = [in_row(block, by) for by, block in zip(shifts, then)] + [middle]
-        *later, loss = lax.optimization_barrier((*later, loss))
-        twin = to_twin(jnp.concatenate([other] + later, axis=0))
-        later_roles = [1 - near_role, 1 - middle_role, 1 - far_role, middle_role]
-        for roles, refs in ((later_roles, later), ([1 - twin_role] + later_roles, [twin])):
-            loss, grads = call(
-                next_kernel, [loss_out, grads_out], len(roles), (scale, bias, jnp.stack(roles)),
-                units, loss, grads, *refs, scratch=stack(len(roles)),
-            )
+        later = [in_row(block, by) for by, block in zip(shifts, then)]
+        *later, sent = lax.optimization_barrier((*later, sent))
+        twin = to_twin(sent)
+        later_twin = to_twin(jnp.concatenate([jnp.where(core == 0, image, text)] + later, axis=0))
+        later_roles = [1 - role for role in got_roles]
+        loss, grads = more([twin_role] + got_roles, [twin], units, loss, grads)
+        loss, grads = more(
+            later_roles + [1 - twin_role] + later_roles, later + [later_twin], units, loss, grads
+        )
         return loss, grads, units, inverses
 
     def skip(_):
@@ -215,8 +246,8 @@
     loss, grads, units, inverses = lax.cond(go > 0, inner, skip, 0)
     block = ((rows, width), F32)
     loss, image_grad, text_grad = call(
-        last_kernel, [((1, rows), F32), block, block], 2, (scale, bias),
-        x, y, y_outer, x_outer, units, inverses, loss, grads,
+        last_kernel, [((1, rows), F32), block, block], 2, (scale, bias, odd[None]),
+        x, y, one, two, units, inverses, loss, grads,
     )
     return (loss[0], image_grad, text_grad)
 

time: 110 us -> 108 us (0.982)
  waiting for transfers between devices: 8.3 us -> 17.7 us
  starting transfers between devices: 69.8 us -> 62 us
  local copies, waits for them, and re-layouts: 5.22 us -> 2.25 us
  other arithmetic: 5.18 us -> 3.52 us
  Pallas kernels: 18.5 us -> 19.8 us
    ppermute x1, starting transfers between devices: 13.7 us -> 1.92 us  [around(): return lax.ppermute(x, 'blk', pairs)]
    ppermute x0 -> x2, starting transfers between devices: none -> 8.35 us  [swapped_along_ring(): return lax.ppermute(x, ('blk', 'group'), pairs)]
    ppermute x1, waiting for transfers between devices: 0.01 us -> 7.56 us  [around(): return lax.ppermute(x, 'blk', pairs)]
    ppermute x0 -> x2, waiting for transfers between devices: none -> 7.06 us  [swapped_along_ring(): return lax.ppermute(x, ('blk', 'group'), pairs)]
    ppermute x4 -> x2, starting transfers between devices: 29.6 us -> 23.6 us  [along_ring(): return lax.ppermute(x, ('blk', 'group'), pairs)]
    ppermute x6, waiting for transfers between devices: 8.28 us -> 3.09 us  [in_row(): return lax.ppermute(x, 'blk', pairs)]
    cond x13 -> x8, local copies, waits for them, and re-layouts: 4.3 us -> 2.15 us
    cond x1 -> x0, other arithmetic: 1.84 us -> none
  transfers between devices with their start and end apart: 13 -> 13, of which waited for: 3 -> 3; matrix products, arithmetic and copies ran while one was open for 6% -> 3% of each run, Pallas kernels for 13% -> 15%
where the time goes in v9:
time: 108 us
  starting transfers between devices  62 us (57%)
  Pallas kernels  19.8 us (18%)
  waiting for transfers between devices  17.7 us (16%)
  other arithmetic  3.52 us (3%)
  local copies, waits for them, and re-layouts  2.25 us (2%)
  between operations  2.16 us (2%)
    ppermute x2, starting transfers between devices, along_ring(): return lax.ppermute(x, ('blk', 'group'), pairs)  23.6 us
    ppermute x6, starting transfers between devices, in_row(): return lax.ppermute(x, 'blk', pairs)  20.7 us
    pallas_call x4, Pallas kernels, call(): pl.pallas_call(kernel, out_shape=[jax.ShapeDtypeStruct(shape, kind) for s...  19.8 us
    ppermute x2, starting transfers between devices, swapped_along_ring(): return lax.ppermute(x, ('blk', 'group'), pairs)  8.35 us
    ppermute x1, waiting for transfers between devices, around(): return lax.ppermute(x, 'blk', pairs)  7.56 us
    ppermute x2, starting transfers between devices, to_twin(): lax.ppermute(x, 'blk', [(i, i ^ 1) for i in range(lax.axis_size('blk'))])  7.41 us
    ppermute x2, waiting for transfers between devices, swapped_along_ring(): return lax.ppermute(x, ('blk', 'group'), pairs)  7.06 us
    ppermute x6, waiting for transfers between devices, in_row(): return lax.ppermute(x, 'blk', pairs)  3.09 us
  transfers between devices with their start and end apart: 13, of which 3 were waited for; matrix products, arithmetic and copies ran while one was open for 3% of the time, Pallas kernels for 15%

profile of v9, /device:TPU:1, one launch (start us, length us, event | category | flops | bytes accessed | tf_op | source)
XLA Modules:
  0.0 107.6 jit_solution(9602474082427359479)
XLA Ops:
  0.6 4.4 %collective-permute-start.5 = (bf16[128,1152]{1,0:T(8,128)(2,1)}, bf16[128,1152]{1,0:T(8,128)(2,1)S(1)}, u32[]{:S(2)}, u32[]{:S(2)}) collective-permute-start(bf16[128,1152]{1,0:T(8,128)(2,1)} %y_ref.1), channel_id=1, source_target_pairs={{0,128},{1,129},{2,130},{3,131},{4,132},{5,133},{6,134},{7,135},{8... | collective-permute-start | bytes 884744 | tf_op jit(solution)/shard_map/ppermute | solution.py:27
  5.0 19.2 %collective-permute-start.6 = (bf16[128,1152]{1,0:T(8,128)(2,1)}, bf16[128,1152]{1,0:T(8,128)(2,1)S(1)}, u32[]{:S(2)}, u32[]{:S(2)}) collective-permute-start(bf16[128,1152]{1,0:T(8,128)(2,1)} %x_ref.1), channel_id=1, source_target_pairs={{0,911},{1,896},{2,897},{3,898},{4,899},{5,900},{6,901},{7,902},{8... | collective-permute-start | bytes 884744 | tf_op jit(solution)/shard_map/ppermute | solution.py:27
  24.3 0.0 copy-start.2
  24.3 0.0 copy-start.3
  24.3 0.0 copy-start.6
  24.3 1.2 %broadcast_select_fusion.6 = (bf16[128,1152]{1,0:T(8,128)(2,1)S(1)}, bf16[128,1152]{1,0:T(8,128)(2,1)S(1)}, bf16[128,1152]{1,0:T(8,128)(2,1)S(1)}, bf16[128,1152]{1,0:T(8,128)(2,1)S(1)}) fusion(bf16[128,1152]{1,0:T(8,128)(2,1)} %y_ref.1, bf16[128,1152]{1,0:T(8,128)(2,1)} %x_ref.1, pred[]{:T(512)S(6)} %lt.51, pred[]{:T(512)S(6)} %lt.50, pred[]{:T(512)S(6)} %lt.49, ...), kind=kLoop, calls=%fused_computation.9 | loop fusion | flops 589824 | bytes 1769476 | tf_op jit(solution)/shard_map/jit(_where)/select_n | solution.py:198
  25.6 1.9 %collective-permute-start.7 = (bf16[128,1152]{1,0:T(8,128)(2,1)S(1)}, bf16[128,1152]{1,0:T(8,128)(2,1)S(1)}, u32[]{:S(2)}, u32[]{:S(2)}) collective-permute-start(bf16[128,1152]{1,0:T(8,128)(2,1)S(1)} %get-tuple-element.116), channel_id=1, source_target_pairs={{896,0},{912,16},{928,32},{944,48},{960,64},{976,80},{992,96},{100... | collective-permute-start | bytes 884744 | tf_op jit(solution)/shard_map/ppermute | solution.py:55
  27.5 3.1 %collective-permute-start.10 = (bf16[128,1152]{1,0:T(8,128)(2,1)S(1)}, bf16[128,1152]{1,0:T(8,128)(2,1)S(1)}, u32[]{:S(2)}, u32[]{:S(2)}) collective-permute-start(bf16[128,1152]{1,0:T(8,128)(2,1)S(1)} %get-tuple-element.114), channel_id=1, source_target_pairs={{0,32},{16,48},{32,64},{48,80},{64,96},{80,112},{96,0},{112,16},{1... | collective-permute-start | bytes 884744 | tf_op jit(solution)/shard_map/ppermute | solution.py:49
  30.6 3.4 %collective-permute-start.12 = (bf16[128,1152]{1,0:T(8,128)(2,1)S(1)}, bf16[128,1152]{1,0:T(8,128)(2,1)S(1)}, u32[]{:S(2)}, u32[]{:S(2)}) collective-permute-start(bf16[128,1152]{1,0:T(8,128)(2,1)S(1)} %get-tuple-element.113), channel_id=1, source_target_pairs={{0,96},{16,112},{32,0},{48,16},{64,32},{80,48},{96,64},{112,80},{1... | collective-permute-start | bytes 884744 | tf_op jit(solution)/shard_map/ppermute | solution.py:49
  34.0 0.0 collective-permute-done.5
  34.0 0.0 collective-permute-done.6
  34.0 7.6 %collective-permute-done.7 = bf16[128,1152]{1,0:T(8,128)(2,1)S(1)} collective-permute-done((bf16[128,1152]{1,0:T(8,128)(2,1)S(1)}, bf16[128,1152]{1,0:T(8,128)(2,1)S(1)}, u32[]{:S(2)}, u32[]{:S(2)}) %collective-permute-start.7) | collective-permute-done | bytes 294944 | tf_op jit(solution)/shard_map/ppermute | solution.py:55
  41.6 0.0 collective-permute-done.10
  41.6 5.0 %collective-permute-start.11 = (bf16[128,1152]{1,0:T(8,128)(2,1)S(1)}, bf16[128,1152]{1,0:T(8,128)(2,1)S(1)}, u32[]{:S(2)}, u32[]{:S(2)}) collective-permute-start(bf16[128,1152]{1,0:T(8,128)(2,1)S(1)} %get-tuple-element.96), channel_id=1, source_target_pairs={{0,64},{16,80},{32,96},{48,112},{64,0},{80,16},{96,32},{112,48},{1... | collective-permute-start | bytes 884744 | tf_op jit(solution)/shard_map/ppermute | solution.py:49
  46.6 0.9 broadcast_select_fusion.9
  47.5 4.6 %collective-permute-start.8 = (bf16[128,1152]{1,0:T(8,128)(2,1)}, bf16[128,1152]{1,0:T(8,128)(2,1)S(1)}, u32[]{:S(2)}, u32[]{:S(2)}) collective-permute-start(bf16[128,1152]{1,0:T(8,128)(2,1)} %get-tuple-element.118), channel_id=1, source_target_pairs={{0,896},{1,897},{2,898},{3,899},{4,900},{5,901},{6,902},{7,903},{8... | collective-permute-start | bytes 884744 | tf_op jit(solution)/shard_map/ppermute | solution.py:41
  52.1 3.8 %collective-permute-start.9 = (bf16[128,1152]{1,0:T(8,128)(2,1)}, bf16[128,1152]{1,0:T(8,128)(2,1)}, u32[]{:S(2)}, u32[]{:S(2)}) collective-permute-start(bf16[128,1152]{1,0:T(8,128)(2,1)} %get-tuple-element.117), channel_id=1, source_target_pairs={{0,143},{1,128},{2,129},{3,130},{4,131},{5,132},{6,133},{7,134},{8... | collective-permute-start | bytes 884744 | tf_op jit(solution)/shard_map/ppermute | solution.py:41
  57.2 0.0 collective-permute-done.12
  57.2 0.0 collective-permute-done.11
  57.2 0.0 copy-done.2
  57.2 0.0 copy-done.3
  57.2 0.0 copy-done.6
  57.2 39.4 %conditional.1 = (f32[128,128]{1,0:T(8,128)}, f32[256,1152]{1,0:T(8,128)}, bf16[256,1152]{1,0:T(8,128)(2,1)}, f32[256,1]{1,0:T(8,128)}) conditional(s32[]{:T(128)} %convert_element_type.12, () %tuple.20, (s32[]{:T(128)}, s32[]{:T(128)}, s32[]{:T(128)}, s32[]{:T(128)}, pred[]{:T(512)}, /*index=5*/f32[1]{0:T(128)}, f32[1]{0:T(128)}, ...), branch_computations={%region_0.1_spmd, %region_1.2_spmd} | conditional | flops 1138065408 | bytes 37192324 | solution.py:246
  57.3 0.7 copy-done.4
  58.0 0.1 broadcast_select_fusion
  58.1 0.1 broadcast_select_fusion.1
  58.2 2.2 %collective-permute-start = (bf16[128,1152]{1,0:T(8,128)(2,1)S(1)}, bf16[128,1152]{1,0:T(8,128)(2,1)S(1)}, u32[]{:S(2)}, u32[]{:S(2)}) collective-permute-start(bf16[128,1152]{1,0:T(8,128)(2,1)S(1)} %get-tuple-element.112), channel_id=1, source_target_pairs={{0,32},{16,48},{32,64},{48,80},{64,96},{80,112},{96,0},{112,16},{1... | collective-permute-start | bytes 884744 | tf_op jit(solution)/shard_map/cond/branch_1_fun/ppermute | solution.py:49
  60.4 3.6 %collective-permute-start.1 = (bf16[128,1152]{1,0:T(8,128)(2,1)S(1)}, bf16[128,1152]{1,0:T(8,128)(2,1)S(1)}, u32[]{:S(2)}, u32[]{:S(2)}) collective-permute-start(bf16[128,1152]{1,0:T(8,128)(2,1)S(1)} %get-tuple-element.111), channel_id=1, source_target_pairs={{0,64},{16,80},{32,96},{48,112},{64,0},{80,16},{96,32},{112,48},{1... | collective-permute-start | bytes 884744 | tf_op jit(solution)/shard_map/cond/branch_1_fun/ppermute | solution.py:49
  64.0 3.4 %collective-permute-start.2 = (bf16[128,1152]{1,0:T(8,128)(2,1)S(1)}, bf16[128,1152]{1,0:T(8,128)(2,1)S(1)}, u32[]{:S(2)}, u32[]{:S(2)}) collective-permute-start(bf16[128,1152]{1,0:T(8,128)(2,1)S(1)} %get-tuple-element.110), channel_id=1, source_target_pairs={{0,96},{16,112},{32,0},{48,16},{64,32},{80,48},{96,64},{112,80},{1... | collective-permute-start | bytes 884744 | tf_op jit(solution)/shard_map/cond/branch_1_fun/ppermute | solution.py:49
  67.4 0.1 pad_add_fusion.roles
  67.5 4.7 %branch_1_fun.3 = (f32[128,128]{1,0:T(8,128)S(1)}, f32[256,1152]{1,0:T(8,128)S(1)}, bf16[256,1152]{1,0:T(8,128)(2,1)}, f32[256,1]{1,0:T(8,128)}, bf16[512,1152]{1,0:T(8,128)(2,1)}) custom-call(f32[1]{0:T(128)} %get-tuple-element.47.scale, f32[1]{0:T(128)} %get-tuple-element.48.bias, s32[4]{0:T(128)S(1)} %pad_add_fusion.roles, ...), custom_call_target="tpu_custom_call" | custom-call | flops 301989888 | bytes 4194304 | tf_op jit(solution)/shard_map/cond/branch_1_fun/pallas_call | solution.py:174
  72.2 0.6 copy-done
  72.8 0.0 collective-permute-done.rest_0_
  72.8 0.0 collective-permute-done.1.rest_1_
  72.8 3.1 %collective-permute-done.2.rest_2_ = bf16[128,1152]{1,0:T(8,128)(2,1)S(1)} collective-permute-done((bf16[128,1152]{1,0:T(8,128)(2,1)S(1)}, bf16[128,1152]{1,0:T(8,128)(2,1)S(1)}, u32[]{:S(2)}, u32[]{:S(2)}) %collective-permute-start.2) | collective-permute-done | bytes 294944 | tf_op jit(solution)/shard_map/cond/branch_1_fun/ppermute | solution.py:49
  75.9 5.5 %collective-permute-start.3 = (bf16[512,1152]{1,0:T(8,128)(2,1)}, bf16[512,1152]{1,0:T(8,128)(2,1)}, u32[]{:S(2)}, u32[]{:S(2)}) collective-permute-start(bf16[512,1152]{1,0:T(8,128)(2,1)} %get-tuple-element.69), channel_id=1, source_target_pairs={{0,16},{16,0},{32,48},{48,32},{64,80},{80,64},{96,112},{112,96},{1... | collective-permute-start | bytes 3538952 | tf_op jit(solution)/shard_map/cond/branch_1_fun/ppermute | solution.py:59
  81.4 1.1 %pad_maximum_fusion = bf16[512,1152]{1,0:T(8,128)(2,1)} fusion(bf16[128,1152]{1,0:T(8,128)(2,1)S(1)} %collective-permute-done.2.rest_2_, bf16[128,1152]{1,0:T(8,128)(2,1)S(1)} %collective-permute-done.1.rest_1_, bf16[128,1152]{1,0:T(8,128)(2,1)S(1)} %collective-permute-done.rest_0_, bf16[128,1152]{1,0:T(8,128)(2,1)S(1)} %get-tuple-element.107), kind=kLoop, calls=%fused_computation | loop fusion | flops 4718592 | bytes 2359296 | tf_op jit(solution)/shard_map/cond/branch_1_fun/concatenate | solution.py:234
  82.5 1.9 %collective-permute-start.4 = (bf16[512,1152]{1,0:T(8,128)(2,1)}, bf16[512,1152]{1,0:T(8,128)(2,1)S(1)}, u32[]{:S(2)}, u32[]{:S(2)}) collective-permute-start(bf16[512,1152]{1,0:T(8,128)(2,1)} %pad_maximum_fusion), channel_id=1, source_target_pairs={{0,16},{16,0},{32,48},{48,32},{64,80},{80,64},{96,112},{112,96},{1... | collective-permute-start | bytes 3538952 | tf_op jit(solution)/shard_map/cond/branch_1_fun/ppermute | solution.py:59
  84.4 0.1 stack.10.roles
  84.5 0.1 pad_add_fusion.1.roles
  84.6 0.0 collective-permute-done.3.rest_0_
  84.6 0.8 copy-done.1
  85.4 4.6 %branch_1_fun.4 = (f32[128,128]{1,0:T(8,128)S(1)}, f32[256,1152]{1,0:T(8,128)S(1)}) custom-call(f32[1]{0:T(128)} %get-tuple-element.47.scale, f32[1]{0:T(128)} %get-tuple-element.48.bias, s32[4]{0:T(128)S(1)} %pad_add_fusion.1.roles, bf16[256,1152]{1,0:T(8,128)(2,1)} %get-tuple-element.125.units_ref, f32[128,128]{1,0:T(8,128)S(1)} %copy-done.1, ...), custom_call_target="tpu_custom_call" | custom-call | flops 301989888 | bytes 4194304 | tf_op jit(solution)/shard_map/cond/branch_1_fun/pallas_call | solution.py:174
  90.1 0.0 collective-permute-done.4.rest_3_
  90.1 6.5 %branch_1_fun.5 = (f32[128,128]{1,0:T(8,128)}, f32[256,1152]{1,0:T(8,128)}) custom-call(f32[1]{0:T(128)} %get-tuple-element.47.scale, f32[1]{0:T(128)} %get-tuple-element.48.bias, s32[7]{0:T(128)S(1)} %stack.10.roles, bf16[256,1152]{1,0:T(8,128)(2,1)} %get-tuple-element.125.units_ref, f32[128,128]{1,0:T(8,128)S(1)} %get-tuple-element.70.loss_in, ...), custom_call_target="tpu_custom_call" | custom-call | flops 528482304 | bytes 7340032 | tf_op jit(solution)/shard_map/cond/branch_1_fun/pallas_call | solution.py:174
  96.6 0.0 collective-permute-done.8.one_ref
  96.6 7.1 %collective-permute-done.9.two_ref = bf16[128,1152]{1,0:T(8,128)(2,1)} collective-permute-done((bf16[128,1152]{1,0:T(8,128)(2,1)}, bf16[128,1152]{1,0:T(8,128)(2,1)}, u32[]{:S(2)}, u32[]{:S(2)}) %collective-permute-start.9) | collective-permute-done | bytes 294944 | tf_op jit(solution)/shard_map/ppermute | solution.py:41
  103.7 4.0 %shard_map.77 = (f32[1,128]{1,0:T(1,128)}, f32[128,1152]{1,0:T(8,128)}, f32[128,1152]{1,0:T(8,128)}) custom-call(f32[1]{0:T(128)S(6)} %copy.17.scale, f32[1]{0:T(128)S(6)} %copy.18.bias, s32[1]{0:T(128)} %bitcast.8.odd, bf16[128,1152]{1,0:T(8,128)(2,1)} %x_ref.1, bf16[128,1152]{1,0:T(8,128)(2,1)} %y_ref.1, ...), custom_call_target="tpu_custom_call" | custom-call | flops 150994944 | bytes 2097152 | tf_op jit(solution)/shard_map/pallas_call | solution.py:174
  (5 shorter events, 0.0 us)
Async XLA Ops:
  0.6 33.4 %collective-permute-start.5 = (bf16[128,1152]{1,0:T(8,128)(2,1)}, bf16[128,1152]{1,0:T(8,128)(2,1)S(1)}, u32[]{:S(2)}, u32[]{:S(2)}) collective-permute-start(bf16[128,1152]{1,0:T(8,128)(2,1)} %y_ref.1), channel_id=1, source_target_pairs={{0,128},{1,129},{2,130},{3,131},{4,132},{5,133},{6,134},{7,135},{8... | collective-permute-start | bytes 884744 | tf_op jit(solution)/shard_map/ppermute | solution.py:27
  5.0 29.0 %collective-permute-start.6 = (bf16[128,1152]{1,0:T(8,128)(2,1)}, bf16[128,1152]{1,0:T(8,128)(2,1)S(1)}, u32[]{:S(2)}, u32[]{:S(2)}) collective-permute-start(bf16[128,1152]{1,0:T(8,128)(2,1)} %x_ref.1), channel_id=1, source_target_pairs={{0,911},{1,896},{2,897},{3,898},{4,899},{5,900},{6,901},{7,902},{8... | collective-permute-start | bytes 884744 | tf_op jit(solution)/shard_map/ppermute | solution.py:27
  24.3 32.9 %copy-start.2 = (bf16[128,1152]{1,0:T(8,128)(2,1)S(1)}, bf16[128,1152]{1,0:T(8,128)(2,1)}, u32[]{:S(2)}) copy-start(bf16[128,1152]{1,0:T(8,128)(2,1)} %x_ref.1) | copy-start | bytes 884740
  24.3 32.9 %copy-start.3 = (bf16[128,1152]{1,0:T(8,128)(2,1)S(1)}, bf16[128,1152]{1,0:T(8,128)(2,1)}, u32[]{:S(2)}) copy-start(bf16[128,1152]{1,0:T(8,128)(2,1)} %y_ref.1) | copy-start | bytes 884740
  24.3 32.9 %copy-start.6 = (s32[1,128]{1,0:T(1,128)S(1)}, s32[1,128]{1,0:T(1,128)}, u32[]{:S(2)}) copy-start(s32[1,128]{1,0:T(1,128)} %param.9) | copy-start | bytes 1540
  25.6 16.1 %collective-permute-start.7 = (bf16[128,1152]{1,0:T(8,128)(2,1)S(1)}, bf16[128,1152]{1,0:T(8,128)(2,1)S(1)}, u32[]{:S(2)}, u32[]{:S(2)}) collective-permute-start(bf16[128,1152]{1,0:T(8,128)(2,1)S(1)} %get-tuple-element.116), channel_id=1, source_target_pairs={{896,0},{912,16},{928,32},{944,48},{960,64},{976,80},{992,96},{100... | collective-permute-start | bytes 884744 | tf_op jit(solution)/shard_map/ppermute | solution.py:55
  27.5 14.1 %collective-permute-start.10 = (bf16[128,1152]{1,0:T(8,128)(2,1)S(1)}, bf16[128,1152]{1,0:T(8,128)(2,1)S(1)}, u32[]{:S(2)}, u32[]{:S(2)}) collective-permute-start(bf16[128,1152]{1,0:T(8,128)(2,1)S(1)} %get-tuple-element.114), channel_id=1, source_target_pairs={{0,32},{16,48},{32,64},{48,80},{64,96},{80,112},{96,0},{112,16},{1... | collective-permute-start | bytes 884744 | tf_op jit(solution)/shard_map/ppermute | solution.py:49
  30.6 26.6 %collective-permute-start.12 = (bf16[128,1152]{1,0:T(8,128)(2,1)S(1)}, bf16[128,1152]{1,0:T(8,128)(2,1)S(1)}, u32[]{:S(2)}, u32[]{:S(2)}) collective-permute-start(bf16[128,1152]{1,0:T(8,128)(2,1)S(1)} %get-tuple-element.113), channel_id=1, source_target_pairs={{0,96},{16,112},{32,0},{48,16},{64,32},{80,48},{96,64},{112,80},{1... | collective-permute-start | bytes 884744 | tf_op jit(solution)/shard_map/ppermute | solution.py:49
  41.6 15.6 %collective-permute-start.11 = (bf16[128,1152]{1,0:T(8,128)(2,1)S(1)}, bf16[128,1152]{1,0:T(8,128)(2,1)S(1)}, u32[]{:S(2)}, u32[]{:S(2)}) collective-permute-start(bf16[128,1152]{1,0:T(8,128)(2,1)S(1)} %get-tuple-element.96), channel_id=1, source_target_pairs={{0,64},{16,80},{32,96},{48,112},{64,0},{80,16},{96,32},{112,48},{1... | collective-permute-start | bytes 884744 | tf_op jit(solution)/shard_map/ppermute | solution.py:49
  47.5 49.1 %collective-permute-start.8 = (bf16[128,1152]{1,0:T(8,128)(2,1)}, bf16[128,1152]{1,0:T(8,128)(2,1)S(1)}, u32[]{:S(2)}, u32[]{:S(2)}) collective-permute-start(bf16[128,1152]{1,0:T(8,128)(2,1)} %get-tuple-element.118), channel_id=1, source_target_pairs={{0,896},{1,897},{2,898},{3,899},{4,900},{5,901},{6,902},{7,903},{8... | collective-permute-start | bytes 884744 | tf_op jit(solution)/shard_map/ppermute | solution.py:41
  52.1 51.6 %collective-permute-start.9 = (bf16[128,1152]{1,0:T(8,128)(2,1)}, bf16[128,1152]{1,0:T(8,128)(2,1)}, u32[]{:S(2)}, u32[]{:S(2)}) collective-permute-start(bf16[128,1152]{1,0:T(8,128)(2,1)} %get-tuple-element.117), channel_id=1, source_target_pairs={{0,143},{1,128},{2,129},{3,130},{4,131},{5,132},{6,133},{7,134},{8... | collective-permute-start | bytes 884744 | tf_op jit(solution)/shard_map/ppermute | solution.py:41
  57.2 0.7 copy-start.4
  58.0 9.4 %copy-start.5 = (bf16[128,1152]{1,0:T(8,128)(2,1)S(1)}, bf16[128,1152]{1,0:T(8,128)(2,1)}, u32[]{:S(2)}) copy-start(bf16[128,1152]{1,0:T(8,128)(2,1)} %copy-done.4) | copy-start | bytes 884740 | tf_op jit(solution)/shard_map/cond
  58.2 14.7 %collective-permute-start = (bf16[128,1152]{1,0:T(8,128)(2,1)S(1)}, bf16[128,1152]{1,0:T(8,128)(2,1)S(1)}, u32[]{:S(2)}, u32[]{:S(2)}) collective-permute-start(bf16[128,1152]{1,0:T(8,128)(2,1)S(1)} %get-tuple-element.112), channel_id=1, source_target_pairs={{0,32},{16,48},{32,64},{48,80},{64,96},{80,112},{96,0},{112,16},{1... | collective-permute-start | bytes 884744 | tf_op jit(solution)/shard_map/cond/branch_1_fun/ppermute | solution.py:49
  60.4 12.4 %collective-permute-start.1 = (bf16[128,1152]{1,0:T(8,128)(2,1)S(1)}, bf16[128,1152]{1,0:T(8,128)(2,1)S(1)}, u32[]{:S(2)}, u32[]{:S(2)}) collective-permute-start(bf16[128,1152]{1,0:T(8,128)(2,1)S(1)} %get-tuple-element.111), channel_id=1, source_target_pairs={{0,64},{16,80},{32,96},{48,112},{64,0},{80,16},{96,32},{112,48},{1... | collective-permute-start | bytes 884744 | tf_op jit(solution)/shard_map/cond/branch_1_fun/ppermute | solution.py:49
  64.0 11.9 %collective-permute-start.2 = (bf16[128,1152]{1,0:T(8,128)(2,1)S(1)}, bf16[128,1152]{1,0:T(8,128)(2,1)S(1)}, u32[]{:S(2)}, u32[]{:S(2)}) collective-permute-start(bf16[128,1152]{1,0:T(8,128)(2,1)S(1)} %get-tuple-element.110), channel_id=1, source_target_pairs={{0,96},{16,112},{32,0},{48,16},{64,32},{80,48},{96,64},{112,80},{1... | collective-permute-start | bytes 884744 | tf_op jit(solution)/shard_map/cond/branch_1_fun/ppermute | solution.py:49
  72.2 0.6 copy-start
  75.9 8.7 %collective-permute-start.3 = (bf16[512,1152]{1,0:T(8,128)(2,1)}, bf16[512,1152]{1,0:T(8,128)(2,1)}, u32[]{:S(2)}, u32[]{:S(2)}) collective-permute-start(bf16[512,1152]{1,0:T(8,128)(2,1)} %get-tuple-element.69), channel_id=1, source_target_pairs={{0,16},{16,0},{32,48},{48,32},{64,80},{80,64},{96,112},{112,96},{1... | collective-permute-start | bytes 3538952 | tf_op jit(solution)/shard_map/cond/branch_1_fun/ppermute | solution.py:59
  82.5 7.6 %collective-permute-start.4 = (bf16[512,1152]{1,0:T(8,128)(2,1)}, bf16[512,1152]{1,0:T(8,128)(2,1)S(1)}, u32[]{:S(2)}, u32[]{:S(2)}) collective-permute-start(bf16[512,1152]{1,0:T(8,128)(2,1)} %pad_maximum_fusion), channel_id=1, source_target_pairs={{0,16},{16,0},{32,48},{48,32},{64,80},{80,64},{96,112},{112,96},{1... | collective-permute-start | bytes 3538952 | tf_op jit(solution)/shard_map/cond/branch_1_fun/ppermute | solution.py:59
  84.6 0.8 copy-start.1

commit v10 on v9

--- a/solution.py
+++ b/solution.py
@@ -113,20 +113,9 @@
 
 
 def first_kernel(scale, bias, roles, x_ref, y_ref, pos_ref, *rest):
-    refs, (loss_ref, grads_ref, units_ref, inverses_ref, sent_ref, stack_ref) = rest[:-6], rest[-6:]
+    refs, (loss_ref, grads_ref, units_ref, inverses_ref, stack_ref) = rest[:-5], rest[-5:]
     tau, offset = scale[0], bias[0]
     rows = x_ref.shape[0]
-
-    @pl.when(roles[len(refs)] == TEXT)
-    def _():
-        sent_ref[:rows, :] = y_ref[...]
-
-    @pl.when(roles[len(refs)] != TEXT)
-    def _():
-        sent_ref[:rows, :] = x_ref[...]
-
-    for i, ref in enumerate(refs, 1):
-        sent_ref[i * rows : (i + 1) * rows, :] = ref[...]
     for i, ref in enumerate((x_ref, y_ref)):
         inverse = row_inverse(ref[...])
         inverses_ref[i * rows : (i + 1) * rows, :] = inverse
@@ -155,18 +144,26 @@
 ):
     tau, offset = scale[0], bias[0]
     rows = x_ref.shape[0]
-    one, two = one_ref[...].astype(F32), two_ref[...].astype(F32)
-    text, image = jnp.where(odd[0] == 1, one, two), jnp.where(odd[0] == 1, two, one)
-    for i, (feats_ref, other, out_ref) in enumerate(((x_ref, text, ix_ref), (y_ref, image, ty_ref))):
-        own = slice(i * rows, (i + 1) * rows)
-        other = unit_rows(other)
-        loss, slope = loss_and_slope(tau * by_rows(other, units_ref[own, :]) + offset)
-        if i == TEXT:
-            loss_ref[...] = jnp.sum(loss_in[...] + loss, axis=0, keepdims=True) / F32((SPAN + 1) * rows)
-        grad = (grads_in[own, :] + by_cols(slope.astype(BF16), other)) * tau
-        inverse = inverses_ref[own, :]
-        norm = feats_ref[...].astype(F32) * inverse
-        out_ref[...] = (grad - norm * jnp.sum(norm * grad, axis=-1, keepdims=True)) * inverse
+
+    def finish(text_ref, image_ref):
+        for i, (feats_ref, other_ref, out_ref) in enumerate(((x_ref, text_ref, ix_ref), (y_ref, image_ref, ty_ref))):
+            own = slice(i * rows, (i + 1) * rows)
+            other = unit_rows(other_ref[...])
+            loss, slope = loss_and_slope(tau * by_rows(other, units_ref[own, :]) + offset)
+            if i == TEXT:
+                loss_ref[...] = jnp.sum(loss_in[...] + loss, axis=0, keepdims=True) / F32((SPAN + 1) * rows)
+            grad = (grads_in[own, :] + by_cols(slope.astype(BF16), other)) * tau
+            inverse = inverses_ref[own, :]
+            norm = feats_ref[...].astype(F32) * inverse
+            out_ref[...] = (grad - norm * jnp.sum(norm * grad, axis=-1, keepdims=True)) * inverse
+
+    @pl.when(odd[0] == 1)
+    def _():
+        finish(one_ref, two_ref)
+
+    @pl.when(odd[0] != 1)
+    def _():
+        finish(two_ref, one_ref)
 
 
 def call(kernel, outs, blocks, scalars, *args, scratch=()):
@@ -196,17 +193,15 @@
     y_back = along_ring(y, 1)
     x_next = along_ring(x, -1)
     first = [jnp.where(chip + by < CHIPS, y, x) for by in shifts]
-    near, far = in_row(first[0], 1), in_row(first[2], 3)
-    first[1], near = lax.optimization_barrier((first[1], near))
-    middle = in_row(first[1], 2)
+    near = in_row(first[0], 1)
+    first[1], first[2], near = lax.optimization_barrier((first[1], first[2], near))
+    middle, far = in_row(first[1], 2), in_row(first[2], 3)
     odd = index // SPAN % 2
-    y_back, x_next, wrapped = lax.optimization_barrier((y_back, x_next, wrapped))
     one = swapped_along_ring(jnp.where(odd == 0, y_back, x_next), length - 1, 0)
     two = swapped_along_ring(jnp.where(odd == 1, y_back, x_next), length - 1, 1)
     double = 2 * rows
     loss_out, grads_out = ((rows, rows), F32), ((double, width), F32)
     units_out, inverses_out = ((double, width), BF16), ((double, 1), F32)
-    sent_out = ((CHIPS * rows, width), BF16)
     near_role, middle_role, far_role = [(chip < by).astype(jnp.int32) for by in shifts]
     twin_role = 1 - core
 
@@ -223,20 +218,19 @@
         text = jnp.where(index < SPAN, wrapped, y_back)
         image = jnp.where(index >= last, wrapped, x_next)
         then = [jnp.where(chip + by < CHIPS, image, text) for by in shifts]
-        got_roles = [near_role, middle_role, far_role]
-        loss, grads, units, inverses, sent = call(
-            first_kernel, [loss_out, grads_out, units_out, inverses_out, sent_out], 4,
-            (scale, bias, jnp.stack(got_roles + [core])), x, y, positive, near, middle, far, scratch=stack(3),
+        got, roles = [near, middle, far], [near_role, middle_role, far_role]
+        twin = to_twin(jnp.concatenate([jnp.where(core == 0, y, x)] + got, axis=0))
+        then[2], twin = lax.optimization_barrier((then[2], twin))
+        later = [in_row(block, by) for by, block in zip(shifts, then)]
+        loss, grads, units, inverses = call(
+            first_kernel, [loss_out, grads_out, units_out, inverses_out], 8,
+            (scale, bias, jnp.stack(roles + [twin_role] + roles)), x, y, positive, *got, twin, scratch=stack(7),
         )
-        later = [in_row(block, by) for by, block in zip(shifts, then)]
-        *later, sent = lax.optimization_barrier((*later, sent))
-        twin = to_twin(sent)
-        later_twin = to_twin(jnp.concatenate([jnp.where(core == 0, image, text)] + later, axis=0))
-        later_roles = [1 - role for role in got_roles]
-        loss, grads = more([twin_role] + got_roles, [twin], units, loss, grads)
-        loss, grads = more(
-            later_roles + [1 - twin_role] + later_roles, later + [later_twin], units, loss, grads
-        )
+        *later, loss = lax.optimization_barrier((*later, loss))
+        twin = to_twin(jnp.concatenate([jnp.where(core == 0, image, text)] + later, axis=0))
+        roles = [1 - role for role in roles]
+        loss, grads = more(roles, later, units, loss, grads)
+        loss, grads = more([1 - twin_role] + roles, [twin], units, loss, grads)
         return loss, grads, units, inverses
 
     def skip(_):

time: 108 us -> 106 us (0.981)
  the two profiles are of different devices: /device:TPU:1 before, /device:TPU:32 now
where the time goes in v10:
time: 106 us; the launch traced here: 105 us
  starting transfers between devices  56.9 us (54%)
  Pallas kernels  18.9 us (18%)
  waiting for transfers between devices  17.7 us (17%)
  other arithmetic  6.48 us (6%)
  local copies, waits for them, and re-layouts  2.77 us (3%)
  between operations  2.18 us (2%)
    ppermute x6, starting transfers between devices, in_row(): return lax.ppermute(x, 'blk', pairs)  20.3 us
    pallas_call x4, Pallas kernels, call(): pl.pallas_call(kernel, out_shape=[jax.ShapeDtypeStruct(shape, kind) for s...  18.9 us
    ppermute x2, starting transfers between devices, swapped_along_ring(): return lax.ppermute(x, ('blk', 'group'), pairs)  16.9 us
    ppermute x2, starting transfers between devices, along_ring(): return lax.ppermute(x, ('blk', 'group'), pairs)  15.1 us
    ppermute x2, waiting for transfers between devices, along_ring(): return lax.ppermute(x, ('blk', 'group'), pairs)  8.12 us
    ppermute x2, waiting for transfers between devices, swapped_along_ring(): return lax.ppermute(x, ('blk', 'group'), pairs)  5.78 us
    ppermute x2, starting transfers between devices, to_twin(): lax.ppermute(x, 'blk', [(i, i ^ 1) for i in range(lax.axis_size('blk'))])  3.86 us
    ppermute x6, waiting for transfers between devices, in_row(): return lax.ppermute(x, 'blk', pairs)  3.78 us
  transfers between devices with their start and end apart: 13, of which 3 were waited for; matrix products, arithmetic and copies ran while one was open for 5% of the time, Pallas kernels for 14%

profile of v10, /device:TPU:32, one launch (start us, length us, event | category | flops | bytes accessed | tf_op | source)
XLA Modules:
  0.0 105.1 jit_solution(4157503603474847827)
XLA Ops:
  0.6 0.0 copy-start.4
  0.6 0.0 copy-start.2
  0.7 1.2 %broadcast_select_fusion.7 = (bf16[128,1152]{1,0:T(8,128)(2,1)S(1)}, bf16[128,1152]{1,0:T(8,128)(2,1)S(1)}, bf16[128,1152]{1,0:T(8,128)(2,1)S(1)}, bf16[128,1152]{1,0:T(8,128)(2,1)S(1)}) fusion(bf16[128,1152]{1,0:T(8,128)(2,1)} %y_ref.1, bf16[128,1152]{1,0:T(8,128)(2,1)} %x_ref.1, pred[]{:T(512)S(6)} %lt.51, pred[]{:T(512)S(6)} %lt.50, pred[]{:T(512)S(6)} %lt.49, ...), kind=kLoop, calls=%fused_computation.11 | loop fusion | flops 589824 | bytes 1769476 | tf_op jit(solution)/shard_map/jit(_where)/select_n | solution.py:195
  1.9 3.4 %collective-permute-start.10 = (bf16[128,1152]{1,0:T(8,128)(2,1)S(1)}, bf16[128,1152]{1,0:T(8,128)(2,1)S(1)}, u32[]{:S(2)}, u32[]{:S(2)}) collective-permute-start(bf16[128,1152]{1,0:T(8,128)(2,1)S(1)} %get-tuple-element.110), channel_id=1, source_target_pairs={{0,32},{16,48},{32,64},{48,80},{64,96},{80,112},{96,0},{112,16},{1... | collective-permute-start | bytes 884744 | tf_op jit(solution)/shard_map/ppermute | solution.py:49
  5.4 13.2 %collective-permute-start.6 = (bf16[128,1152]{1,0:T(8,128)(2,1)S(1)}, bf16[128,1152]{1,0:T(8,128)(2,1)S(1)}, u32[]{:S(2)}, u32[]{:S(2)}) collective-permute-start(bf16[128,1152]{1,0:T(8,128)(2,1)S(1)} %copy-done.2), channel_id=1, source_target_pairs={{0,911},{1,896},{2,897},{3,898},{4,899},{5,900},{6,901},{7,902},{8... | collective-permute-start | bytes 884744 | tf_op jit(solution)/shard_map/ppermute | solution.py:27
  18.6 1.9 %collective-permute-start.5 = (bf16[128,1152]{1,0:T(8,128)(2,1)S(1)}, bf16[128,1152]{1,0:T(8,128)(2,1)S(1)}, u32[]{:S(2)}, u32[]{:S(2)}) collective-permute-start(bf16[128,1152]{1,0:T(8,128)(2,1)S(1)} %copy-done.4), channel_id=1, source_target_pairs={{0,128},{1,129},{2,130},{3,131},{4,132},{5,133},{6,134},{7,135},{8... | collective-permute-start | bytes 884744 | tf_op jit(solution)/shard_map/ppermute | solution.py:27
  20.5 0.7 collective-permute-start.9
  21.2 0.0 collective-permute-done.10
  21.2 1.9 %collective-permute-start.11 = (bf16[128,1152]{1,0:T(8,128)(2,1)S(1)}, bf16[128,1152]{1,0:T(8,128)(2,1)S(1)}, u32[]{:S(2)}, u32[]{:S(2)}) collective-permute-start(bf16[128,1152]{1,0:T(8,128)(2,1)S(1)} %get-tuple-element.93), channel_id=1, source_target_pairs={{0,64},{16,80},{32,96},{48,112},{64,0},{80,16},{96,32},{112,48},{1... | collective-permute-start | bytes 884744 | tf_op jit(solution)/shard_map/ppermute | solution.py:49
  23.1 5.1 %collective-permute-start.12 = (bf16[128,1152]{1,0:T(8,128)(2,1)S(1)}, bf16[128,1152]{1,0:T(8,128)(2,1)S(1)}, u32[]{:S(2)}, u32[]{:S(2)}) collective-permute-start(bf16[128,1152]{1,0:T(8,128)(2,1)S(1)} %get-tuple-element.94), channel_id=1, source_target_pairs={{0,96},{16,112},{32,0},{48,16},{64,32},{80,48},{96,64},{112,80},{1... | collective-permute-start | bytes 884744 | tf_op jit(solution)/shard_map/ppermute | solution.py:49
  28.3 0.0 collective-permute-done.6
  28.3 8.1 %collective-permute-done.5 = bf16[128,1152]{1,0:T(8,128)(2,1)S(1)} collective-permute-done((bf16[128,1152]{1,0:T(8,128)(2,1)S(1)}, bf16[128,1152]{1,0:T(8,128)(2,1)S(1)}, u32[]{:S(2)}, u32[]{:S(2)}) %collective-permute-start.5) | collective-permute-done | bytes 294944 | tf_op jit(solution)/shard_map/ppermute | solution.py:27
  36.4 0.9 broadcast_select_fusion.11
  37.3 11.6 %collective-permute-start.8 = (bf16[128,1152]{1,0:T(8,128)(2,1)}, bf16[128,1152]{1,0:T(8,128)(2,1)S(1)}, u32[]{:S(2)}, u32[]{:S(2)}) collective-permute-start(bf16[128,1152]{1,0:T(8,128)(2,1)} %get-tuple-element.114), channel_id=1, source_target_pairs={{0,143},{1,128},{2,129},{3,130},{4,131},{5,132},{6,133},{7,134},{8... | collective-permute-start | bytes 884744 | tf_op jit(solution)/shard_map/ppermute | solution.py:41
  48.9 5.3 %collective-permute-start.7 = (bf16[128,1152]{1,0:T(8,128)(2,1)}, bf16[128,1152]{1,0:T(8,128)(2,1)}, u32[]{:S(2)}, u32[]{:S(2)}) collective-permute-start(bf16[128,1152]{1,0:T(8,128)(2,1)} %get-tuple-element.115), channel_id=1, source_target_pairs={{0,896},{1,897},{2,898},{3,899},{4,900},{5,901},{6,902},{7,903},{8... | collective-permute-start | bytes 884744 | tf_op jit(solution)/shard_map/ppermute | solution.py:41
  55.5 0.0 collective-permute-done.9
  55.5 0.0 collective-permute-done.12
  55.5 39.0 %conditional.1 = (f32[128,128]{1,0:T(8,128)S(1)}, f32[256,1152]{1,0:T(8,128)}, bf16[256,1152]{1,0:T(8,128)(2,1)}, f32[256,1]{1,0:T(8,128)}) conditional(s32[]{:T(128)} %convert_element_type.12, () %tuple.19, (s32[]{:T(128)}, pred[]{:T(512)}, s32[]{:T(128)}, s32[]{:T(128)}, s32[]{:T(128)}, /*index=5*/s32[]{:T(128)}, s32[]{:T(128)}, ...), branch_computations={%region_0.1_spmd, %region_1.2_spmd} | conditional | flops 1142931456 | bytes 47514404 | solution.py:240
  55.7 0.6 copy-done.3
  56.3 0.1 copy-done.5
  56.4 0.1 copy-done.6
  56.5 0.1 copy-done.7
  56.6 0.1 copy-done.8
  56.7 0.1 copy-done.11
  56.8 0.1 copy-done.12
  56.9 0.1 pad_maximum_fusion
  57.0 1.9 %collective-permute-start = (bf16[512,1152]{1,0:T(8,128)(2,1)S(1)}, bf16[512,1152]{1,0:T(8,128)(2,1)S(1)}, u32[]{:S(2)}, u32[]{:S(2)}) collective-permute-start(bf16[512,1152]{1,0:T(8,128)(2,1)S(1)} %pad_maximum_fusion), channel_id=1, source_target_pairs={{0,16},{16,0},{32,48},{48,32},{64,80},{80,64},{96,112},{112,96},{1... | collective-permute-start | bytes 3538952 | tf_op jit(solution)/shard_map/cond/branch_1_fun/ppermute | solution.py:59
  58.9 1.9 %broadcast_select_fusion.2 = (bf16[128,1152]{1,0:T(8,128)(2,1)}, bf16[128,1152]{1,0:T(8,128)(2,1)S(1)}, bf16[128,1152]{1,0:T(8,128)(2,1)S(1)}) fusion(pred[]{:T(512)S(6)} %eq.11, bf16[128,1152]{1,0:T(8,128)(2,1)} %copy-done.12, bf16[128,1152]{1,0:T(8,128)(2,1)} %copy-done.11, pred[]{:T(512)S(6)} %lt.33, bf16[128,1152]{1,0:T(8,128)(2,1)} %get-tuple-element.63, ...), kind=kLoop, calls=%fused_computation.4 | loop fusion | flops 442368 | bytes 1769475 | tf_op jit(solution)/shard_map/cond/branch_1_fun/jit(_where)/select_n | solution.py:230
  60.8 1.0 broadcast_select_fusion
  61.9 2.8 %collective-permute-start.2 = (bf16[128,1152]{1,0:T(8,128)(2,1)}, bf16[128,1152]{1,0:T(8,128)(2,1)S(1)}, u32[]{:S(2)}, u32[]{:S(2)}) collective-permute-start(bf16[128,1152]{1,0:T(8,128)(2,1)} %get-tuple-element.107), channel_id=1, source_target_pairs={{0,64},{16,80},{32,96},{48,112},{64,0},{80,16},{96,32},{112,48},{1... | collective-permute-start | bytes 884744 | tf_op jit(solution)/shard_map/cond/branch_1_fun/ppermute | solution.py:49
  64.7 2.4 %collective-permute-start.1 = (bf16[128,1152]{1,0:T(8,128)(2,1)}, bf16[128,1152]{1,0:T(8,128)(2,1)S(1)}, u32[]{:S(2)}, u32[]{:S(2)}) collective-permute-start(bf16[128,1152]{1,0:T(8,128)(2,1)} %get-tuple-element.108), channel_id=1, source_target_pairs={{0,32},{16,48},{32,64},{48,80},{64,96},{80,112},{96,0},{112,16},{1... | collective-permute-start | bytes 884744 | tf_op jit(solution)/shard_map/cond/branch_1_fun/ppermute | solution.py:49
  67.1 4.7 %collective-permute-start.3 = (bf16[128,1152]{1,0:T(8,128)(2,1)}, bf16[128,1152]{1,0:T(8,128)(2,1)S(1)}, u32[]{:S(2)}, u32[]{:S(2)}) collective-permute-start(bf16[128,1152]{1,0:T(8,128)(2,1)} %get-tuple-element.67), channel_id=1, source_target_pairs={{0,96},{16,112},{32,0},{48,16},{64,32},{80,48},{96,64},{112,80},{1... | collective-permute-start | bytes 884744 | tf_op jit(solution)/shard_map/cond/branch_1_fun/ppermute | solution.py:49
  71.8 0.1 stack.37.roles
  71.9 5.5 %branch_1_fun.3 = (f32[128,128]{1,0:T(8,128)S(1)}, f32[256,1152]{1,0:T(8,128)S(1)}, bf16[256,1152]{1,0:T(8,128)(2,1)}, f32[256,1]{1,0:T(8,128)}) custom-call(f32[1]{0:T(128)} %get-tuple-element.47.scale, f32[1]{0:T(128)} %get-tuple-element.48.bias, s32[7]{0:T(128)S(1)} %stack.37.roles, bf16[128,1152]{1,0:T(8,128)(2,1)} %copy-done.3, ...), custom_call_target="tpu_custom_call" | custom-call | flops 603979776 | bytes 8388608 | tf_op jit(solution)/shard_map/cond/branch_1_fun/pallas_call | solution.py:171
  77.4 0.0 collective-permute-done.2.rest_1_
  77.4 3.8 %collective-permute-done.1.rest_0_ = bf16[128,1152]{1,0:T(8,128)(2,1)S(1)} collective-permute-done((bf16[128,1152]{1,0:T(8,128)(2,1)}, bf16[128,1152]{1,0:T(8,128)(2,1)S(1)}, u32[]{:S(2)}, u32[]{:S(2)}) %collective-permute-start.1) | collective-permute-done | bytes 294944 | tf_op jit(solution)/shard_map/cond/branch_1_fun/ppermute | solution.py:49
  81.2 0.0 collective-permute-done.3.rest_2_
  81.2 1.1 %pad_maximum_fusion.1 = bf16[512,1152]{1,0:T(8,128)(2,1)} fusion(bf16[128,1152]{1,0:T(8,128)(2,1)S(1)} %collective-permute-done.3.rest_2_, bf16[128,1152]{1,0:T(8,128)(2,1)S(1)} %collective-permute-done.2.rest_1_, bf16[128,1152]{1,0:T(8,128)(2,1)S(1)} %collective-permute-done.1.rest_0_, bf16[128,1152]{1,0:T(8,128)(2,1)S(1)} %copy-done.9), kind=kLoop, calls=%fused_computation.1 | loop fusion | flops 4718592 | bytes 2359296 | tf_op jit(solution)/shard_map/cond/branch_1_fun/concatenate | solution.py:230
  82.4 1.9 %collective-permute-start.4 = (bf16[512,1152]{1,0:T(8,128)(2,1)}, bf16[512,1152]{1,0:T(8,128)(2,1)S(1)}, u32[]{:S(2)}, u32[]{:S(2)}) collective-permute-start(bf16[512,1152]{1,0:T(8,128)(2,1)} %pad_maximum_fusion.1), channel_id=1, source_target_pairs={{0,16},{16,0},{32,48},{48,32},{64,80},{80,64},{96,112},{112,96},{1... | collective-permute-start | bytes 3538952 | tf_op jit(solution)/shard_map/cond/branch_1_fun/ppermute | solution.py:59
  84.3 0.1 pad_add_fusion.1.roles
  84.4 0.1 pad_add_fusion.roles
  84.5 0.8 copy-done.1
  85.3 4.0 %branch_1_fun.4 = (f32[128,128]{1,0:T(8,128)S(1)}, f32[256,1152]{1,0:T(8,128)S(1)}) custom-call(f32[1]{0:T(128)} %get-tuple-element.47.scale, f32[1]{0:T(128)} %get-tuple-element.48.bias, s32[3]{0:T(128)S(1)} %pad_add_fusion.1.roles, bf16[256,1152]{1,0:T(8,128)(2,1)} %get-tuple-element.122.units_ref, f32[128,128]{1,0:T(8,128)S(1)} %copy-done.1, ...), custom_call_target="tpu_custom_call" | custom-call | flops 226492416 | bytes 3145728 | tf_op jit(solution)/shard_map/cond/branch_1_fun/pallas_call | solution.py:171
  89.3 0.0 collective-permute-done.4.rest_0_
  89.3 5.3 %branch_1_fun.5 = (f32[128,128]{1,0:T(8,128)S(1)}, f32[256,1152]{1,0:T(8,128)}) custom-call(f32[1]{0:T(128)} %get-tuple-element.47.scale, f32[1]{0:T(128)} %get-tuple-element.48.bias, s32[4]{0:T(128)S(1)} %pad_add_fusion.roles, bf16[256,1152]{1,0:T(8,128)(2,1)} %get-tuple-element.122.units_ref, f32[128,128]{1,0:T(8,128)S(1)} %get-tuple-element.74.loss_in, ...), custom_call_target="tpu_custom_call" | custom-call | flops 301989888 | bytes 4194304 | tf_op jit(solution)/shard_map/cond/branch_1_fun/pallas_call | solution.py:171
  94.6 0.6 copy-done.13
  95.2 5.8 %collective-permute-done.7.one_ref = bf16[128,1152]{1,0:T(8,128)(2,1)} collective-permute-done((bf16[128,1152]{1,0:T(8,128)(2,1)}, bf16[128,1152]{1,0:T(8,128)(2,1)}, u32[]{:S(2)}, u32[]{:S(2)}) %collective-permute-start.7) | collective-permute-done | bytes 294944 | tf_op jit(solution)/shard_map/ppermute | solution.py:41
  101.0 4.1 %shard_map.77 = (f32[1,128]{1,0:T(1,128)}, f32[128,1152]{1,0:T(8,128)}, f32[128,1152]{1,0:T(8,128)}) custom-call(f32[1]{0:T(128)S(6)} %copy.17.scale, f32[1]{0:T(128)S(6)} %copy.18.bias, s32[1]{0:T(128)} %bitcast.8.odd, bf16[128,1152]{1,0:T(8,128)(2,1)} %x_ref.1, bf16[128,1152]{1,0:T(8,128)(2,1)} %y_ref.1, bf16[128,1152]{1,0:T(8,128)(2,1)} %collective-permute-done.7.one_ref, ...), custom_call_target="tpu_custom_call" | custom-call | flops 150994944 | bytes 2097152 | tf_op jit(solution)/shard_map/pallas_call | solution.py:171
  (23 shorter events, 0.1 us)
Async XLA Ops:
  0.6 17.9 %copy-start.4 = (bf16[128,1152]{1,0:T(8,128)(2,1)S(1)}, bf16[128,1152]{1,0:T(8,128)(2,1)}, u32[]{:S(2)}) copy-start(bf16[128,1152]{1,0:T(8,128)(2,1)} %y_ref.1) | copy-start | bytes 884740
  0.6 4.7 %copy-start.2 = (bf16[128,1152]{1,0:T(8,128)(2,1)S(1)}, bf16[128,1152]{1,0:T(8,128)(2,1)}, u32[]{:S(2)}) copy-start(bf16[128,1152]{1,0:T(8,128)(2,1)} %x_ref.1) | copy-start | bytes 884740
  0.7 54.8 %copy-start.14 = (s32[1,128]{1,0:T(1,128)S(1)}, s32[1,128]{1,0:T(1,128)}, u32[]{:S(2)}) copy-start(s32[1,128]{1,0:T(1,128)} %param.9) | copy-start | bytes 1540
  1.9 19.3 %collective-permute-start.10 = (bf16[128,1152]{1,0:T(8,128)(2,1)S(1)}, bf16[128,1152]{1,0:T(8,128)(2,1)S(1)}, u32[]{:S(2)}, u32[]{:S(2)}) collective-permute-start(bf16[128,1152]{1,0:T(8,128)(2,1)S(1)} %get-tuple-element.110), channel_id=1, source_target_pairs={{0,32},{16,48},{32,64},{48,80},{64,96},{80,112},{96,0},{112,16},{1... | collective-permute-start | bytes 884744 | tf_op jit(solution)/shard_map/ppermute | solution.py:49
  5.4 22.9 %collective-permute-start.6 = (bf16[128,1152]{1,0:T(8,128)(2,1)S(1)}, bf16[128,1152]{1,0:T(8,128)(2,1)S(1)}, u32[]{:S(2)}, u32[]{:S(2)}) collective-permute-start(bf16[128,1152]{1,0:T(8,128)(2,1)S(1)} %copy-done.2), channel_id=1, source_target_pairs={{0,911},{1,896},{2,897},{3,898},{4,899},{5,900},{6,901},{7,902},{8... | collective-permute-start | bytes 884744 | tf_op jit(solution)/shard_map/ppermute | solution.py:27
  18.6 17.9 %collective-permute-start.5 = (bf16[128,1152]{1,0:T(8,128)(2,1)S(1)}, bf16[128,1152]{1,0:T(8,128)(2,1)S(1)}, u32[]{:S(2)}, u32[]{:S(2)}) collective-permute-start(bf16[128,1152]{1,0:T(8,128)(2,1)S(1)} %copy-done.4), channel_id=1, source_target_pairs={{0,128},{1,129},{2,130},{3,131},{4,132},{5,133},{6,134},{7,135},{8... | collective-permute-start | bytes 884744 | tf_op jit(solution)/shard_map/ppermute | solution.py:27
  20.5 35.0 %collective-permute-start.9 = (bf16[128,1152]{1,0:T(8,128)(2,1)S(1)}, bf16[128,1152]{1,0:T(8,128)(2,1)S(1)}, u32[]{:S(2)}, u32[]{:S(2)}) collective-permute-start(bf16[128,1152]{1,0:T(8,128)(2,1)S(1)} %get-tuple-element.113), channel_id=1, source_target_pairs={{896,0},{912,16},{928,32},{944,48},{960,64},{976,80},{992,96},{100... | collective-permute-start | bytes 884744 | tf_op jit(solution)/shard_map/ppermute | solution.py:55
  21.2 34.3 %collective-permute-start.11 = (bf16[128,1152]{1,0:T(8,128)(2,1)S(1)}, bf16[128,1152]{1,0:T(8,128)(2,1)S(1)}, u32[]{:S(2)}, u32[]{:S(2)}) collective-permute-start(bf16[128,1152]{1,0:T(8,128)(2,1)S(1)} %get-tuple-element.93), channel_id=1, source_target_pairs={{0,64},{16,80},{32,96},{48,112},{64,0},{80,16},{96,32},{112,48},{1... | collective-permute-start | bytes 884744 | tf_op jit(solution)/shard_map/ppermute | solution.py:49
  23.1 32.4 %collective-permute-start.12 = (bf16[128,1152]{1,0:T(8,128)(2,1)S(1)}, bf16[128,1152]{1,0:T(8,128)(2,1)S(1)}, u32[]{:S(2)}, u32[]{:S(2)}) collective-permute-start(bf16[128,1152]{1,0:T(8,128)(2,1)S(1)} %get-tuple-element.94), channel_id=1, source_target_pairs={{0,96},{16,112},{32,0},{48,16},{64,32},{80,48},{96,64},{112,80},{1... | collective-permute-start | bytes 884744 | tf_op jit(solution)/shard_map/ppermute | solution.py:49
  28.3 9.0 %copy-start.10 = (bf16[128,1152]{1,0:T(8,128)(2,1)}, bf16[128,1152]{1,0:T(8,128)(2,1)S(1)}, u32[]{:S(2)}) copy-start(bf16[128,1152]{1,0:T(8,128)(2,1)S(1)} %collective-permute-done.6) | copy-start | bytes 884740
  37.3 57.3 %collective-permute-start.8 = (bf16[128,1152]{1,0:T(8,128)(2,1)}, bf16[128,1152]{1,0:T(8,128)(2,1)S(1)}, u32[]{:S(2)}, u32[]{:S(2)}) collective-permute-start(bf16[128,1152]{1,0:T(8,128)(2,1)} %get-tuple-element.114), channel_id=1, source_target_pairs={{0,143},{1,128},{2,129},{3,130},{4,131},{5,132},{6,133},{7,134},{8... | collective-permute-start | bytes 884744 | tf_op jit(solution)/shard_map/ppermute | solution.py:41
  48.9 52.1 %collective-permute-start.7 = (bf16[128,1152]{1,0:T(8,128)(2,1)}, bf16[128,1152]{1,0:T(8,128)(2,1)}, u32[]{:S(2)}, u32[]{:S(2)}) collective-permute-start(bf16[128,1152]{1,0:T(8,128)(2,1)} %get-tuple-element.115), channel_id=1, source_target_pairs={{0,896},{1,897},{2,898},{3,899},{4,900},{5,901},{6,902},{7,903},{8... | collective-permute-start | bytes 884744 | tf_op jit(solution)/shard_map/ppermute | solution.py:41
  55.6 0.7 copy-start.3
  55.6 0.8 copy-start.5
  55.6 0.9 copy-start.6
  55.6 1.0 copy-start.7
  55.6 1.1 %copy-start.8 = (bf16[128,1152]{1,0:T(8,128)(2,1)}, bf16[128,1152]{1,0:T(8,128)(2,1)S(1)}, u32[]{:S(2)}) copy-start(bf16[128,1152]{1,0:T(8,128)(2,1)S(1)} %get-tuple-element.59.rest_2_) | copy-start | bytes 884740 | tf_op jit(solution)/shard_map/cond
  55.6 1.2 %copy-start.11 = (bf16[128,1152]{1,0:T(8,128)(2,1)}, bf16[128,1152]{1,0:T(8,128)(2,1)S(1)}, u32[]{:S(2)}) copy-start(bf16[128,1152]{1,0:T(8,128)(2,1)S(1)} %get-tuple-element.64) | copy-start | bytes 884740 | tf_op jit(solution)/shard_map/cond
  55.6 1.3 %copy-start.12 = (bf16[128,1152]{1,0:T(8,128)(2,1)}, bf16[128,1152]{1,0:T(8,128)(2,1)S(1)}, u32[]{:S(2)}) copy-start(bf16[128,1152]{1,0:T(8,128)(2,1)S(1)} %get-tuple-element.62) | copy-start | bytes 884740 | tf_op jit(solution)/shard_map/cond
  57.0 10.1 %collective-permute-start = (bf16[512,1152]{1,0:T(8,128)(2,1)S(1)}, bf16[512,1152]{1,0:T(8,128)(2,1)S(1)}, u32[]{:S(2)}, u32[]{:S(2)}) collective-permute-start(bf16[512,1152]{1,0:T(8,128)(2,1)S(1)} %pad_maximum_fusion), channel_id=1, source_target_pairs={{0,16},{16,0},{32,48},{48,32},{64,80},{80,64},{96,112},{112,96},{1... | collective-permute-start | bytes 3538952 | tf_op jit(solution)/shard_map/cond/branch_1_fun/ppermute | solution.py:59
  61.9 15.6 %collective-permute-start.2 = (bf16[128,1152]{1,0:T(8,128)(2,1)}, bf16[128,1152]{1,0:T(8,128)(2,1)S(1)}, u32[]{:S(2)}, u32[]{:S(2)}) collective-permute-start(bf16[128,1152]{1,0:T(8,128)(2,1)} %get-tuple-element.107), channel_id=1, source_target_pairs={{0,64},{16,80},{32,96},{48,112},{64,0},{80,16},{96,32},{112,48},{1... | collective-permute-start | bytes 884744 | tf_op jit(solution)/shard_map/cond/branch_1_fun/ppermute | solution.py:49
  64.7 16.5 %collective-permute-start.1 = (bf16[128,1152]{1,0:T(8,128)(2,1)}, bf16[128,1152]{1,0:T(8,128)(2,1)S(1)}, u32[]{:S(2)}, u32[]{:S(2)}) collective-permute-start(bf16[128,1152]{1,0:T(8,128)(2,1)} %get-tuple-element.108), channel_id=1, source_target_pairs={{0,32},{16,48},{32,64},{48,80},{64,96},{80,112},{96,0},{112,16},{1... | collective-permute-start | bytes 884744 | tf_op jit(solution)/shard_map/cond/branch_1_fun/ppermute | solution.py:49
  67.1 14.1 %collective-permute-start.3 = (bf16[128,1152]{1,0:T(8,128)(2,1)}, bf16[128,1152]{1,0:T(8,128)(2,1)S(1)}, u32[]{:S(2)}, u32[]{:S(2)}) collective-permute-start(bf16[128,1152]{1,0:T(8,128)(2,1)} %get-tuple-element.67), channel_id=1, source_target_pairs={{0,96},{16,112},{32,0},{48,16},{64,32},{80,48},{96,64},{112,80},{1... | collective-permute-start | bytes 884744 | tf_op jit(solution)/shard_map/cond/branch_1_fun/ppermute | solution.py:49
  71.9 9.3 %copy-start.9 = (bf16[128,1152]{1,0:T(8,128)(2,1)S(1)}, bf16[128,1152]{1,0:T(8,128)(2,1)}, u32[]{:S(2)}) copy-start(bf16[128,1152]{1,0:T(8,128)(2,1)} %get-tuple-element.104) | copy-start | bytes 884740 | tf_op jit(solution)/shard_map/cond
  77.4 4.9 %copy-start = (f32[128,128]{1,0:T(8,128)}, f32[128,128]{1,0:T(8,128)S(1)}, u32[]{:S(2)}) copy-start(f32[128,128]{1,0:T(8,128)S(1)} %get-tuple-element.69.loss_in) | copy-start | bytes 196612 | tf_op jit(solution)/shard_map/cond
  82.4 6.9 %collective-permute-start.4 = (bf16[512,1152]{1,0:T(8,128)(2,1)}, bf16[512,1152]{1,0:T(8,128)(2,1)S(1)}, u32[]{:S(2)}, u32[]{:S(2)}) collective-permute-start(bf16[512,1152]{1,0:T(8,128)(2,1)} %pad_maximum_fusion.1), channel_id=1, source_target_pairs={{0,16},{16,0},{32,48},{48,32},{64,80},{80,64},{96,112},{112,96},{1... | collective-permute-start | bytes 3538952 | tf_op jit(solution)/shard_map/cond/branch_1_fun/ppermute | solution.py:59
  84.5 0.8 copy-start.1
  94.6 0.6 copy-start.13

commit v11 on v7

--- a/solution.py
+++ b/solution.py
@@ -115,14 +115,16 @@
     loss_ref[...] = loss
     grads_ref[:rows, :] = by_cols(slope, y)
     grads_ref[rows:, :] = product(slope, x)
-    add_blocks(roles, refs, tau, offset, units, loss_ref, grads_ref, stack_ref)
-
-
-def next_kernel(scale, bias, roles, units_ref, loss_in, grads_in, *rest):
+    add_blocks([roles[i] for i in range(2 * CHIPS - 1)], refs, tau, offset, units, loss_ref, grads_ref, stack_ref)
+
+
+def next_kernel(first, scale, bias, roles, units_ref, loss_in, grads_in, *rest):
     refs, (loss_ref, grads_ref, stack_ref) = rest[:-3], rest[-3:]
     loss_ref[...] = loss_in[...]
     grads_ref[...] = grads_in[...]
-    add_blocks(roles, refs, scale[0], bias[0], units_ref[...], loss_ref, grads_ref, stack_ref)
+    count = stack_ref.shape[0] * 2 // units_ref.shape[0]
+    flipped = [1 - roles[first + i] for i in range(count)]
+    add_blocks(flipped, refs, scale[0], bias[0], units_ref[...], loss_ref, grads_ref, stack_ref)
 
 
 def last_kernel(
@@ -169,42 +171,42 @@
     y_back = along_ring(y, 1)
     x_next = along_ring(x, -1)
     first = [jnp.where(chip + by < CHIPS, y, x) for by in shifts]
-    nearest = in_row(first[0], 1)
+    near = in_row(first[0], 1)
+    first[1], first[2], near = lax.optimization_barrier((first[1], first[2], near))
+    middle, far = in_row(first[1], 2), in_row(first[2], 3)
     y_outer = along_ring(y_back, length - 1)
     x_outer = along_ring(x_next, 1 - length)
     double = 2 * rows
     loss_out, grads_out = ((rows, rows), F32), ((double, width), F32)
     units_out, inverses_out = ((double, width), BF16), ((double, 1), F32)
-    from_chips = [(chip < by).astype(jnp.int32) for by in shifts]
-    roles = jnp.stack(from_chips + [1 - core] + from_chips)
+    near_role, middle_role, far_role = [(chip < by).astype(jnp.int32) for by in shifts]
+    roles = jnp.stack([near_role, middle_role, far_role, 1 - core, near_role, middle_role, far_role])
 
     def stack(blocks):
         return [pltpu.VMEM((blocks * rows, width), BF16)]
+
+    def more(first, count, refs, units, loss, grads):
+        return call(
+            functools.partial(next_kernel, first), [loss_out, grads_out], count, (scale, bias, roles),
+            units, loss, grads, *refs, scratch=stack(count),
+        )
 
     def inner(_):
         text = jnp.where(index < SPAN, wrapped, y_back)
         image = jnp.where(index >= last, wrapped, x_next)
         then = [jnp.where(chip + by < CHIPS, image, text) for by in shifts]
-        got = [nearest, in_row(first[1], 2), in_row(first[2], 3)]
-        then[2], got[2] = lax.optimization_barrier((then[2], got[2]))
+        got = [near, middle, far]
         twin = to_twin(jnp.concatenate([jnp.where(core == 0, y, x)] + got, axis=0))
-        then[1], twin = lax.optimization_barrier((then[1], twin))
+        then[2], twin = lax.optimization_barrier((then[2], twin))
+        later = [in_row(block, by) for by, block in zip(shifts, then)]
         loss, grads, units, inverses = call(
-            first_kernel, [loss_out, grads_out, units_out, inverses_out], 8, (scale, bias, roles),
-            x, y, positive, *got, twin, scratch=stack(7),
+            first_kernel, [loss_out, grads_out, units_out, inverses_out], 8,
+            (scale, bias, roles), x, y, positive, *got, twin, scratch=stack(2 * CHIPS - 1),
         )
-        later = [in_row(block, by) for by, block in zip(shifts, then)]
         *later, loss = lax.optimization_barrier((*later, loss))
         twin = to_twin(jnp.concatenate([jnp.where(core == 0, image, text)] + later, axis=0))
-        outs, count = [loss_out, grads_out], len(later)
-        loss, grads = call(
-            next_kernel, outs, count, (scale, bias, 1 - roles[:count]),
-            units, loss, grads, *later, scratch=stack(count),
-        )
-        loss, grads = call(
-            next_kernel, outs, count + 1, (scale, bias, 1 - roles[count:]),
-            units, loss, grads, twin, scratch=stack(count + 1),
-        )
+        loss, grads = more(0, len(later), later, units, loss, grads)
+        loss, grads = more(len(later), CHIPS, [twin], units, loss, grads)
         return loss, grads, units, inverses
 
     def skip(_):

time: 123 us -> 104 us (0.85)
  the two profiles are of different devices: /device:TPU:1 before, /device:TPU:36 now
where the time goes in v11:
time: 104 us
  starting transfers between devices  59.2 us (57%)
  waiting for transfers between devices  22.1 us (21%)
  Pallas kernels  16.3 us (16%)
  other arithmetic  2.77 us (3%)
  between operations  2.15 us (2%)
    ppermute x6, starting transfers between devices, in_row(): return lax.ppermute(x, 'blk', pairs)  29.6 us
    ppermute x4, starting transfers between devices, along_ring(): return lax.ppermute(x, ('blk', 'group'), pairs)  25.1 us
    ppermute x4, waiting for transfers between devices, along_ring(): return lax.ppermute(x, ('blk', 'group'), pairs)  16.8 us
    pallas_call x4, Pallas kernels, call(): pl.pallas_call(kernel, out_shape=[jax.ShapeDtypeStruct(shape, kind) for s...  16.3 us
    ppermute x6, waiting for transfers between devices, in_row(): return lax.ppermute(x, 'blk', pairs)  5.23 us
    ppermute x2, starting transfers between devices, to_twin(): lax.ppermute(x, 'blk', [(i, i ^ 1) for i in range(lax.axis_size('blk'))])  3.84 us
  transfers between devices with their start and end apart: 13, of which 4 were waited for; matrix products, arithmetic and copies ran while one was open for 2% of the time, Pallas kernels for 12%

profile of v11, /device:TPU:36, one launch (start us, length us, event | category | flops | bytes accessed | tf_op | source)
XLA Modules:
  0.0 103.7 jit_solution(1436013537946952253)
XLA Ops:
  0.6 0.0 copy-start.1
  0.6 0.0 copy-start
  0.7 0.0 copy-start.9
  0.7 1.2 %broadcast_select_fusion.7 = (bf16[128,1152]{1,0:T(8,128)(2,1)S(1)}, bf16[128,1152]{1,0:T(8,128)(2,1)S(1)}, bf16[128,1152]{1,0:T(8,128)(2,1)S(1)}, bf16[128,1152]{1,0:T(8,128)(2,1)S(1)}) fusion(bf16[128,1152]{1,0:T(8,128)(2,1)} %y_ref.1, bf16[128,1152]{1,0:T(8,128)(2,1)} %x_ref.1, pred[]{:T(512)S(6)} %lt.44, pred[]{:T(512)S(6)} %lt.43, pred[]{:T(512)S(6)} %lt.42, ...), kind=kLoop, calls=%fused_computation.9 | loop fusion | flops 589824 | bytes 1769476 | tf_op jit(solution)/shard_map/jit(_where)/select_n | solution.py:173
  1.9 3.1 %collective-permute-start.10 = (bf16[128,1152]{1,0:T(8,128)(2,1)S(1)}, bf16[128,1152]{1,0:T(8,128)(2,1)S(1)}, u32[]{:S(2)}, u32[]{:S(2)}) collective-permute-start(bf16[128,1152]{1,0:T(8,128)(2,1)S(1)} %get-tuple-element.90), channel_id=1, source_target_pairs={{0,32},{16,48},{32,64},{48,80},{64,96},{80,112},{96,0},{112,16},{1... | collective-permute-start | bytes 884744 | tf_op jit(solution)/shard_map/ppermute | solution.py:35
  5.1 2.0 %collective-permute-start.7 = (bf16[128,1152]{1,0:T(8,128)(2,1)S(1)}, bf16[128,1152]{1,0:T(8,128)(2,1)}, u32[]{:S(2)}, u32[]{:S(2)}) collective-permute-start(bf16[128,1152]{1,0:T(8,128)(2,1)S(1)} %copy-done), channel_id=1, source_target_pairs={{0,911},{1,896},{2,897},{3,898},{4,899},{5,900},{6,901},{7,902},{8... | collective-permute-start | bytes 884744 | tf_op jit(solution)/shard_map/ppermute | solution.py:27
  7.1 3.8 %collective-permute-start.5 = (bf16[128,1152]{1,0:T(8,128)(2,1)S(1)}, bf16[128,1152]{1,0:T(8,128)(2,1)}, u32[]{:S(2)}, u32[]{:S(2)}) collective-permute-start(bf16[128,1152]{1,0:T(8,128)(2,1)S(1)} %copy-done.1), channel_id=1, source_target_pairs={{0,128},{1,129},{2,130},{3,131},{4,132},{5,133},{6,134},{7,135},{8... | collective-permute-start | bytes 884744 | tf_op jit(solution)/shard_map/ppermute | solution.py:27
  10.9 0.7 collective-permute-start.9
  11.6 1.0 collective-permute-done.10
  12.6 11.0 %collective-permute-start.11 = (bf16[128,1152]{1,0:T(8,128)(2,1)S(1)}, bf16[128,1152]{1,0:T(8,128)(2,1)S(1)}, u32[]{:S(2)}, u32[]{:S(2)}) collective-permute-start(bf16[128,1152]{1,0:T(8,128)(2,1)S(1)} %get-tuple-element.73), channel_id=1, source_target_pairs={{0,64},{16,80},{32,96},{48,112},{64,0},{80,16},{96,32},{112,48},{1... | collective-permute-start | bytes 884744 | tf_op jit(solution)/shard_map/ppermute | solution.py:35
  23.6 4.5 %collective-permute-start.12 = (bf16[128,1152]{1,0:T(8,128)(2,1)S(1)}, bf16[128,1152]{1,0:T(8,128)(2,1)S(1)}, u32[]{:S(2)}, u32[]{:S(2)}) collective-permute-start(bf16[128,1152]{1,0:T(8,128)(2,1)S(1)} %get-tuple-element.74), channel_id=1, source_target_pairs={{0,96},{16,112},{32,0},{48,16},{64,32},{80,48},{96,64},{112,80},{1... | collective-permute-start | bytes 884744 | tf_op jit(solution)/shard_map/ppermute | solution.py:35
  28.1 0.0 collective-permute-done.7
  28.2 15.0 %collective-permute-start.8 = (bf16[128,1152]{1,0:T(8,128)(2,1)}, bf16[128,1152]{1,0:T(8,128)(2,1)S(1)}, u32[]{:S(2)}, u32[]{:S(2)}) collective-permute-start(bf16[128,1152]{1,0:T(8,128)(2,1)} %collective-permute-done.7), channel_id=1, source_target_pairs={{0,143},{1,128},{2,129},{3,130},{4,131},{5,132},{6,133},{7,134},{8... | collective-permute-start | bytes 884744 | tf_op jit(solution)/shard_map/ppermute | solution.py:27
  43.2 0.0 collective-permute-done.5
  43.2 4.2 %collective-permute-start.6 = (bf16[128,1152]{1,0:T(8,128)(2,1)}, bf16[128,1152]{1,0:T(8,128)(2,1)S(1)}, u32[]{:S(2)}, u32[]{:S(2)}) collective-permute-start(bf16[128,1152]{1,0:T(8,128)(2,1)} %collective-permute-done.5), channel_id=1, source_target_pairs={{0,896},{1,897},{2,898},{3,899},{4,900},{5,901},{6,902},{7,903},{8... | collective-permute-start | bytes 884744 | tf_op jit(solution)/shard_map/ppermute | solution.py:27
  48.7 0.1 stack.34
  48.8 0.0 collective-permute-done.9
  48.8 0.0 collective-permute-done.11
  48.8 0.0 collective-permute-done.12
  48.8 34.6 %conditional.1 = (f32[128,128]{1,0:T(8,128)}, f32[256,1152]{1,0:T(8,128)S(1)}, bf16[256,1152]{1,0:T(8,128)(2,1)}, f32[256,1]{1,0:T(8,128)}) conditional(s32[]{:T(128)} %convert_element_type.2, () %tuple.19, (s32[]{:T(128)}, s32[]{:T(128)}, bf16[128,1152]{1,0:T(8,128)(2,1)S(1)}, bf16[128,1152]{1,0:T(8,128)(2,1)}, bf16[128,1152]{1,0:T(8,128)(2,1)}, ...), branch_computations={%region_0.1_spmd, %region_1.2_spmd} | conditional | flops 1142931456 | bytes 45810188 | solution.py:216
  48.9 0.0 copy-start.2
  48.9 0.0 copy-start.4
  48.9 0.7 copy-done.8
  49.6 0.1 copy-done.2
  49.7 0.1 copy-done.4
  49.8 0.1 copy-done.6
  49.9 0.1 pad_maximum_fusion
  49.9 1.9 %collective-permute-start = (bf16[512,1152]{1,0:T(8,128)(2,1)S(1)}, bf16[512,1152]{1,0:T(8,128)(2,1)S(1)}, u32[]{:S(2)}, u32[]{:S(2)}) collective-permute-start(bf16[512,1152]{1,0:T(8,128)(2,1)S(1)} %pad_maximum_fusion), channel_id=1, source_target_pairs={{0,16},{16,0},{32,48},{48,32},{64,80},{80,64},{96,112},{112,96},{1... | collective-permute-start | bytes 3538952 | tf_op jit(solution)/shard_map/cond/branch_1_fun/ppermute | solution.py:45
  51.9 1.2 %broadcast_select_fusion.2 = (bf16[128,1152]{1,0:T(8,128)(2,1)S(1)}, bf16[128,1152]{1,0:T(8,128)(2,1)S(1)}, bf16[128,1152]{1,0:T(8,128)(2,1)S(1)}) fusion(pred[]{:T(512)S(6)} %eq.6, bf16[128,1152]{1,0:T(8,128)(2,1)} %copy-done.8, bf16[128,1152]{1,0:T(8,128)(2,1)} %get-tuple-element.43, pred[]{:T(512)S(6)} %lt.29, bf16[128,1152]{1,0:T(8,128)(2,1)} %get-tuple-element.42, ...), kind=kLoop, calls=%fused_computation.4 | loop fusion | flops 442368 | bytes 1769475 | tf_op jit(solution)/shard_map/cond/branch_1_fun/jit(_where)/select_n | solution.py:207
  53.1 0.0 copy-start.3
  53.1 0.0 copy-start.5
  53.2 0.1 broadcast_select_fusion
  53.3 5.1 %collective-permute-start.2 = (bf16[128,1152]{1,0:T(8,128)(2,1)S(1)}, bf16[128,1152]{1,0:T(8,128)(2,1)S(1)}, u32[]{:S(2)}, u32[]{:S(2)}) collective-permute-start(bf16[128,1152]{1,0:T(8,128)(2,1)S(1)} %get-tuple-element.87), channel_id=1, source_target_pairs={{0,64},{16,80},{32,96},{48,112},{64,0},{80,16},{96,32},{112,48},{1... | collective-permute-start | bytes 884744 | tf_op jit(solution)/shard_map/cond/branch_1_fun/ppermute | solution.py:35
  58.3 3.1 %collective-permute-start.1 = (bf16[128,1152]{1,0:T(8,128)(2,1)S(1)}, bf16[128,1152]{1,0:T(8,128)(2,1)S(1)}, u32[]{:S(2)}, u32[]{:S(2)}) collective-permute-start(bf16[128,1152]{1,0:T(8,128)(2,1)S(1)} %get-tuple-element.88), channel_id=1, source_target_pairs={{0,32},{16,48},{32,64},{48,80},{64,96},{80,112},{96,0},{112,16},{1... | collective-permute-start | bytes 884744 | tf_op jit(solution)/shard_map/cond/branch_1_fun/ppermute | solution.py:35
  61.4 0.0 collective-permute-done.rest_3_
  61.5 2.7 %collective-permute-start.3 = (bf16[128,1152]{1,0:T(8,128)(2,1)S(1)}, bf16[128,1152]{1,0:T(8,128)(2,1)S(1)}, u32[]{:S(2)}, u32[]{:S(2)}) collective-permute-start(bf16[128,1152]{1,0:T(8,128)(2,1)S(1)} %get-tuple-element.47), channel_id=1, source_target_pairs={{0,96},{16,112},{32,0},{48,16},{64,32},{80,48},{96,64},{112,80},{1... | collective-permute-start | bytes 884744 | tf_op jit(solution)/shard_map/cond/branch_1_fun/ppermute | solution.py:35
  64.2 4.7 %branch_1_fun.3 = (f32[128,128]{1,0:T(8,128)S(1)}, f32[256,1152]{1,0:T(8,128)S(1)}, bf16[256,1152]{1,0:T(8,128)(2,1)}, f32[256,1]{1,0:T(8,128)}) custom-call(f32[1]{0:T(128)} %get-tuple-element.30.scale, f32[1]{0:T(128)} %get-tuple-element.31.bias, s32[7]{0:T(128)S(1)} %get-tuple-element.32.roles, bf16[128,1152]{1,0:T(8,128)(2,1)S(1)} %get-tuple-element.33.x_ref, ...), custom_call_target="tpu_custom_call" | custom-call | flops 603979776 | bytes 8388608 | tf_op jit(solution)/shard_map/cond/branch_1_fun/pallas_call | solution.py:149
  68.9 0.0 collective-permute-done.2.rest_1_
  68.9 3.6 %collective-permute-done.1.rest_0_ = bf16[128,1152]{1,0:T(8,128)(2,1)S(1)} collective-permute-done((bf16[128,1152]{1,0:T(8,128)(2,1)S(1)}, bf16[128,1152]{1,0:T(8,128)(2,1)S(1)}, u32[]{:S(2)}, u32[]{:S(2)}) %collective-permute-start.1) | collective-permute-done | bytes 294944 | tf_op jit(solution)/shard_map/cond/branch_1_fun/ppermute | solution.py:35
  72.5 0.7 collective-permute-done.3.rest_2_
  73.2 0.1 pad_maximum_fusion.1
  73.3 1.9 %collective-permute-start.4 = (bf16[512,1152]{1,0:T(8,128)(2,1)S(1)}, bf16[512,1152]{1,0:T(8,128)(2,1)S(1)}, u32[]{:S(2)}, u32[]{:S(2)}) collective-permute-start(bf16[512,1152]{1,0:T(8,128)(2,1)S(1)} %pad_maximum_fusion.1), channel_id=1, source_target_pairs={{0,16},{16,0},{32,48},{48,32},{64,80},{80,64},{96,112},{112,96},{1... | collective-permute-start | bytes 3538952 | tf_op jit(solution)/shard_map/cond/branch_1_fun/ppermute | solution.py:45
  75.2 4.0 %branch_1_fun.4 = (f32[128,128]{1,0:T(8,128)S(1)}, f32[256,1152]{1,0:T(8,128)S(1)}) custom-call(f32[1]{0:T(128)} %get-tuple-element.30.scale, f32[1]{0:T(128)} %get-tuple-element.31.bias, s32[7]{0:T(128)S(1)} %get-tuple-element.32.roles, bf16[256,1152]{1,0:T(8,128)(2,1)} %get-tuple-element.100.units_ref, f32[128,128]{1,0:T(8,128)S(1)} %get-tuple-element.49.loss_in, ...), custom_call_target="tpu_custom_call" | custom-call | flops 226492416 | bytes 3145728 | tf_op jit(solution)/shard_map/cond/branch_1_fun/pallas_call | solution.py:149
  79.2 0.0 collective-permute-done.4.rest_0_
  79.2 4.3 %branch_1_fun.5 = (f32[128,128]{1,0:T(8,128)}, f32[256,1152]{1,0:T(8,128)S(1)}) custom-call(f32[1]{0:T(128)} %get-tuple-element.30.scale, f32[1]{0:T(128)} %get-tuple-element.31.bias, s32[7]{0:T(128)S(1)} %get-tuple-element.32.roles, bf16[256,1152]{1,0:T(8,128)(2,1)} %get-tuple-element.100.units_ref, f32[128,128]{1,0:T(8,128)S(1)} %get-tuple-element.54.loss_in, ...), custom_call_target="tpu_custom_call" | custom-call | flops 301989888 | bytes 4194304 | tf_op jit(solution)/shard_map/cond/branch_1_fun/pallas_call | solution.py:149
  83.5 0.0 collective-permute-done.8.xg_ref
  83.5 16.8 %collective-permute-done.6.yg_ref = bf16[128,1152]{1,0:T(8,128)(2,1)S(1)} collective-permute-done((bf16[128,1152]{1,0:T(8,128)(2,1)}, bf16[128,1152]{1,0:T(8,128)(2,1)S(1)}, u32[]{:S(2)}, u32[]{:S(2)}) %collective-permute-start.6) | collective-permute-done | bytes 294944 | tf_op jit(solution)/shard_map/ppermute | solution.py:27
  100.3 3.3 %shard_map.77 = (f32[1,128]{1,0:T(1,128)}, f32[128,1152]{1,0:T(8,128)}, f32[128,1152]{1,0:T(8,128)}) custom-call(f32[1]{0:T(128)S(6)} %copy.17.scale, f32[1]{0:T(128)S(6)} %copy.18.bias, bf16[128,1152]{1,0:T(8,128)(2,1)S(1)} %copy-done, bf16[128,1152]{1,0:T(8,128)(2,1)S(1)} %copy-done.1, bf16[128,1152]{1,0:T(8,128)(2,1)S(1)} %collective-permute-done.6.yg_ref, ...), custom_call_target="tpu_custom_call" | custom-call | flops 150994944 | bytes 2097152 | tf_op jit(solution)/shard_map/pallas_call | solution.py:149
  (10 shorter events, 0.1 us)
Async XLA Ops:
  0.6 6.5 %copy-start.1 = (bf16[128,1152]{1,0:T(8,128)(2,1)S(1)}, bf16[128,1152]{1,0:T(8,128)(2,1)}, u32[]{:S(2)}) copy-start(bf16[128,1152]{1,0:T(8,128)(2,1)} %y_ref.1) | copy-start | bytes 884740
  0.6 4.4 %copy-start = (bf16[128,1152]{1,0:T(8,128)(2,1)S(1)}, bf16[128,1152]{1,0:T(8,128)(2,1)}, u32[]{:S(2)}) copy-start(bf16[128,1152]{1,0:T(8,128)(2,1)} %x_ref.1) | copy-start | bytes 884740
  0.7 48.2 %copy-start.9 = (s32[1,128]{1,0:T(1,128)S(1)}, s32[1,128]{1,0:T(1,128)}, u32[]{:S(2)}) copy-start(s32[1,128]{1,0:T(1,128)} %param.9) | copy-start | bytes 1540
  1.9 10.6 %collective-permute-start.10 = (bf16[128,1152]{1,0:T(8,128)(2,1)S(1)}, bf16[128,1152]{1,0:T(8,128)(2,1)S(1)}, u32[]{:S(2)}, u32[]{:S(2)}) collective-permute-start(bf16[128,1152]{1,0:T(8,128)(2,1)S(1)} %get-tuple-element.90), channel_id=1, source_target_pairs={{0,32},{16,48},{32,64},{48,80},{64,96},{80,112},{96,0},{112,16},{1... | collective-permute-start | bytes 884744 | tf_op jit(solution)/shard_map/ppermute | solution.py:35
  5.1 23.1 %collective-permute-start.7 = (bf16[128,1152]{1,0:T(8,128)(2,1)S(1)}, bf16[128,1152]{1,0:T(8,128)(2,1)}, u32[]{:S(2)}, u32[]{:S(2)}) collective-permute-start(bf16[128,1152]{1,0:T(8,128)(2,1)S(1)} %copy-done), channel_id=1, source_target_pairs={{0,911},{1,896},{2,897},{3,898},{4,899},{5,900},{6,901},{7,902},{8... | collective-permute-start | bytes 884744 | tf_op jit(solution)/shard_map/ppermute | solution.py:27
  7.1 36.1 %collective-permute-start.5 = (bf16[128,1152]{1,0:T(8,128)(2,1)S(1)}, bf16[128,1152]{1,0:T(8,128)(2,1)}, u32[]{:S(2)}, u32[]{:S(2)}) collective-permute-start(bf16[128,1152]{1,0:T(8,128)(2,1)S(1)} %copy-done.1), channel_id=1, source_target_pairs={{0,128},{1,129},{2,130},{3,131},{4,132},{5,133},{6,134},{7,135},{8... | collective-permute-start | bytes 884744 | tf_op jit(solution)/shard_map/ppermute | solution.py:27
  10.9 37.9 %collective-permute-start.9 = (bf16[128,1152]{1,0:T(8,128)(2,1)S(1)}, bf16[128,1152]{1,0:T(8,128)(2,1)S(1)}, u32[]{:S(2)}, u32[]{:S(2)}) collective-permute-start(bf16[128,1152]{1,0:T(8,128)(2,1)S(1)} %get-tuple-element.93), channel_id=1, source_target_pairs={{896,0},{912,16},{928,32},{944,48},{960,64},{976,80},{992,96},{100... | collective-permute-start | bytes 884744 | tf_op jit(solution)/shard_map/ppermute | solution.py:41
  12.6 36.2 %collective-permute-start.11 = (bf16[128,1152]{1,0:T(8,128)(2,1)S(1)}, bf16[128,1152]{1,0:T(8,128)(2,1)S(1)}, u32[]{:S(2)}, u32[]{:S(2)}) collective-permute-start(bf16[128,1152]{1,0:T(8,128)(2,1)S(1)} %get-tuple-element.73), channel_id=1, source_target_pairs={{0,64},{16,80},{32,96},{48,112},{64,0},{80,16},{96,32},{112,48},{1... | collective-permute-start | bytes 884744 | tf_op jit(solution)/shard_map/ppermute | solution.py:35
  23.6 25.2 %collective-permute-start.12 = (bf16[128,1152]{1,0:T(8,128)(2,1)S(1)}, bf16[128,1152]{1,0:T(8,128)(2,1)S(1)}, u32[]{:S(2)}, u32[]{:S(2)}) collective-permute-start(bf16[128,1152]{1,0:T(8,128)(2,1)S(1)} %get-tuple-element.74), channel_id=1, source_target_pairs={{0,96},{16,112},{32,0},{48,16},{64,32},{80,48},{96,64},{112,80},{1... | collective-permute-start | bytes 884744 | tf_op jit(solution)/shard_map/ppermute | solution.py:35
  28.2 55.3 %collective-permute-start.8 = (bf16[128,1152]{1,0:T(8,128)(2,1)}, bf16[128,1152]{1,0:T(8,128)(2,1)S(1)}, u32[]{:S(2)}, u32[]{:S(2)}) collective-permute-start(bf16[128,1152]{1,0:T(8,128)(2,1)} %collective-permute-done.7), channel_id=1, source_target_pairs={{0,143},{1,128},{2,129},{3,130},{4,131},{5,132},{6,133},{7,134},{8... | collective-permute-start | bytes 884744 | tf_op jit(solution)/shard_map/ppermute | solution.py:27
  43.2 57.1 %collective-permute-start.6 = (bf16[128,1152]{1,0:T(8,128)(2,1)}, bf16[128,1152]{1,0:T(8,128)(2,1)S(1)}, u32[]{:S(2)}, u32[]{:S(2)}) collective-permute-start(bf16[128,1152]{1,0:T(8,128)(2,1)} %collective-permute-done.5), channel_id=1, source_target_pairs={{0,896},{1,897},{2,898},{3,899},{4,900},{5,901},{6,902},{7,903},{8... | collective-permute-start | bytes 884744 | tf_op jit(solution)/shard_map/ppermute | solution.py:27
  48.9 0.7 copy-start.8
  48.9 0.8 copy-start.2
  48.9 0.9 copy-start.4
  48.9 1.0 copy-start.6
  49.9 11.5 %collective-permute-start = (bf16[512,1152]{1,0:T(8,128)(2,1)S(1)}, bf16[512,1152]{1,0:T(8,128)(2,1)S(1)}, u32[]{:S(2)}, u32[]{:S(2)}) collective-permute-start(bf16[512,1152]{1,0:T(8,128)(2,1)S(1)} %pad_maximum_fusion), channel_id=1, source_target_pairs={{0,16},{16,0},{32,48},{48,32},{64,80},{80,64},{96,112},{112,96},{1... | collective-permute-start | bytes 3538952 | tf_op jit(solution)/shard_map/cond/branch_1_fun/ppermute | solution.py:45
  53.1 11.1 %copy-start.3 = (bf16[128,1152]{1,0:T(8,128)(2,1)S(1)}, bf16[128,1152]{1,0:T(8,128)(2,1)}, u32[]{:S(2)}) copy-start(bf16[128,1152]{1,0:T(8,128)(2,1)} %copy-done.2) | copy-start | bytes 884740 | tf_op jit(solution)/shard_map/cond
  53.1 11.1 %copy-start.5 = (bf16[128,1152]{1,0:T(8,128)(2,1)S(1)}, bf16[128,1152]{1,0:T(8,128)(2,1)}, u32[]{:S(2)}) copy-start(bf16[128,1152]{1,0:T(8,128)(2,1)} %copy-done.4) | copy-start | bytes 884740 | tf_op jit(solution)/shard_map/cond
  53.1 11.1 %copy-start.7 = (bf16[128,1152]{1,0:T(8,128)(2,1)S(1)}, bf16[128,1152]{1,0:T(8,128)(2,1)}, u32[]{:S(2)}) copy-start(bf16[128,1152]{1,0:T(8,128)(2,1)} %copy-done.6) | copy-start | bytes 884740 | tf_op jit(solution)/shard_map/cond
  53.3 15.7 %collective-permute-start.2 = (bf16[128,1152]{1,0:T(8,128)(2,1)S(1)}, bf16[128,1152]{1,0:T(8,128)(2,1)S(1)}, u32[]{:S(2)}, u32[]{:S(2)}) collective-permute-start(bf16[128,1152]{1,0:T(8,128)(2,1)S(1)} %get-tuple-element.87), channel_id=1, source_target_pairs={{0,64},{16,80},{32,96},{48,112},{64,0},{80,16},{96,32},{112,48},{1... | collective-permute-start | bytes 884744 | tf_op jit(solution)/shard_map/cond/branch_1_fun/ppermute | solution.py:35
  58.3 14.2 %collective-permute-start.1 = (bf16[128,1152]{1,0:T(8,128)(2,1)S(1)}, bf16[128,1152]{1,0:T(8,128)(2,1)S(1)}, u32[]{:S(2)}, u32[]{:S(2)}) collective-permute-start(bf16[128,1152]{1,0:T(8,128)(2,1)S(1)} %get-tuple-element.88), channel_id=1, source_target_pairs={{0,32},{16,48},{32,64},{48,80},{64,96},{80,112},{96,0},{112,16},{1... | collective-permute-start | bytes 884744 | tf_op jit(solution)/shard_map/cond/branch_1_fun/ppermute | solution.py:35
  61.5 11.8 %collective-permute-start.3 = (bf16[128,1152]{1,0:T(8,128)(2,1)S(1)}, bf16[128,1152]{1,0:T(8,128)(2,1)S(1)}, u32[]{:S(2)}, u32[]{:S(2)}) collective-permute-start(bf16[128,1152]{1,0:T(8,128)(2,1)S(1)} %get-tuple-element.47), channel_id=1, source_target_pairs={{0,96},{16,112},{32,0},{48,16},{64,32},{80,48},{96,64},{112,80},{1... | collective-permute-start | bytes 884744 | tf_op jit(solution)/shard_map/cond/branch_1_fun/ppermute | solution.py:35
  73.3 5.9 %collective-permute-start.4 = (bf16[512,1152]{1,0:T(8,128)(2,1)S(1)}, bf16[512,1152]{1,0:T(8,128)(2,1)S(1)}, u32[]{:S(2)}, u32[]{:S(2)}) collective-permute-start(bf16[512,1152]{1,0:T(8,128)(2,1)S(1)} %pad_maximum_fusion.1), channel_id=1, source_target_pairs={{0,16},{16,0},{32,48},{48,32},{64,80},{80,64},{96,112},{112,96},{1... | collective-permute-start | bytes 3538952 | tf_op jit(solution)/shard_map/cond/branch_1_fun/ppermute | solution.py:45

commit v12 on v11

--- a/solution.py
+++ b/solution.py
@@ -115,7 +115,8 @@
     loss_ref[...] = loss
     grads_ref[:rows, :] = by_cols(slope, y)
     grads_ref[rows:, :] = product(slope, x)
-    add_blocks([roles[i] for i in range(2 * CHIPS - 1)], refs, tau, offset, units, loss_ref, grads_ref, stack_ref)
+    count = stack_ref.shape[0] // rows
+    add_blocks([roles[i] for i in range(count)], refs, tau, offset, units, loss_ref, grads_ref, stack_ref)
 
 
 def next_kernel(first, scale, bias, roles, units_ref, loss_in, grads_in, *rest):
@@ -123,25 +124,32 @@
     loss_ref[...] = loss_in[...]
     grads_ref[...] = grads_in[...]
     count = stack_ref.shape[0] * 2 // units_ref.shape[0]
-    flipped = [1 - roles[first + i] for i in range(count)]
-    add_blocks(flipped, refs, scale[0], bias[0], units_ref[...], loss_ref, grads_ref, stack_ref)
-
-
-def last_kernel(
-    scale, bias, x_ref, y_ref, yg_ref, xg_ref, units_ref, inverses_ref, loss_in, grads_in, loss_ref, ix_ref, ty_ref
-):
-    tau, offset = scale[0], bias[0]
+    add_blocks([roles[first + i] for i in range(count)], refs, scale[0], bias[0], units_ref[...], loss_ref, grads_ref, stack_ref)
+
+
+def outer_grad(tau, offset, feats_ref, other_ref, unit, inverse, before):
+    other = unit_rows(other_ref[...])
+    loss, slope = loss_and_slope(tau * by_rows(other, unit) + offset)
+    grad = (before + by_cols(slope.astype(BF16), other)) * tau
+    norm = feats_ref[...].astype(F32) * inverse
+    return loss, (grad - norm * jnp.sum(norm * grad, axis=-1, keepdims=True)) * inverse
+
+
+def image_kernel(scale, bias, x_ref, other_ref, units_ref, inverses_ref, loss_in, grads_in, loss_ref, out_ref):
     rows = x_ref.shape[0]
-    for i, (feats_ref, other_ref, out_ref) in enumerate(((x_ref, yg_ref, ix_ref), (y_ref, xg_ref, ty_ref))):
-        own = slice(i * rows, (i + 1) * rows)
-        other = unit_rows(other_ref[...])
-        loss, slope = loss_and_slope(tau * by_rows(other, units_ref[own, :]) + offset)
-        if i == TEXT:
-            loss_ref[...] = jnp.sum(loss_in[...] + loss, axis=0, keepdims=True) / F32((SPAN + 1) * rows)
-        grad = (grads_in[own, :] + by_cols(slope.astype(BF16), other)) * tau
-        inverse = inverses_ref[own, :]
-        norm = feats_ref[...].astype(F32) * inverse
-        out_ref[...] = (grad - norm * jnp.sum(norm * grad, axis=-1, keepdims=True)) * inverse
+    own = slice(0, rows)
+    loss, out_ref[...] = outer_grad(
+        scale[0], bias[0], x_ref, other_ref, units_ref[own, :], inverses_ref[own, :], grads_in[own, :]
+    )
+    loss_ref[...] = jnp.sum(loss_in[...] + loss, axis=0, keepdims=True) / F32((SPAN + 1) * rows)
+
+
+def text_kernel(scale, bias, y_ref, other_ref, units_ref, inverses_ref, grads_in, out_ref):
+    rows = y_ref.shape[0]
+    own = slice(rows, 2 * rows)
+    _, out_ref[...] = outer_grad(
+        scale[0], bias[0], y_ref, other_ref, units_ref[own, :], inverses_ref[own, :], grads_in[own, :]
+    )
 
 
 def call(kernel, outs, blocks, scalars, *args, scratch=()):
@@ -171,16 +179,16 @@
     y_back = along_ring(y, 1)
     x_next = along_ring(x, -1)
     first = [jnp.where(chip + by < CHIPS, y, x) for by in shifts]
-    near = in_row(first[0], 1)
-    first[1], first[2], near = lax.optimization_barrier((first[1], first[2], near))
-    middle, far = in_row(first[1], 2), in_row(first[2], 3)
+    near, far = in_row(first[0], 1), in_row(first[2], 3)
     y_outer = along_ring(y_back, length - 1)
     x_outer = along_ring(x_next, 1 - length)
     double = 2 * rows
     loss_out, grads_out = ((rows, rows), F32), ((double, width), F32)
     units_out, inverses_out = ((double, width), BF16), ((double, 1), F32)
     near_role, middle_role, far_role = [(chip < by).astype(jnp.int32) for by in shifts]
-    roles = jnp.stack([near_role, middle_role, far_role, 1 - core, near_role, middle_role, far_role])
+    early = [near_role, far_role, 1 - core, near_role, far_role]
+    late = [middle_role, 1 - middle_role, 1 - near_role, 1 - far_role, core]
+    roles = jnp.stack(early + late + late[:-1])
 
     def stack(blocks):
         return [pltpu.VMEM((blocks * rows, width), BF16)]
@@ -195,18 +203,17 @@
         text = jnp.where(index < SPAN, wrapped, y_back)
         image = jnp.where(index >= last, wrapped, x_next)
         then = [jnp.where(chip + by < CHIPS, image, text) for by in shifts]
-        got = [near, middle, far]
-        twin = to_twin(jnp.concatenate([jnp.where(core == 0, y, x)] + got, axis=0))
+        twin = to_twin(jnp.concatenate([jnp.where(core == 0, y, x), near, far], axis=0))
         then[2], twin = lax.optimization_barrier((then[2], twin))
-        later = [in_row(block, by) for by, block in zip(shifts, then)]
+        later = [in_row(jnp.concatenate([first[1], then[1]], axis=0), 2), in_row(then[0], 1), in_row(then[2], 3)]
         loss, grads, units, inverses = call(
-            first_kernel, [loss_out, grads_out, units_out, inverses_out], 8,
-            (scale, bias, roles), x, y, positive, *got, twin, scratch=stack(2 * CHIPS - 1),
+            first_kernel, [loss_out, grads_out, units_out, inverses_out], 6,
+            (scale, bias, roles), x, y, positive, near, far, twin, scratch=stack(5),
         )
         *later, loss = lax.optimization_barrier((*later, loss))
         twin = to_twin(jnp.concatenate([jnp.where(core == 0, image, text)] + later, axis=0))
-        loss, grads = more(0, len(later), later, units, loss, grads)
-        loss, grads = more(len(later), CHIPS, [twin], units, loss, grads)
+        loss, grads = more(5, 4, later, units, loss, grads)
+        loss, grads = more(9, 5, [twin], units, loss, grads)
         return loss, grads, units, inverses
 
     def skip(_):
@@ -215,10 +222,10 @@
     go = lax.optimization_barrier(jnp.int32(1))
     loss, grads, units, inverses = lax.cond(go > 0, inner, skip, 0)
     block = ((rows, width), F32)
-    loss, image_grad, text_grad = call(
-        last_kernel, [((1, rows), F32), block, block], 2, (scale, bias),
-        x, y, y_outer, x_outer, units, inverses, loss, grads,
-    )
+    loss, image_grad = call(
+        image_kernel, [((1, rows), F32), block], 1, (scale, bias), x, y_outer, units, inverses, loss, grads
+    )
+    (text_grad,) = call(text_kernel, [block], 1, (scale, bias), y, x_outer, units, inverses, grads)
     return (loss[0], image_grad, text_grad)
 
 

time: 104 us -> 123 us (1.18)
  the two profiles are of different devices: /device:TPU:36 before, /device:TPU:25 now
where the time goes in v12:
time: 123 us; the launch traced here: 122 us
  starting transfers between devices  76.6 us (62%)
  waiting for transfers between devices  19.6 us (16%)
  Pallas kernels  18.6 us (15%)
  other arithmetic  5.25 us (4%)
  between operations  2.13 us (2%)
    ppermute x5, starting transfers between devices, in_row(): return lax.ppermute(x, 'blk', pairs)  34.2 us
    ppermute x4, starting transfers between devices, along_ring(): return lax.ppermute(x, ('blk', 'group'), pairs)  32.5 us
    pallas_call x5, Pallas kernels, call(): pl.pallas_call(kernel, out_shape=[jax.ShapeDtypeStruct(shape, kind) for s...  18.6 us
    ppermute x1, waiting for transfers between devices, around(): return lax.ppermute(x, 'blk', pairs)  10.1 us
    ppermute x5, waiting for transfers between devices, in_row(): return lax.ppermute(x, 'blk', pairs)  9.46 us
    ppermute x2, starting transfers between devices, to_twin(): lax.ppermute(x, 'blk', [(i, i ^ 1) for i in range(lax.axis_size('blk'))])  8.01 us
    select_n x2, other arithmetic, local(): first = [jnp.where(chip + by < CHIPS, y, x) for by in shifts]  3.05 us
  transfers between devices with their start and end apart: 12, of which 2 were waited for; matrix products, arithmetic and copies ran while one was open for 4% of the time, Pallas kernels for 13%

profile of v12, /device:TPU:25, one launch (start us, length us, event | category | flops | bytes accessed | tf_op | source)
XLA Modules:
  0.0 122.4 jit_solution(13671864764100908389)
XLA Ops:
  0.6 0.0 copy-start.1
  0.6 0.0 copy-start
  0.7 0.0 copy-start.4
  0.7 3.7 %collective-permute-start.5 = (bf16[128,1152]{1,0:T(8,128)(2,1)}, bf16[128,1152]{1,0:T(8,128)(2,1)}, u32[]{:S(2)}, u32[]{:S(2)}) collective-permute-start(bf16[128,1152]{1,0:T(8,128)(2,1)} %y_ref.1), channel_id=1, source_target_pairs={{0,128},{1,129},{2,130},{3,131},{4,132},{5,133},{6,134},{7,135},{8... | collective-permute-start | bytes 884744 | tf_op jit(solution)/shard_map/ppermute | solution.py:27
  4.3 17.0 %collective-permute-start.8 = (bf16[128,1152]{1,0:T(8,128)(2,1)}, bf16[128,1152]{1,0:T(8,128)(2,1)}, u32[]{:S(2)}, u32[]{:S(2)}) collective-permute-start(bf16[128,1152]{1,0:T(8,128)(2,1)} %x_ref.1), channel_id=1, source_target_pairs={{0,911},{1,896},{2,897},{3,898},{4,899},{5,900},{6,901},{7,902},{8... | collective-permute-start | bytes 884744 | tf_op jit(solution)/shard_map/ppermute | solution.py:27
  21.4 1.1 broadcast_select_fusion.8
  22.5 1.9 %collective-permute-start.7 = (bf16[128,1152]{1,0:T(8,128)(2,1)S(1)}, bf16[128,1152]{1,0:T(8,128)(2,1)S(1)}, u32[]{:S(2)}, u32[]{:S(2)}) collective-permute-start(bf16[128,1152]{1,0:T(8,128)(2,1)S(1)} %get-tuple-element.95), channel_id=1, source_target_pairs={{896,0},{912,16},{928,32},{944,48},{960,64},{976,80},{992,96},{100... | collective-permute-start | bytes 884744 | tf_op jit(solution)/shard_map/ppermute | solution.py:41
  24.4 3.1 %collective-permute-start.9 = (bf16[128,1152]{1,0:T(8,128)(2,1)S(1)}, bf16[128,1152]{1,0:T(8,128)(2,1)S(1)}, u32[]{:S(2)}, u32[]{:S(2)}) collective-permute-start(bf16[128,1152]{1,0:T(8,128)(2,1)S(1)} %get-tuple-element.94), channel_id=1, source_target_pairs={{0,32},{16,48},{32,64},{48,80},{64,96},{80,112},{96,0},{112,16},{1... | collective-permute-start | bytes 884744 | tf_op jit(solution)/shard_map/ppermute | solution.py:35
  27.5 3.4 %collective-permute-start.10 = (bf16[128,1152]{1,0:T(8,128)(2,1)S(1)}, bf16[128,1152]{1,0:T(8,128)(2,1)S(1)}, u32[]{:S(2)}, u32[]{:S(2)}) collective-permute-start(bf16[128,1152]{1,0:T(8,128)(2,1)S(1)} %get-tuple-element.93), channel_id=1, source_target_pairs={{0,96},{16,112},{32,0},{48,16},{64,32},{80,48},{96,64},{112,80},{1... | collective-permute-start | bytes 884744 | tf_op jit(solution)/shard_map/ppermute | solution.py:35
  30.9 0.0 collective-permute-done.8
  30.9 6.0 %collective-permute-start.11 = (bf16[128,1152]{1,0:T(8,128)(2,1)}, bf16[128,1152]{1,0:T(8,128)(2,1)S(1)}, u32[]{:S(2)}, u32[]{:S(2)}) collective-permute-start(bf16[128,1152]{1,0:T(8,128)(2,1)} %collective-permute-done.8), channel_id=1, source_target_pairs={{0,143},{1,128},{2,129},{3,130},{4,131},{5,132},{6,133},{7,134},{8... | collective-permute-start | bytes 884744 | tf_op jit(solution)/shard_map/ppermute | solution.py:27
  36.9 0.0 collective-permute-done.5
  37.0 5.9 %collective-permute-start.6 = (bf16[128,1152]{1,0:T(8,128)(2,1)}, bf16[128,1152]{1,0:T(8,128)(2,1)S(1)}, u32[]{:S(2)}, u32[]{:S(2)}) collective-permute-start(bf16[128,1152]{1,0:T(8,128)(2,1)} %collective-permute-done.5), channel_id=1, source_target_pairs={{0,896},{1,897},{2,898},{3,899},{4,900},{5,901},{6,902},{7,903},{8... | collective-permute-start | bytes 884744 | tf_op jit(solution)/shard_map/ppermute | solution.py:27
  44.2 0.1 stack.41
  44.3 10.1 %collective-permute-done.7 = bf16[128,1152]{1,0:T(8,128)(2,1)S(1)} collective-permute-done((bf16[128,1152]{1,0:T(8,128)(2,1)S(1)}, bf16[128,1152]{1,0:T(8,128)(2,1)S(1)}, u32[]{:S(2)}, u32[]{:S(2)}) %collective-permute-start.7) | collective-permute-done | bytes 294944 | tf_op jit(solution)/shard_map/ppermute | solution.py:41
  54.4 0.0 collective-permute-done.9
  54.4 0.0 collective-permute-done.10
  54.4 0.0 copy-done.1
  54.4 0.0 copy-done
  54.4 0.0 copy-done.4
  54.4 62.5 %conditional.1 = (f32[128,128]{1,0:T(8,128)}, f32[256,1152]{1,0:T(8,128)S(1)}, bf16[256,1152]{1,0:T(8,128)(2,1)}, f32[256,1]{1,0:T(8,128)}) conditional(s32[]{:T(128)} %convert_element_type.12, () %tuple.18, (s32[]{:T(128)}, s32[]{:T(128)}, bf16[128,1152]{1,0:T(8,128)(2,1)S(1)}, bf16[128,1152]{1,0:T(8,128)(2,1)}, bf16[128,1152]{1,0:T(8,128)(2,1)}, ...), branch_computations={%region_0.1_spmd, %region_1.2_spmd} | conditional | flops 1143373824 | bytes 42566016 | solution.py:223
  54.4 0.0 copy-start.2
  54.4 1.9 %broadcast_select_fusion.2 = (bf16[128,1152]{1,0:T(8,128)(2,1)S(1)}, bf16[128,1152]{1,0:T(8,128)(2,1)S(1)}, bf16[128,1152]{1,0:T(8,128)(2,1)S(1)}, bf16[128,1152]{1,0:T(8,128)(2,1)S(1)}, bf16[128,1152]{1,0:T(8,128)(2,1)}) fusion(bf16[128,1152]{1,0:T(8,128)(2,1)S(1)} %get-tuple-element.41.y_ref, bf16[128,1152]{1,0:T(8,128)(2,1)S(1)} %get-tuple-element.40.x_ref, ...), kind=kLoop, calls=%fused_computation.5 | loop fusion | flops 737280 | bytes 2949124 | tf_op jit(solution)/shard_map/jit(_where)/select_n | solution.py:181
  56.4 0.0 copy-done.2
  56.4 1.0 pad_maximum_fusion.1
  57.4 0.0 copy-start.3
  57.4 5.3 %collective-permute-start = (bf16[384,1152]{1,0:T(8,128)(2,1)}, bf16[384,1152]{1,0:T(8,128)(2,1)S(1)}, u32[]{:S(2)}, u32[]{:S(2)}) collective-permute-start(bf16[384,1152]{1,0:T(8,128)(2,1)} %pad_maximum_fusion.1), channel_id=1, source_target_pairs={{0,16},{16,0},{32,48},{48,32},{64,80},{80,64},{96,112},{112,96},{1... | collective-permute-start | bytes 2654216 | tf_op jit(solution)/shard_map/cond/branch_1_fun/ppermute | solution.py:45
  62.7 1.0 broadcast_select_fusion
  63.8 21.2 %collective-permute-start.1 = (bf16[256,1152]{1,0:T(8,128)(2,1)S(1)}, bf16[256,1152]{1,0:T(8,128)(2,1)S(1)}, u32[]{:S(2)}, u32[]{:S(2)}) collective-permute-start(bf16[256,1152]{1,0:T(8,128)(2,1)S(1)} %pad_maximum_fusion.2), channel_id=1, source_target_pairs={{0,64},{16,80},{32,96},{48,112},{64,0},{80,16},{96,32},{112,48},{1... | collective-permute-start | bytes 1769480 | tf_op jit(solution)/shard_map/cond/branch_1_fun/ppermute | solution.py:35
  85.0 2.2 %collective-permute-start.2 = (bf16[128,1152]{1,0:T(8,128)(2,1)S(1)}, bf16[128,1152]{1,0:T(8,128)(2,1)S(1)}, u32[]{:S(2)}, u32[]{:S(2)}) collective-permute-start(bf16[128,1152]{1,0:T(8,128)(2,1)S(1)} %get-tuple-element.85), channel_id=1, source_target_pairs={{0,32},{16,48},{32,64},{48,80},{64,96},{80,112},{96,0},{112,16},{1... | collective-permute-start | bytes 884744 | tf_op jit(solution)/shard_map/cond/branch_1_fun/ppermute | solution.py:35
  87.2 0.0 collective-permute-done.rest_2_
  87.2 4.3 %collective-permute-start.3 = (bf16[128,1152]{1,0:T(8,128)(2,1)S(1)}, bf16[128,1152]{1,0:T(8,128)(2,1)S(1)}, u32[]{:S(2)}, u32[]{:S(2)}) collective-permute-start(bf16[128,1152]{1,0:T(8,128)(2,1)S(1)} %get-tuple-element.53), channel_id=1, source_target_pairs={{0,96},{16,112},{32,0},{48,16},{64,32},{80,48},{96,64},{112,80},{1... | collective-permute-start | bytes 884744 | tf_op jit(solution)/shard_map/cond/branch_1_fun/ppermute | solution.py:35
  91.5 0.0 copy-done.3
  91.5 4.1 %branch_1_fun.3 = (f32[128,128]{1,0:T(8,128)S(1)}, f32[256,1152]{1,0:T(8,128)S(1)}, bf16[256,1152]{1,0:T(8,128)(2,1)}, f32[256,1]{1,0:T(8,128)}) custom-call(f32[1]{0:T(128)} %get-tuple-element.37.scale, f32[1]{0:T(128)} %get-tuple-element.38.bias, s32[14]{0:T(128)S(1)} %get-tuple-element.39.roles, bf16[128,1152]{1,0:T(8,128)(2,1)S(1)} %get-tuple-element.40.x_ref, ...), custom_call_target="tpu_custom_call" | custom-call | flops 452984832 | bytes 6291456 | tf_op jit(solution)/shard_map/cond/branch_1_fun/pallas_call | solution.py:157
  95.7 9.4 %collective-permute-done.2.rest_1_ = bf16[128,1152]{1,0:T(8,128)(2,1)S(1)} collective-permute-done((bf16[128,1152]{1,0:T(8,128)(2,1)S(1)}, bf16[128,1152]{1,0:T(8,128)(2,1)S(1)}, u32[]{:S(2)}, u32[]{:S(2)}) %collective-permute-start.2) | collective-permute-done | bytes 294944 | tf_op jit(solution)/shard_map/cond/branch_1_fun/ppermute | solution.py:35
  105.1 0.0 collective-permute-done.1.rest_0_
  105.1 0.0 collective-permute-done.3.rest_2_
  105.1 0.1 pad_maximum_fusion
  105.2 2.7 %collective-permute-start.4 = (bf16[640,1152]{1,0:T(8,128)(2,1)S(1)}, bf16[640,1152]{1,0:T(8,128)(2,1)S(1)}, u32[]{:S(2)}, u32[]{:S(2)}) collective-permute-start(bf16[640,1152]{1,0:T(8,128)(2,1)S(1)} %pad_maximum_fusion), channel_id=1, source_target_pairs={{0,16},{16,0},{32,48},{48,32},{64,80},{80,64},{96,112},{112,96},{1... | collective-permute-start | bytes 4423688 | tf_op jit(solution)/shard_map/cond/branch_1_fun/ppermute | solution.py:45
  107.9 4.3 %branch_1_fun.4 = (f32[128,128]{1,0:T(8,128)S(1)}, f32[256,1152]{1,0:T(8,128)S(1)}) custom-call(f32[1]{0:T(128)} %get-tuple-element.37.scale, f32[1]{0:T(128)} %get-tuple-element.38.bias, s32[14]{0:T(128)S(1)} %get-tuple-element.39.roles, bf16[256,1152]{1,0:T(8,128)(2,1)} %get-tuple-element.102.units_ref, f32[128,128]{1,0:T(8,128)S(1)} %get-tuple-element.55.loss_in, ...), custom_call_target="tpu_custom_call" | custom-call | flops 301989888 | bytes 4194304 | tf_op jit(solution)/shard_map/cond/branch_1_fun/pallas_call | solution.py:157
  112.2 0.0 collective-permute-done.4.rest_0_
  112.2 4.7 %branch_1_fun.5 = (f32[128,128]{1,0:T(8,128)}, f32[256,1152]{1,0:T(8,128)S(1)}) custom-call(f32[1]{0:T(128)} %get-tuple-element.37.scale, f32[1]{0:T(128)} %get-tuple-element.38.bias, s32[14]{0:T(128)S(1)} %get-tuple-element.39.roles, bf16[256,1152]{1,0:T(8,128)(2,1)} %get-tuple-element.102.units_ref, f32[128,128]{1,0:T(8,128)S(1)} %get-tuple-element.60.loss_in, ...), custom_call_target="tpu_custom_call" | custom-call | flops 377487360 | bytes 5242880 | tf_op jit(solution)/shard_map/cond/branch_1_fun/pallas_call | solution.py:157
  116.9 0.0 collective-permute-done.11.other_ref
  117.0 2.7 %shard_map.78 = f32[128,1152]{1,0:T(8,128)} custom-call(f32[1]{0:T(128)S(6)} %copy.17.scale, f32[1]{0:T(128)S(6)} %copy.18.bias, bf16[128,1152]{1,0:T(8,128)(2,1)S(1)} %copy-done.1, bf16[128,1152]{1,0:T(8,128)(2,1)S(1)} %collective-permute-done.11.other_ref, bf16[256,1152]{1,0:T(8,128)(2,1)} %get-tuple-element.74.units_ref, ...), custom_call_target="tpu_custom_call" | custom-call | flops 75497472 | bytes 1048576 | tf_op jit(solution)/shard_map/pallas_call | solution.py:157
  119.7 0.0 collective-permute-done.6.other_ref
  119.7 2.8 %shard_map.77 = (f32[1,128]{1,0:T(1,128)}, f32[128,1152]{1,0:T(8,128)}) custom-call(f32[1]{0:T(128)S(6)} %copy.17.scale, f32[1]{0:T(128)S(6)} %copy.18.bias, bf16[128,1152]{1,0:T(8,128)(2,1)S(1)} %copy-done, bf16[128,1152]{1,0:T(8,128)(2,1)S(1)} %collective-permute-done.6.other_ref, bf16[256,1152]{1,0:T(8,128)(2,1)} %get-tuple-element.74.units_ref, ...), custom_call_target="tpu_custom_call" | custom-call | flops 75497472 | bytes 1048576 | tf_op jit(solution)/shard_map/pallas_call | solution.py:157
  (1 shorter events, 0.0 us)
Async XLA Ops:
  0.6 53.8 %copy-start.1 = (bf16[128,1152]{1,0:T(8,128)(2,1)S(1)}, bf16[128,1152]{1,0:T(8,128)(2,1)}, u32[]{:S(2)}) copy-start(bf16[128,1152]{1,0:T(8,128)(2,1)} %y_ref.1) | copy-start | bytes 884740
  0.6 53.8 %copy-start = (bf16[128,1152]{1,0:T(8,128)(2,1)S(1)}, bf16[128,1152]{1,0:T(8,128)(2,1)}, u32[]{:S(2)}) copy-start(bf16[128,1152]{1,0:T(8,128)(2,1)} %x_ref.1) | copy-start | bytes 884740
  0.7 53.8 %copy-start.4 = (s32[1,128]{1,0:T(1,128)S(1)}, s32[1,128]{1,0:T(1,128)}, u32[]{:S(2)}) copy-start(s32[1,128]{1,0:T(1,128)} %param.9) | copy-start | bytes 1540
  0.7 36.3 %collective-permute-start.5 = (bf16[128,1152]{1,0:T(8,128)(2,1)}, bf16[128,1152]{1,0:T(8,128)(2,1)}, u32[]{:S(2)}, u32[]{:S(2)}) collective-permute-start(bf16[128,1152]{1,0:T(8,128)(2,1)} %y_ref.1), channel_id=1, source_target_pairs={{0,128},{1,129},{2,130},{3,131},{4,132},{5,133},{6,134},{7,135},{8... | collective-permute-start | bytes 884744 | tf_op jit(solution)/shard_map/ppermute | solution.py:27
  4.3 26.6 %collective-permute-start.8 = (bf16[128,1152]{1,0:T(8,128)(2,1)}, bf16[128,1152]{1,0:T(8,128)(2,1)}, u32[]{:S(2)}, u32[]{:S(2)}) collective-permute-start(bf16[128,1152]{1,0:T(8,128)(2,1)} %x_ref.1), channel_id=1, source_target_pairs={{0,911},{1,896},{2,897},{3,898},{4,899},{5,900},{6,901},{7,902},{8... | collective-permute-start | bytes 884744 | tf_op jit(solution)/shard_map/ppermute | solution.py:27
  22.5 31.9 %collective-permute-start.7 = (bf16[128,1152]{1,0:T(8,128)(2,1)S(1)}, bf16[128,1152]{1,0:T(8,128)(2,1)S(1)}, u32[]{:S(2)}, u32[]{:S(2)}) collective-permute-start(bf16[128,1152]{1,0:T(8,128)(2,1)S(1)} %get-tuple-element.95), channel_id=1, source_target_pairs={{896,0},{912,16},{928,32},{944,48},{960,64},{976,80},{992,96},{100... | collective-permute-start | bytes 884744 | tf_op jit(solution)/shard_map/ppermute | solution.py:41
  24.4 30.0 %collective-permute-start.9 = (bf16[128,1152]{1,0:T(8,128)(2,1)S(1)}, bf16[128,1152]{1,0:T(8,128)(2,1)S(1)}, u32[]{:S(2)}, u32[]{:S(2)}) collective-permute-start(bf16[128,1152]{1,0:T(8,128)(2,1)S(1)} %get-tuple-element.94), channel_id=1, source_target_pairs={{0,32},{16,48},{32,64},{48,80},{64,96},{80,112},{96,0},{112,16},{1... | collective-permute-start | bytes 884744 | tf_op jit(solution)/shard_map/ppermute | solution.py:35
  27.5 26.8 %collective-permute-start.10 = (bf16[128,1152]{1,0:T(8,128)(2,1)S(1)}, bf16[128,1152]{1,0:T(8,128)(2,1)S(1)}, u32[]{:S(2)}, u32[]{:S(2)}) collective-permute-start(bf16[128,1152]{1,0:T(8,128)(2,1)S(1)} %get-tuple-element.93), channel_id=1, source_target_pairs={{0,96},{16,112},{32,0},{48,16},{64,32},{80,48},{96,64},{112,80},{1... | collective-permute-start | bytes 884744 | tf_op jit(solution)/shard_map/ppermute | solution.py:35
  30.9 86.0 %collective-permute-start.11 = (bf16[128,1152]{1,0:T(8,128)(2,1)}, bf16[128,1152]{1,0:T(8,128)(2,1)S(1)}, u32[]{:S(2)}, u32[]{:S(2)}) collective-permute-start(bf16[128,1152]{1,0:T(8,128)(2,1)} %collective-permute-done.8), channel_id=1, source_target_pairs={{0,143},{1,128},{2,129},{3,130},{4,131},{5,132},{6,133},{7,134},{8... | collective-permute-start | bytes 884744 | tf_op jit(solution)/shard_map/ppermute | solution.py:27
  37.0 82.7 %collective-permute-start.6 = (bf16[128,1152]{1,0:T(8,128)(2,1)}, bf16[128,1152]{1,0:T(8,128)(2,1)S(1)}, u32[]{:S(2)}, u32[]{:S(2)}) collective-permute-start(bf16[128,1152]{1,0:T(8,128)(2,1)} %collective-permute-done.5), channel_id=1, source_target_pairs={{0,896},{1,897},{2,898},{3,899},{4,900},{5,901},{6,902},{7,903},{8... | collective-permute-start | bytes 884744 | tf_op jit(solution)/shard_map/ppermute | solution.py:27
  54.4 1.9 %copy-start.2 = (bf16[128,1152]{1,0:T(8,128)(2,1)}, bf16[128,1152]{1,0:T(8,128)(2,1)S(1)}, u32[]{:S(2)}) copy-start(bf16[128,1152]{1,0:T(8,128)(2,1)S(1)} %get-tuple-element.44.rest_1_) | copy-start | bytes 884740 | tf_op jit(solution)/shard_map/cond
  57.4 34.1 %copy-start.3 = (bf16[128,1152]{1,0:T(8,128)(2,1)S(1)}, bf16[128,1152]{1,0:T(8,128)(2,1)}, u32[]{:S(2)}) copy-start(bf16[128,1152]{1,0:T(8,128)(2,1)} %copy-done.2) | copy-start | bytes 884740 | tf_op jit(solution)/shard_map/cond
  57.4 29.8 %collective-permute-start = (bf16[384,1152]{1,0:T(8,128)(2,1)}, bf16[384,1152]{1,0:T(8,128)(2,1)S(1)}, u32[]{:S(2)}, u32[]{:S(2)}) collective-permute-start(bf16[384,1152]{1,0:T(8,128)(2,1)} %pad_maximum_fusion.1), channel_id=1, source_target_pairs={{0,16},{16,0},{32,48},{48,32},{64,80},{80,64},{96,112},{112,96},{1... | collective-permute-start | bytes 2654216 | tf_op jit(solution)/shard_map/cond/branch_1_fun/ppermute | solution.py:45
  63.8 41.3 %collective-permute-start.1 = (bf16[256,1152]{1,0:T(8,128)(2,1)S(1)}, bf16[256,1152]{1,0:T(8,128)(2,1)S(1)}, u32[]{:S(2)}, u32[]{:S(2)}) collective-permute-start(bf16[256,1152]{1,0:T(8,128)(2,1)S(1)} %pad_maximum_fusion.2), channel_id=1, source_target_pairs={{0,64},{16,80},{32,96},{48,112},{64,0},{80,16},{96,32},{112,48},{1... | collective-permute-start | bytes 1769480 | tf_op jit(solution)/shard_map/cond/branch_1_fun/ppermute | solution.py:35
  85.0 20.1 %collective-permute-start.2 = (bf16[128,1152]{1,0:T(8,128)(2,1)S(1)}, bf16[128,1152]{1,0:T(8,128)(2,1)S(1)}, u32[]{:S(2)}, u32[]{:S(2)}) collective-permute-start(bf16[128,1152]{1,0:T(8,128)(2,1)S(1)} %get-tuple-element.85), channel_id=1, source_target_pairs={{0,32},{16,48},{32,64},{48,80},{64,96},{80,112},{96,0},{112,16},{1... | collective-permute-start | bytes 884744 | tf_op jit(solution)/shard_map/cond/branch_1_fun/ppermute | solution.py:35
  87.2 17.9 %collective-permute-start.3 = (bf16[128,1152]{1,0:T(8,128)(2,1)S(1)}, bf16[128,1152]{1,0:T(8,128)(2,1)S(1)}, u32[]{:S(2)}, u32[]{:S(2)}) collective-permute-start(bf16[128,1152]{1,0:T(8,128)(2,1)S(1)} %get-tuple-element.53), channel_id=1, source_target_pairs={{0,96},{16,112},{32,0},{48,16},{64,32},{80,48},{96,64},{112,80},{1... | collective-permute-start | bytes 884744 | tf_op jit(solution)/shard_map/cond/branch_1_fun/ppermute | solution.py:35
  105.2 7.0 %collective-permute-start.4 = (bf16[640,1152]{1,0:T(8,128)(2,1)S(1)}, bf16[640,1152]{1,0:T(8,128)(2,1)S(1)}, u32[]{:S(2)}, u32[]{:S(2)}) collective-permute-start(bf16[640,1152]{1,0:T(8,128)(2,1)S(1)} %pad_maximum_fusion), channel_id=1, source_target_pairs={{0,16},{16,0},{32,48},{48,32},{64,80},{80,64},{96,112},{112,96},{1... | collective-permute-start | bytes 4423688 | tf_op jit(solution)/shard_map/cond/branch_1_fun/ppermute | solution.py:45
